TPU v7x, 32 devices: a whole 2x2x4 slice. The times are simulated.
32 devices in a mesh: depth: 8 (over y, x, core), chan: 4 (over z).
Axes of the slice: x: 2, y: 2, z: 4, core: 2. Of those that a mesh axis runs over, the one named last changes fastest.
Arguments:
- grad_out: bfloat16 [128, 8, 32, 128], P('chan', 'depth'), may hold values from -6 to 6
- volume: bfloat16 [64, 16, 64, 256], P('chan', 'depth'), may hold values from -6 to 6
- weight: bfloat16 [27, 64, 128], replicated, may hold values from -0.15625 to 0.15625
Outputs:
- input_grad: bfloat16 [64, 16, 64, 256], P('chan', 'depth')
- weight_grad: float32 [27, 64, 128], P(None, 'chan', 'depth')
All inputs are finite; a program needn't handle non-finite values.
Results may differ from a plain program's by a relative error of at most 0.001.
Values may be sent and summed in bfloat16 or wider, within the bound.
No kernel may reach another device: no remote copies, remote signals or barrier semaphores. Data moves between devices by JAX's collectives and lax.ppermute only.
A program may use at most 192 MiB of HBM per device.

v0:
```python
import math

import jax
import jax.numpy as jnp
from jax import lax
from jax.experimental import pallas as pl
from jax.experimental.pallas import tpu as pltpu
from jax.sharding import PartitionSpec as P

F32 = jnp.float32
BF16 = jnp.bfloat16
VMEM = pl.BlockSpec(memory_space=pltpu.VMEM)
SMEM = pl.BlockSpec(memory_space=pltpu.SMEM)
LIMIT = 48 * 1024 * 1024


def ring_order(count):
    return [0] + list(range(1, count, 2)) + list(range(2, count, 2))[::-1]


def matmul(left, right):
    return jnp.dot(left, right, preferred_element_type=F32)


def one_hot(rows, cols, source):
    row = lax.broadcasted_iota(jnp.int32, (rows, cols), 0)
    col = lax.broadcasted_iota(jnp.int32, (rows, cols), 1)
    return jnp.where(source(row, col), 1.0, 0.0).astype(BF16)


def swap_rows(major, minor):
    bits = minor.bit_length() - 1
    return one_hot(
        major * minor,
        major * minor,
        lambda row, col: col == (row & (minor - 1)) * major + (row >> bits),
    )


def place_views(plane, views_ref, base):
    chans, rows, cols = plane.shape
    half = cols // 2
    group = 256 // chans
    swap = swap_rows(group, chans)
    split = one_hot(cols, cols, lambda row, col: row == 2 * (col & (half - 1)) + col // half)
    inner = lax.broadcasted_iota(jnp.int32, (group * chans, half), 1) > 0
    for start in range(0, rows, group):
        block = plane[:, start : start + group, :].reshape(chans * group, cols)
        parted = matmul(matmul(swap, block).astype(BF16), split)
        odd = parted[:, half:]
        before = jnp.where(inner, pltpu.roll(odd, 1, 1), 0.0)
        views = [view.astype(BF16) for view in (before, parted[:, :half], odd)]
        for at in range(group):
            row = start + at
            lanes = slice(row // 2 * half, (row // 2 + 1) * half)
            for e in range(3):
                lo = base + (3 * (row % 2) + e) * chans
                views_ref[lo : lo + chans, lanes] = views[e][at * chans : (at + 1) * chans]


def owner_of(seats, slot):
    here = lax.axis_index("chan")
    owner = jnp.int32(seats[0][slot])
    for chip in range(1, len(seats)):
        owner = jnp.where(here == chip, seats[chip][slot], owner)
    return owner


def own_views_kernel(seats, depth, volume_ref, weight_ref, views_ref, taps_ref, odd_ref):
    chans = volume_ref.shape[0]
    channels = weight_ref.shape[2]
    odd_ref[...] = volume_ref[:, 1:]
    place_views(volume_ref.at[:, 0], views_ref, 0)
    place_views(volume_ref.at[:, 1], views_ref, 6 * chans)
    part = channels // len(seats)
    row = lax.broadcasted_iota(jnp.int32, (channels, channels), 0)
    col = lax.broadcasted_iota(jnp.int32, (channels, channels), 1)
    order = jnp.zeros((channels, channels), F32)
    for slot in range(len(seats)):
        moved = (owner_of(seats, slot) - slot) * part
        inside = (col >= slot * part) & (col < (slot + 1) * part)
        order = jnp.where(inside & (row == col + moved), 1.0, order)
    ordered = matmul(weight_ref[...].reshape(27 * chans, channels), order.astype(BF16)).astype(BF16)
    beyond = jnp.where(lax.axis_index("depth") == depth - 1, 0.0, 1.0).astype(BF16)
    zero = jnp.zeros((chans, channels), BF16)
    for k, e in enumerate((1, 2, 0)):
        for b in range(3):
            pick = lambda a: ordered[(9 * a + 3 * b + e) * chans : (9 * a + 3 * b + e + 1) * chans]
            for plane, line in enumerate(((zero, pick(1)), (pick(0) * beyond, pick(2)))):
                lo = ((3 * plane + k) * 3 + b) * chans
                taps_ref[lo : lo + chans, :] = jnp.concatenate(line, axis=1)


def behind_views_kernel(behind_ref, views_ref):
    first = lax.axis_index("depth") == 0

    @pl.when(jnp.logical_not(first))
    def _():
        place_views(behind_ref.at[:, 0], views_ref, 0)

    @pl.when(first)
    def _():
        views_ref[...] = jnp.zeros(views_ref.shape, BF16)


def place_lines(part, out_ref, at, wide_ref):
    outs, _, rows, cols = part.shape
    wide_ref[...] = part[...].reshape(outs * rows, cols).astype(F32)
    for row in range(rows):
        line = wide_ref[pl.ds(row, outs, stride=rows), :].astype(BF16)
        out_ref[at : at + outs, row * cols : (row + 1) * cols] = line


def lines_kernel(*refs):
    *parts, out_ref, wide_ref = refs
    at = 0
    for part in parts:
        place_lines(part, out_ref, at, wide_ref)
        at += part.shape[0]


def weight_kernel(seats, own_ref, behind_ref, near_ref, far_ref, out_ref, grads_ref, terms_ref, placed_ref):
    channels = out_ref.shape[0]
    chans = behind_ref.shape[0] // 6
    cells = own_ref.shape[1]
    cols = grads_ref.shape[1] - cells
    known = near_ref.shape[0]
    grads_ref[:known, :cells] = near_ref[...]
    grads_ref[known:, :cells] = far_ref[...]
    grads_ref[:, cells:] = jnp.zeros((channels, cols), BF16)
    both = jnp.concatenate([grads_ref[:, :cells], grads_ref[:, cols:]], axis=0)
    contract = (((1,), (1,)), ((), ()))
    for a, (ref, at) in enumerate(((behind_ref, 0), (own_ref, 0), (own_ref, 6 * chans))):
        terms = lax.dot_general(ref[at : at + 6 * chans], both, contract, preferred_element_type=F32)
        even, odd = terms[: 3 * chans, :channels], terms[3 * chans :]
        for b, block in enumerate((odd[:, channels:], even, odd[:, :channels])):
            lo = (9 * a + 3 * b) * chans
            terms_ref[lo : lo + 3 * chans, :] = block
    terms_ref[27 * chans :, :] = jnp.zeros((5 * chans, channels), F32)
    for c in range(chans):
        placed_ref[32 * c : 32 * c + 32, :] = terms_ref[pl.ds(c, 32, stride=chans), :]
    turned = placed_ref[...].T
    part = channels // len(seats)
    for slot in range(len(seats)):
        place = pl.multiple_of(owner_of(seats, slot) * part, part)
        out_ref[pl.ds(place, part), :] = turned[slot * part : (slot + 1) * part]


def input_kernel(taps_ref, next_near_ref, next_far_ref, near_ref, far_ref, out_ref, cells_ref, lines_ref):
    chans, _, rows, cols = out_ref.shape
    half = cols // 2
    grid_cells = half * rows // 2
    grads = [ref[...] for ref in (next_near_ref, next_far_ref, near_ref, far_ref)]
    cells_ref[:, :grid_cells] = matmul(taps_ref[...], jnp.concatenate(grads, axis=0))
    cells_ref[:, grid_cells:] = jnp.zeros((cells_ref.shape[0], half), F32)
    group = 256 // chans
    weave = one_hot(cols, cols, lambda row, col: col == 2 * (row & (half - 1)) + row // half)
    inner = lax.broadcasted_iota(jnp.int32, (chans, half), 1) < half - 1

    def cells(plane, kind, b, r):
        lo = ((3 * plane + kind) * 3 + b) * chans
        return cells_ref[lo : lo + chans, r * half : (r + 1) * half]

    for plane in range(2):
        for start in range(0, rows, group):
            pieces = []
            for row in range(start, start + group):
                r = row // 2
                if row % 2 == 0:
                    even, odd, next_odd = [cells(plane, kind, 1, r) for kind in range(3)]
                else:
                    even, odd, next_odd = [
                        cells(plane, kind, 0, r + 1) + cells(plane, kind, 2, r) for kind in range(3)
                    ]
                odd = odd + jnp.where(inner, pltpu.roll(next_odd, half - 1, 1), 0.0)
                pieces.append(jnp.concatenate([even, odd], axis=1).astype(BF16))
            woven = matmul(jnp.concatenate(pieces, axis=0), weave)
            for side in range(2):
                lanes = slice(side * half, (side + 1) * half)
                lines_ref[side] = woven[:, lanes]
                for c in range(chans):
                    line = lines_ref[side, pl.ds(c, group, stride=chans), :].astype(BF16)
                    out_ref[c, plane, start : start + group, lanes] = line


def total_kernel(scale, terms_ref, out_ref):
    chans, outs, taps = out_ref.shape
    total = terms_ref[0]
    for source in range(1, terms_ref.shape[0]):
        total = total + terms_ref[source]
    total = total * scale
    for c in range(chans):
        out_ref[c] = total[:, 32 * c : 32 * c + taps]


def from_behind(shard, axis, by):
    count = lax.axis_size(axis)
    pairs = [(i, i + by) for i in range(count) if 0 <= i + by < count]
    return lax.ppermute(shard, axis, pairs)


def upsample(stacked, axis, extended):
    tap_zero, tap_one, tap_two = (stacked[0], stacked[1], stacked[2])
    coord_axis = axis - 1
    length = tap_zero.shape[coord_axis]
    if extended:
        outer = length - 1
        even_cells = lax.slice_in_dim(tap_one, 0, outer, axis=coord_axis)
        odd_cells = lax.slice_in_dim(tap_zero, 1, length, axis=coord_axis) + lax.slice_in_dim(
            tap_two, 0, outer, axis=coord_axis
        )
    else:
        outer = length
        shifted = lax.slice_in_dim(tap_zero, 1, length, axis=coord_axis)
        shifted = jnp.concatenate(
            [shifted, jnp.zeros_like(lax.slice_in_dim(tap_zero, 0, 1, axis=coord_axis))],
            axis=coord_axis,
        )
        even_cells = tap_one
        odd_cells = shifted + tap_two
    paired = jnp.stack([even_cells, odd_cells], axis=coord_axis + 1)
    new_shape = list(even_cells.shape)
    new_shape[coord_axis] = 2 * outer
    return paired.reshape(new_shape)


def phase_grads(weight_rows, grads_ext):
    local_in = weight_rows.shape[0] // 27
    channels_out, planes, rows, cols = grads_ext.shape
    taps_out = jnp.dot(
        weight_rows, grads_ext.reshape(channels_out, -1), preferred_element_type=jnp.float32
    )
    taps_out = taps_out.reshape(3, 3, 3, local_in, planes, rows, cols)
    along_w = upsample(jnp.moveaxis(taps_out, 2, 0), 6, False)
    along_h = upsample(jnp.moveaxis(along_w, 1, 0), 4, False)
    return upsample(along_h, 2, True)


def weight_terms(inputs, grads_ext):
    row_extra = 0
    weight_cube = lax.conv_general_dilated(
        inputs[None],
        grads_ext[:, None],
        (1, 1, 1),
        ((1, 2), (1, row_extra), (1, 0)),
        rhs_dilation=(2, 2, 2),
        dimension_numbers=("CNDHW", "OIDHW", "NCDHW"),
        preferred_element_type=jnp.float32,
    )
    return jnp.transpose(weight_cube, (2, 3, 4, 0, 1)).reshape(
        27, weight_cube.shape[0], weight_cube.shape[1]
    )


def plain_shards(grad_out, volume, weight):
    plane_next = from_behind(grad_out, "depth", -1)
    grads_ext = jnp.concatenate([grad_out, plane_next], axis=1)
    channels_out = weight.shape[2]
    local_in = volume.shape[0]
    every_channel = lax.all_gather(grads_ext, "chan", axis=0, tiled=True)
    own_weight = lax.dynamic_slice_in_dim(weight, lax.axis_index("chan") * local_in, local_in, 1)
    input_part = phase_grads(own_weight.reshape(27 * local_in, channels_out), every_channel)
    weight_part = weight_terms(volume, every_channel)
    input_grad = input_part.astype(jnp.bfloat16)
    summed = lax.psum_scatter(weight_part, "depth", scatter_dimension=2, tiled=True)
    cell_count = grad_out.shape[1] * lax.axis_size("depth") * grad_out.shape[2] * grad_out.shape[3]
    return (input_grad, summed * (1.0 / math.sqrt(cell_count)))


def call(kernel, out_shape, *args, specs=None, scratch=(), cost=None):
    flops, moved = cost
    return pl.pallas_call(
        kernel,
        out_shape=out_shape,
        in_specs=specs or [VMEM] * len(args),
        out_specs=jax.tree.map(lambda _: VMEM, out_shape),
        scratch_shapes=scratch,
        compiler_params=pltpu.CompilerParams(vmem_limit_bytes=LIMIT),
        cost_estimate=pl.CostEstimate(flops=flops, bytes_accessed=moved, transcendentals=0),
    )(*args)


def shards(grad_out, volume, weight):
    count = lax.axis_size("chan")
    depth = lax.axis_size("depth")
    own_outs, _, rows, cols = grad_out.shape
    chans = volume.shape[0]
    channels = weight.shape[2]
    cells = rows * cols
    order = ring_order(count)
    ahead = [(order[i], order[(i + 1) % count]) for i in range(count)]
    back = [(b, a) for a, b in ahead]
    farther = [(i, (i + 1) % depth) for i in range(depth)]
    nearer = [(b, a) for a, b in farther]
    own_weight = lax.dynamic_slice_in_dim(weight, lax.axis_index("chan") * local_in, local_in, 1)
    input_part = phase_grads(own_weight.reshape(27 * local_in, channels_out), every_channel)
    weight_part = weight_terms(volume, every_channel)
    input_grad = input_part.astype(jnp.bfloat16)
    summed = lax.psum_scatter(weight_part, "depth", scatter_dimension=2, tiled=True)
    cell_count = grad_out.shape[1] * lax.axis_size("depth") * grad_out.shape[2] * grad_out.shape[3]
    return (input_grad, summed * (1.0 / math.sqrt(cell_count)))


def call(kernel, out_shape, *args, specs=None, scratch=(), cost=None):
    flops, moved = cost
    return pl.pallas_call(
        kernel,
        out_shape=out_shape,
        in_specs=specs or [VMEM] * len(args),
        out_specs=jax.tree.map(lambda _: VMEM, out_shape),
        scratch_shapes=scratch,
        compiler_params=pltpu.CompilerParams(vmem_limit_bytes=LIMIT),
        cost_estimate=pl.CostEstimate(flops=flops, bytes_accessed=moved, transcendentals=0),
    )(*args)


def shards(grad_out, volume, weight):
    count = lax.axis_size("chan")
    depth = lax.axis_size("depth")
    own_outs, _, rows, cols = grad_out.shape
    chans = volume.shape[0]
    channels = weight.shape[2]
    cells = rows * cols
    order = ring_order(count)
    ahead = [(order[i], order[(i + 1) % count]) for i in range(count)]
    back = [(b, a) for a, b in ahead]
    farther = [(i, (i + 1) % depth) for i in range(depth)]
    nearer = [(b, a) for a, b in farther]
    own_weight = lax.dynamic_slice_in_dim(weight, lax.axis_index("chan") * local_in, local_in, 1)
    input_part = phase_grads(own_weight.reshape(27 * local_in, channels_out), every_channel)
    weight_part = weight_terms(volume, every_channel)
    input_grad = input_part.astype(jnp.bfloat16)
    summed = lax.psum_scatter(weight_part, "depth", scatter_dimension=2, tiled=True)
    cell_count = grad_out.shape[1] * lax.axis_size("depth") * grad_out.shape[2] * grad_out.shape[3]
    return (input_grad, summed * (1.0 / math.sqrt(cell_count)))


def call(kernel, out_shape, *args, specs=None, scratch=(), cost=None):
    flops, moved = cost
    return pl.pallas_call(
        kernel,
        out_shape=out_shape,
        in_specs=specs or [VMEM] * len(args),
        out_specs=jax.tree.map(lambda _: VMEM, out_shape),
        scratch_shapes=scratch,
        compiler_params=pltpu.CompilerParams(vmem_limit_bytes=LIMIT),
        cost_estimate=pl.CostEstimate(flops=flops, bytes_accessed=moved, transcendentals=0),
    )(*args)


def shards(grad_out, volume, weight):
    count = lax.axis_size("chan")
    depth = lax.axis_size("depth")
    own_outs, _, rows, cols = grad_out.shape
    chans = volume.shape[0]
    channels = weight.shape[2]
    cells = rows * cols
    order = ring_order(count)
    ahead = [(order[i], order[(i + 1) % count]) for i in range(count)]
    back = [(b, a) for a, b in ahead]
    farther = [(i, (i + 1) % depth) for i in range(depth)]
    nearer = [(b, a) for a, b in farther]
    own_weight = lax.dynamic_slice_in_dim(weight, lax.axis_index("chan") * local_in, local_in, 1)
    input_part = phase_grads(own_weight.reshape(27 * local_in, channels_out), every_channel)
    weight_part = weight_terms(volume, every_channel)
    input_grad = input_part.astype(jnp.bfloat16)
    summed = lax.psum_scatter(weight_part, "depth", scatter_dimension=2, tiled=True)
    cell_count = grad_out.shape[1] * lax.axis_size("depth") * grad_out.shape[2] * grad_out.shape[3]
    return (input_grad, summed * (1.0 / math.sqrt(cell_count)))


def call(kernel, out_shape, *args, specs=None, scratch=(), cost=None):
    flops, moved = cost
    return pl.pallas_call(
        kernel,
        out_shape=out_shape,
        in_specs=specs or [VMEM] * len(args),
        out_specs=jax.tree.map(lambda _: VMEM, out_shape),
        scratch_shapes=scratch,
        compiler_params=pltpu.CompilerParams(vmem_limit_bytes=LIMIT),
        cost_estimate=pl.CostEstimate(flops=flops, bytes_accessed=moved, transcendentals=0),
    )(*args)


def shards(grad_out, volume, weight):
    count = lax.axis_size("chan")
    depth = lax.axis_size("depth")
    own_outs, _, rows, cols = grad_out.shape
    chans = volume.shape[0]
    channels = weight.shape[2]
    cells = rows * cols
    order = ring_order(count)
    ahead = [(order[i], order[(i + 1) % count]) for i in range(count)]
    back = [(b, a) for a, b in ahead]
    farther = [(i, (i + 1) % depth) for i in range(depth)]
    nearer = [(b, a) for a, b in farther]
    shifts = [0]

    near = []
    up = down = grad_out
    for step in range(1, (count - 1) // 2 + 1):
        up = lax.ppermute(up, "chan", ahead)
        down = lax.ppermute(down, "chan", back)
        near += [up, down]
        shifts += [-step, step]
    last = lax.ppermute(up, "chan", ahead)
    shifts += [count // 2]
    seats = [[order[(order.index(chip) + s) % count] for s in shifts] for chip in range(count)]

    shifts = [0, -1]
    for step in range(1, count // 2):
        shifts += [step, -step - 1]
    seats = [[order[(order.index(chip) + s) % count] for s in shifts] for chip in range(count)]

    own_weight = lax.dynamic_slice_in_dim(weight, lax.axis_index("chan") * chans, chans, 1)
    views, taps, odd = call(
        lambda *refs: own_views_kernel(seats, depth, *refs),
        (
            jax.ShapeDtypeStruct((12 * chans, cells), BF16),
            jax.ShapeDtypeStruct((18 * chans, 2 * channels), BF16),
            jax.ShapeDtypeStruct((chans, 1, 2 * rows, 2 * cols), BF16),
        ),
        volume,
        own_weight,
        cost=(2 * 2 * 2 * cells * chans * 8 * cols, 4 << 20),
    )
    first = lax.ppermute(grad_out, "chan", ahead)
    first, views = lax.optimization_barrier((first, views))
    up, down, far = first, grad_out, []
    for step in range(1, count // 2):
        down = lax.ppermute(down, "chan", back)
        up = lax.ppermute(up, "chan", ahead)
        far += [down, up]
    lines = lambda *parts: call(
        lines_kernel,
        jax.ShapeDtypeStruct((len(parts) * own_outs, cells), BF16),
        *parts,
        scratch=(pltpu.VMEM((own_outs * rows, cols), F32),),
        cost=(1 << 20, 2 << 20),
    )
    near_lines = lines(grad_out, first)
    far[0], odd = lax.optimization_barrier((far[0], odd))
    next_near_lines = lax.ppermute(near_lines, "depth", nearer)
    behind = lax.ppermute(odd, "depth", farther)
    behind_views = call(
        behind_views_kernel,
        jax.ShapeDtypeStruct((6 * chans, cells), BF16),
        behind,
        cost=(2 * 2 * cells * chans * 8 * cols, 2 << 20),
    )
    far_lines = lines(*far)
    next_far_lines = lax.ppermute(far_lines, "depth", nearer)
    partial = call(
        lambda *refs: weight_kernel(seats, *refs),
        jax.ShapeDtypeStruct((channels, 32 * chans), F32),
        views,
        behind_views,
        near_lines,
        far_lines,
        scratch=(
            pltpu.VMEM((channels, cells + cols), BF16),
            pltpu.VMEM((32 * chans, channels), F32),
            pltpu.VMEM((32 * chans, channels), F32),
        ),
        cost=(2 * 27 * chans * channels * cells, 8 << 20),
    )
    terms = lax.all_to_all(partial, "depth", split_axis=0, concat_axis=0, tiled=True)
    input_grad = call(
        input_kernel,
        jax.ShapeDtypeStruct(volume.shape, BF16),
        taps,
        next_near_lines,
        next_far_lines,
        near_lines,
        far_lines,
        scratch=(
            pltpu.VMEM((18 * chans, cells + cols), F32),
            pltpu.VMEM((2, 256, cols), F32),
        ),
        cost=(2 * 18 * chans * 2 * channels * cells, 8 << 20),
    )
    terms, input_grad = lax.optimization_barrier((terms, input_grad))
    scale = 1.0 / math.sqrt(depth * cells)
    outs = channels // depth
    weight_grad = call(
        lambda *refs: total_kernel(scale, *refs),
        jax.ShapeDtypeStruct((chans, outs, 27), F32),
        terms.reshape(depth, outs, 32 * chans),
        cost=(1 << 20, 1 << 20),
    )
    return input_grad, jnp.transpose(weight_grad, (2, 0, 1))


def solution(mesh):
    in_specs = (P("chan", "depth", None, None), P("chan", "depth", None, None), P())
    out_specs = (P("chan", "depth", None, None), P(None, "chan", "depth"))
    ring = mesh.shape["chan"]

    def either(grad_out, volume, weight):
        fits = (
            grad_out.shape[0] % 16 == 0
            and volume.shape[0] == 16
            and grad_out.shape[1] == 1
            and ring % 2 == 0
            and ring >= 4
        )
        return (shards if fits else plain_shards)(grad_out, volume, weight)

    return jax.shard_map(either, mesh=mesh, in_specs=in_specs, out_specs=out_specs, check_vma=False)
```

profile of v0, /device:TPU:0, one launch (start us, length us, event | category | flops | bytes accessed | tf_op | source)
XLA Modules:
  0.0 46.3 jit_solution(4591422502026742698)
XLA Ops:
  0.6 0.0 copy-start
  0.6 0.0 copy-start.1
  0.7 3.1 %collective-permute-start = (bf16[32,1,32,128]{3,2,1,0:T(8,128)(2,1)}, bf16[32,1,32,128]{3,2,1,0:T(8,128)(2,1)S(1)}, u32[]{:S(2)}, u32[]{:S(2)}) collective-permute-start(bf16[32,1,32,128]{3,2,1,0:T(8,128)(2,1)} %refs_0_.3), channel_id=1, source_target_pairs={{0,1},{1,3},{3,2},{2,0},{4,5},{5,7},{7,6},{6,4},{8,9},{9,11},{11,1... | collective-permute-start | bytes 786440 | tf_op jit(solution)/shard_map/ppermute | solution.py:427
  3.7 1.1 %collective-permute-start.1 = (bf16[32,1,32,128]{3,2,1,0:T(8,128)(2,1)}, bf16[32,1,32,128]{3,2,1,0:T(8,128)(2,1)S(1)}, u32[]{:S(2)}, u32[]{:S(2)}) collective-permute-start(bf16[32,1,32,128]{3,2,1,0:T(8,128)(2,1)} %refs_0_.3), channel_id=1, source_target_pairs={{1,0},{3,1},{2,3},{0,2},{5,4},{7,5},{6,7},{4,6},{9,8},{11,9},{10,1... | collective-permute-start | bytes 786440 | tf_op jit(solution)/shard_map/ppermute | solution.py:431
  4.8 0.0 copy-done
  4.8 0.0 copy-start.2
  4.8 1.2 %copy-done.2 = bf16[16,2,64,256]{3,2,1,0:T(8,128)(2,1)S(1)} copy-done((bf16[16,2,64,256]{3,2,1,0:T(8,128)(2,1)S(1)}, bf16[16,2,64,256]{3,2,1,0:T(8,128)(2,1)}, u32[]{:S(2)}) %copy-start.2) | copy-done | bytes 1048600
  6.1 0.9 %shard_map.50 = (bf16[192,4096]{1,0:T(8,128)(2,1)S(1)}, bf16[288,256]{1,0:T(8,128)(2,1)S(1)}, bf16[16,1,64,256]{3,2,1,0:T(8,128)(2,1)S(1)}) custom-call(bf16[16,2,64,256]{3,2,1,0:T(8,128)(2,1)S(1)} %copy-done.2, bf16[27,16,128]{2,1,0:T(8,128)(2,1)S(1)} %constant_dynamic-slice_fusion.refs_1_), custom_call_target="tpu_custom_call" | custom-call | flops 536870912 | bytes 4194304 | tf_op jit(solution)/shard_map/pallas_call | solution.py:374
  7.0 4.4 %collective-permute-done.refs_1_ = bf16[32,1,32,128]{3,2,1,0:T(8,128)(2,1)S(1)} collective-permute-done((bf16[32,1,32,128]{3,2,1,0:T(8,128)(2,1)}, bf16[32,1,32,128]{3,2,1,0:T(8,128)(2,1)S(1)}, u32[]{:S(2)}, u32[]{:S(2)}) %collective-permute-start) | collective-permute-done | bytes 262176 | tf_op jit(solution)/shard_map/ppermute | solution.py:427
  11.4 7.4 %collective-permute-start.3 = (bf16[32,1,32,128]{3,2,1,0:T(8,128)(2,1)S(1)}, bf16[32,1,32,128]{3,2,1,0:T(8,128)(2,1)S(1)}, u32[]{:S(2)}, u32[]{:S(2)}) collective-permute-start(bf16[32,1,32,128]{3,2,1,0:T(8,128)(2,1)S(1)} %collective-permute-done.refs_1_), channel_id=1, source_target_pairs={{0,1},{1,3},{3,2},{2,0},{4,5},{5,7},{7,6},{6,4},{8,9},{9,11},{11,1... | collective-permute-start | bytes 786440 | tf_op jit(solution)/shard_map/ppermute | solution.py:432
  18.8 0.0 collective-permute-done.1.refs_0_
  18.8 0.0 collective-permute-start.2
  18.8 0.0 copy-done.1
  18.8 0.7 %shard_map.52.refs_2_.near_ref = bf16[64,4096]{1,0:T(8,128)(2,1)S(1)} custom-call(bf16[32,1,32,128]{3,2,1,0:T(8,128)(2,1)S(1)} %copy-done.1, bf16[32,1,32,128]{3,2,1,0:T(8,128)(2,1)S(1)} %collective-permute-done.refs_1_), custom_call_target="tpu_custom_call" | custom-call | flops 1048576 | bytes 2097152 | tf_op jit(solution)/shard_map/pallas_call | solution.py:374
  19.5 2.7 %collective-permute-start.4 = (bf16[64,4096]{1,0:T(8,128)(2,1)S(1)}, bf16[64,4096]{1,0:T(8,128)(2,1)S(1)}, u32[]{:S(2)}, u32[]{:S(2)}) collective-permute-start(bf16[64,4096]{1,0:T(8,128)(2,1)S(1)} %shard_map.52.refs_2_.near_ref), channel_id=1, source_target_pairs={{4,0},{8,4},{12,8},{16,12},{20,16},{24,20},{28,24},{0,28},{5,1},{9... | collective-permute-start | bytes 1572872 | tf_op jit(solution)/shard_map/ppermute | solution.py:443
  22.1 1.5 %collective-permute-done.3.refs_1_ = bf16[32,1,32,128]{3,2,1,0:T(8,128)(2,1)S(1)} collective-permute-done((bf16[32,1,32,128]{3,2,1,0:T(8,128)(2,1)S(1)}, bf16[32,1,32,128]{3,2,1,0:T(8,128)(2,1)S(1)}, u32[]{:S(2)}, u32[]{:S(2)}) %collective-permute-start.3) | collective-permute-done | bytes 262176 | tf_op jit(solution)/shard_map/ppermute | solution.py:432
  23.7 0.7 %shard_map.53.refs_3_.far_ref = bf16[64,4096]{1,0:T(8,128)(2,1)S(1)} custom-call(bf16[32,1,32,128]{3,2,1,0:T(8,128)(2,1)S(1)} %collective-permute-done.1.refs_0_, bf16[32,1,32,128]{3,2,1,0:T(8,128)(2,1)S(1)} %collective-permute-done.3.refs_1_), custom_call_target="tpu_custom_call" | custom-call | flops 1048576 | bytes 2097152 | tf_op jit(solution)/shard_map/pallas_call | solution.py:374
  24.3 2.1 %collective-permute-start.5 = (bf16[64,4096]{1,0:T(8,128)(2,1)S(1)}, bf16[64,4096]{1,0:T(8,128)(2,1)S(1)}, u32[]{:S(2)}, u32[]{:S(2)}) collective-permute-start(bf16[64,4096]{1,0:T(8,128)(2,1)S(1)} %shard_map.53.refs_3_.far_ref), channel_id=1, source_target_pairs={{4,0},{8,4},{12,8},{16,12},{20,16},{24,20},{28,24},{0,28},{5,1},{9... | collective-permute-start | bytes 1572872 | tf_op jit(solution)/shard_map/ppermute | solution.py:452
  26.5 4.8 %collective-permute-done.2.behind_ref = bf16[16,1,64,256]{3,2,1,0:T(8,128)(2,1)S(1)} collective-permute-done((bf16[16,1,64,256]{3,2,1,0:T(8,128)(2,1)S(1)}, bf16[16,1,64,256]{3,2,1,0:T(8,128)(2,1)S(1)}, u32[]{:S(2)}, u32[]{:S(2)}) %collective-permute-start.2) | collective-permute-done | bytes 524320 | tf_op jit(solution)/shard_map/ppermute | solution.py:444
  31.2 0.1 shard_map.51.refs_1_
  31.3 2.9 %shard_map.54 = f32[128,512]{1,0:T(8,128)} custom-call(bf16[192,4096]{1,0:T(8,128)(2,1)S(1)} %get-tuple-element.12.refs_0_, bf16[96,4096]{1,0:T(8,128)(2,1)S(1)} %shard_map.51.refs_1_, bf16[64,4096]{1,0:T(8,128)(2,1)S(1)} %shard_map.52.refs_2_.near_ref, bf16[64,4096]{1,0:T(8,128)(2,1)S(1)} %shard_map.53.refs_3_.far_ref), custom_call_target="tpu_custom_call" | custom-call | flops 452984832 | bytes 8388608 | tf_op jit(solution)/shard_map/pallas_call | solution.py:374
  34.2 4.4 %all-to-all-start = ((f32[8,16,512]{2,1,0:T(8,128)}), f32[8,16,512]{2,1,0:T(8,128)S(1)}, u32[]{:S(2)}, u32[]{:S(2)}) async-start(f32[8,16,512]{2,1,0:T(8,128)} %bitcast), calls=%async_computation | async-start | bytes 524288 | tf_op jit(solution)/shard_map/all_to_all | solution.py:467
  38.6 0.0 collective-permute-done.4.next_near_ref
  38.6 0.0 collective-permute-done.5.next_far_ref
  38.6 2.9 %shard_map.55 = bf16[16,2,64,256]{3,2,1,0:T(8,128)(2,1)} custom-call(bf16[288,256]{1,0:T(8,128)(2,1)S(1)} %get-tuple-element.17.taps_ref, bf16[64,4096]{1,0:T(8,128)(2,1)S(1)} %collective-permute-done.4.next_near_ref, bf16[64,4096]{1,0:T(8,128)(2,1)S(1)} %collective-permute-done.5.next_far_ref, bf16[64,4096]{1,0:T(8,128)(2,1)S(1)} %shard_map.52.refs_2_.near_ref, ...), custom_call_target="tpu_custom_call" | custom-call | flops 603979776 | bytes 8388608 | tf_op jit(solution)/shard_map/pallas_call | solution.py:374
  41.5 4.0 %all-to-all-done = f32[8,16,512]{2,1,0:T(8,128)S(1)} async-done(((f32[8,16,512]{2,1,0:T(8,128)}), f32[8,16,512]{2,1,0:T(8,128)S(1)}, u32[]{:S(2)}, u32[]{:S(2)}) %all-to-all-start) | async-done | bytes 262176 | tf_op jit(solution)/shard_map/all_to_all | solution.py:467
  45.5 0.8 %shard_map.56 = f32[16,16,27]{2,1,0:T(8,128)} custom-call(f32[8,16,512]{2,1,0:T(8,128)S(1)} %all-to-all-done), custom_call_target="tpu_custom_call" | custom-call | flops 1048576 | bytes 1048576 | tf_op jit(solution)/shard_map/pallas_call | solution.py:374
  (1 shorter events, 0.0 us)
Async XLA Ops:
  0.6 4.2 %copy-start = (bf16[27,64,128]{2,1,0:T(8,128)(2,1)S(1)}, bf16[27,64,128]{2,1,0:T(8,128)(2,1)}, u32[]{:S(2)}) copy-start(bf16[27,64,128]{2,1,0:T(8,128)(2,1)} %param.5) | copy-start | bytes 1327108
  0.6 18.1 %copy-start.1 = (bf16[32,1,32,128]{3,2,1,0:T(8,128)(2,1)S(1)}, bf16[32,1,32,128]{3,2,1,0:T(8,128)(2,1)}, u32[]{:S(2)}) copy-start(bf16[32,1,32,128]{3,2,1,0:T(8,128)(2,1)} %refs_0_.3) | copy-start | bytes 786436
  0.7 10.7 %collective-permute-start = (bf16[32,1,32,128]{3,2,1,0:T(8,128)(2,1)}, bf16[32,1,32,128]{3,2,1,0:T(8,128)(2,1)S(1)}, u32[]{:S(2)}, u32[]{:S(2)}) collective-permute-start(bf16[32,1,32,128]{3,2,1,0:T(8,128)(2,1)} %refs_0_.3), channel_id=1, source_target_pairs={{0,1},{1,3},{3,2},{2,0},{4,5},{5,7},{7,6},{6,4},{8,9},{9,11},{11,1... | collective-permute-start | bytes 786440 | tf_op jit(solution)/shard_map/ppermute | solution.py:427
  3.7 15.0 %collective-permute-start.1 = (bf16[32,1,32,128]{3,2,1,0:T(8,128)(2,1)}, bf16[32,1,32,128]{3,2,1,0:T(8,128)(2,1)S(1)}, u32[]{:S(2)}, u32[]{:S(2)}) collective-permute-start(bf16[32,1,32,128]{3,2,1,0:T(8,128)(2,1)} %refs_0_.3), channel_id=1, source_target_pairs={{1,0},{3,1},{2,3},{0,2},{5,4},{7,5},{6,7},{4,6},{9,8},{11,9},{10,1... | collective-permute-start | bytes 786440 | tf_op jit(solution)/shard_map/ppermute | solution.py:431
  4.8 1.2 %copy-start.2 = (bf16[16,2,64,256]{3,2,1,0:T(8,128)(2,1)S(1)}, bf16[16,2,64,256]{3,2,1,0:T(8,128)(2,1)}, u32[]{:S(2)}) copy-start(bf16[16,2,64,256]{3,2,1,0:T(8,128)(2,1)} %refs_0_.2) | copy-start | bytes 3145732
  11.4 12.3 %collective-permute-start.3 = (bf16[32,1,32,128]{3,2,1,0:T(8,128)(2,1)S(1)}, bf16[32,1,32,128]{3,2,1,0:T(8,128)(2,1)S(1)}, u32[]{:S(2)}, u32[]{:S(2)}) collective-permute-start(bf16[32,1,32,128]{3,2,1,0:T(8,128)(2,1)S(1)} %collective-permute-done.refs_1_), channel_id=1, source_target_pairs={{0,1},{1,3},{3,2},{2,0},{4,5},{5,7},{7,6},{6,4},{8,9},{9,11},{11,1... | collective-permute-start | bytes 786440 | tf_op jit(solution)/shard_map/ppermute | solution.py:432
  18.8 12.5 %collective-permute-start.2 = (bf16[16,1,64,256]{3,2,1,0:T(8,128)(2,1)S(1)}, bf16[16,1,64,256]{3,2,1,0:T(8,128)(2,1)S(1)}, u32[]{:S(2)}, u32[]{:S(2)}) collective-permute-start(bf16[16,1,64,256]{3,2,1,0:T(8,128)(2,1)S(1)} %get-tuple-element.14), channel_id=1, source_target_pairs={{0,4},{4,8},{8,12},{12,16},{16,20},{20,24},{24,28},{28,0},{1,5},{5... | collective-permute-start | bytes 1572872 | tf_op jit(solution)/shard_map/ppermute | solution.py:444
  19.5 19.1 %collective-permute-start.4 = (bf16[64,4096]{1,0:T(8,128)(2,1)S(1)}, bf16[64,4096]{1,0:T(8,128)(2,1)S(1)}, u32[]{:S(2)}, u32[]{:S(2)}) collective-permute-start(bf16[64,4096]{1,0:T(8,128)(2,1)S(1)} %shard_map.52.refs_2_.near_ref), channel_id=1, source_target_pairs={{4,0},{8,4},{12,8},{16,12},{20,16},{24,20},{28,24},{0,28},{5,1},{9... | collective-permute-start | bytes 1572872 | tf_op jit(solution)/shard_map/ppermute | solution.py:443
  24.3 14.2 %collective-permute-start.5 = (bf16[64,4096]{1,0:T(8,128)(2,1)S(1)}, bf16[64,4096]{1,0:T(8,128)(2,1)S(1)}, u32[]{:S(2)}, u32[]{:S(2)}) collective-permute-start(bf16[64,4096]{1,0:T(8,128)(2,1)S(1)} %shard_map.53.refs_3_.far_ref), channel_id=1, source_target_pairs={{4,0},{8,4},{12,8},{16,12},{20,16},{24,20},{28,24},{0,28},{5,1},{9... | collective-permute-start | bytes 1572872 | tf_op jit(solution)/shard_map/ppermute | solution.py:452
  34.2 11.3 %all-to-all-start = ((f32[8,16,512]{2,1,0:T(8,128)}), f32[8,16,512]{2,1,0:T(8,128)S(1)}, u32[]{:S(2)}, u32[]{:S(2)}) async-start(f32[8,16,512]{2,1,0:T(8,128)} %bitcast), calls=%async_computation | async-start | bytes 524288 | tf_op jit(solution)/shard_map/all_to_all | solution.py:467
where the time goes:
time: 46.8 us; the launch traced here: 46.3 us
  starting transfers between devices  20.7 us (44%)
  waiting for transfers between devices  14.7 us (31%)
  Pallas kernels  8.89 us (19%)
  local copies, waits for them, and re-layouts  1.25 us (3%)
  between operations  0.7 us (1%)
    pallas_call x7, Pallas kernels, call(): pl.pallas_call(kernel, out_shape=out_shape, in_specs=specs or [VMEM] * le...  8.89 us
    ppermute x1, starting transfers between devices, shards(): up = lax.ppermute(up, 'chan', ahead)  7.4 us
    ppermute x1, waiting for transfers between devices, shards(): behind = lax.ppermute(odd, 'depth', farther)  4.78 us
    all_to_all x1, starting transfers between devices, shards(): lax.all_to_all(partial, 'depth', split_axis=0, concat_axis=0, tiled=True)  4.37 us
    ppermute x1, waiting for transfers between devices, shards(): first = lax.ppermute(grad_out, 'chan', ahead)  4.37 us
    all_to_all x1, waiting for transfers between devices, shards(): lax.all_to_all(partial, 'depth', split_axis=0, concat_axis=0, tiled=True)  4.01 us
    ppermute x1, starting transfers between devices, shards(): first = lax.ppermute(grad_out, 'chan', ahead)  3.08 us
    ppermute x1, starting transfers between devices, shards(): next_near_lines = lax.ppermute(near_lines, 'depth', nearer)  2.69 us
  transfers between devices with their start and end apart: 7, of which 4 were waited for; matrix products, arithmetic and copies ran while one was open for 0% of the time, Pallas kernels for 18%

commit v1 on v0

--- a/solution.py
+++ b/solution.py
@@ -119,8 +119,10 @@
         at += part.shape[0]
 
 
-def weight_kernel(seats, own_ref, behind_ref, near_ref, far_ref, out_ref, grads_ref, terms_ref, placed_ref):
-    channels = out_ref.shape[0]
+def weight_kernel(
+    seats, outs, own_ref, behind_ref, near_ref, far_ref, keep_ref, send_ref, grads_ref, terms_ref, placed_ref
+):
+    channels = grads_ref.shape[0]
     chans = behind_ref.shape[0] // 6
     cells = own_ref.shape[1]
     cols = grads_ref.shape[1] - cells
@@ -141,9 +143,23 @@
         placed_ref[32 * c : 32 * c + 32, :] = terms_ref[pl.ds(c, 32, stride=chans), :]
     turned = placed_ref[...].T
     part = channels // len(seats)
+    odd_core = lax.axis_index("depth") % 2 == 1
     for slot in range(len(seats)):
-        place = pl.multiple_of(owner_of(seats, slot) * part, part)
-        out_ref[pl.ds(place, part), :] = turned[slot * part : (slot + 1) * part]
+        start = owner_of(seats, slot) * (part // 2)
+        for at in range(0, part // 2, outs):
+            lo = slot * part + 2 * at
+            even, odd = turned[lo : lo + outs], turned[lo + outs : lo + 2 * outs]
+            place = pl.ds(pl.multiple_of(start + at, outs), outs)
+            keep_ref[place, :] = jnp.where(odd_core, odd, even)
+            send_ref[place, :] = jnp.where(odd_core, even, odd)
+
+
+def pair_kernel(keep_ref, other_ref, *out_refs):
+    chip = lax.axis_index("depth") // 2
+    outs = out_refs[0].shape[0]
+    for k, out_ref in enumerate(out_refs):
+        place = pl.ds(pl.multiple_of((chip ^ k) * outs, outs), outs)
+        out_ref[...] = keep_ref[place, :] + other_ref[place, :]
 
 
 def input_kernel(taps_ref, next_near_ref, next_far_ref, near_ref, far_ref, out_ref, cells_ref, lines_ref):
@@ -183,11 +199,12 @@
                     out_ref[c, plane, start : start + group, lanes] = line
 
 
-def total_kernel(scale, terms_ref, out_ref):
+def total_kernel(scale, *refs):
+    *term_refs, out_ref = refs
     chans, outs, taps = out_ref.shape
-    total = terms_ref[0]
-    for source in range(1, terms_ref.shape[0]):
-        total = total + terms_ref[source]
+    total = term_refs[0][...]
+    for ref in term_refs[1:]:
+        total = total + ref[...]
     total = total * scale
     for c in range(chans):
         out_ref[c] = total[:, 32 * c : 32 * c + taps]
@@ -439,7 +456,6 @@
         cost=(1 << 20, 2 << 20),
     )
     near_lines = lines(grad_out, first)
-    far[0], odd = lax.optimization_barrier((far[0], odd))
     next_near_lines = lax.ppermute(near_lines, "depth", nearer)
     behind = lax.ppermute(odd, "depth", farther)
     behind_views = call(
@@ -450,9 +466,11 @@
     )
     far_lines = lines(*far)
     next_far_lines = lax.ppermute(far_lines, "depth", nearer)
-    partial = call(
-        lambda *refs: weight_kernel(seats, *refs),
-        jax.ShapeDtypeStruct((channels, 32 * chans), F32),
+    outs = channels // depth
+    half_terms = jax.ShapeDtypeStruct((channels // 2, 32 * chans), F32)
+    keep, send = call(
+        lambda *refs: weight_kernel(seats, outs, *refs),
+        (half_terms, half_terms),
         views,
         behind_views,
         near_lines,
@@ -464,7 +482,16 @@
         ),
         cost=(2 * 27 * chans * channels * cells, 8 << 20),
     )
-    terms = lax.all_to_all(partial, "depth", split_axis=0, concat_axis=0, tiled=True)
+    chips = depth // 2
+    other = lax.ppermute(send, "depth", [(i, i ^ 1) for i in range(depth)])
+    own_terms, *terms = call(
+        pair_kernel,
+        [jax.ShapeDtypeStruct((outs, 32 * chans), F32)] * chips,
+        keep,
+        other,
+        cost=(1 << 16, 1 << 19),
+    )
+    terms = [lax.ppermute(term, "depth", [(i, i ^ (2 * k + 2)) for i in range(depth)]) for k, term in enumerate(terms)]
     input_grad = call(
         input_kernel,
         jax.ShapeDtypeStruct(volume.shape, BF16),
@@ -479,14 +506,14 @@
         ),
         cost=(2 * 18 * chans * 2 * channels * cells, 8 << 20),
     )
-    terms, input_grad = lax.optimization_barrier((terms, input_grad))
+    own_terms, input_grad = lax.optimization_barrier((own_terms, input_grad))
     scale = 1.0 / math.sqrt(depth * cells)
-    outs = channels // depth
     weight_grad = call(
         lambda *refs: total_kernel(scale, *refs),
         jax.ShapeDtypeStruct((chans, outs, 27), F32),
-        terms.reshape(depth, outs, 32 * chans),
-        cost=(1 << 20, 1 << 20),
+        own_terms,
+        *terms,
+        cost=(1 << 16, 1 << 19),
     )
     return input_grad, jnp.transpose(weight_grad, (2, 0, 1))
 
@@ -494,7 +521,7 @@
 def solution(mesh):
     in_specs = (P("chan", "depth", None, None), P("chan", "depth", None, None), P())
     out_specs = (P("chan", "depth", None, None), P(None, "chan", "depth"))
-    ring = mesh.shape["chan"]
+    ring, depth = mesh.shape["chan"], mesh.shape["depth"]
 
     def either(grad_out, volume, weight):
         fits = (
@@ -503,6 +530,8 @@
             and grad_out.shape[1] == 1
             and ring % 2 == 0
             and ring >= 4
+            and depth & (depth - 1) == 0
+            and depth % (2 * ring) == 0
         )
         return (shards if fits else plain_shards)(grad_out, volume, weight)
 

time: 46.8 us -> 44.6 us (0.953)
  waiting for transfers between devices: 14.7 us -> 12.5 us
  Pallas kernels: 8.89 us -> 8.18 us
    ppermute x0 -> x4, starting transfers between devices: none -> 4.69 us  [the longest x3 4.62 us: shards(): lax.ppermute(term, 'depth', [(i, i ^ 2 * k + 2) for i in range(depth)])]
    all_to_all x1 -> x0, starting transfers between devices: 4.37 us -> none  [shards(): lax.all_to_all(partial, 'depth', split_axis=0, concat_axis=0, tiled=True)]
    all_to_all x1 -> x0, waiting for transfers between devices: 4.01 us -> none  [shards(): lax.all_to_all(partial, 'depth', split_axis=0, concat_axis=0, tiled=True)]
    ppermute x0 -> x4, waiting for transfers between devices: none -> 1.85 us  [the longest x1 1.33 us: shards(): other = lax.ppermute(send, 'depth', [(i, i ^ 1) for i in range(depth)])]
    pallas_call x7 -> x8, Pallas kernels: 8.89 us -> 8.18 us  [call(): pl.pallas_call(kernel, out_shape=out_shape, in_specs=specs or [VMEM] * le...]
  transfers between devices with their start and end apart: 7 -> 10, of which waited for: 4 -> 5; matrix products, arithmetic and copies ran while one was open for 0% -> 0% of each run, Pallas kernels for 18% -> 17%
where the time goes in v1:
time: 44.6 us; the launch traced here: 43.7 us
  starting transfers between devices  21.1 us (47%)
  waiting for transfers between devices  12.5 us (28%)
  Pallas kernels  8.18 us (18%)
  local copies, waits for them, and re-layouts  1.25 us (3%)
  between operations  0.71 us (2%)
    pallas_call x8, Pallas kernels, call(): pl.pallas_call(kernel, out_shape=out_shape, in_specs=specs or [VMEM] * le...  8.18 us
    ppermute x1, starting transfers between devices, shards(): up = lax.ppermute(up, 'chan', ahead)  7.4 us
    ppermute x1, waiting for transfers between devices, shards(): behind = lax.ppermute(odd, 'depth', farther)  4.77 us
    ppermute x3, starting transfers between devices, shards(): lax.ppermute(term, 'depth', [(i, i ^ 2 * k + 2) for i in range(depth)])  4.62 us
    ppermute x1, waiting for transfers between devices, shards(): first = lax.ppermute(grad_out, 'chan', ahead)  4.37 us
    ppermute x1, starting transfers between devices, shards(): first = lax.ppermute(grad_out, 'chan', ahead)  3.08 us
    ppermute x1, starting transfers between devices, shards(): next_near_lines = lax.ppermute(near_lines, 'depth', nearer)  2.69 us
    ppermute x1, starting transfers between devices, shards(): next_far_lines = lax.ppermute(far_lines, 'depth', nearer)  2.12 us
  transfers between devices with their start and end apart: 10, of which 5 were waited for; matrix products, arithmetic and copies ran while one was open for 0% of the time, Pallas kernels for 17%

profile of v1, /device:TPU:0, one launch (start us, length us, event | category | flops | bytes accessed | tf_op | source)
XLA Modules:
  0.0 43.7 jit_solution(18122603442146271775)
XLA Ops:
  0.6 0.0 copy-start
  0.6 0.0 copy-start.1
  0.7 3.1 %collective-permute-start = (bf16[32,1,32,128]{3,2,1,0:T(8,128)(2,1)}, bf16[32,1,32,128]{3,2,1,0:T(8,128)(2,1)S(1)}, u32[]{:S(2)}, u32[]{:S(2)}) collective-permute-start(bf16[32,1,32,128]{3,2,1,0:T(8,128)(2,1)} %refs_0_.3), channel_id=1, source_target_pairs={{0,1},{1,3},{3,2},{2,0},{4,5},{5,7},{7,6},{6,4},{8,9},{9,11},{11,1... | collective-permute-start | bytes 786440 | tf_op jit(solution)/shard_map/ppermute | solution.py:444
  3.7 1.1 %collective-permute-start.2 = (bf16[32,1,32,128]{3,2,1,0:T(8,128)(2,1)}, bf16[32,1,32,128]{3,2,1,0:T(8,128)(2,1)S(1)}, u32[]{:S(2)}, u32[]{:S(2)}) collective-permute-start(bf16[32,1,32,128]{3,2,1,0:T(8,128)(2,1)} %refs_0_.3), channel_id=1, source_target_pairs={{1,0},{3,1},{2,3},{0,2},{5,4},{7,5},{6,7},{4,6},{9,8},{11,9},{10,1... | collective-permute-start | bytes 786440 | tf_op jit(solution)/shard_map/ppermute | solution.py:448
  4.8 0.0 copy-done
  4.8 0.0 copy-start.2
  4.8 1.2 %copy-done.2 = bf16[16,2,64,256]{3,2,1,0:T(8,128)(2,1)S(1)} copy-done((bf16[16,2,64,256]{3,2,1,0:T(8,128)(2,1)S(1)}, bf16[16,2,64,256]{3,2,1,0:T(8,128)(2,1)}, u32[]{:S(2)}) %copy-start.2) | copy-done | bytes 1048600
  6.1 0.9 %shard_map.50 = (bf16[192,4096]{1,0:T(8,128)(2,1)S(1)}, bf16[288,256]{1,0:T(8,128)(2,1)S(1)}, bf16[16,1,64,256]{3,2,1,0:T(8,128)(2,1)S(1)}) custom-call(bf16[16,2,64,256]{3,2,1,0:T(8,128)(2,1)S(1)} %copy-done.2, bf16[27,16,128]{2,1,0:T(8,128)(2,1)S(1)} %constant_dynamic-slice_fusion.refs_1_), custom_call_target="tpu_custom_call" | custom-call | flops 536870912 | bytes 4194304 | tf_op jit(solution)/shard_map/pallas_call | solution.py:391
  7.0 4.4 %collective-permute-done.refs_1_ = bf16[32,1,32,128]{3,2,1,0:T(8,128)(2,1)S(1)} collective-permute-done((bf16[32,1,32,128]{3,2,1,0:T(8,128)(2,1)}, bf16[32,1,32,128]{3,2,1,0:T(8,128)(2,1)S(1)}, u32[]{:S(2)}, u32[]{:S(2)}) %collective-permute-start) | collective-permute-done | bytes 262176 | tf_op jit(solution)/shard_map/ppermute | solution.py:444
  11.4 7.4 %collective-permute-start.3 = (bf16[32,1,32,128]{3,2,1,0:T(8,128)(2,1)S(1)}, bf16[32,1,32,128]{3,2,1,0:T(8,128)(2,1)S(1)}, u32[]{:S(2)}, u32[]{:S(2)}) collective-permute-start(bf16[32,1,32,128]{3,2,1,0:T(8,128)(2,1)S(1)} %collective-permute-done.refs_1_), channel_id=1, source_target_pairs={{0,1},{1,3},{3,2},{2,0},{4,5},{5,7},{7,6},{6,4},{8,9},{9,11},{11,1... | collective-permute-start | bytes 786440 | tf_op jit(solution)/shard_map/ppermute | solution.py:449
  18.8 0.0 collective-permute-start.1
  18.8 0.0 copy-done.1
  18.8 0.7 %shard_map.52.refs_2_.near_ref = bf16[64,4096]{1,0:T(8,128)(2,1)S(1)} custom-call(bf16[32,1,32,128]{3,2,1,0:T(8,128)(2,1)S(1)} %copy-done.1, bf16[32,1,32,128]{3,2,1,0:T(8,128)(2,1)S(1)} %collective-permute-done.refs_1_), custom_call_target="tpu_custom_call" | custom-call | flops 1048576 | bytes 2097152 | tf_op jit(solution)/shard_map/pallas_call | solution.py:391
  19.4 2.7 %collective-permute-start.5 = (bf16[64,4096]{1,0:T(8,128)(2,1)S(1)}, bf16[64,4096]{1,0:T(8,128)(2,1)S(1)}, u32[]{:S(2)}, u32[]{:S(2)}) collective-permute-start(bf16[64,4096]{1,0:T(8,128)(2,1)S(1)} %shard_map.52.refs_2_.near_ref), channel_id=1, source_target_pairs={{4,0},{8,4},{12,8},{16,12},{20,16},{24,20},{28,24},{0,28},{5,1},{9... | collective-permute-start | bytes 1572872 | tf_op jit(solution)/shard_map/ppermute | solution.py:459
  22.1 0.0 collective-permute-done.2.refs_0_
  22.1 1.5 %collective-permute-done.3.refs_1_ = bf16[32,1,32,128]{3,2,1,0:T(8,128)(2,1)S(1)} collective-permute-done((bf16[32,1,32,128]{3,2,1,0:T(8,128)(2,1)S(1)}, bf16[32,1,32,128]{3,2,1,0:T(8,128)(2,1)S(1)}, u32[]{:S(2)}, u32[]{:S(2)}) %collective-permute-start.3) | collective-permute-done | bytes 262176 | tf_op jit(solution)/shard_map/ppermute | solution.py:449
  23.7 0.7 %shard_map.53.refs_3_.far_ref = bf16[64,4096]{1,0:T(8,128)(2,1)S(1)} custom-call(bf16[32,1,32,128]{3,2,1,0:T(8,128)(2,1)S(1)} %collective-permute-done.2.refs_0_, bf16[32,1,32,128]{3,2,1,0:T(8,128)(2,1)S(1)} %collective-permute-done.3.refs_1_), custom_call_target="tpu_custom_call" | custom-call | flops 1048576 | bytes 2097152 | tf_op jit(solution)/shard_map/pallas_call | solution.py:391
  24.3 2.1 %collective-permute-start.6 = (bf16[64,4096]{1,0:T(8,128)(2,1)S(1)}, bf16[64,4096]{1,0:T(8,128)(2,1)S(1)}, u32[]{:S(2)}, u32[]{:S(2)}) collective-permute-start(bf16[64,4096]{1,0:T(8,128)(2,1)S(1)} %shard_map.53.refs_3_.far_ref), channel_id=1, source_target_pairs={{4,0},{8,4},{12,8},{16,12},{20,16},{24,20},{28,24},{0,28},{5,1},{9... | collective-permute-start | bytes 1572872 | tf_op jit(solution)/shard_map/ppermute | solution.py:468
  26.5 4.8 %collective-permute-done.1.behind_ref = bf16[16,1,64,256]{3,2,1,0:T(8,128)(2,1)S(1)} collective-permute-done((bf16[16,1,64,256]{3,2,1,0:T(8,128)(2,1)S(1)}, bf16[16,1,64,256]{3,2,1,0:T(8,128)(2,1)S(1)}, u32[]{:S(2)}, u32[]{:S(2)}) %collective-permute-start.1) | collective-permute-done | bytes 524320 | tf_op jit(solution)/shard_map/ppermute | solution.py:460
  31.2 0.1 shard_map.51.refs_1_
  31.3 2.2 %shard_map.54 = (f32[64,512]{1,0:T(8,128)S(1)}, f32[64,512]{1,0:T(8,128)S(1)}) custom-call(bf16[192,4096]{1,0:T(8,128)(2,1)S(1)} %get-tuple-element.16.refs_0_, bf16[96,4096]{1,0:T(8,128)(2,1)S(1)} %shard_map.51.refs_1_, bf16[64,4096]{1,0:T(8,128)(2,1)S(1)} %shard_map.52.refs_2_.near_ref, bf16[64,4096]{1,0:T(8,128)(2,1)S(1)} %shard_map.53.refs_3_.far_ref), custom_call_target="tpu_custom_call" | custom-call | flops 452984832 | bytes 8388608 | tf_op jit(solution)/shard_map/pallas_call | solution.py:391
  33.5 0.1 collective-permute-start.4
  33.6 1.3 %collective-permute-done.4.other_ref = f32[64,512]{1,0:T(8,128)S(1)} collective-permute-done((f32[64,512]{1,0:T(8,128)S(1)}, f32[64,512]{1,0:T(8,128)S(1)}, u32[]{:S(2)}, u32[]{:S(2)}) %collective-permute-start.4) | collective-permute-done | bytes 131104 | tf_op jit(solution)/shard_map/ppermute | solution.py:486
  34.9 1.3 %collective-permute-start.7 = (f32[16,512]{1,0:T(8,128)S(1)}, f32[16,512]{1,0:T(8,128)S(1)}, u32[]{:S(2)}, u32[]{:S(2)}) collective-permute-start(f32[16,512]{1,0:T(8,128)S(1)} %get-tuple-element.25), channel_id=1, source_target_pairs={{0,8},{4,12},{8,0},{12,4},{16,24},{20,28},{24,16},{28,20},{1,9},{5... | collective-permute-start | bytes 98312 | tf_op jit(solution)/shard_map/ppermute | solution.py:494
  36.3 1.9 %collective-permute-start.8 = (f32[16,512]{1,0:T(8,128)S(1)}, f32[16,512]{1,0:T(8,128)S(1)}, u32[]{:S(2)}, u32[]{:S(2)}) collective-permute-start(f32[16,512]{1,0:T(8,128)S(1)} %get-tuple-element.26), channel_id=1, source_target_pairs={{0,16},{4,20},{8,24},{12,28},{16,0},{20,4},{24,8},{28,12},{1,17},{... | collective-permute-start | bytes 98312 | tf_op jit(solution)/shard_map/ppermute | solution.py:494
  38.2 1.4 %collective-permute-start.9 = (f32[16,512]{1,0:T(8,128)S(1)}, f32[16,512]{1,0:T(8,128)S(1)}, u32[]{:S(2)}, u32[]{:S(2)}) collective-permute-start(f32[16,512]{1,0:T(8,128)S(1)} %get-tuple-element.27), channel_id=1, source_target_pairs={{0,24},{4,28},{8,16},{12,20},{16,8},{20,12},{24,0},{28,4},{1,25},{... | collective-permute-start | bytes 98312 | tf_op jit(solution)/shard_map/ppermute | solution.py:494
  39.5 0.0 collective-permute-done.5.next_near_ref
  39.5 0.0 collective-permute-done.6.next_far_ref
  39.6 2.9 %shard_map.56 = bf16[16,2,64,256]{3,2,1,0:T(8,128)(2,1)} custom-call(bf16[288,256]{1,0:T(8,128)(2,1)S(1)} %get-tuple-element.22.taps_ref, bf16[64,4096]{1,0:T(8,128)(2,1)S(1)} %collective-permute-done.5.next_near_ref, bf16[64,4096]{1,0:T(8,128)(2,1)S(1)} %collective-permute-done.6.next_far_ref, bf16[64,4096]{1,0:T(8,128)(2,1)S(1)} %shard_map.52.refs_2_.near_ref, ...), custom_call_target="tpu_custom_call" | custom-call | flops 603979776 | bytes 8388608 | tf_op jit(solution)/shard_map/pallas_call | solution.py:391
  42.5 0.0 collective-permute-done.7.refs_1_
  42.5 0.0 collective-permute-done.8.refs_2_
  42.5 0.5 %collective-permute-done.9.refs_3_ = f32[16,512]{1,0:T(8,128)S(1)} collective-permute-done((f32[16,512]{1,0:T(8,128)S(1)}, f32[16,512]{1,0:T(8,128)S(1)}, u32[]{:S(2)}, u32[]{:S(2)}) %collective-permute-start.9) | collective-permute-done | bytes 32800 | tf_op jit(solution)/shard_map/ppermute | solution.py:494
  43.0 0.8 %shard_map.57 = f32[16,16,27]{2,1,0:T(8,128)} custom-call(f32[16,512]{1,0:T(8,128)S(1)} %get-tuple-element.24.refs_0_, f32[16,512]{1,0:T(8,128)S(1)} %collective-permute-done.7.refs_1_, f32[16,512]{1,0:T(8,128)S(1)} %collective-permute-done.8.refs_2_, f32[16,512]{1,0:T(8,128)S(1)} %collective-permute-done.9.refs_3_), custom_call_target="tpu_custom_call" | custom-call | flops 65536 | bytes 524288 | tf_op jit(solution)/shard_map/pallas_call | solution.py:391
  (2 shorter events, 0.0 us)
Async XLA Ops:
  0.6 4.2 %copy-start = (bf16[27,64,128]{2,1,0:T(8,128)(2,1)S(1)}, bf16[27,64,128]{2,1,0:T(8,128)(2,1)}, u32[]{:S(2)}) copy-start(bf16[27,64,128]{2,1,0:T(8,128)(2,1)} %param.5) | copy-start | bytes 1327108
  0.6 18.1 %copy-start.1 = (bf16[32,1,32,128]{3,2,1,0:T(8,128)(2,1)S(1)}, bf16[32,1,32,128]{3,2,1,0:T(8,128)(2,1)}, u32[]{:S(2)}) copy-start(bf16[32,1,32,128]{3,2,1,0:T(8,128)(2,1)} %refs_0_.3) | copy-start | bytes 786436
  0.7 10.7 %collective-permute-start = (bf16[32,1,32,128]{3,2,1,0:T(8,128)(2,1)}, bf16[32,1,32,128]{3,2,1,0:T(8,128)(2,1)S(1)}, u32[]{:S(2)}, u32[]{:S(2)}) collective-permute-start(bf16[32,1,32,128]{3,2,1,0:T(8,128)(2,1)} %refs_0_.3), channel_id=1, source_target_pairs={{0,1},{1,3},{3,2},{2,0},{4,5},{5,7},{7,6},{6,4},{8,9},{9,11},{11,1... | collective-permute-start | bytes 786440 | tf_op jit(solution)/shard_map/ppermute | solution.py:444
  3.7 18.4 %collective-permute-start.2 = (bf16[32,1,32,128]{3,2,1,0:T(8,128)(2,1)}, bf16[32,1,32,128]{3,2,1,0:T(8,128)(2,1)S(1)}, u32[]{:S(2)}, u32[]{:S(2)}) collective-permute-start(bf16[32,1,32,128]{3,2,1,0:T(8,128)(2,1)} %refs_0_.3), channel_id=1, source_target_pairs={{1,0},{3,1},{2,3},{0,2},{5,4},{7,5},{6,7},{4,6},{9,8},{11,9},{10,1... | collective-permute-start | bytes 786440 | tf_op jit(solution)/shard_map/ppermute | solution.py:448
  4.8 1.2 %copy-start.2 = (bf16[16,2,64,256]{3,2,1,0:T(8,128)(2,1)S(1)}, bf16[16,2,64,256]{3,2,1,0:T(8,128)(2,1)}, u32[]{:S(2)}) copy-start(bf16[16,2,64,256]{3,2,1,0:T(8,128)(2,1)} %refs_0_.2) | copy-start | bytes 3145732
  11.4 12.3 %collective-permute-start.3 = (bf16[32,1,32,128]{3,2,1,0:T(8,128)(2,1)S(1)}, bf16[32,1,32,128]{3,2,1,0:T(8,128)(2,1)S(1)}, u32[]{:S(2)}, u32[]{:S(2)}) collective-permute-start(bf16[32,1,32,128]{3,2,1,0:T(8,128)(2,1)S(1)} %collective-permute-done.refs_1_), channel_id=1, source_target_pairs={{0,1},{1,3},{3,2},{2,0},{4,5},{5,7},{7,6},{6,4},{8,9},{9,11},{11,1... | collective-permute-start | bytes 786440 | tf_op jit(solution)/shard_map/ppermute | solution.py:449
  18.8 12.5 %collective-permute-start.1 = (bf16[16,1,64,256]{3,2,1,0:T(8,128)(2,1)S(1)}, bf16[16,1,64,256]{3,2,1,0:T(8,128)(2,1)S(1)}, u32[]{:S(2)}, u32[]{:S(2)}) collective-permute-start(bf16[16,1,64,256]{3,2,1,0:T(8,128)(2,1)S(1)} %get-tuple-element.17), channel_id=1, source_target_pairs={{0,4},{4,8},{8,12},{12,16},{16,20},{20,24},{24,28},{28,0},{1,5},{5... | collective-permute-start | bytes 1572872 | tf_op jit(solution)/shard_map/ppermute | solution.py:460
  19.4 20.1 %collective-permute-start.5 = (bf16[64,4096]{1,0:T(8,128)(2,1)S(1)}, bf16[64,4096]{1,0:T(8,128)(2,1)S(1)}, u32[]{:S(2)}, u32[]{:S(2)}) collective-permute-start(bf16[64,4096]{1,0:T(8,128)(2,1)S(1)} %shard_map.52.refs_2_.near_ref), channel_id=1, source_target_pairs={{4,0},{8,4},{12,8},{16,12},{20,16},{24,20},{28,24},{0,28},{5,1},{9... | collective-permute-start | bytes 1572872 | tf_op jit(solution)/shard_map/ppermute | solution.py:459
  24.3 15.2 %collective-permute-start.6 = (bf16[64,4096]{1,0:T(8,128)(2,1)S(1)}, bf16[64,4096]{1,0:T(8,128)(2,1)S(1)}, u32[]{:S(2)}, u32[]{:S(2)}) collective-permute-start(bf16[64,4096]{1,0:T(8,128)(2,1)S(1)} %shard_map.53.refs_3_.far_ref), channel_id=1, source_target_pairs={{4,0},{8,4},{12,8},{16,12},{20,16},{24,20},{28,24},{0,28},{5,1},{9... | collective-permute-start | bytes 1572872 | tf_op jit(solution)/shard_map/ppermute | solution.py:468
  33.5 1.4 %collective-permute-start.4 = (f32[64,512]{1,0:T(8,128)S(1)}, f32[64,512]{1,0:T(8,128)S(1)}, u32[]{:S(2)}, u32[]{:S(2)}) collective-permute-start(f32[64,512]{1,0:T(8,128)S(1)} %get-tuple-element.20), channel_id=1, source_target_pairs={{0,4},{4,0},{8,12},{12,8},{16,20},{20,16},{24,28},{28,24},{1,5},{5... | collective-permute-start | bytes 393224 | tf_op jit(solution)/shard_map/ppermute | solution.py:486
  34.9 7.5 %collective-permute-start.7 = (f32[16,512]{1,0:T(8,128)S(1)}, f32[16,512]{1,0:T(8,128)S(1)}, u32[]{:S(2)}, u32[]{:S(2)}) collective-permute-start(f32[16,512]{1,0:T(8,128)S(1)} %get-tuple-element.25), channel_id=1, source_target_pairs={{0,8},{4,12},{8,0},{12,4},{16,24},{20,28},{24,16},{28,20},{1,9},{5... | collective-permute-start | bytes 98312 | tf_op jit(solution)/shard_map/ppermute | solution.py:494
  36.3 6.2 %collective-permute-start.8 = (f32[16,512]{1,0:T(8,128)S(1)}, f32[16,512]{1,0:T(8,128)S(1)}, u32[]{:S(2)}, u32[]{:S(2)}) collective-permute-start(f32[16,512]{1,0:T(8,128)S(1)} %get-tuple-element.26), channel_id=1, source_target_pairs={{0,16},{4,20},{8,24},{12,28},{16,0},{20,4},{24,8},{28,12},{1,17},{... | collective-permute-start | bytes 98312 | tf_op jit(solution)/shard_map/ppermute | solution.py:494
  38.2 4.8 %collective-permute-start.9 = (f32[16,512]{1,0:T(8,128)S(1)}, f32[16,512]{1,0:T(8,128)S(1)}, u32[]{:S(2)}, u32[]{:S(2)}) collective-permute-start(f32[16,512]{1,0:T(8,128)S(1)} %get-tuple-element.27), channel_id=1, source_target_pairs={{0,24},{4,28},{8,16},{12,20},{16,8},{20,12},{24,0},{28,4},{1,25},{... | collective-permute-start | bytes 98312 | tf_op jit(solution)/shard_map/ppermute | solution.py:494

commit v2 on v1

--- a/solution.py
+++ b/solution.py
@@ -442,8 +442,8 @@
         cost=(2 * 2 * 2 * cells * chans * 8 * cols, 4 << 20),
     )
     first = lax.ppermute(grad_out, "chan", ahead)
-    first, views = lax.optimization_barrier((first, views))
-    up, down, far = first, grad_out, []
+    down, views = lax.optimization_barrier((grad_out, views))
+    up, far = first, []
     for step in range(1, count // 2):
         down = lax.ppermute(down, "chan", back)
         up = lax.ppermute(up, "chan", ahead)

time: 44.6 us -> 44.6 us (level)
  waiting for transfers between devices: 12.5 us -> 11.6 us
  starting transfers between devices: 21.1 us -> 22 us
    ppermute x1, waiting for transfers between devices: 4.37 us -> 3.43 us  [shards(): first = lax.ppermute(grad_out, 'chan', ahead)]
    ppermute x1, starting transfers between devices: 1.08 us -> 2 us  [shards(): down = lax.ppermute(down, 'chan', back)]
where the time goes in v2:
time: 44.6 us; the launch traced here: 43.7 us
  starting transfers between devices  22 us (49%)
  waiting for transfers between devices  11.6 us (26%)
  Pallas kernels  8.18 us (18%)
  local copies, waits for them, and re-layouts  1.25 us (3%)
  between operations  0.72 us (2%)
    pallas_call x8, Pallas kernels, call(): pl.pallas_call(kernel, out_shape=out_shape, in_specs=specs or [VMEM] * le...  8.18 us
    ppermute x1, starting transfers between devices, shards(): up = lax.ppermute(up, 'chan', ahead)  7.38 us
    ppermute x1, waiting for transfers between devices, shards(): behind = lax.ppermute(odd, 'depth', farther)  4.76 us
    ppermute x3, starting transfers between devices, shards(): lax.ppermute(term, 'depth', [(i, i ^ 2 * k + 2) for i in range(depth)])  4.63 us
    ppermute x1, waiting for transfers between devices, shards(): first = lax.ppermute(grad_out, 'chan', ahead)  3.43 us
    ppermute x1, starting transfers between devices, shards(): first = lax.ppermute(grad_out, 'chan', ahead)  3.08 us
    ppermute x1, starting transfers between devices, shards(): next_near_lines = lax.ppermute(near_lines, 'depth', nearer)  2.69 us
    ppermute x1, starting transfers between devices, shards(): next_far_lines = lax.ppermute(far_lines, 'depth', nearer)  2.12 us
  transfers between devices with their start and end apart: 10, of which 5 were waited for; matrix products, arithmetic and copies ran while one was open for 0% of the time, Pallas kernels for 17%

profile of v2, /device:TPU:0, one launch (start us, length us, event | category | flops | bytes accessed | tf_op | source)
XLA Modules:
  0.0 43.7 jit_solution(15961640365213933985)
XLA Ops:
  0.6 0.0 copy-start
  0.6 0.0 copy-start.1
  0.7 3.1 %collective-permute-start.1 = (bf16[32,1,32,128]{3,2,1,0:T(8,128)(2,1)}, bf16[32,1,32,128]{3,2,1,0:T(8,128)(2,1)S(1)}, u32[]{:S(2)}, u32[]{:S(2)}) collective-permute-start(bf16[32,1,32,128]{3,2,1,0:T(8,128)(2,1)} %refs_0_.3), channel_id=1, source_target_pairs={{0,1},{1,3},{3,2},{2,0},{4,5},{5,7},{7,6},{6,4},{8,9},{9,11},{11,1... | collective-permute-start | bytes 786440 | tf_op jit(solution)/shard_map/ppermute | solution.py:444
  3.7 0.0 copy-done
  3.8 0.0 copy-start.2
  3.8 1.2 %copy-done.2 = bf16[16,2,64,256]{3,2,1,0:T(8,128)(2,1)S(1)} copy-done((bf16[16,2,64,256]{3,2,1,0:T(8,128)(2,1)S(1)}, bf16[16,2,64,256]{3,2,1,0:T(8,128)(2,1)}, u32[]{:S(2)}) %copy-start.2) | copy-done | bytes 1048600
  5.0 0.9 %shard_map.50 = (bf16[192,4096]{1,0:T(8,128)(2,1)S(1)}, bf16[288,256]{1,0:T(8,128)(2,1)S(1)}, bf16[16,1,64,256]{3,2,1,0:T(8,128)(2,1)S(1)}) custom-call(bf16[16,2,64,256]{3,2,1,0:T(8,128)(2,1)S(1)} %copy-done.2, bf16[27,16,128]{2,1,0:T(8,128)(2,1)S(1)} %constant_dynamic-slice_fusion.refs_1_), custom_call_target="tpu_custom_call" | custom-call | flops 536870912 | bytes 4194304 | tf_op jit(solution)/shard_map/pallas_call | solution.py:391
  5.9 0.0 copy-done.1
  5.9 2.0 %collective-permute-start.2 = (bf16[32,1,32,128]{3,2,1,0:T(8,128)(2,1)S(1)}, bf16[32,1,32,128]{3,2,1,0:T(8,128)(2,1)S(1)}, u32[]{:S(2)}, u32[]{:S(2)}) collective-permute-start(bf16[32,1,32,128]{3,2,1,0:T(8,128)(2,1)S(1)} %copy-done.1), channel_id=1, source_target_pairs={{1,0},{3,1},{2,3},{0,2},{5,4},{7,5},{6,7},{4,6},{9,8},{11,9},{10,1... | collective-permute-start | bytes 786440 | tf_op jit(solution)/shard_map/ppermute | solution.py:448
  7.9 3.4 %collective-permute-done.1.refs_1_ = bf16[32,1,32,128]{3,2,1,0:T(8,128)(2,1)S(1)} collective-permute-done((bf16[32,1,32,128]{3,2,1,0:T(8,128)(2,1)}, bf16[32,1,32,128]{3,2,1,0:T(8,128)(2,1)S(1)}, u32[]{:S(2)}, u32[]{:S(2)}) %collective-permute-start.1) | collective-permute-done | bytes 262176 | tf_op jit(solution)/shard_map/ppermute | solution.py:444
  11.4 7.4 %collective-permute-start.3 = (bf16[32,1,32,128]{3,2,1,0:T(8,128)(2,1)S(1)}, bf16[32,1,32,128]{3,2,1,0:T(8,128)(2,1)S(1)}, u32[]{:S(2)}, u32[]{:S(2)}) collective-permute-start(bf16[32,1,32,128]{3,2,1,0:T(8,128)(2,1)S(1)} %collective-permute-done.1.refs_1_), channel_id=1, source_target_pairs={{0,1},{1,3},{3,2},{2,0},{4,5},{5,7},{7,6},{6,4},{8,9},{9,11},{11,1... | collective-permute-start | bytes 786440 | tf_op jit(solution)/shard_map/ppermute | solution.py:449
  18.7 0.0 collective-permute-start
  18.7 0.7 %shard_map.52.refs_2_.near_ref = bf16[64,4096]{1,0:T(8,128)(2,1)S(1)} custom-call(bf16[32,1,32,128]{3,2,1,0:T(8,128)(2,1)S(1)} %copy-done.1, bf16[32,1,32,128]{3,2,1,0:T(8,128)(2,1)S(1)} %collective-permute-done.1.refs_1_), custom_call_target="tpu_custom_call" | custom-call | flops 1048576 | bytes 2097152 | tf_op jit(solution)/shard_map/pallas_call | solution.py:391
  19.4 2.7 %collective-permute-start.5 = (bf16[64,4096]{1,0:T(8,128)(2,1)S(1)}, bf16[64,4096]{1,0:T(8,128)(2,1)S(1)}, u32[]{:S(2)}, u32[]{:S(2)}) collective-permute-start(bf16[64,4096]{1,0:T(8,128)(2,1)S(1)} %shard_map.52.refs_2_.near_ref), channel_id=1, source_target_pairs={{4,0},{8,4},{12,8},{16,12},{20,16},{24,20},{28,24},{0,28},{5,1},{9... | collective-permute-start | bytes 1572872 | tf_op jit(solution)/shard_map/ppermute | solution.py:459
  22.1 0.0 collective-permute-done.2.refs_0_
  22.1 1.6 %collective-permute-done.3.refs_1_ = bf16[32,1,32,128]{3,2,1,0:T(8,128)(2,1)S(1)} collective-permute-done((bf16[32,1,32,128]{3,2,1,0:T(8,128)(2,1)S(1)}, bf16[32,1,32,128]{3,2,1,0:T(8,128)(2,1)S(1)}, u32[]{:S(2)}, u32[]{:S(2)}) %collective-permute-start.3) | collective-permute-done | bytes 262176 | tf_op jit(solution)/shard_map/ppermute | solution.py:449
  23.7 0.7 %shard_map.53.refs_3_.far_ref = bf16[64,4096]{1,0:T(8,128)(2,1)S(1)} custom-call(bf16[32,1,32,128]{3,2,1,0:T(8,128)(2,1)S(1)} %collective-permute-done.2.refs_0_, bf16[32,1,32,128]{3,2,1,0:T(8,128)(2,1)S(1)} %collective-permute-done.3.refs_1_), custom_call_target="tpu_custom_call" | custom-call | flops 1048576 | bytes 2097152 | tf_op jit(solution)/shard_map/pallas_call | solution.py:391
  24.3 2.1 %collective-permute-start.6 = (bf16[64,4096]{1,0:T(8,128)(2,1)S(1)}, bf16[64,4096]{1,0:T(8,128)(2,1)S(1)}, u32[]{:S(2)}, u32[]{:S(2)}) collective-permute-start(bf16[64,4096]{1,0:T(8,128)(2,1)S(1)} %shard_map.53.refs_3_.far_ref), channel_id=1, source_target_pairs={{4,0},{8,4},{12,8},{16,12},{20,16},{24,20},{28,24},{0,28},{5,1},{9... | collective-permute-start | bytes 1572872 | tf_op jit(solution)/shard_map/ppermute | solution.py:468
  26.5 4.8 %collective-permute-done.behind_ref = bf16[16,1,64,256]{3,2,1,0:T(8,128)(2,1)S(1)} collective-permute-done((bf16[16,1,64,256]{3,2,1,0:T(8,128)(2,1)S(1)}, bf16[16,1,64,256]{3,2,1,0:T(8,128)(2,1)S(1)}, u32[]{:S(2)}, u32[]{:S(2)}) %collective-permute-start) | collective-permute-done | bytes 524320 | tf_op jit(solution)/shard_map/ppermute | solution.py:460
  31.2 0.1 shard_map.51.refs_1_
  31.3 2.2 %shard_map.54 = (f32[64,512]{1,0:T(8,128)S(1)}, f32[64,512]{1,0:T(8,128)S(1)}) custom-call(bf16[192,4096]{1,0:T(8,128)(2,1)S(1)} %get-tuple-element.16.refs_0_, bf16[96,4096]{1,0:T(8,128)(2,1)S(1)} %shard_map.51.refs_1_, bf16[64,4096]{1,0:T(8,128)(2,1)S(1)} %shard_map.52.refs_2_.near_ref, bf16[64,4096]{1,0:T(8,128)(2,1)S(1)} %shard_map.53.refs_3_.far_ref), custom_call_target="tpu_custom_call" | custom-call | flops 452984832 | bytes 8388608 | tf_op jit(solution)/shard_map/pallas_call | solution.py:391
  33.5 0.1 collective-permute-start.4
  33.5 1.3 %collective-permute-done.4.other_ref = f32[64,512]{1,0:T(8,128)S(1)} collective-permute-done((f32[64,512]{1,0:T(8,128)S(1)}, f32[64,512]{1,0:T(8,128)S(1)}, u32[]{:S(2)}, u32[]{:S(2)}) %collective-permute-start.4) | collective-permute-done | bytes 131104 | tf_op jit(solution)/shard_map/ppermute | solution.py:486
  34.9 1.3 %collective-permute-start.7 = (f32[16,512]{1,0:T(8,128)S(1)}, f32[16,512]{1,0:T(8,128)S(1)}, u32[]{:S(2)}, u32[]{:S(2)}) collective-permute-start(f32[16,512]{1,0:T(8,128)S(1)} %get-tuple-element.25), channel_id=1, source_target_pairs={{0,8},{4,12},{8,0},{12,4},{16,24},{20,28},{24,16},{28,20},{1,9},{5... | collective-permute-start | bytes 98312 | tf_op jit(solution)/shard_map/ppermute | solution.py:494
  36.2 1.9 %collective-permute-start.8 = (f32[16,512]{1,0:T(8,128)S(1)}, f32[16,512]{1,0:T(8,128)S(1)}, u32[]{:S(2)}, u32[]{:S(2)}) collective-permute-start(f32[16,512]{1,0:T(8,128)S(1)} %get-tuple-element.26), channel_id=1, source_target_pairs={{0,16},{4,20},{8,24},{12,28},{16,0},{20,4},{24,8},{28,12},{1,17},{... | collective-permute-start | bytes 98312 | tf_op jit(solution)/shard_map/ppermute | solution.py:494
  38.1 1.4 %collective-permute-start.9 = (f32[16,512]{1,0:T(8,128)S(1)}, f32[16,512]{1,0:T(8,128)S(1)}, u32[]{:S(2)}, u32[]{:S(2)}) collective-permute-start(f32[16,512]{1,0:T(8,128)S(1)} %get-tuple-element.27), channel_id=1, source_target_pairs={{0,24},{4,28},{8,16},{12,20},{16,8},{20,12},{24,0},{28,4},{1,25},{... | collective-permute-start | bytes 98312 | tf_op jit(solution)/shard_map/ppermute | solution.py:494
  39.5 0.0 collective-permute-done.5.next_near_ref
  39.5 0.0 collective-permute-done.6.next_far_ref
  39.5 2.9 %shard_map.56 = bf16[16,2,64,256]{3,2,1,0:T(8,128)(2,1)} custom-call(bf16[288,256]{1,0:T(8,128)(2,1)S(1)} %get-tuple-element.22.taps_ref, bf16[64,4096]{1,0:T(8,128)(2,1)S(1)} %collective-permute-done.5.next_near_ref, bf16[64,4096]{1,0:T(8,128)(2,1)S(1)} %collective-permute-done.6.next_far_ref, bf16[64,4096]{1,0:T(8,128)(2,1)S(1)} %shard_map.52.refs_2_.near_ref, ...), custom_call_target="tpu_custom_call" | custom-call | flops 603979776 | bytes 8388608 | tf_op jit(solution)/shard_map/pallas_call | solution.py:391
  42.5 0.0 collective-permute-done.7.refs_1_
  42.5 0.0 collective-permute-done.8.refs_2_
  42.5 0.5 %collective-permute-done.9.refs_3_ = f32[16,512]{1,0:T(8,128)S(1)} collective-permute-done((f32[16,512]{1,0:T(8,128)S(1)}, f32[16,512]{1,0:T(8,128)S(1)}, u32[]{:S(2)}, u32[]{:S(2)}) %collective-permute-start.9) | collective-permute-done | bytes 32800 | tf_op jit(solution)/shard_map/ppermute | solution.py:494
  43.0 0.8 %shard_map.57 = f32[16,16,27]{2,1,0:T(8,128)} custom-call(f32[16,512]{1,0:T(8,128)S(1)} %get-tuple-element.24.refs_0_, f32[16,512]{1,0:T(8,128)S(1)} %collective-permute-done.7.refs_1_, f32[16,512]{1,0:T(8,128)S(1)} %collective-permute-done.8.refs_2_, f32[16,512]{1,0:T(8,128)S(1)} %collective-permute-done.9.refs_3_), custom_call_target="tpu_custom_call" | custom-call | flops 65536 | bytes 524288 | tf_op jit(solution)/shard_map/pallas_call | solution.py:391
  (2 shorter events, 0.0 us)
Async XLA Ops:
  0.6 3.1 %copy-start = (bf16[27,64,128]{2,1,0:T(8,128)(2,1)S(1)}, bf16[27,64,128]{2,1,0:T(8,128)(2,1)}, u32[]{:S(2)}) copy-start(bf16[27,64,128]{2,1,0:T(8,128)(2,1)} %param.5) | copy-start | bytes 1327108
  0.6 5.3 %copy-start.1 = (bf16[32,1,32,128]{3,2,1,0:T(8,128)(2,1)S(1)}, bf16[32,1,32,128]{3,2,1,0:T(8,128)(2,1)}, u32[]{:S(2)}) copy-start(bf16[32,1,32,128]{3,2,1,0:T(8,128)(2,1)} %refs_0_.3) | copy-start | bytes 786436
  0.7 10.7 %collective-permute-start.1 = (bf16[32,1,32,128]{3,2,1,0:T(8,128)(2,1)}, bf16[32,1,32,128]{3,2,1,0:T(8,128)(2,1)S(1)}, u32[]{:S(2)}, u32[]{:S(2)}) collective-permute-start(bf16[32,1,32,128]{3,2,1,0:T(8,128)(2,1)} %refs_0_.3), channel_id=1, source_target_pairs={{0,1},{1,3},{3,2},{2,0},{4,5},{5,7},{7,6},{6,4},{8,9},{9,11},{11,1... | collective-permute-start | bytes 786440 | tf_op jit(solution)/shard_map/ppermute | solution.py:444
  3.8 1.2 %copy-start.2 = (bf16[16,2,64,256]{3,2,1,0:T(8,128)(2,1)S(1)}, bf16[16,2,64,256]{3,2,1,0:T(8,128)(2,1)}, u32[]{:S(2)}) copy-start(bf16[16,2,64,256]{3,2,1,0:T(8,128)(2,1)} %refs_0_.2) | copy-start | bytes 3145732
  5.9 16.2 %collective-permute-start.2 = (bf16[32,1,32,128]{3,2,1,0:T(8,128)(2,1)S(1)}, bf16[32,1,32,128]{3,2,1,0:T(8,128)(2,1)S(1)}, u32[]{:S(2)}, u32[]{:S(2)}) collective-permute-start(bf16[32,1,32,128]{3,2,1,0:T(8,128)(2,1)S(1)} %copy-done.1), channel_id=1, source_target_pairs={{1,0},{3,1},{2,3},{0,2},{5,4},{7,5},{6,7},{4,6},{9,8},{11,9},{10,1... | collective-permute-start | bytes 786440 | tf_op jit(solution)/shard_map/ppermute | solution.py:448
  11.4 12.3 %collective-permute-start.3 = (bf16[32,1,32,128]{3,2,1,0:T(8,128)(2,1)S(1)}, bf16[32,1,32,128]{3,2,1,0:T(8,128)(2,1)S(1)}, u32[]{:S(2)}, u32[]{:S(2)}) collective-permute-start(bf16[32,1,32,128]{3,2,1,0:T(8,128)(2,1)S(1)} %collective-permute-done.1.refs_1_), channel_id=1, source_target_pairs={{0,1},{1,3},{3,2},{2,0},{4,5},{5,7},{7,6},{6,4},{8,9},{9,11},{11,1... | collective-permute-start | bytes 786440 | tf_op jit(solution)/shard_map/ppermute | solution.py:449
  18.7 12.5 %collective-permute-start = (bf16[16,1,64,256]{3,2,1,0:T(8,128)(2,1)S(1)}, bf16[16,1,64,256]{3,2,1,0:T(8,128)(2,1)S(1)}, u32[]{:S(2)}, u32[]{:S(2)}) collective-permute-start(bf16[16,1,64,256]{3,2,1,0:T(8,128)(2,1)S(1)} %get-tuple-element.17), channel_id=1, source_target_pairs={{0,4},{4,8},{8,12},{12,16},{16,20},{20,24},{24,28},{28,0},{1,5},{5... | collective-permute-start | bytes 1572872 | tf_op jit(solution)/shard_map/ppermute | solution.py:460
  19.4 20.1 %collective-permute-start.5 = (bf16[64,4096]{1,0:T(8,128)(2,1)S(1)}, bf16[64,4096]{1,0:T(8,128)(2,1)S(1)}, u32[]{:S(2)}, u32[]{:S(2)}) collective-permute-start(bf16[64,4096]{1,0:T(8,128)(2,1)S(1)} %shard_map.52.refs_2_.near_ref), channel_id=1, source_target_pairs={{4,0},{8,4},{12,8},{16,12},{20,16},{24,20},{28,24},{0,28},{5,1},{9... | collective-permute-start | bytes 1572872 | tf_op jit(solution)/shard_map/ppermute | solution.py:459
  24.3 15.2 %collective-permute-start.6 = (bf16[64,4096]{1,0:T(8,128)(2,1)S(1)}, bf16[64,4096]{1,0:T(8,128)(2,1)S(1)}, u32[]{:S(2)}, u32[]{:S(2)}) collective-permute-start(bf16[64,4096]{1,0:T(8,128)(2,1)S(1)} %shard_map.53.refs_3_.far_ref), channel_id=1, source_target_pairs={{4,0},{8,4},{12,8},{16,12},{20,16},{24,20},{28,24},{0,28},{5,1},{9... | collective-permute-start | bytes 1572872 | tf_op jit(solution)/shard_map/ppermute | solution.py:468
  33.5 1.4 %collective-permute-start.4 = (f32[64,512]{1,0:T(8,128)S(1)}, f32[64,512]{1,0:T(8,128)S(1)}, u32[]{:S(2)}, u32[]{:S(2)}) collective-permute-start(f32[64,512]{1,0:T(8,128)S(1)} %get-tuple-element.20), channel_id=1, source_target_pairs={{0,4},{4,0},{8,12},{12,8},{16,20},{20,16},{24,28},{28,24},{1,5},{5... | collective-permute-start | bytes 393224 | tf_op jit(solution)/shard_map/ppermute | solution.py:486
  34.9 7.6 %collective-permute-start.7 = (f32[16,512]{1,0:T(8,128)S(1)}, f32[16,512]{1,0:T(8,128)S(1)}, u32[]{:S(2)}, u32[]{:S(2)}) collective-permute-start(f32[16,512]{1,0:T(8,128)S(1)} %get-tuple-element.25), channel_id=1, source_target_pairs={{0,8},{4,12},{8,0},{12,4},{16,24},{20,28},{24,16},{28,20},{1,9},{5... | collective-permute-start | bytes 98312 | tf_op jit(solution)/shard_map/ppermute | solution.py:494
  36.2 6.2 %collective-permute-start.8 = (f32[16,512]{1,0:T(8,128)S(1)}, f32[16,512]{1,0:T(8,128)S(1)}, u32[]{:S(2)}, u32[]{:S(2)}) collective-permute-start(f32[16,512]{1,0:T(8,128)S(1)} %get-tuple-element.26), channel_id=1, source_target_pairs={{0,16},{4,20},{8,24},{12,28},{16,0},{20,4},{24,8},{28,12},{1,17},{... | collective-permute-start | bytes 98312 | tf_op jit(solution)/shard_map/ppermute | solution.py:494
  38.1 4.8 %collective-permute-start.9 = (f32[16,512]{1,0:T(8,128)S(1)}, f32[16,512]{1,0:T(8,128)S(1)}, u32[]{:S(2)}, u32[]{:S(2)}) collective-permute-start(f32[16,512]{1,0:T(8,128)S(1)} %get-tuple-element.27), channel_id=1, source_target_pairs={{0,24},{4,28},{8,16},{12,20},{16,8},{20,12},{24,0},{28,4},{1,25},{... | collective-permute-start | bytes 98312 | tf_op jit(solution)/shard_map/ppermute | solution.py:494

commit v3 on v2

--- a/solution.py
+++ b/solution.py
@@ -10,7 +10,7 @@
 F32 = jnp.float32
 BF16 = jnp.bfloat16
 VMEM = pl.BlockSpec(memory_space=pltpu.VMEM)
-SMEM = pl.BlockSpec(memory_space=pltpu.SMEM)
+HBM = pl.BlockSpec(memory_space=pltpu.HBM)
 LIMIT = 48 * 1024 * 1024
 
 
@@ -66,10 +66,15 @@
     return owner
 
 
-def own_views_kernel(seats, depth, volume_ref, weight_ref, views_ref, taps_ref, odd_ref):
+def odd_plane_kernel(volume_ref, odd_ref, sem):
+    copy = pltpu.make_async_copy(volume_ref.at[:, 1:], odd_ref, sem)
+    copy.start()
+    copy.wait()
+
+
+def own_views_kernel(seats, depth, volume_ref, weight_ref, views_ref, taps_ref):
     chans = volume_ref.shape[0]
     channels = weight_ref.shape[2]
-    odd_ref[...] = volume_ref[:, 1:]
     place_views(volume_ref.at[:, 0], views_ref, 0)
     place_views(volume_ref.at[:, 1], views_ref, 6 * chans)
     part = channels // len(seats)
@@ -105,7 +110,7 @@
 
 def place_lines(part, out_ref, at, wide_ref):
     outs, _, rows, cols = part.shape
-    wide_ref[...] = part[...].reshape(outs * rows, cols).astype(F32)
+    wide_ref[: outs * rows, :] = part[...].reshape(outs * rows, cols).astype(F32)
     for row in range(rows):
         line = wide_ref[pl.ds(row, outs, stride=rows), :].astype(BF16)
         out_ref[at : at + outs, row * cols : (row + 1) * cols] = line
@@ -120,15 +125,17 @@
 
 
 def weight_kernel(
-    seats, outs, own_ref, behind_ref, near_ref, far_ref, keep_ref, send_ref, grads_ref, terms_ref, placed_ref
+    seats, outs, own_ref, behind_ref, *refs
 ):
+    *line_refs, keep_ref, send_ref, grads_ref, terms_ref, placed_ref = refs
     channels = grads_ref.shape[0]
     chans = behind_ref.shape[0] // 6
     cells = own_ref.shape[1]
     cols = grads_ref.shape[1] - cells
-    known = near_ref.shape[0]
-    grads_ref[:known, :cells] = near_ref[...]
-    grads_ref[known:, :cells] = far_ref[...]
+    at = 0
+    for ref in line_refs:
+        grads_ref[at : at + ref.shape[0], :cells] = ref[...]
+        at += ref.shape[0]
     grads_ref[:, cells:] = jnp.zeros((channels, cols), BF16)
     both = jnp.concatenate([grads_ref[:, :cells], grads_ref[:, cols:]], axis=0)
     contract = (((1,), (1,)), ((), ()))
@@ -162,11 +169,12 @@
         out_ref[...] = keep_ref[place, :] + other_ref[place, :]
 
 
-def input_kernel(taps_ref, next_near_ref, next_far_ref, near_ref, far_ref, out_ref, cells_ref, lines_ref):
+def input_kernel(taps_ref, *refs):
+    *line_refs, out_ref, cells_ref, lines_ref = refs
     chans, _, rows, cols = out_ref.shape
     half = cols // 2
     grid_cells = half * rows // 2
-    grads = [ref[...] for ref in (next_near_ref, next_far_ref, near_ref, far_ref)]
+    grads = [ref[...] for ref in line_refs]
     cells_ref[:, :grid_cells] = matmul(taps_ref[...], jnp.concatenate(grads, axis=0))
     cells_ref[:, grid_cells:] = jnp.zeros((cells_ref.shape[0], half), F32)
     group = 256 // chans
@@ -284,12 +292,12 @@
     return (input_grad, summed * (1.0 / math.sqrt(cell_count)))
 
 
-def call(kernel, out_shape, *args, specs=None, scratch=(), cost=None):
+def call(kernel, out_shape, *args, scratch=(), cost=None):
     flops, moved = cost
     return pl.pallas_call(
         kernel,
         out_shape=out_shape,
-        in_specs=specs or [VMEM] * len(args),
+        in_specs=[VMEM] * len(args),
         out_specs=jax.tree.map(lambda _: VMEM, out_shape),
         scratch_shapes=scratch,
         compiler_params=pltpu.CompilerParams(vmem_limit_bytes=LIMIT),
@@ -306,157 +314,42 @@
     cells = rows * cols
     order = ring_order(count)
     ahead = [(order[i], order[(i + 1) % count]) for i in range(count)]
-    back = [(b, a) for a, b in ahead]
     farther = [(i, (i + 1) % depth) for i in range(depth)]
     nearer = [(b, a) for a, b in farther]
-    own_weight = lax.dynamic_slice_in_dim(weight, lax.axis_index("chan") * local_in, local_in, 1)
-    input_part = phase_grads(own_weight.reshape(27 * local_in, channels_out), every_channel)
-    weight_part = weight_terms(volume, every_channel)
-    input_grad = input_part.astype(jnp.bfloat16)
-    summed = lax.psum_scatter(weight_part, "depth", scatter_dimension=2, tiled=True)
-    cell_count = grad_out.shape[1] * lax.axis_size("depth") * grad_out.shape[2] * grad_out.shape[3]
-    return (input_grad, summed * (1.0 / math.sqrt(cell_count)))
-
-
-def call(kernel, out_shape, *args, specs=None, scratch=(), cost=None):
-    flops, moved = cost
-    return pl.pallas_call(
-        kernel,
-        out_shape=out_shape,
-        in_specs=specs or [VMEM] * len(args),
-        out_specs=jax.tree.map(lambda _: VMEM, out_shape),
-        scratch_shapes=scratch,
-        compiler_params=pltpu.CompilerParams(vmem_limit_bytes=LIMIT),
-        cost_estimate=pl.CostEstimate(flops=flops, bytes_accessed=moved, transcendentals=0),
-    )(*args)
-
-
-def shards(grad_out, volume, weight):
-    count = lax.axis_size("chan")
-    depth = lax.axis_size("depth")
-    own_outs, _, rows, cols = grad_out.shape
-    chans = volume.shape[0]
-    channels = weight.shape[2]
-    cells = rows * cols
-    order = ring_order(count)
-    ahead = [(order[i], order[(i + 1) % count]) for i in range(count)]
-    back = [(b, a) for a, b in ahead]
-    farther = [(i, (i + 1) % depth) for i in range(depth)]
-    nearer = [(b, a) for a, b in farther]
-    own_weight = lax.dynamic_slice_in_dim(weight, lax.axis_index("chan") * local_in, local_in, 1)
-    input_part = phase_grads(own_weight.reshape(27 * local_in, channels_out), every_channel)
-    weight_part = weight_terms(volume, every_channel)
-    input_grad = input_part.astype(jnp.bfloat16)
-    summed = lax.psum_scatter(weight_part, "depth", scatter_dimension=2, tiled=True)
-    cell_count = grad_out.shape[1] * lax.axis_size("depth") * grad_out.shape[2] * grad_out.shape[3]
-    return (input_grad, summed * (1.0 / math.sqrt(cell_count)))
-
-
-def call(kernel, out_shape, *args, specs=None, scratch=(), cost=None):
-    flops, moved = cost
-    return pl.pallas_call(
-        kernel,
-        out_shape=out_shape,
-        in_specs=specs or [VMEM] * len(args),
-        out_specs=jax.tree.map(lambda _: VMEM, out_shape),
-        scratch_shapes=scratch,
-        compiler_params=pltpu.CompilerParams(vmem_limit_bytes=LIMIT),
-        cost_estimate=pl.CostEstimate(flops=flops, bytes_accessed=moved, transcendentals=0),
-    )(*args)
-
-
-def shards(grad_out, volume, weight):
-    count = lax.axis_size("chan")
-    depth = lax.axis_size("depth")
-    own_outs, _, rows, cols = grad_out.shape
-    chans = volume.shape[0]
-    channels = weight.shape[2]
-    cells = rows * cols
-    order = ring_order(count)
-    ahead = [(order[i], order[(i + 1) % count]) for i in range(count)]
-    back = [(b, a) for a, b in ahead]
-    farther = [(i, (i + 1) % depth) for i in range(depth)]
-    nearer = [(b, a) for a, b in farther]
-    own_weight = lax.dynamic_slice_in_dim(weight, lax.axis_index("chan") * local_in, local_in, 1)
-    input_part = phase_grads(own_weight.reshape(27 * local_in, channels_out), every_channel)
-    weight_part = weight_terms(volume, every_channel)
-    input_grad = input_part.astype(jnp.bfloat16)
-    summed = lax.psum_scatter(weight_part, "depth", scatter_dimension=2, tiled=True)
-    cell_count = grad_out.shape[1] * lax.axis_size("depth") * grad_out.shape[2] * grad_out.shape[3]
-    return (input_grad, summed * (1.0 / math.sqrt(cell_count)))
-
-
-def call(kernel, out_shape, *args, specs=None, scratch=(), cost=None):
-    flops, moved = cost
-    return pl.pallas_call(
-        kernel,
-        out_shape=out_shape,
-        in_specs=specs or [VMEM] * len(args),
-        out_specs=jax.tree.map(lambda _: VMEM, out_shape),
-        scratch_shapes=scratch,
-        compiler_params=pltpu.CompilerParams(vmem_limit_bytes=LIMIT),
-        cost_estimate=pl.CostEstimate(flops=flops, bytes_accessed=moved, transcendentals=0),
-    )(*args)
-
-
-def shards(grad_out, volume, weight):
-    count = lax.axis_size("chan")
-    depth = lax.axis_size("depth")
-    own_outs, _, rows, cols = grad_out.shape
-    chans = volume.shape[0]
-    channels = weight.shape[2]
-    cells = rows * cols
-    order = ring_order(count)
-    ahead = [(order[i], order[(i + 1) % count]) for i in range(count)]
-    back = [(b, a) for a, b in ahead]
-    farther = [(i, (i + 1) % depth) for i in range(depth)]
-    nearer = [(b, a) for a, b in farther]
-    shifts = [0]
-
-    near = []
-    up = down = grad_out
-    for step in range(1, (count - 1) // 2 + 1):
-        up = lax.ppermute(up, "chan", ahead)
-        down = lax.ppermute(down, "chan", back)
-        near += [up, down]
-        shifts += [-step, step]
-    last = lax.ppermute(up, "chan", ahead)
-    shifts += [count // 2]
-    seats = [[order[(order.index(chip) + s) % count] for s in shifts] for chip in range(count)]
-
-    shifts = [0, -1]
-    for step in range(1, count // 2):
-        shifts += [step, -step - 1]
-    seats = [[order[(order.index(chip) + s) % count] for s in shifts] for chip in range(count)]
+    seats = [[order[(order.index(chip) - step) % count] for step in range(count)] for chip in range(count)]
 
     own_weight = lax.dynamic_slice_in_dim(weight, lax.axis_index("chan") * chans, chans, 1)
-    views, taps, odd = call(
+    odd = pl.pallas_call(
+        odd_plane_kernel,
+        out_shape=jax.ShapeDtypeStruct((chans, 1, 2 * rows, 2 * cols), BF16),
+        in_specs=[HBM],
+        out_specs=HBM,
+        scratch_shapes=[pltpu.SemaphoreType.DMA],
+        compiler_params=pltpu.CompilerParams(vmem_limit_bytes=63 * 1024 * 1024),
+        cost_estimate=pl.CostEstimate(flops=0, bytes_accessed=1 << 20, transcendentals=0),
+    )(volume)
+    views, taps = call(
         lambda *refs: own_views_kernel(seats, depth, *refs),
         (
             jax.ShapeDtypeStruct((12 * chans, cells), BF16),
             jax.ShapeDtypeStruct((18 * chans, 2 * channels), BF16),
-            jax.ShapeDtypeStruct((chans, 1, 2 * rows, 2 * cols), BF16),
         ),
         volume,
         own_weight,
         cost=(2 * 2 * 2 * cells * chans * 8 * cols, 4 << 20),
     )
-    first = lax.ppermute(grad_out, "chan", ahead)
-    down, views = lax.optimization_barrier((grad_out, views))
-    up, far = first, []
-    for step in range(1, count // 2):
-        down = lax.ppermute(down, "chan", back)
-        up = lax.ppermute(up, "chan", ahead)
-        far += [down, up]
+    halves = [grad_out[: own_outs // 2], grad_out[own_outs // 2 :]]
+    steps = []
+    for step in range(1, count):
+        halves = [lax.ppermute(half, "chan", ahead) for half in halves]
+        steps.append(halves)
     lines = lambda *parts: call(
         lines_kernel,
-        jax.ShapeDtypeStruct((len(parts) * own_outs, cells), BF16),
+        jax.ShapeDtypeStruct((sum(part.shape[0] for part in parts), cells), BF16),
         *parts,
         scratch=(pltpu.VMEM((own_outs * rows, cols), F32),),
         cost=(1 << 20, 2 << 20),
     )
-    near_lines = lines(grad_out, first)
-    next_near_lines = lax.ppermute(near_lines, "depth", nearer)
     behind = lax.ppermute(odd, "depth", farther)
     behind_views = call(
         behind_views_kernel,
@@ -464,8 +357,9 @@
         behind,
         cost=(2 * 2 * cells * chans * 8 * cols, 2 << 20),
     )
-    far_lines = lines(*far)
-    next_far_lines = lax.ppermute(far_lines, "depth", nearer)
+    *steps[0], views = lax.optimization_barrier((*steps[0], views))
+    own_lines = [lines(grad_out, *steps[0])] + [lines(*step) for step in steps[1:]]
+    next_lines = [lax.ppermute(part, "depth", nearer) for part in own_lines]
     outs = channels // depth
     half_terms = jax.ShapeDtypeStruct((channels // 2, 32 * chans), F32)
     keep, send = call(
@@ -473,8 +367,7 @@
         (half_terms, half_terms),
         views,
         behind_views,
-        near_lines,
-        far_lines,
+        *own_lines,
         scratch=(
             pltpu.VMEM((channels, cells + cols), BF16),
             pltpu.VMEM((32 * chans, channels), F32),
@@ -496,10 +389,8 @@
         input_kernel,
         jax.ShapeDtypeStruct(volume.shape, BF16),
         taps,
-        next_near_lines,
-        next_far_lines,
-        near_lines,
-        far_lines,
+        *next_lines,
+        *own_lines,
         scratch=(
             pltpu.VMEM((18 * chans, cells + cols), F32),
             pltpu.VMEM((2, 256, cols), F32),
@@ -525,11 +416,10 @@
 
     def either(grad_out, volume, weight):
         fits = (
-            grad_out.shape[0] % 16 == 0
+            grad_out.shape[0] % 32 == 0
             and volume.shape[0] == 16
             and grad_out.shape[1] == 1
-            and ring % 2 == 0
-            and ring >= 4
+            and ring >= 2
             and depth & (depth - 1) == 0
             and depth % (2 * ring) == 0
         )

time: 44.6 us -> 57.9 us (1.30); the launches traced: 43.7 us -> 57.7 us
  Pallas kernels: 8.18 us -> 25.1 us
  waiting for transfers between devices: 11.6 us -> 9.84 us
  starting transfers between devices: 22 us -> 20.8 us
    pallas_call x8 -> x10, Pallas kernels: 8.18 us -> 25.1 us  [the longest x1 17 us: shards(): pl.pallas_call(odd_plane_kernel, out_shape=jax.ShapeDtypeStruct((chans, 1...]
    ppermute x1, waiting for transfers between devices: 4.76 us -> 0.01 us  [shards(): behind = lax.ppermute(odd, 'depth', farther)]
    ppermute x5 -> x9, waiting for transfers between devices: 4.99 us -> 7.41 us  [the longest x6 7.4 us: shards(): halves = [lax.ppermute(half, 'chan', ahead) for half in halves]]
    ppermute x5 -> x9, starting transfers between devices: 17.3 us -> 15.8 us  [the longest x6 13.8 us: shards(): halves = [lax.ppermute(half, 'chan', ahead) for half in halves]]
    ppermute x3, waiting for transfers between devices: 0.51 us -> 1.45 us  [shards(): lax.ppermute(term, 'depth', [(i, i ^ 2 * k + 2) for i in range(depth)])]
    ppermute x3, starting transfers between devices: 4.63 us -> 3.72 us  [shards(): lax.ppermute(term, 'depth', [(i, i ^ 2 * k + 2) for i in range(depth)])]
    ppermute x1, starting transfers between devices: 0.07 us -> 0.76 us  [shards(): other = lax.ppermute(send, 'depth', [(i, i ^ 1) for i in range(depth)])]
  transfers between devices with their start and end apart: 10 -> 14, of which waited for: 5 -> 7; matrix products, arithmetic and copies ran while one was open for 0% -> 0% of each run, Pallas kernels for 17% -> 13%
where the time goes in v3:
time: 57.9 us; the launch traced here: 57.7 us
  Pallas kernels  25.1 us (43%)
  starting transfers between devices  20.8 us (36%)
  waiting for transfers between devices  9.84 us (17%)
  local copies, waits for them, and re-layouts  1.27 us (2%)
  between operations  0.73 us (1%)
    pallas_call x1, Pallas kernels, shards(): pl.pallas_call(odd_plane_kernel, out_shape=jax.ShapeDtypeStruct((chans, 1...  17 us
    ppermute x6, starting transfers between devices, shards(): halves = [lax.ppermute(half, 'chan', ahead) for half in halves]  13.8 us
    pallas_call x9, Pallas kernels, call(): pl.pallas_call(kernel, out_shape=out_shape, in_specs=[VMEM] * len(args),...  8.15 us
    ppermute x6, waiting for transfers between devices, shards(): halves = [lax.ppermute(half, 'chan', ahead) for half in halves]  7.4 us
    ppermute x3, starting transfers between devices, shards(): lax.ppermute(term, 'depth', [(i, i ^ 2 * k + 2) for i in range(depth)])  3.72 us
    ppermute x3, starting transfers between devices, shards(): next_lines = [lax.ppermute(part, 'depth', nearer) for part in own_lines]  1.95 us
    ppermute x3, waiting for transfers between devices, shards(): lax.ppermute(term, 'depth', [(i, i ^ 2 * k + 2) for i in range(depth)])  1.45 us
    unnamed x6, local copies, waits for them, and re-layouts  1.23 us
  transfers between devices with their start and end apart: 14, of which 7 were waited for; matrix products, arithmetic and copies ran while one was open for 0% of the time, Pallas kernels for 13%

profile of v3, /device:TPU:0, one launch (start us, length us, event | category | flops | bytes accessed | tf_op | source)
XLA Modules:
  0.0 57.7 jit_solution(12925003389027397635)
XLA Ops:
  0.6 0.0 copy-start
  0.6 0.0 copy-start.2
  0.7 17.0 %shard_map.51 = bf16[16,1,64,256]{3,2,1,0:T(8,128)(2,1)} custom-call(bf16[16,2,64,256]{3,2,1,0:T(8,128)(2,1)} %volume_ref.1), custom_call_target="tpu_custom_call" | custom-call | bytes 1048576 | tf_op jit(solution)/shard_map/pallas_call | solution.py:322
  17.7 0.5 collective-permute-start.2
  18.2 0.0 copy-done.2
  18.2 2.6 %collective-permute-start = (bf16[16,1,32,128]{3,2,1,0:T(8,128)(2,1)S(1)}, bf16[16,1,32,128]{3,2,1,0:T(8,128)(2,1)S(1)}, u32[]{:S(2)}, u32[]{:S(2)}) collective-permute-start(bf16[16,1,32,128]{3,2,1,0:T(8,128)(2,1)S(1)} %get-tuple-element.29), channel_id=1, source_target_pairs={{0,1},{1,3},{3,2},{2,0},{4,5},{5,7},{7,6},{6,4},{8,9},{9,11},{11,1... | collective-permute-start | bytes 393224 | tf_op jit(solution)/shard_map/ppermute | solution.py:344
  20.8 2.6 %collective-permute-start.1 = (bf16[16,1,32,128]{3,2,1,0:T(8,128)(2,1)S(1)}, bf16[16,1,32,128]{3,2,1,0:T(8,128)(2,1)S(1)}, u32[]{:S(2)}, u32[]{:S(2)}) collective-permute-start(bf16[16,1,32,128]{3,2,1,0:T(8,128)(2,1)S(1)} %get-tuple-element.28), channel_id=1, source_target_pairs={{0,1},{1,3},{3,2},{2,0},{4,5},{5,7},{7,6},{6,4},{8,9},{9,11},{11,1... | collective-permute-start | bytes 393224 | tf_op jit(solution)/shard_map/ppermute | solution.py:344
  23.4 0.0 copy-done
  23.4 0.0 copy-start.1
  23.5 1.2 %copy-done.1 = bf16[16,2,64,256]{3,2,1,0:T(8,128)(2,1)S(1)} copy-done((bf16[16,2,64,256]{3,2,1,0:T(8,128)(2,1)S(1)}, bf16[16,2,64,256]{3,2,1,0:T(8,128)(2,1)}, u32[]{:S(2)}) %copy-start.1) | copy-done | bytes 1048600
  24.7 0.9 %shard_map.50 = (bf16[192,4096]{1,0:T(8,128)(2,1)S(1)}, bf16[288,256]{1,0:T(8,128)(2,1)S(1)}) custom-call(bf16[16,2,64,256]{3,2,1,0:T(8,128)(2,1)S(1)} %copy-done.1, bf16[27,16,128]{2,1,0:T(8,128)(2,1)S(1)} %constant_dynamic-slice_fusion.refs_1_), custom_call_target="tpu_custom_call" | custom-call | flops 536870912 | bytes 4194304 | tf_op jit(solution)/shard_map/pallas_call | solution.py:297
  25.6 0.0 collective-permute-done.refs_1_
  25.6 2.5 %collective-permute-done.1.refs_2_ = bf16[16,1,32,128]{3,2,1,0:T(8,128)(2,1)S(1)} collective-permute-done((bf16[16,1,32,128]{3,2,1,0:T(8,128)(2,1)S(1)}, bf16[16,1,32,128]{3,2,1,0:T(8,128)(2,1)S(1)}, u32[]{:S(2)}, u32[]{:S(2)}) %collective-permute-start.1) | collective-permute-done | bytes 131104 | tf_op jit(solution)/shard_map/ppermute | solution.py:344
  28.1 1.8 %collective-permute-start.3 = (bf16[16,1,32,128]{3,2,1,0:T(8,128)(2,1)S(1)}, bf16[16,1,32,128]{3,2,1,0:T(8,128)(2,1)S(1)}, u32[]{:S(2)}, u32[]{:S(2)}) collective-permute-start(bf16[16,1,32,128]{3,2,1,0:T(8,128)(2,1)S(1)} %collective-permute-done.refs_1_), channel_id=1, source_target_pairs={{0,1},{1,3},{3,2},{2,0},{4,5},{5,7},{7,6},{6,4},{8,9},{9,11},{11,1... | collective-permute-start | bytes 393224 | tf_op jit(solution)/shard_map/ppermute | solution.py:344
  29.9 3.1 %collective-permute-start.4 = (bf16[16,1,32,128]{3,2,1,0:T(8,128)(2,1)S(1)}, bf16[16,1,32,128]{3,2,1,0:T(8,128)(2,1)S(1)}, u32[]{:S(2)}, u32[]{:S(2)}) collective-permute-start(bf16[16,1,32,128]{3,2,1,0:T(8,128)(2,1)S(1)} %collective-permute-done.1.refs_2_), channel_id=1, source_target_pairs={{0,1},{1,3},{3,2},{2,0},{4,5},{5,7},{7,6},{6,4},{8,9},{9,11},{11,1... | collective-permute-start | bytes 393224 | tf_op jit(solution)/shard_map/ppermute | solution.py:344
  33.0 0.7 %shard_map.53.refs_2_.refs_3_ = bf16[64,4096]{1,0:T(8,128)(2,1)S(1)} custom-call(bf16[32,1,32,128]{3,2,1,0:T(8,128)(2,1)S(1)} %copy-done.2, bf16[16,1,32,128]{3,2,1,0:T(8,128)(2,1)S(1)} %collective-permute-done.refs_1_, bf16[16,1,32,128]{3,2,1,0:T(8,128)(2,1)S(1)} %collective-permute-done.1.refs_2_), custom_call_target="tpu_custom_call" | custom-call | flops 1048576 | bytes 2097152 | tf_op jit(solution)/shard_map/pallas_call | solution.py:297
  33.7 1.5 %collective-permute-start.8 = (bf16[64,4096]{1,0:T(8,128)(2,1)S(1)}, bf16[64,4096]{1,0:T(8,128)(2,1)S(1)}, u32[]{:S(2)}, u32[]{:S(2)}) collective-permute-start(bf16[64,4096]{1,0:T(8,128)(2,1)S(1)} %shard_map.53.refs_2_.refs_3_), channel_id=1, source_target_pairs={{4,0},{8,4},{12,8},{16,12},{20,16},{24,20},{28,24},{0,28},{5,1},{9... | collective-permute-start | bytes 1572872 | tf_op jit(solution)/shard_map/ppermute | solution.py:362
  35.1 0.3 collective-permute-done.3.refs_0_
  35.4 1.4 %collective-permute-start.5 = (bf16[16,1,32,128]{3,2,1,0:T(8,128)(2,1)S(1)}, bf16[16,1,32,128]{3,2,1,0:T(8,128)(2,1)S(1)}, u32[]{:S(2)}, u32[]{:S(2)}) collective-permute-start(bf16[16,1,32,128]{3,2,1,0:T(8,128)(2,1)S(1)} %collective-permute-done.3.refs_0_), channel_id=1, source_target_pairs={{0,1},{1,3},{3,2},{2,0},{4,5},{5,7},{7,6},{6,4},{8,9},{9,11},{11,1... | collective-permute-start | bytes 393224 | tf_op jit(solution)/shard_map/ppermute | solution.py:344
  36.8 1.1 %collective-permute-done.4.refs_1_ = bf16[16,1,32,128]{3,2,1,0:T(8,128)(2,1)S(1)} collective-permute-done((bf16[16,1,32,128]{3,2,1,0:T(8,128)(2,1)S(1)}, bf16[16,1,32,128]{3,2,1,0:T(8,128)(2,1)S(1)}, u32[]{:S(2)}, u32[]{:S(2)}) %collective-permute-start.4) | collective-permute-done | bytes 131104 | tf_op jit(solution)/shard_map/ppermute | solution.py:344
  37.9 2.3 %collective-permute-start.6 = (bf16[16,1,32,128]{3,2,1,0:T(8,128)(2,1)S(1)}, bf16[16,1,32,128]{3,2,1,0:T(8,128)(2,1)S(1)}, u32[]{:S(2)}, u32[]{:S(2)}) collective-permute-start(bf16[16,1,32,128]{3,2,1,0:T(8,128)(2,1)S(1)} %collective-permute-done.4.refs_1_), channel_id=1, source_target_pairs={{0,1},{1,3},{3,2},{2,0},{4,5},{5,7},{7,6},{6,4},{8,9},{9,11},{11,1... | collective-permute-start | bytes 393224 | tf_op jit(solution)/shard_map/ppermute | solution.py:344
  40.2 0.3 shard_map.54.refs_3_.refs_4_
  40.5 0.1 collective-permute-start.9
  40.6 0.7 %collective-permute-done.5.refs_0_ = bf16[16,1,32,128]{3,2,1,0:T(8,128)(2,1)S(1)} collective-permute-done((bf16[16,1,32,128]{3,2,1,0:T(8,128)(2,1)S(1)}, bf16[16,1,32,128]{3,2,1,0:T(8,128)(2,1)S(1)}, u32[]{:S(2)}, u32[]{:S(2)}) %collective-permute-start.5) | collective-permute-done | bytes 131104 | tf_op jit(solution)/shard_map/ppermute | solution.py:344
  41.3 2.8 %collective-permute-done.6.refs_1_ = bf16[16,1,32,128]{3,2,1,0:T(8,128)(2,1)S(1)} collective-permute-done((bf16[16,1,32,128]{3,2,1,0:T(8,128)(2,1)S(1)}, bf16[16,1,32,128]{3,2,1,0:T(8,128)(2,1)S(1)}, u32[]{:S(2)}, u32[]{:S(2)}) %collective-permute-start.6) | collective-permute-done | bytes 131104 | tf_op jit(solution)/shard_map/ppermute | solution.py:344
  44.1 0.3 shard_map.55.refs_4_.refs_5_
  44.5 0.4 collective-permute-start.10
  44.9 0.0 collective-permute-done.2.behind_ref
  44.9 0.1 shard_map.52.refs_1_
  45.0 2.2 %shard_map.56 = (f32[64,512]{1,0:T(8,128)S(1)}, f32[64,512]{1,0:T(8,128)S(1)}) custom-call(bf16[192,4096]{1,0:T(8,128)(2,1)S(1)} %get-tuple-element.16.refs_0_, bf16[96,4096]{1,0:T(8,128)(2,1)S(1)} %shard_map.52.refs_1_, bf16[64,4096]{1,0:T(8,128)(2,1)S(1)} %shard_map.53.refs_2_.refs_3_, bf16[32,4096]{1,0:T(8,128)(2,1)S(1)} %shard_map.54.refs_3_.refs_4_, ...), custom_call_target="tpu_custom_call" | custom-call | flops 452984832 | bytes 8388608 | tf_op jit(solution)/shard_map/pallas_call | solution.py:297
  47.1 0.8 %collective-permute-start.7 = (f32[64,512]{1,0:T(8,128)S(1)}, f32[64,512]{1,0:T(8,128)S(1)}, u32[]{:S(2)}, u32[]{:S(2)}) collective-permute-start(f32[64,512]{1,0:T(8,128)S(1)} %get-tuple-element.20), channel_id=1, source_target_pairs={{0,4},{4,0},{8,12},{12,8},{16,20},{20,16},{24,28},{28,24},{1,5},{5... | collective-permute-start | bytes 393224 | tf_op jit(solution)/shard_map/ppermute | solution.py:379
  47.9 1.0 %collective-permute-done.7.other_ref = f32[64,512]{1,0:T(8,128)S(1)} collective-permute-done((f32[64,512]{1,0:T(8,128)S(1)}, f32[64,512]{1,0:T(8,128)S(1)}, u32[]{:S(2)}, u32[]{:S(2)}) %collective-permute-start.7) | collective-permute-done | bytes 131104 | tf_op jit(solution)/shard_map/ppermute | solution.py:379
  48.9 2.1 %collective-permute-start.11 = (f32[16,512]{1,0:T(8,128)S(1)}, f32[16,512]{1,0:T(8,128)S(1)}, u32[]{:S(2)}, u32[]{:S(2)}) collective-permute-start(f32[16,512]{1,0:T(8,128)S(1)} %get-tuple-element.25), channel_id=1, source_target_pairs={{0,8},{4,12},{8,0},{12,4},{16,24},{20,28},{24,16},{28,20},{1,9},{5... | collective-permute-start | bytes 98312 | tf_op jit(solution)/shard_map/ppermute | solution.py:387
  51.0 1.1 %collective-permute-start.12 = (f32[16,512]{1,0:T(8,128)S(1)}, f32[16,512]{1,0:T(8,128)S(1)}, u32[]{:S(2)}, u32[]{:S(2)}) collective-permute-start(f32[16,512]{1,0:T(8,128)S(1)} %get-tuple-element.26), channel_id=1, source_target_pairs={{0,16},{4,20},{8,24},{12,28},{16,0},{20,4},{24,8},{28,12},{1,17},{... | collective-permute-start | bytes 98312 | tf_op jit(solution)/shard_map/ppermute | solution.py:387
  52.2 0.0 collective-permute-done.9.refs_1_
  52.2 0.5 collective-permute-start.13
  52.6 0.0 collective-permute-done.8.refs_0_
  52.6 0.0 collective-permute-done.10.refs_2_
  52.6 2.9 %shard_map.58 = bf16[16,2,64,256]{3,2,1,0:T(8,128)(2,1)} custom-call(bf16[288,256]{1,0:T(8,128)(2,1)S(1)} %get-tuple-element.22.taps_ref, bf16[64,4096]{1,0:T(8,128)(2,1)S(1)} %collective-permute-done.8.refs_0_, bf16[32,4096]{1,0:T(8,128)(2,1)S(1)} %collective-permute-done.9.refs_1_, bf16[32,4096]{1,0:T(8,128)(2,1)S(1)} %collective-permute-done.10.refs_2_, ...), custom_call_target="tpu_custom_call" | custom-call | flops 603979776 | bytes 8388608 | tf_op jit(solution)/shard_map/pallas_call | solution.py:297
  55.5 0.0 collective-permute-done.11.refs_1_
  55.5 0.0 collective-permute-done.12.refs_2_
  55.5 1.4 %collective-permute-done.13.refs_3_ = f32[16,512]{1,0:T(8,128)S(1)} collective-permute-done((f32[16,512]{1,0:T(8,128)S(1)}, f32[16,512]{1,0:T(8,128)S(1)}, u32[]{:S(2)}, u32[]{:S(2)}) %collective-permute-start.13) | collective-permute-done | bytes 32800 | tf_op jit(solution)/shard_map/ppermute | solution.py:387
  57.0 0.8 %shard_map.59 = f32[16,16,27]{2,1,0:T(8,128)} custom-call(f32[16,512]{1,0:T(8,128)S(1)} %get-tuple-element.24.refs_0_, f32[16,512]{1,0:T(8,128)S(1)} %collective-permute-done.11.refs_1_, f32[16,512]{1,0:T(8,128)S(1)} %collective-permute-done.12.refs_2_, f32[16,512]{1,0:T(8,128)S(1)} %collective-permute-done.13.refs_3_), custom_call_target="tpu_custom_call" | custom-call | flops 65536 | bytes 524288 | tf_op jit(solution)/shard_map/pallas_call | solution.py:297
  (3 shorter events, 0.0 us)
Async XLA Ops:
  0.6 22.8 %copy-start = (bf16[27,64,128]{2,1,0:T(8,128)(2,1)S(1)}, bf16[27,64,128]{2,1,0:T(8,128)(2,1)}, u32[]{:S(2)}) copy-start(bf16[27,64,128]{2,1,0:T(8,128)(2,1)} %param.5) | copy-start | bytes 1327108
  0.6 17.5 %copy-start.2 = (bf16[32,1,32,128]{3,2,1,0:T(8,128)(2,1)S(1)}, bf16[32,1,32,128]{3,2,1,0:T(8,128)(2,1)}, u32[]{:S(2)}) copy-start(bf16[32,1,32,128]{3,2,1,0:T(8,128)(2,1)} %refs_0_.3) | copy-start | bytes 786436
  17.7 27.2 %collective-permute-start.2 = (bf16[16,1,64,256]{3,2,1,0:T(8,128)(2,1)}, bf16[16,1,64,256]{3,2,1,0:T(8,128)(2,1)S(1)}, u32[]{:S(2)}, u32[]{:S(2)}) collective-permute-start(bf16[16,1,64,256]{3,2,1,0:T(8,128)(2,1)} %shard_map.51), channel_id=1, source_target_pairs={{0,4},{4,8},{8,12},{12,16},{16,20},{20,24},{24,28},{28,0},{1,5},{5... | collective-permute-start | bytes 1572872 | tf_op jit(solution)/shard_map/ppermute | solution.py:353
  18.2 7.4 %collective-permute-start = (bf16[16,1,32,128]{3,2,1,0:T(8,128)(2,1)S(1)}, bf16[16,1,32,128]{3,2,1,0:T(8,128)(2,1)S(1)}, u32[]{:S(2)}, u32[]{:S(2)}) collective-permute-start(bf16[16,1,32,128]{3,2,1,0:T(8,128)(2,1)S(1)} %get-tuple-element.29), channel_id=1, source_target_pairs={{0,1},{1,3},{3,2},{2,0},{4,5},{5,7},{7,6},{6,4},{8,9},{9,11},{11,1... | collective-permute-start | bytes 393224 | tf_op jit(solution)/shard_map/ppermute | solution.py:344
  20.8 7.3 %collective-permute-start.1 = (bf16[16,1,32,128]{3,2,1,0:T(8,128)(2,1)S(1)}, bf16[16,1,32,128]{3,2,1,0:T(8,128)(2,1)S(1)}, u32[]{:S(2)}, u32[]{:S(2)}) collective-permute-start(bf16[16,1,32,128]{3,2,1,0:T(8,128)(2,1)S(1)} %get-tuple-element.28), channel_id=1, source_target_pairs={{0,1},{1,3},{3,2},{2,0},{4,5},{5,7},{7,6},{6,4},{8,9},{9,11},{11,1... | collective-permute-start | bytes 393224 | tf_op jit(solution)/shard_map/ppermute | solution.py:344
  23.4 1.2 %copy-start.1 = (bf16[16,2,64,256]{3,2,1,0:T(8,128)(2,1)S(1)}, bf16[16,2,64,256]{3,2,1,0:T(8,128)(2,1)}, u32[]{:S(2)}) copy-start(bf16[16,2,64,256]{3,2,1,0:T(8,128)(2,1)} %volume_ref.1) | copy-start | bytes 3145732
  28.1 7.3 %collective-permute-start.3 = (bf16[16,1,32,128]{3,2,1,0:T(8,128)(2,1)S(1)}, bf16[16,1,32,128]{3,2,1,0:T(8,128)(2,1)S(1)}, u32[]{:S(2)}, u32[]{:S(2)}) collective-permute-start(bf16[16,1,32,128]{3,2,1,0:T(8,128)(2,1)S(1)} %collective-permute-done.refs_1_), channel_id=1, source_target_pairs={{0,1},{1,3},{3,2},{2,0},{4,5},{5,7},{7,6},{6,4},{8,9},{9,11},{11,1... | collective-permute-start | bytes 393224 | tf_op jit(solution)/shard_map/ppermute | solution.py:344
  29.9 8.1 %collective-permute-start.4 = (bf16[16,1,32,128]{3,2,1,0:T(8,128)(2,1)S(1)}, bf16[16,1,32,128]{3,2,1,0:T(8,128)(2,1)S(1)}, u32[]{:S(2)}, u32[]{:S(2)}) collective-permute-start(bf16[16,1,32,128]{3,2,1,0:T(8,128)(2,1)S(1)} %collective-permute-done.1.refs_2_), channel_id=1, source_target_pairs={{0,1},{1,3},{3,2},{2,0},{4,5},{5,7},{7,6},{6,4},{8,9},{9,11},{11,1... | collective-permute-start | bytes 393224 | tf_op jit(solution)/shard_map/ppermute | solution.py:344
  33.7 19.0 %collective-permute-start.8 = (bf16[64,4096]{1,0:T(8,128)(2,1)S(1)}, bf16[64,4096]{1,0:T(8,128)(2,1)S(1)}, u32[]{:S(2)}, u32[]{:S(2)}) collective-permute-start(bf16[64,4096]{1,0:T(8,128)(2,1)S(1)} %shard_map.53.refs_2_.refs_3_), channel_id=1, source_target_pairs={{4,0},{8,4},{12,8},{16,12},{20,16},{24,20},{28,24},{0,28},{5,1},{9... | collective-permute-start | bytes 1572872 | tf_op jit(solution)/shard_map/ppermute | solution.py:362
  35.4 5.9 %collective-permute-start.5 = (bf16[16,1,32,128]{3,2,1,0:T(8,128)(2,1)S(1)}, bf16[16,1,32,128]{3,2,1,0:T(8,128)(2,1)S(1)}, u32[]{:S(2)}, u32[]{:S(2)}) collective-permute-start(bf16[16,1,32,128]{3,2,1,0:T(8,128)(2,1)S(1)} %collective-permute-done.3.refs_0_), channel_id=1, source_target_pairs={{0,1},{1,3},{3,2},{2,0},{4,5},{5,7},{7,6},{6,4},{8,9},{9,11},{11,1... | collective-permute-start | bytes 393224 | tf_op jit(solution)/shard_map/ppermute | solution.py:344
  37.9 6.2 %collective-permute-start.6 = (bf16[16,1,32,128]{3,2,1,0:T(8,128)(2,1)S(1)}, bf16[16,1,32,128]{3,2,1,0:T(8,128)(2,1)S(1)}, u32[]{:S(2)}, u32[]{:S(2)}) collective-permute-start(bf16[16,1,32,128]{3,2,1,0:T(8,128)(2,1)S(1)} %collective-permute-done.4.refs_1_), channel_id=1, source_target_pairs={{0,1},{1,3},{3,2},{2,0},{4,5},{5,7},{7,6},{6,4},{8,9},{9,11},{11,1... | collective-permute-start | bytes 393224 | tf_op jit(solution)/shard_map/ppermute | solution.py:344
  40.5 11.6 %collective-permute-start.9 = (bf16[32,4096]{1,0:T(8,128)(2,1)S(1)}, bf16[32,4096]{1,0:T(8,128)(2,1)S(1)}, u32[]{:S(2)}, u32[]{:S(2)}) collective-permute-start(bf16[32,4096]{1,0:T(8,128)(2,1)S(1)} %shard_map.54.refs_3_.refs_4_), channel_id=1, source_target_pairs={{4,0},{8,4},{12,8},{16,12},{20,16},{24,20},{28,24},{0,28},{5,1},{9... | collective-permute-start | bytes 786440 | tf_op jit(solution)/shard_map/ppermute | solution.py:362
  44.5 8.2 %collective-permute-start.10 = (bf16[32,4096]{1,0:T(8,128)(2,1)S(1)}, bf16[32,4096]{1,0:T(8,128)(2,1)S(1)}, u32[]{:S(2)}, u32[]{:S(2)}) collective-permute-start(bf16[32,4096]{1,0:T(8,128)(2,1)S(1)} %shard_map.55.refs_4_.refs_5_), channel_id=1, source_target_pairs={{4,0},{8,4},{12,8},{16,12},{20,16},{24,20},{28,24},{0,28},{5,1},{9... | collective-permute-start | bytes 786440 | tf_op jit(solution)/shard_map/ppermute | solution.py:362
  47.1 1.7 %collective-permute-start.7 = (f32[64,512]{1,0:T(8,128)S(1)}, f32[64,512]{1,0:T(8,128)S(1)}, u32[]{:S(2)}, u32[]{:S(2)}) collective-permute-start(f32[64,512]{1,0:T(8,128)S(1)} %get-tuple-element.20), channel_id=1, source_target_pairs={{0,4},{4,0},{8,12},{12,8},{16,20},{20,16},{24,28},{28,24},{1,5},{5... | collective-permute-start | bytes 393224 | tf_op jit(solution)/shard_map/ppermute | solution.py:379
  48.9 6.6 %collective-permute-start.11 = (f32[16,512]{1,0:T(8,128)S(1)}, f32[16,512]{1,0:T(8,128)S(1)}, u32[]{:S(2)}, u32[]{:S(2)}) collective-permute-start(f32[16,512]{1,0:T(8,128)S(1)} %get-tuple-element.25), channel_id=1, source_target_pairs={{0,8},{4,12},{8,0},{12,4},{16,24},{20,28},{24,16},{28,20},{1,9},{5... | collective-permute-start | bytes 98312 | tf_op jit(solution)/shard_map/ppermute | solution.py:387
  51.0 4.5 %collective-permute-start.12 = (f32[16,512]{1,0:T(8,128)S(1)}, f32[16,512]{1,0:T(8,128)S(1)}, u32[]{:S(2)}, u32[]{:S(2)}) collective-permute-start(f32[16,512]{1,0:T(8,128)S(1)} %get-tuple-element.26), channel_id=1, source_target_pairs={{0,16},{4,20},{8,24},{12,28},{16,0},{20,4},{24,8},{28,12},{1,17},{... | collective-permute-start | bytes 98312 | tf_op jit(solution)/shard_map/ppermute | solution.py:387
  52.2 4.8 %collective-permute-start.13 = (f32[16,512]{1,0:T(8,128)S(1)}, f32[16,512]{1,0:T(8,128)S(1)}, u32[]{:S(2)}, u32[]{:S(2)}) collective-permute-start(f32[16,512]{1,0:T(8,128)S(1)} %get-tuple-element.27), channel_id=1, source_target_pairs={{0,24},{4,28},{8,16},{12,20},{16,8},{20,12},{24,0},{28,4},{1,25},{... | collective-permute-start | bytes 98312 | tf_op jit(solution)/shard_map/ppermute | solution.py:387

commit v4 on v3

--- a/solution.py
+++ b/solution.py
@@ -10,12 +10,7 @@
 F32 = jnp.float32
 BF16 = jnp.bfloat16
 VMEM = pl.BlockSpec(memory_space=pltpu.VMEM)
-HBM = pl.BlockSpec(memory_space=pltpu.HBM)
 LIMIT = 48 * 1024 * 1024
-
-
-def ring_order(count):
-    return [0] + list(range(1, count, 2)) + list(range(2, count, 2))[::-1]
 
 
 def matmul(left, right):
@@ -58,31 +53,20 @@
                 views_ref[lo : lo + chans, lanes] = views[e][at * chans : (at + 1) * chans]
 
 
-def owner_of(seats, slot):
-    here = lax.axis_index("chan")
-    owner = jnp.int32(seats[0][slot])
-    for chip in range(1, len(seats)):
-        owner = jnp.where(here == chip, seats[chip][slot], owner)
-    return owner
-
-
-def odd_plane_kernel(volume_ref, odd_ref, sem):
-    copy = pltpu.make_async_copy(volume_ref.at[:, 1:], odd_ref, sem)
-    copy.start()
-    copy.wait()
-
-
-def own_views_kernel(seats, depth, volume_ref, weight_ref, views_ref, taps_ref):
+def own_views_kernel(depth, volume_ref, weight_ref, views_ref, taps_ref, odd_ref):
     chans = volume_ref.shape[0]
     channels = weight_ref.shape[2]
+    odd_ref[...] = volume_ref[:, 1:]
     place_views(volume_ref.at[:, 0], views_ref, 0)
     place_views(volume_ref.at[:, 1], views_ref, 6 * chans)
-    part = channels // len(seats)
+    count = lax.axis_size("chan")
+    part = channels // count
+    here = lax.axis_index("chan")
     row = lax.broadcasted_iota(jnp.int32, (channels, channels), 0)
     col = lax.broadcasted_iota(jnp.int32, (channels, channels), 1)
     order = jnp.zeros((channels, channels), F32)
-    for slot in range(len(seats)):
-        moved = (owner_of(seats, slot) - slot) * part
+    for slot in range(count):
+        moved = ((here ^ slot) - slot) * part
         inside = (col >= slot * part) & (col < (slot + 1) * part)
         order = jnp.where(inside & (row == col + moved), 1.0, order)
     ordered = matmul(weight_ref[...].reshape(27 * chans, channels), order.astype(BF16)).astype(BF16)
@@ -125,7 +109,7 @@
 
 
 def weight_kernel(
-    seats, outs, own_ref, behind_ref, *refs
+    outs, own_ref, behind_ref, *refs
 ):
     *line_refs, keep_ref, send_ref, grads_ref, terms_ref, placed_ref = refs
     channels = grads_ref.shape[0]
@@ -149,10 +133,11 @@
     for c in range(chans):
         placed_ref[32 * c : 32 * c + 32, :] = terms_ref[pl.ds(c, 32, stride=chans), :]
     turned = placed_ref[...].T
-    part = channels // len(seats)
+    count = lax.axis_size("chan")
+    part = channels // count
     odd_core = lax.axis_index("depth") % 2 == 1
-    for slot in range(len(seats)):
-        start = owner_of(seats, slot) * (part // 2)
+    for slot in range(count):
+        start = (lax.axis_index("chan") ^ slot) * (part // 2)
         for at in range(0, part // 2, outs):
             lo = slot * part + 2 * at
             even, odd = turned[lo : lo + outs], turned[lo + outs : lo + 2 * outs]
@@ -312,37 +297,26 @@
     chans = volume.shape[0]
     channels = weight.shape[2]
     cells = rows * cols
-    order = ring_order(count)
-    ahead = [(order[i], order[(i + 1) % count]) for i in range(count)]
     farther = [(i, (i + 1) % depth) for i in range(depth)]
     nearer = [(b, a) for a, b in farther]
-    seats = [[order[(order.index(chip) - step) % count] for step in range(count)] for chip in range(count)]
 
     own_weight = lax.dynamic_slice_in_dim(weight, lax.axis_index("chan") * chans, chans, 1)
-    odd = pl.pallas_call(
-        odd_plane_kernel,
-        out_shape=jax.ShapeDtypeStruct((chans, 1, 2 * rows, 2 * cols), BF16),
-        in_specs=[HBM],
-        out_specs=HBM,
-        scratch_shapes=[pltpu.SemaphoreType.DMA],
-        compiler_params=pltpu.CompilerParams(vmem_limit_bytes=63 * 1024 * 1024),
-        cost_estimate=pl.CostEstimate(flops=0, bytes_accessed=1 << 20, transcendentals=0),
-    )(volume)
-    views, taps = call(
-        lambda *refs: own_views_kernel(seats, depth, *refs),
+    views, taps, odd = call(
+        lambda *refs: own_views_kernel(depth, *refs),
         (
             jax.ShapeDtypeStruct((12 * chans, cells), BF16),
             jax.ShapeDtypeStruct((18 * chans, 2 * channels), BF16),
+            jax.ShapeDtypeStruct((chans, 1, 2 * rows, 2 * cols), BF16),
         ),
         volume,
         own_weight,
         cost=(2 * 2 * 2 * cells * chans * 8 * cols, 4 << 20),
     )
-    halves = [grad_out[: own_outs // 2], grad_out[own_outs // 2 :]]
-    steps = []
-    for step in range(1, count):
-        halves = [lax.ppermute(half, "chan", ahead) for half in halves]
-        steps.append(halves)
+    got = {0: grad_out}
+    for mask in sorted(range(1, count), key=lambda mask: (mask & (mask - 1) > 0, -mask)):
+        low = mask & -mask
+        got[mask] = lax.ppermute(got[mask - low], "chan", [(i, i ^ low) for i in range(count)])
+    got[1], odd = lax.optimization_barrier((got[1], odd))
     lines = lambda *parts: call(
         lines_kernel,
         jax.ShapeDtypeStruct((sum(part.shape[0] for part in parts), cells), BF16),
@@ -357,13 +331,12 @@
         behind,
         cost=(2 * 2 * cells * chans * 8 * cols, 2 << 20),
     )
-    *steps[0], views = lax.optimization_barrier((*steps[0], views))
-    own_lines = [lines(grad_out, *steps[0])] + [lines(*step) for step in steps[1:]]
+    own_lines = [lines(got[0], got[1])] + [lines(got[mask]) for mask in range(2, count)]
     next_lines = [lax.ppermute(part, "depth", nearer) for part in own_lines]
     outs = channels // depth
     half_terms = jax.ShapeDtypeStruct((channels // 2, 32 * chans), F32)
     keep, send = call(
-        lambda *refs: weight_kernel(seats, outs, *refs),
+        lambda *refs: weight_kernel(outs, *refs),
         (half_terms, half_terms),
         views,
         behind_views,
@@ -420,6 +393,7 @@
             and volume.shape[0] == 16
             and grad_out.shape[1] == 1
             and ring >= 2
+            and ring & (ring - 1) == 0
             and depth & (depth - 1) == 0
             and depth % (2 * ring) == 0
         )

time: 57.9 us -> 40.4 us (0.70)
  Pallas kernels: 25.1 us -> 8.2 us
  starting transfers between devices: 20.8 us -> 14.1 us
  waiting for transfers between devices: 9.84 us -> 16 us
    pallas_call x1 -> x0, Pallas kernels: 17 us -> none  [shards(): pl.pallas_call(odd_plane_kernel, out_shape=jax.ShapeDtypeStruct((chans, 1...]
    ppermute x6 -> x3, starting transfers between devices: 13.8 us -> 6.11 us  [shards(): lax.ppermute(got[mask - low], 'chan', [(i, i ^ low) for i in range(count)])]
    ppermute x6 -> x3, waiting for transfers between devices: 7.4 us -> 13.1 us  [shards(): lax.ppermute(got[mask - low], 'chan', [(i, i ^ low) for i in range(count)])]
    ppermute x3, starting transfers between devices: 3.72 us -> 4.96 us  [shards(): lax.ppermute(term, 'depth', [(i, i ^ 2 * k + 2) for i in range(depth)])]
    ppermute x1, waiting for transfers between devices: 0.01 us -> 0.83 us  [shards(): behind = lax.ppermute(odd, 'depth', farther)]
    ppermute x3, starting transfers between devices: 1.95 us -> 2.72 us  [shards(): next_lines = [lax.ppermute(part, 'depth', nearer) for part in own_lines]]
  transfers between devices with their start and end apart: 14 -> 11, of which waited for: 7 -> 6; matrix products, arithmetic and copies ran while one was open for 0% -> 0% of each run, Pallas kernels for 13% -> 18%
where the time goes in v4:
time: 40.4 us; the launch traced here: 40.3 us
  waiting for transfers between devices  16 us (40%)
  starting transfers between devices  14.1 us (35%)
  Pallas kernels  8.2 us (20%)
  local copies, waits for them, and re-layouts  1.25 us (3%)
  between operations  0.72 us (2%)
    ppermute x3, waiting for transfers between devices, shards(): lax.ppermute(got[mask - low], 'chan', [(i, i ^ low) for i in range(count)])  13.1 us
    pallas_call x9, Pallas kernels, call(): pl.pallas_call(kernel, out_shape=out_shape, in_specs=[VMEM] * len(args),...  8.2 us
    ppermute x3, starting transfers between devices, shards(): lax.ppermute(got[mask - low], 'chan', [(i, i ^ low) for i in range(count)])  6.11 us
    ppermute x3, starting transfers between devices, shards(): lax.ppermute(term, 'depth', [(i, i ^ 2 * k + 2) for i in range(depth)])  4.96 us
    ppermute x3, starting transfers between devices, shards(): next_lines = [lax.ppermute(part, 'depth', nearer) for part in own_lines]  2.72 us
    unnamed x6, local copies, waits for them, and re-layouts  1.23 us
    ppermute x1, waiting for transfers between devices, shards(): other = lax.ppermute(send, 'depth', [(i, i ^ 1) for i in range(depth)])  1.12 us
    ppermute x3, waiting for transfers between devices, shards(): lax.ppermute(term, 'depth', [(i, i ^ 2 * k + 2) for i in range(depth)])  0.99 us
  transfers between devices with their start and end apart: 11, of which 6 were waited for; matrix products, arithmetic and copies ran while one was open for 0% of the time, Pallas kernels for 18%

profile of v4, /device:TPU:0, one launch (start us, length us, event | category | flops | bytes accessed | tf_op | source)
XLA Modules:
  0.0 40.3 jit_solution(4701756980076506231)
XLA Ops:
  0.6 0.0 copy-start
  0.6 0.0 copy-start.1
  0.7 3.1 %collective-permute-start = (bf16[32,1,32,128]{3,2,1,0:T(8,128)(2,1)}, bf16[32,1,32,128]{3,2,1,0:T(8,128)(2,1)S(1)}, u32[]{:S(2)}, u32[]{:S(2)}) collective-permute-start(bf16[32,1,32,128]{3,2,1,0:T(8,128)(2,1)} %refs_0_.3), channel_id=1, source_target_pairs={{0,1},{1,0},{2,3},{3,2},{4,5},{5,4},{6,7},{7,6},{8,9},{9,8},{10,11... | collective-permute-start | bytes 786440 | tf_op jit(solution)/shard_map/ppermute | solution.py:318
  3.7 2.6 %collective-permute-start.2 = (bf16[32,1,32,128]{3,2,1,0:T(8,128)(2,1)}, bf16[32,1,32,128]{3,2,1,0:T(8,128)(2,1)S(1)}, u32[]{:S(2)}, u32[]{:S(2)}) collective-permute-start(bf16[32,1,32,128]{3,2,1,0:T(8,128)(2,1)} %refs_0_.3), channel_id=1, source_target_pairs={{0,2},{1,3},{2,0},{3,1},{4,6},{5,7},{6,4},{7,5},{8,10},{9,11},{10,... | collective-permute-start | bytes 786440 | tf_op jit(solution)/shard_map/ppermute | solution.py:318
  6.3 0.0 copy-done
  6.4 0.0 copy-start.2
  6.4 1.2 %copy-done.2 = bf16[16,2,64,256]{3,2,1,0:T(8,128)(2,1)S(1)} copy-done((bf16[16,2,64,256]{3,2,1,0:T(8,128)(2,1)S(1)}, bf16[16,2,64,256]{3,2,1,0:T(8,128)(2,1)}, u32[]{:S(2)}) %copy-start.2) | copy-done | bytes 1048600
  7.6 0.9 %shard_map.50 = (bf16[192,4096]{1,0:T(8,128)(2,1)S(1)}, bf16[288,256]{1,0:T(8,128)(2,1)S(1)}, bf16[16,1,64,256]{3,2,1,0:T(8,128)(2,1)S(1)}) custom-call(bf16[16,2,64,256]{3,2,1,0:T(8,128)(2,1)S(1)} %copy-done.2, bf16[27,16,128]{2,1,0:T(8,128)(2,1)S(1)} %constant_dynamic-slice_fusion.refs_1_), custom_call_target="tpu_custom_call" | custom-call | flops 536870912 | bytes 4194304 | tf_op jit(solution)/shard_map/pallas_call | solution.py:282
  8.5 7.2 %collective-permute-done.refs_1_ = bf16[32,1,32,128]{3,2,1,0:T(8,128)(2,1)S(1)} collective-permute-done((bf16[32,1,32,128]{3,2,1,0:T(8,128)(2,1)}, bf16[32,1,32,128]{3,2,1,0:T(8,128)(2,1)S(1)}, u32[]{:S(2)}, u32[]{:S(2)}) %collective-permute-start) | collective-permute-done | bytes 262176 | tf_op jit(solution)/shard_map/ppermute | solution.py:318
  15.7 0.0 collective-permute-start.1
  15.7 2.6 %collective-permute-done.2.refs_0_ = bf16[32,1,32,128]{3,2,1,0:T(8,128)(2,1)S(1)} collective-permute-done((bf16[32,1,32,128]{3,2,1,0:T(8,128)(2,1)}, bf16[32,1,32,128]{3,2,1,0:T(8,128)(2,1)S(1)}, u32[]{:S(2)}, u32[]{:S(2)}) %collective-permute-start.2) | collective-permute-done | bytes 262176 | tf_op jit(solution)/shard_map/ppermute | solution.py:318
  18.3 0.4 %collective-permute-start.3 = (bf16[32,1,32,128]{3,2,1,0:T(8,128)(2,1)S(1)}, bf16[32,1,32,128]{3,2,1,0:T(8,128)(2,1)S(1)}, u32[]{:S(2)}, u32[]{:S(2)}) collective-permute-start(bf16[32,1,32,128]{3,2,1,0:T(8,128)(2,1)S(1)} %collective-permute-done.2.refs_0_), channel_id=1, source_target_pairs={{0,1},{1,0},{2,3},{3,2},{4,5},{5,4},{6,7},{7,6},{8,9},{9,8},{10,11... | collective-permute-start | bytes 786440 | tf_op jit(solution)/shard_map/ppermute | solution.py:318
  18.7 0.0 copy-done.1
  18.7 0.7 %shard_map.52.refs_2_.refs_3_ = bf16[64,4096]{1,0:T(8,128)(2,1)S(1)} custom-call(bf16[32,1,32,128]{3,2,1,0:T(8,128)(2,1)S(1)} %copy-done.1, bf16[32,1,32,128]{3,2,1,0:T(8,128)(2,1)S(1)} %collective-permute-done.refs_1_), custom_call_target="tpu_custom_call" | custom-call | flops 1048576 | bytes 2097152 | tf_op jit(solution)/shard_map/pallas_call | solution.py:282
  19.4 0.7 %collective-permute-start.5 = (bf16[64,4096]{1,0:T(8,128)(2,1)S(1)}, bf16[64,4096]{1,0:T(8,128)(2,1)S(1)}, u32[]{:S(2)}, u32[]{:S(2)}) collective-permute-start(bf16[64,4096]{1,0:T(8,128)(2,1)S(1)} %shard_map.52.refs_2_.refs_3_), channel_id=1, source_target_pairs={{4,0},{8,4},{12,8},{16,12},{20,16},{24,20},{28,24},{0,28},{5,1},{9... | collective-permute-start | bytes 1572872 | tf_op jit(solution)/shard_map/ppermute | solution.py:335
  20.1 0.3 shard_map.53.refs_3_.refs_4_
  20.5 1.9 %collective-permute-start.6 = (bf16[32,4096]{1,0:T(8,128)(2,1)S(1)}, bf16[32,4096]{1,0:T(8,128)(2,1)S(1)}, u32[]{:S(2)}, u32[]{:S(2)}) collective-permute-start(bf16[32,4096]{1,0:T(8,128)(2,1)S(1)} %shard_map.53.refs_3_.refs_4_), channel_id=1, source_target_pairs={{4,0},{8,4},{12,8},{16,12},{20,16},{24,20},{28,24},{0,28},{5,1},{9... | collective-permute-start | bytes 786440 | tf_op jit(solution)/shard_map/ppermute | solution.py:335
  22.4 3.3 %collective-permute-done.3.refs_0_ = bf16[32,1,32,128]{3,2,1,0:T(8,128)(2,1)S(1)} collective-permute-done((bf16[32,1,32,128]{3,2,1,0:T(8,128)(2,1)S(1)}, bf16[32,1,32,128]{3,2,1,0:T(8,128)(2,1)S(1)}, u32[]{:S(2)}, u32[]{:S(2)}) %collective-permute-start.3) | collective-permute-done | bytes 262176 | tf_op jit(solution)/shard_map/ppermute | solution.py:318
  25.7 0.3 shard_map.54.refs_4_.refs_5_
  26.1 0.1 collective-permute-start.7
  26.1 0.8 %collective-permute-done.1.behind_ref = bf16[16,1,64,256]{3,2,1,0:T(8,128)(2,1)S(1)} collective-permute-done((bf16[16,1,64,256]{3,2,1,0:T(8,128)(2,1)S(1)}, bf16[16,1,64,256]{3,2,1,0:T(8,128)(2,1)S(1)}, u32[]{:S(2)}, u32[]{:S(2)}) %collective-permute-start.1) | collective-permute-done | bytes 524320 | tf_op jit(solution)/shard_map/ppermute | solution.py:327
  27.0 0.1 shard_map.51.refs_1_
  27.0 2.2 %shard_map.55 = (f32[64,512]{1,0:T(8,128)S(1)}, f32[64,512]{1,0:T(8,128)S(1)}) custom-call(bf16[192,4096]{1,0:T(8,128)(2,1)S(1)} %get-tuple-element.15.refs_0_, bf16[96,4096]{1,0:T(8,128)(2,1)S(1)} %shard_map.51.refs_1_, bf16[64,4096]{1,0:T(8,128)(2,1)S(1)} %shard_map.52.refs_2_.refs_3_, bf16[32,4096]{1,0:T(8,128)(2,1)S(1)} %shard_map.53.refs_3_.refs_4_, ...), custom_call_target="tpu_custom_call" | custom-call | flops 452984832 | bytes 8388608 | tf_op jit(solution)/shard_map/pallas_call | solution.py:282
  29.2 0.3 collective-permute-start.4
  29.5 1.1 %collective-permute-done.4.other_ref = f32[64,512]{1,0:T(8,128)S(1)} collective-permute-done((f32[64,512]{1,0:T(8,128)S(1)}, f32[64,512]{1,0:T(8,128)S(1)}, u32[]{:S(2)}, u32[]{:S(2)}) %collective-permute-start.4) | collective-permute-done | bytes 131104 | tf_op jit(solution)/shard_map/ppermute | solution.py:352
  30.7 3.5 %collective-permute-start.10 = (f32[16,512]{1,0:T(8,128)S(1)}, f32[16,512]{1,0:T(8,128)S(1)}, u32[]{:S(2)}, u32[]{:S(2)}) collective-permute-start(f32[16,512]{1,0:T(8,128)S(1)} %get-tuple-element.27), channel_id=1, source_target_pairs={{0,24},{4,28},{8,16},{12,20},{16,8},{20,12},{24,0},{28,4},{1,25},{... | collective-permute-start | bytes 98312 | tf_op jit(solution)/shard_map/ppermute | solution.py:360
  34.2 1.4 %collective-permute-start.8 = (f32[16,512]{1,0:T(8,128)S(1)}, f32[16,512]{1,0:T(8,128)S(1)}, u32[]{:S(2)}, u32[]{:S(2)}) collective-permute-start(f32[16,512]{1,0:T(8,128)S(1)} %get-tuple-element.25), channel_id=1, source_target_pairs={{0,8},{4,12},{8,0},{12,4},{16,24},{20,28},{24,16},{28,20},{1,9},{5... | collective-permute-start | bytes 98312 | tf_op jit(solution)/shard_map/ppermute | solution.py:360
  35.6 0.0 collective-permute-done.6.refs_1_
  35.6 0.0 collective-permute-start.9
  35.6 0.0 collective-permute-done.5.refs_0_
  35.6 0.0 collective-permute-done.7.refs_2_
  35.6 2.9 %shard_map.57 = bf16[16,2,64,256]{3,2,1,0:T(8,128)(2,1)} custom-call(bf16[288,256]{1,0:T(8,128)(2,1)S(1)} %get-tuple-element.22.taps_ref, bf16[64,4096]{1,0:T(8,128)(2,1)S(1)} %collective-permute-done.5.refs_0_, bf16[32,4096]{1,0:T(8,128)(2,1)S(1)} %collective-permute-done.6.refs_1_, bf16[32,4096]{1,0:T(8,128)(2,1)S(1)} %collective-permute-done.7.refs_2_, ...), custom_call_target="tpu_custom_call" | custom-call | flops 603979776 | bytes 8388608 | tf_op jit(solution)/shard_map/pallas_call | solution.py:282
  38.5 0.0 collective-permute-done.10.refs_3_
  38.5 0.0 collective-permute-done.8.refs_1_
  38.6 1.0 %collective-permute-done.9.refs_2_ = f32[16,512]{1,0:T(8,128)S(1)} collective-permute-done((f32[16,512]{1,0:T(8,128)S(1)}, f32[16,512]{1,0:T(8,128)S(1)}, u32[]{:S(2)}, u32[]{:S(2)}) %collective-permute-start.9) | collective-permute-done | bytes 32800 | tf_op jit(solution)/shard_map/ppermute | solution.py:360
  39.5 0.8 %shard_map.58 = f32[16,16,27]{2,1,0:T(8,128)} custom-call(f32[16,512]{1,0:T(8,128)S(1)} %get-tuple-element.24.refs_0_, f32[16,512]{1,0:T(8,128)S(1)} %collective-permute-done.8.refs_1_, f32[16,512]{1,0:T(8,128)S(1)} %collective-permute-done.9.refs_2_, f32[16,512]{1,0:T(8,128)S(1)} %collective-permute-done.10.refs_3_), custom_call_target="tpu_custom_call" | custom-call | flops 65536 | bytes 524288 | tf_op jit(solution)/shard_map/pallas_call | solution.py:282
  (2 shorter events, 0.0 us)
Async XLA Ops:
  0.6 5.7 %copy-start = (bf16[27,64,128]{2,1,0:T(8,128)(2,1)S(1)}, bf16[27,64,128]{2,1,0:T(8,128)(2,1)}, u32[]{:S(2)}) copy-start(bf16[27,64,128]{2,1,0:T(8,128)(2,1)} %param.5) | copy-start | bytes 1327108
  0.6 18.1 %copy-start.1 = (bf16[32,1,32,128]{3,2,1,0:T(8,128)(2,1)S(1)}, bf16[32,1,32,128]{3,2,1,0:T(8,128)(2,1)}, u32[]{:S(2)}) copy-start(bf16[32,1,32,128]{3,2,1,0:T(8,128)(2,1)} %refs_0_.3) | copy-start | bytes 786436
  0.7 15.1 %collective-permute-start = (bf16[32,1,32,128]{3,2,1,0:T(8,128)(2,1)}, bf16[32,1,32,128]{3,2,1,0:T(8,128)(2,1)S(1)}, u32[]{:S(2)}, u32[]{:S(2)}) collective-permute-start(bf16[32,1,32,128]{3,2,1,0:T(8,128)(2,1)} %refs_0_.3), channel_id=1, source_target_pairs={{0,1},{1,0},{2,3},{3,2},{4,5},{5,4},{6,7},{7,6},{8,9},{9,8},{10,11... | collective-permute-start | bytes 786440 | tf_op jit(solution)/shard_map/ppermute | solution.py:318
  3.7 14.6 %collective-permute-start.2 = (bf16[32,1,32,128]{3,2,1,0:T(8,128)(2,1)}, bf16[32,1,32,128]{3,2,1,0:T(8,128)(2,1)S(1)}, u32[]{:S(2)}, u32[]{:S(2)}) collective-permute-start(bf16[32,1,32,128]{3,2,1,0:T(8,128)(2,1)} %refs_0_.3), channel_id=1, source_target_pairs={{0,2},{1,3},{2,0},{3,1},{4,6},{5,7},{6,4},{7,5},{8,10},{9,11},{10,... | collective-permute-start | bytes 786440 | tf_op jit(solution)/shard_map/ppermute | solution.py:318
  6.4 1.2 %copy-start.2 = (bf16[16,2,64,256]{3,2,1,0:T(8,128)(2,1)S(1)}, bf16[16,2,64,256]{3,2,1,0:T(8,128)(2,1)}, u32[]{:S(2)}) copy-start(bf16[16,2,64,256]{3,2,1,0:T(8,128)(2,1)} %refs_0_.2) | copy-start | bytes 3145732
  15.7 11.2 %collective-permute-start.1 = (bf16[16,1,64,256]{3,2,1,0:T(8,128)(2,1)S(1)}, bf16[16,1,64,256]{3,2,1,0:T(8,128)(2,1)S(1)}, u32[]{:S(2)}, u32[]{:S(2)}) collective-permute-start(bf16[16,1,64,256]{3,2,1,0:T(8,128)(2,1)S(1)} %get-tuple-element.17), channel_id=1, source_target_pairs={{0,4},{4,8},{8,12},{12,16},{16,20},{20,24},{24,28},{28,0},{1,5},{5... | collective-permute-start | bytes 1572872 | tf_op jit(solution)/shard_map/ppermute | solution.py:327
  18.3 7.4 %collective-permute-start.3 = (bf16[32,1,32,128]{3,2,1,0:T(8,128)(2,1)S(1)}, bf16[32,1,32,128]{3,2,1,0:T(8,128)(2,1)S(1)}, u32[]{:S(2)}, u32[]{:S(2)}) collective-permute-start(bf16[32,1,32,128]{3,2,1,0:T(8,128)(2,1)S(1)} %collective-permute-done.2.refs_0_), channel_id=1, source_target_pairs={{0,1},{1,0},{2,3},{3,2},{4,5},{5,4},{6,7},{7,6},{8,9},{9,8},{10,11... | collective-permute-start | bytes 786440 | tf_op jit(solution)/shard_map/ppermute | solution.py:318
  19.4 16.2 %collective-permute-start.5 = (bf16[64,4096]{1,0:T(8,128)(2,1)S(1)}, bf16[64,4096]{1,0:T(8,128)(2,1)S(1)}, u32[]{:S(2)}, u32[]{:S(2)}) collective-permute-start(bf16[64,4096]{1,0:T(8,128)(2,1)S(1)} %shard_map.52.refs_2_.refs_3_), channel_id=1, source_target_pairs={{4,0},{8,4},{12,8},{16,12},{20,16},{24,20},{28,24},{0,28},{5,1},{9... | collective-permute-start | bytes 1572872 | tf_op jit(solution)/shard_map/ppermute | solution.py:335
  20.5 15.1 %collective-permute-start.6 = (bf16[32,4096]{1,0:T(8,128)(2,1)S(1)}, bf16[32,4096]{1,0:T(8,128)(2,1)S(1)}, u32[]{:S(2)}, u32[]{:S(2)}) collective-permute-start(bf16[32,4096]{1,0:T(8,128)(2,1)S(1)} %shard_map.53.refs_3_.refs_4_), channel_id=1, source_target_pairs={{4,0},{8,4},{12,8},{16,12},{20,16},{24,20},{28,24},{0,28},{5,1},{9... | collective-permute-start | bytes 786440 | tf_op jit(solution)/shard_map/ppermute | solution.py:335
  26.1 9.6 %collective-permute-start.7 = (bf16[32,4096]{1,0:T(8,128)(2,1)S(1)}, bf16[32,4096]{1,0:T(8,128)(2,1)S(1)}, u32[]{:S(2)}, u32[]{:S(2)}) collective-permute-start(bf16[32,4096]{1,0:T(8,128)(2,1)S(1)} %shard_map.54.refs_4_.refs_5_), channel_id=1, source_target_pairs={{4,0},{8,4},{12,8},{16,12},{20,16},{24,20},{28,24},{0,28},{5,1},{9... | collective-permute-start | bytes 786440 | tf_op jit(solution)/shard_map/ppermute | solution.py:335
  29.2 1.4 %collective-permute-start.4 = (f32[64,512]{1,0:T(8,128)S(1)}, f32[64,512]{1,0:T(8,128)S(1)}, u32[]{:S(2)}, u32[]{:S(2)}) collective-permute-start(f32[64,512]{1,0:T(8,128)S(1)} %get-tuple-element.20), channel_id=1, source_target_pairs={{0,4},{4,0},{8,12},{12,8},{16,20},{20,16},{24,28},{28,24},{1,5},{5... | collective-permute-start | bytes 393224 | tf_op jit(solution)/shard_map/ppermute | solution.py:352
  30.7 7.9 %collective-permute-start.10 = (f32[16,512]{1,0:T(8,128)S(1)}, f32[16,512]{1,0:T(8,128)S(1)}, u32[]{:S(2)}, u32[]{:S(2)}) collective-permute-start(f32[16,512]{1,0:T(8,128)S(1)} %get-tuple-element.27), channel_id=1, source_target_pairs={{0,24},{4,28},{8,16},{12,20},{16,8},{20,12},{24,0},{28,4},{1,25},{... | collective-permute-start | bytes 98312 | tf_op jit(solution)/shard_map/ppermute | solution.py:360
  34.2 4.4 %collective-permute-start.8 = (f32[16,512]{1,0:T(8,128)S(1)}, f32[16,512]{1,0:T(8,128)S(1)}, u32[]{:S(2)}, u32[]{:S(2)}) collective-permute-start(f32[16,512]{1,0:T(8,128)S(1)} %get-tuple-element.25), channel_id=1, source_target_pairs={{0,8},{4,12},{8,0},{12,4},{16,24},{20,28},{24,16},{28,20},{1,9},{5... | collective-permute-start | bytes 98312 | tf_op jit(solution)/shard_map/ppermute | solution.py:360
  35.6 3.9 %collective-permute-start.9 = (f32[16,512]{1,0:T(8,128)S(1)}, f32[16,512]{1,0:T(8,128)S(1)}, u32[]{:S(2)}, u32[]{:S(2)}) collective-permute-start(f32[16,512]{1,0:T(8,128)S(1)} %get-tuple-element.26), channel_id=1, source_target_pairs={{0,16},{4,20},{8,24},{12,28},{16,0},{20,4},{24,8},{28,12},{1,17},{... | collective-permute-start | bytes 98312 | tf_op jit(solution)/shard_map/ppermute | solution.py:360

commit v5 on v4

--- a/solution.py
+++ b/solution.py
@@ -1,3 +1,4 @@
+import functools
 import math
 
 import jax
@@ -10,6 +11,7 @@
 F32 = jnp.float32
 BF16 = jnp.bfloat16
 VMEM = pl.BlockSpec(memory_space=pltpu.VMEM)
+HBM = pl.BlockSpec(memory_space=pltpu.HBM)
 LIMIT = 48 * 1024 * 1024
 
 
@@ -53,10 +55,9 @@
                 views_ref[lo : lo + chans, lanes] = views[e][at * chans : (at + 1) * chans]
 
 
-def own_views_kernel(depth, volume_ref, weight_ref, views_ref, taps_ref, odd_ref):
+def own_views_kernel(depth, volume_ref, weight_ref, views_ref, even_ref, odd_ref):
     chans = volume_ref.shape[0]
     channels = weight_ref.shape[2]
-    odd_ref[...] = volume_ref[:, 1:]
     place_views(volume_ref.at[:, 0], views_ref, 0)
     place_views(volume_ref.at[:, 1], views_ref, 6 * chans)
     count = lax.axis_size("chan")
@@ -71,13 +72,12 @@
         order = jnp.where(inside & (row == col + moved), 1.0, order)
     ordered = matmul(weight_ref[...].reshape(27 * chans, channels), order.astype(BF16)).astype(BF16)
     beyond = jnp.where(lax.axis_index("depth") == depth - 1, 0.0, 1.0).astype(BF16)
-    zero = jnp.zeros((chans, channels), BF16)
     for k, e in enumerate((1, 2, 0)):
         for b in range(3):
             pick = lambda a: ordered[(9 * a + 3 * b + e) * chans : (9 * a + 3 * b + e + 1) * chans]
-            for plane, line in enumerate(((zero, pick(1)), (pick(0) * beyond, pick(2)))):
-                lo = ((3 * plane + k) * 3 + b) * chans
-                taps_ref[lo : lo + chans, :] = jnp.concatenate(line, axis=1)
+            lo = (3 * k + b) * chans
+            even_ref[lo : lo + chans, :] = pick(1)
+            odd_ref[lo : lo + chans, :] = jnp.concatenate([pick(0) * beyond, pick(2)], axis=1)
 
 
 def behind_views_kernel(behind_ref, views_ref):
@@ -85,7 +85,7 @@
 
     @pl.when(jnp.logical_not(first))
     def _():
-        place_views(behind_ref.at[:, 0], views_ref, 0)
+        place_views(behind_ref.at[:, 1], views_ref, 0)
 
     @pl.when(first)
     def _():
@@ -109,22 +109,29 @@
 
 
 def weight_kernel(
-    outs, own_ref, behind_ref, *refs
+    outs, cols, chunk, own_ref, behind_ref, *refs
 ):
-    *line_refs, keep_ref, send_ref, grads_ref, terms_ref, placed_ref = refs
-    channels = grads_ref.shape[0]
+    *line_refs, keep_ref, send_ref, terms_ref, placed_ref = refs
+    channels = terms_ref.shape[1]
     chans = behind_ref.shape[0] // 6
     cells = own_ref.shape[1]
-    cols = grads_ref.shape[1] - cells
-    at = 0
-    for ref in line_refs:
-        grads_ref[at : at + ref.shape[0], :cells] = ref[...]
-        at += ref.shape[0]
-    grads_ref[:, cells:] = jnp.zeros((channels, cols), BF16)
-    both = jnp.concatenate([grads_ref[:, :cells], grads_ref[:, cols:]], axis=0)
     contract = (((1,), (1,)), ((), ()))
-    for a, (ref, at) in enumerate(((behind_ref, 0), (own_ref, 0), (own_ref, 6 * chans))):
-        terms = lax.dot_general(ref[at : at + 6 * chans], both, contract, preferred_element_type=F32)
+
+    def grads(lo, hi):
+        return jnp.concatenate([ref[:, lo:hi] for ref in line_refs], axis=0)
+
+    sums = None
+    for lo in range(0, cells, chunk):
+        hi = lo + chunk
+        below = grads(lo + cols, min(hi + cols, cells))
+        if hi == cells:
+            below = jnp.concatenate([below, jnp.zeros((channels, cols), BF16)], axis=1)
+        both = jnp.concatenate([grads(lo, hi), below], axis=0)
+        views = jnp.concatenate([behind_ref[:, lo:hi], own_ref[:, lo:hi]], axis=0)
+        part = lax.dot_general(views, both, contract, preferred_element_type=F32)
+        sums = part if sums is None else sums + part
+    for a in range(3):
+        terms = sums[6 * a * chans : 6 * (a + 1) * chans]
         even, odd = terms[: 3 * chans, :channels], terms[3 * chans :]
         for b, block in enumerate((odd[:, channels:], even, odd[:, :channels])):
             lo = (9 * a + 3 * b) * chans
@@ -154,42 +161,49 @@
         out_ref[...] = keep_ref[place, :] + other_ref[place, :]
 
 
-def input_kernel(taps_ref, *refs):
-    *line_refs, out_ref, cells_ref, lines_ref = refs
-    chans, _, rows, cols = out_ref.shape
+def input_kernel(plane, *refs):
+    taps_ref, *line_refs, out_ref, cells_ref, lines_ref, rows_ref, sems = refs
+    chans, rows, cols = rows_ref.shape
     half = cols // 2
     grid_cells = half * rows // 2
-    grads = [ref[...] for ref in line_refs]
-    cells_ref[:, :grid_cells] = matmul(taps_ref[...], jnp.concatenate(grads, axis=0))
+    grads = jnp.concatenate([ref[...] for ref in line_refs], axis=0)
+    cells_ref[:, :grid_cells] = matmul(taps_ref[...], grads)
     cells_ref[:, grid_cells:] = jnp.zeros((cells_ref.shape[0], half), F32)
     group = 256 // chans
     weave = one_hot(cols, cols, lambda row, col: col == 2 * (row & (half - 1)) + row // half)
     inner = lax.broadcasted_iota(jnp.int32, (chans, half), 1) < half - 1
 
-    def cells(plane, kind, b, r):
-        lo = ((3 * plane + kind) * 3 + b) * chans
+    def cells(kind, b, r):
+        lo = (3 * kind + b) * chans
         return cells_ref[lo : lo + chans, r * half : (r + 1) * half]
 
-    for plane in range(2):
-        for start in range(0, rows, group):
-            pieces = []
-            for row in range(start, start + group):
-                r = row // 2
-                if row % 2 == 0:
-                    even, odd, next_odd = [cells(plane, kind, 1, r) for kind in range(3)]
-                else:
-                    even, odd, next_odd = [
-                        cells(plane, kind, 0, r + 1) + cells(plane, kind, 2, r) for kind in range(3)
-                    ]
-                odd = odd + jnp.where(inner, pltpu.roll(next_odd, half - 1, 1), 0.0)
-                pieces.append(jnp.concatenate([even, odd], axis=1).astype(BF16))
-            woven = matmul(jnp.concatenate(pieces, axis=0), weave)
-            for side in range(2):
-                lanes = slice(side * half, (side + 1) * half)
-                lines_ref[side] = woven[:, lanes]
-                for c in range(chans):
-                    line = lines_ref[side, pl.ds(c, group, stride=chans), :].astype(BF16)
-                    out_ref[c, plane, start : start + group, lanes] = line
+    copies = []
+    for start in range(0, rows, group):
+        pieces = []
+        for row in range(start, start + group):
+            r = row // 2
+            if row % 2 == 0:
+                even, odd, next_odd = [cells(kind, 1, r) for kind in range(3)]
+            else:
+                even, odd, next_odd = [cells(kind, 0, r + 1) + cells(kind, 2, r) for kind in range(3)]
+            odd = odd + jnp.where(inner, pltpu.roll(next_odd, half - 1, 1), 0.0)
+            pieces.append(jnp.concatenate([even, odd], axis=1).astype(BF16))
+        woven = matmul(jnp.concatenate(pieces, axis=0), weave)
+        for side in range(2):
+            lanes = slice(side * half, (side + 1) * half)
+            lines_ref[side] = woven[:, lanes]
+            for c in range(chans):
+                line = lines_ref[side, pl.ds(c, group, stride=chans), :].astype(BF16)
+                rows_ref[c, start : start + group, lanes] = line
+        place = pl.ds(start, group)
+        copies.append(
+            pltpu.make_async_copy(
+                rows_ref.at[:, place], out_ref.at[:, plane, place], sems.at[start // group]
+            )
+        )
+        copies[-1].start()
+    for copy in copies:
+        copy.wait()
 
 
 def total_kernel(scale, *refs):
@@ -301,12 +315,12 @@
     nearer = [(b, a) for a, b in farther]
 
     own_weight = lax.dynamic_slice_in_dim(weight, lax.axis_index("chan") * chans, chans, 1)
-    views, taps, odd = call(
+    views, even_taps, odd_taps = call(
         lambda *refs: own_views_kernel(depth, *refs),
         (
             jax.ShapeDtypeStruct((12 * chans, cells), BF16),
-            jax.ShapeDtypeStruct((18 * chans, 2 * channels), BF16),
-            jax.ShapeDtypeStruct((chans, 1, 2 * rows, 2 * cols), BF16),
+            jax.ShapeDtypeStruct((9 * chans, channels), BF16),
+            jax.ShapeDtypeStruct((9 * chans, 2 * channels), BF16),
         ),
         volume,
         own_weight,
@@ -316,7 +330,6 @@
     for mask in sorted(range(1, count), key=lambda mask: (mask & (mask - 1) > 0, -mask)):
         low = mask & -mask
         got[mask] = lax.ppermute(got[mask - low], "chan", [(i, i ^ low) for i in range(count)])
-    got[1], odd = lax.optimization_barrier((got[1], odd))
     lines = lambda *parts: call(
         lines_kernel,
         jax.ShapeDtypeStruct((sum(part.shape[0] for part in parts), cells), BF16),
@@ -324,25 +337,25 @@
         scratch=(pltpu.VMEM((own_outs * rows, cols), F32),),
         cost=(1 << 20, 2 << 20),
     )
-    behind = lax.ppermute(odd, "depth", farther)
+    behind = lax.ppermute(volume, "depth", farther)
     behind_views = call(
         behind_views_kernel,
         jax.ShapeDtypeStruct((6 * chans, cells), BF16),
         behind,
         cost=(2 * 2 * cells * chans * 8 * cols, 2 << 20),
     )
+    got[1], views, behind_views = lax.optimization_barrier((got[1], views, behind_views))
     own_lines = [lines(got[0], got[1])] + [lines(got[mask]) for mask in range(2, count)]
     next_lines = [lax.ppermute(part, "depth", nearer) for part in own_lines]
     outs = channels // depth
     half_terms = jax.ShapeDtypeStruct((channels // 2, 32 * chans), F32)
     keep, send = call(
-        lambda *refs: weight_kernel(outs, *refs),
+        lambda *refs: weight_kernel(outs, cols, 4 * cols, *refs),
         (half_terms, half_terms),
         views,
         behind_views,
         *own_lines,
         scratch=(
-            pltpu.VMEM((channels, cells + cols), BF16),
             pltpu.VMEM((32 * chans, channels), F32),
             pltpu.VMEM((32 * chans, channels), F32),
         ),
@@ -350,6 +363,29 @@
     )
     chips = depth // 2
     other = lax.ppermute(send, "depth", [(i, i ^ 1) for i in range(depth)])
+    def input_plane(plane, taps, lines, before):
+        kernel = functools.partial(input_kernel, plane)
+        earlier = [] if before is None else [before]
+        return pl.pallas_call(
+            kernel if before is None else lambda before, *refs: kernel(*refs),
+            out_shape=jax.ShapeDtypeStruct(volume.shape, BF16),
+            in_specs=[HBM] * len(earlier) + [VMEM] * (1 + len(lines)),
+            out_specs=HBM,
+            input_output_aliases={} if before is None else {0: 0},
+            scratch_shapes=(
+                pltpu.VMEM((9 * chans, cells + cols), F32),
+                pltpu.VMEM((2, 256, cols), F32),
+                pltpu.VMEM((chans, 2 * rows, 2 * cols), BF16),
+                pltpu.SemaphoreType.DMA((2 * rows * chans // 256,)),
+            ),
+            compiler_params=pltpu.CompilerParams(vmem_limit_bytes=LIMIT),
+            cost_estimate=pl.CostEstimate(
+                flops=2 * 9 * chans * taps.shape[1] * cells, bytes_accessed=4 << 20, transcendentals=0
+            ),
+        )(*earlier, taps, *lines)
+
+    half_grad = input_plane(0, even_taps, own_lines, None)
+    other, half_grad = lax.optimization_barrier((other, half_grad))
     own_terms, *terms = call(
         pair_kernel,
         [jax.ShapeDtypeStruct((outs, 32 * chans), F32)] * chips,
@@ -358,18 +394,7 @@
         cost=(1 << 16, 1 << 19),
     )
     terms = [lax.ppermute(term, "depth", [(i, i ^ (2 * k + 2)) for i in range(depth)]) for k, term in enumerate(terms)]
-    input_grad = call(
-        input_kernel,
-        jax.ShapeDtypeStruct(volume.shape, BF16),
-        taps,
-        *next_lines,
-        *own_lines,
-        scratch=(
-            pltpu.VMEM((18 * chans, cells + cols), F32),
-            pltpu.VMEM((2, 256, cols), F32),
-        ),
-        cost=(2 * 18 * chans * 2 * channels * cells, 8 << 20),
-    )
+    input_grad = input_plane(1, odd_taps, next_lines + own_lines, half_grad)
     own_terms, input_grad = lax.optimization_barrier((own_terms, input_grad))
     scale = 1.0 / math.sqrt(depth * cells)
     weight_grad = call(

time: 40.4 us -> 38.1 us (0.943)
  waiting for transfers between devices: 16 us -> 13.8 us
  Pallas kernels: 8.2 us -> 7.51 us
  starting transfers between devices: 14.1 us -> 14.6 us
    pallas_call x9 -> x8, Pallas kernels: 8.2 us -> 4.05 us  [call(): pl.pallas_call(kernel, out_shape=out_shape, in_specs=[VMEM] * len(args),...]
    pallas_call x0 -> x2, Pallas kernels: none -> 3.47 us  [input_plane(): pl.pallas_call(kernel if before is None else lambda before, *refs: kernel...]
    ppermute x3, waiting for transfers between devices: 13.1 us -> 11.7 us  [shards(): lax.ppermute(got[mask - low], 'chan', [(i, i ^ low) for i in range(count)])]
    ppermute x3, starting transfers between devices: 4.96 us -> 3.57 us  [shards(): lax.ppermute(term, 'depth', [(i, i ^ 2 * k + 2) for i in range(depth)])]
    ppermute x3, waiting for transfers between devices: 0.01 us -> 1.14 us  [shards(): next_lines = [lax.ppermute(part, 'depth', nearer) for part in own_lines]]
    ppermute x1, waiting for transfers between devices: 1.12 us -> 0.01 us  [shards(): other = lax.ppermute(send, 'depth', [(i, i ^ 1) for i in range(depth)])]
    ppermute x3, starting transfers between devices: 6.11 us -> 7.05 us  [shards(): lax.ppermute(got[mask - low], 'chan', [(i, i ^ low) for i in range(count)])]
    ppermute x1, waiting for transfers between devices: 0.83 us -> 0.01 us  [shards(): behind = lax.ppermute(volume, 'depth', farther)]
  transfers between devices with their start and end apart: 11 -> 11, of which waited for: 6 -> 4; matrix products, arithmetic and copies ran while one was open for 0% -> 0% of each run, Pallas kernels for 18% -> 18%
where the time goes in v5:
time: 38.1 us; the launch traced here: 37.9 us
  starting transfers between devices  14.6 us (38%)
  waiting for transfers between devices  13.8 us (36%)
  Pallas kernels  7.51 us (20%)
  local copies, waits for them, and re-layouts  1.25 us (3%)
  between operations  0.75 us (2%)
    ppermute x3, waiting for transfers between devices, shards(): lax.ppermute(got[mask - low], 'chan', [(i, i ^ low) for i in range(count)])  11.7 us
    ppermute x3, starting transfers between devices, shards(): lax.ppermute(got[mask - low], 'chan', [(i, i ^ low) for i in range(count)])  7.05 us
    pallas_call x8, Pallas kernels, call(): pl.pallas_call(kernel, out_shape=out_shape, in_specs=[VMEM] * len(args),...  4.05 us
    ppermute x3, starting transfers between devices, shards(): lax.ppermute(term, 'depth', [(i, i ^ 2 * k + 2) for i in range(depth)])  3.57 us
    pallas_call x2, Pallas kernels, input_plane(): pl.pallas_call(kernel if before is None else lambda before, *refs: kernel...  3.47 us
    ppermute x3, starting transfers between devices, shards(): next_lines = [lax.ppermute(part, 'depth', nearer) for part in own_lines]  3.25 us
    unnamed x6, local copies, waits for them, and re-layouts  1.23 us
    ppermute x3, waiting for transfers between devices, shards(): next_lines = [lax.ppermute(part, 'depth', nearer) for part in own_lines]  1.14 us
  transfers between devices with their start and end apart: 11, of which 4 were waited for; matrix products, arithmetic and copies ran while one was open for 0% of the time, Pallas kernels for 18%

profile of v5, /device:TPU:0, one launch (start us, length us, event | category | flops | bytes accessed | tf_op | source)
XLA Modules:
  0.0 37.9 jit_solution(11385033094569651501)
XLA Ops:
  0.6 0.0 copy-start
  0.6 0.5 %collective-permute-start.1 = (bf16[16,2,64,256]{3,2,1,0:T(8,128)(2,1)}, bf16[16,2,64,256]{3,2,1,0:T(8,128)(2,1)S(1)}, u32[]{:S(2)}, u32[]{:S(2)}) collective-permute-start(bf16[16,2,64,256]{3,2,1,0:T(8,128)(2,1)} %refs_0_.2), channel_id=1, source_target_pairs={{0,4},{4,8},{8,12},{12,16},{16,20},{20,24},{24,28},{28,0},{1,5},{5... | collective-permute-start | bytes 3145736 | tf_op jit(solution)/shard_map/ppermute | solution.py:340
  1.1 3.7 %collective-permute-start.2 = (bf16[32,1,32,128]{3,2,1,0:T(8,128)(2,1)}, bf16[32,1,32,128]{3,2,1,0:T(8,128)(2,1)S(1)}, u32[]{:S(2)}, u32[]{:S(2)}) collective-permute-start(bf16[32,1,32,128]{3,2,1,0:T(8,128)(2,1)} %refs_0_.3), channel_id=1, source_target_pairs={{0,2},{1,3},{2,0},{3,1},{4,6},{5,7},{6,4},{7,5},{8,10},{9,11},{10,... | collective-permute-start | bytes 786440 | tf_op jit(solution)/shard_map/ppermute | solution.py:332
  4.8 1.6 %collective-permute-start = (bf16[32,1,32,128]{3,2,1,0:T(8,128)(2,1)}, bf16[32,1,32,128]{3,2,1,0:T(8,128)(2,1)S(1)}, u32[]{:S(2)}, u32[]{:S(2)}) collective-permute-start(bf16[32,1,32,128]{3,2,1,0:T(8,128)(2,1)} %refs_0_.3), channel_id=1, source_target_pairs={{0,1},{1,0},{2,3},{3,2},{4,5},{5,4},{6,7},{7,6},{8,9},{9,8},{10,11... | collective-permute-start | bytes 786440 | tf_op jit(solution)/shard_map/ppermute | solution.py:332
  6.4 0.0 copy-done
  6.4 0.0 copy-start.2
  6.4 1.2 %copy-done.2 = bf16[16,2,64,256]{3,2,1,0:T(8,128)(2,1)S(1)} copy-done((bf16[16,2,64,256]{3,2,1,0:T(8,128)(2,1)S(1)}, bf16[16,2,64,256]{3,2,1,0:T(8,128)(2,1)}, u32[]{:S(2)}) %copy-start.2) | copy-done | bytes 1048600
  7.6 0.0 copy-start.1
  7.6 0.9 %shard_map.50 = (bf16[192,4096]{1,0:T(8,128)(2,1)S(1)}, bf16[144,128]{1,0:T(8,128)(2,1)S(1)}, bf16[144,256]{1,0:T(8,128)(2,1)S(1)}) custom-call(bf16[16,2,64,256]{3,2,1,0:T(8,128)(2,1)S(1)} %copy-done.2, bf16[27,16,128]{2,1,0:T(8,128)(2,1)S(1)} %constant_dynamic-slice_fusion.refs_1_), custom_call_target="tpu_custom_call" | custom-call | flops 536870912 | bytes 4194304 | tf_op jit(solution)/shard_map/pallas_call | solution.py:296
  8.5 8.5 %collective-permute-done.2.refs_0_ = bf16[32,1,32,128]{3,2,1,0:T(8,128)(2,1)S(1)} collective-permute-done((bf16[32,1,32,128]{3,2,1,0:T(8,128)(2,1)}, bf16[32,1,32,128]{3,2,1,0:T(8,128)(2,1)S(1)}, u32[]{:S(2)}, u32[]{:S(2)}) %collective-permute-start.2) | collective-permute-done | bytes 262176 | tf_op jit(solution)/shard_map/ppermute | solution.py:332
  17.0 1.8 %collective-permute-start.3 = (bf16[32,1,32,128]{3,2,1,0:T(8,128)(2,1)S(1)}, bf16[32,1,32,128]{3,2,1,0:T(8,128)(2,1)S(1)}, u32[]{:S(2)}, u32[]{:S(2)}) collective-permute-start(bf16[32,1,32,128]{3,2,1,0:T(8,128)(2,1)S(1)} %collective-permute-done.2.refs_0_), channel_id=1, source_target_pairs={{0,1},{1,0},{2,3},{3,2},{4,5},{5,4},{6,7},{7,6},{8,9},{9,8},{10,11... | collective-permute-start | bytes 786440 | tf_op jit(solution)/shard_map/ppermute | solution.py:332
  18.9 0.0 collective-permute-done.1.behind_ref
  18.9 0.1 shard_map.51.refs_1_
  18.9 0.0 collective-permute-done.refs_1_
  18.9 0.0 copy-done.1
  18.9 0.7 %shard_map.52.refs_2_.refs_1_.refs_4_ = bf16[64,4096]{1,0:T(8,128)(2,1)S(1)} custom-call(bf16[32,1,32,128]{3,2,1,0:T(8,128)(2,1)S(1)} %copy-done.1, bf16[32,1,32,128]{3,2,1,0:T(8,128)(2,1)S(1)} %collective-permute-done.refs_1_), custom_call_target="tpu_custom_call" | custom-call | flops 1048576 | bytes 2097152 | tf_op jit(solution)/shard_map/pallas_call | solution.py:296
  19.6 2.1 %collective-permute-start.5 = (bf16[64,4096]{1,0:T(8,128)(2,1)S(1)}, bf16[64,4096]{1,0:T(8,128)(2,1)S(1)}, u32[]{:S(2)}, u32[]{:S(2)}) collective-permute-start(bf16[64,4096]{1,0:T(8,128)(2,1)S(1)} %shard_map.52.refs_2_.refs_1_.refs_4_), channel_id=1, source_target_pairs={{4,0},{8,4},{12,8},{16,12},{20,16},{24,20},{28,24},{0,28},{5,1},{9... | collective-permute-start | bytes 1572872 | tf_op jit(solution)/shard_map/ppermute | solution.py:349
  21.7 0.3 shard_map.53.refs_3_.refs_2_.refs_5_
  22.0 0.8 %collective-permute-start.6 = (bf16[32,4096]{1,0:T(8,128)(2,1)S(1)}, bf16[32,4096]{1,0:T(8,128)(2,1)S(1)}, u32[]{:S(2)}, u32[]{:S(2)}) collective-permute-start(bf16[32,4096]{1,0:T(8,128)(2,1)S(1)} %shard_map.53.refs_3_.refs_2_.refs_5_), channel_id=1, source_target_pairs={{4,0},{8,4},{12,8},{16,12},{20,16},{24,20},{28,24},{0,28},{5,1},{9... | collective-permute-start | bytes 786440 | tf_op jit(solution)/shard_map/ppermute | solution.py:349
  22.8 3.2 %collective-permute-done.3.refs_0_ = bf16[32,1,32,128]{3,2,1,0:T(8,128)(2,1)S(1)} collective-permute-done((bf16[32,1,32,128]{3,2,1,0:T(8,128)(2,1)S(1)}, bf16[32,1,32,128]{3,2,1,0:T(8,128)(2,1)S(1)}, u32[]{:S(2)}, u32[]{:S(2)}) %collective-permute-start.3) | collective-permute-done | bytes 262176 | tf_op jit(solution)/shard_map/ppermute | solution.py:332
  25.9 0.3 shard_map.54.refs_4_.refs_3_.refs_6_
  26.3 0.4 %collective-permute-start.7 = (bf16[32,4096]{1,0:T(8,128)(2,1)S(1)}, bf16[32,4096]{1,0:T(8,128)(2,1)S(1)}, u32[]{:S(2)}, u32[]{:S(2)}) collective-permute-start(bf16[32,4096]{1,0:T(8,128)(2,1)S(1)} %shard_map.54.refs_4_.refs_3_.refs_6_), channel_id=1, source_target_pairs={{4,0},{8,4},{12,8},{16,12},{20,16},{24,20},{28,24},{0,28},{5,1},{9... | collective-permute-start | bytes 786440 | tf_op jit(solution)/shard_map/ppermute | solution.py:349
  26.7 0.9 %shard_map.55 = (f32[64,512]{1,0:T(8,128)S(1)}, f32[64,512]{1,0:T(8,128)S(1)}) custom-call(bf16[192,4096]{1,0:T(8,128)(2,1)S(1)} %get-tuple-element.19.refs_0_, bf16[96,4096]{1,0:T(8,128)(2,1)S(1)} %shard_map.51.refs_1_, bf16[64,4096]{1,0:T(8,128)(2,1)S(1)} %shard_map.52.refs_2_.refs_1_.refs_4_, bf16[32,4096]{1,0:T(8,128)(2,1)S(1)} %shard_map.53.refs_3_.refs_2_.refs_5_, ...), custom_call_target="tpu_custom_call" | custom-call | flops 452984832 | bytes 8388608 | tf_op jit(solution)/shard_map/pallas_call | solution.py:296
  27.7 0.2 collective-permute-start.4
  27.9 1.7 %shard_map.56.before = bf16[16,2,64,256]{3,2,1,0:T(8,128)(2,1)} custom-call(bf16[144,128]{1,0:T(8,128)(2,1)S(1)} %get-tuple-element.24.refs_0_, bf16[64,4096]{1,0:T(8,128)(2,1)S(1)} %shard_map.52.refs_2_.refs_1_.refs_4_, bf16[32,4096]{1,0:T(8,128)(2,1)S(1)} %shard_map.53.refs_3_.refs_2_.refs_5_, bf16[32,4096]{1,0:T(8,128)(2,1)S(1)} %shard_map.54.refs_4_.refs_3_.refs_6_), custom_call_target="tpu_custom_call" | custom-call | flops 150994944 | bytes 4194304 | tf_op jit(solution)/shard_map/pallas_call | solution.py:369
  29.6 0.0 collective-permute-done.4.other_ref
  29.7 1.9 %collective-permute-start.8 = (f32[16,512]{1,0:T(8,128)S(1)}, f32[16,512]{1,0:T(8,128)S(1)}, u32[]{:S(2)}, u32[]{:S(2)}) collective-permute-start(f32[16,512]{1,0:T(8,128)S(1)} %get-tuple-element.31), channel_id=1, source_target_pairs={{0,8},{4,12},{8,0},{12,4},{16,24},{20,28},{24,16},{28,20},{1,9},{5... | collective-permute-start | bytes 98312 | tf_op jit(solution)/shard_map/ppermute | solution.py:396
  31.5 0.8 %collective-permute-start.9 = (f32[16,512]{1,0:T(8,128)S(1)}, f32[16,512]{1,0:T(8,128)S(1)}, u32[]{:S(2)}, u32[]{:S(2)}) collective-permute-start(f32[16,512]{1,0:T(8,128)S(1)} %get-tuple-element.32), channel_id=1, source_target_pairs={{0,16},{4,20},{8,24},{12,28},{16,0},{20,4},{24,8},{28,12},{1,17},{... | collective-permute-start | bytes 98312 | tf_op jit(solution)/shard_map/ppermute | solution.py:396
  32.4 0.0 collective-permute-done.6.refs_2_
  32.4 0.9 %collective-permute-start.10 = (f32[16,512]{1,0:T(8,128)S(1)}, f32[16,512]{1,0:T(8,128)S(1)}, u32[]{:S(2)}, u32[]{:S(2)}) collective-permute-start(f32[16,512]{1,0:T(8,128)S(1)} %get-tuple-element.33), channel_id=1, source_target_pairs={{0,24},{4,28},{8,16},{12,20},{16,8},{20,12},{24,0},{28,4},{1,25},{... | collective-permute-start | bytes 98312 | tf_op jit(solution)/shard_map/ppermute | solution.py:396
  33.2 1.1 %collective-permute-done.7.refs_3_ = bf16[32,4096]{1,0:T(8,128)(2,1)S(1)} collective-permute-done((bf16[32,4096]{1,0:T(8,128)(2,1)S(1)}, bf16[32,4096]{1,0:T(8,128)(2,1)S(1)}, u32[]{:S(2)}, u32[]{:S(2)}) %collective-permute-start.7) | collective-permute-done | bytes 262176 | tf_op jit(solution)/shard_map/ppermute | solution.py:349
  34.4 0.0 collective-permute-done.5.refs_1_
  34.4 1.7 %shard_map.58 = bf16[16,2,64,256]{3,2,1,0:T(8,128)(2,1)} custom-call(bf16[16,2,64,256]{3,2,1,0:T(8,128)(2,1)} %shard_map.56.before, bf16[144,256]{1,0:T(8,128)(2,1)S(1)} %get-tuple-element.28.refs_0_, bf16[64,4096]{1,0:T(8,128)(2,1)S(1)} %collective-permute-done.5.refs_1_, ...), custom_call_target="tpu_custom_call", output_to_operand_aliasing={{}: (0, {})} | custom-call | flops 301989888 | bytes 4194304 | tf_op jit(solution)/shard_map/pallas_call | solution.py:369
  36.1 0.0 collective-permute-done.8.refs_1_
  36.1 0.0 collective-permute-done.9.refs_2_
  36.1 1.0 %collective-permute-done.10.refs_3_ = f32[16,512]{1,0:T(8,128)S(1)} collective-permute-done((f32[16,512]{1,0:T(8,128)S(1)}, f32[16,512]{1,0:T(8,128)S(1)}, u32[]{:S(2)}, u32[]{:S(2)}) %collective-permute-start.10) | collective-permute-done | bytes 32800 | tf_op jit(solution)/shard_map/ppermute | solution.py:396
  37.2 0.8 %shard_map.59 = f32[16,16,27]{2,1,0:T(8,128)} custom-call(f32[16,512]{1,0:T(8,128)S(1)} %get-tuple-element.30.refs_0_, f32[16,512]{1,0:T(8,128)S(1)} %collective-permute-done.8.refs_1_, f32[16,512]{1,0:T(8,128)S(1)} %collective-permute-done.9.refs_2_, f32[16,512]{1,0:T(8,128)S(1)} %collective-permute-done.10.refs_3_), custom_call_target="tpu_custom_call" | custom-call | flops 65536 | bytes 524288 | tf_op jit(solution)/shard_map/pallas_call | solution.py:296
  (2 shorter events, 0.0 us)
Async XLA Ops:
  0.6 5.8 %copy-start = (bf16[27,64,128]{2,1,0:T(8,128)(2,1)S(1)}, bf16[27,64,128]{2,1,0:T(8,128)(2,1)}, u32[]{:S(2)}) copy-start(bf16[27,64,128]{2,1,0:T(8,128)(2,1)} %param.5) | copy-start | bytes 1327108
  0.6 18.2 %collective-permute-start.1 = (bf16[16,2,64,256]{3,2,1,0:T(8,128)(2,1)}, bf16[16,2,64,256]{3,2,1,0:T(8,128)(2,1)S(1)}, u32[]{:S(2)}, u32[]{:S(2)}) collective-permute-start(bf16[16,2,64,256]{3,2,1,0:T(8,128)(2,1)} %refs_0_.2), channel_id=1, source_target_pairs={{0,4},{4,8},{8,12},{12,16},{16,20},{20,24},{24,28},{28,0},{1,5},{5... | collective-permute-start | bytes 3145736 | tf_op jit(solution)/shard_map/ppermute | solution.py:340
  1.1 15.9 %collective-permute-start.2 = (bf16[32,1,32,128]{3,2,1,0:T(8,128)(2,1)}, bf16[32,1,32,128]{3,2,1,0:T(8,128)(2,1)S(1)}, u32[]{:S(2)}, u32[]{:S(2)}) collective-permute-start(bf16[32,1,32,128]{3,2,1,0:T(8,128)(2,1)} %refs_0_.3), channel_id=1, source_target_pairs={{0,2},{1,3},{2,0},{3,1},{4,6},{5,7},{6,4},{7,5},{8,10},{9,11},{10,... | collective-permute-start | bytes 786440 | tf_op jit(solution)/shard_map/ppermute | solution.py:332
  4.8 14.1 %collective-permute-start = (bf16[32,1,32,128]{3,2,1,0:T(8,128)(2,1)}, bf16[32,1,32,128]{3,2,1,0:T(8,128)(2,1)S(1)}, u32[]{:S(2)}, u32[]{:S(2)}) collective-permute-start(bf16[32,1,32,128]{3,2,1,0:T(8,128)(2,1)} %refs_0_.3), channel_id=1, source_target_pairs={{0,1},{1,0},{2,3},{3,2},{4,5},{5,4},{6,7},{7,6},{8,9},{9,8},{10,11... | collective-permute-start | bytes 786440 | tf_op jit(solution)/shard_map/ppermute | solution.py:332
  6.4 1.2 %copy-start.2 = (bf16[16,2,64,256]{3,2,1,0:T(8,128)(2,1)S(1)}, bf16[16,2,64,256]{3,2,1,0:T(8,128)(2,1)}, u32[]{:S(2)}) copy-start(bf16[16,2,64,256]{3,2,1,0:T(8,128)(2,1)} %refs_0_.2) | copy-start | bytes 3145732
  7.6 11.3 %copy-start.1 = (bf16[32,1,32,128]{3,2,1,0:T(8,128)(2,1)S(1)}, bf16[32,1,32,128]{3,2,1,0:T(8,128)(2,1)}, u32[]{:S(2)}) copy-start(bf16[32,1,32,128]{3,2,1,0:T(8,128)(2,1)} %refs_0_.3) | copy-start | bytes 786436
  17.0 8.9 %collective-permute-start.3 = (bf16[32,1,32,128]{3,2,1,0:T(8,128)(2,1)S(1)}, bf16[32,1,32,128]{3,2,1,0:T(8,128)(2,1)S(1)}, u32[]{:S(2)}, u32[]{:S(2)}) collective-permute-start(bf16[32,1,32,128]{3,2,1,0:T(8,128)(2,1)S(1)} %collective-permute-done.2.refs_0_), channel_id=1, source_target_pairs={{0,1},{1,0},{2,3},{3,2},{4,5},{5,4},{6,7},{7,6},{8,9},{9,8},{10,11... | collective-permute-start | bytes 786440 | tf_op jit(solution)/shard_map/ppermute | solution.py:332
  19.6 14.8 %collective-permute-start.5 = (bf16[64,4096]{1,0:T(8,128)(2,1)S(1)}, bf16[64,4096]{1,0:T(8,128)(2,1)S(1)}, u32[]{:S(2)}, u32[]{:S(2)}) collective-permute-start(bf16[64,4096]{1,0:T(8,128)(2,1)S(1)} %shard_map.52.refs_2_.refs_1_.refs_4_), channel_id=1, source_target_pairs={{4,0},{8,4},{12,8},{16,12},{20,16},{24,20},{28,24},{0,28},{5,1},{9... | collective-permute-start | bytes 1572872 | tf_op jit(solution)/shard_map/ppermute | solution.py:349
  22.0 10.3 %collective-permute-start.6 = (bf16[32,4096]{1,0:T(8,128)(2,1)S(1)}, bf16[32,4096]{1,0:T(8,128)(2,1)S(1)}, u32[]{:S(2)}, u32[]{:S(2)}) collective-permute-start(bf16[32,4096]{1,0:T(8,128)(2,1)S(1)} %shard_map.53.refs_3_.refs_2_.refs_5_), channel_id=1, source_target_pairs={{4,0},{8,4},{12,8},{16,12},{20,16},{24,20},{28,24},{0,28},{5,1},{9... | collective-permute-start | bytes 786440 | tf_op jit(solution)/shard_map/ppermute | solution.py:349
  26.3 8.1 %collective-permute-start.7 = (bf16[32,4096]{1,0:T(8,128)(2,1)S(1)}, bf16[32,4096]{1,0:T(8,128)(2,1)S(1)}, u32[]{:S(2)}, u32[]{:S(2)}) collective-permute-start(bf16[32,4096]{1,0:T(8,128)(2,1)S(1)} %shard_map.54.refs_4_.refs_3_.refs_6_), channel_id=1, source_target_pairs={{4,0},{8,4},{12,8},{16,12},{20,16},{24,20},{28,24},{0,28},{5,1},{9... | collective-permute-start | bytes 786440 | tf_op jit(solution)/shard_map/ppermute | solution.py:349
  27.7 1.9 %collective-permute-start.4 = (f32[64,512]{1,0:T(8,128)S(1)}, f32[64,512]{1,0:T(8,128)S(1)}, u32[]{:S(2)}, u32[]{:S(2)}) collective-permute-start(f32[64,512]{1,0:T(8,128)S(1)} %get-tuple-element.23), channel_id=1, source_target_pairs={{0,4},{4,0},{8,12},{12,8},{16,20},{20,16},{24,28},{28,24},{1,5},{5... | collective-permute-start | bytes 393224 | tf_op jit(solution)/shard_map/ppermute | solution.py:365
  29.7 6.5 %collective-permute-start.8 = (f32[16,512]{1,0:T(8,128)S(1)}, f32[16,512]{1,0:T(8,128)S(1)}, u32[]{:S(2)}, u32[]{:S(2)}) collective-permute-start(f32[16,512]{1,0:T(8,128)S(1)} %get-tuple-element.31), channel_id=1, source_target_pairs={{0,8},{4,12},{8,0},{12,4},{16,24},{20,28},{24,16},{28,20},{1,9},{5... | collective-permute-start | bytes 98312 | tf_op jit(solution)/shard_map/ppermute | solution.py:396
  31.5 4.6 %collective-permute-start.9 = (f32[16,512]{1,0:T(8,128)S(1)}, f32[16,512]{1,0:T(8,128)S(1)}, u32[]{:S(2)}, u32[]{:S(2)}) collective-permute-start(f32[16,512]{1,0:T(8,128)S(1)} %get-tuple-element.32), channel_id=1, source_target_pairs={{0,16},{4,20},{8,24},{12,28},{16,0},{20,4},{24,8},{28,12},{1,17},{... | collective-permute-start | bytes 98312 | tf_op jit(solution)/shard_map/ppermute | solution.py:396
  32.4 4.8 %collective-permute-start.10 = (f32[16,512]{1,0:T(8,128)S(1)}, f32[16,512]{1,0:T(8,128)S(1)}, u32[]{:S(2)}, u32[]{:S(2)}) collective-permute-start(f32[16,512]{1,0:T(8,128)S(1)} %get-tuple-element.33), channel_id=1, source_target_pairs={{0,24},{4,28},{8,16},{12,20},{16,8},{20,12},{24,0},{28,4},{1,25},{... | collective-permute-start | bytes 98312 | tf_op jit(solution)/shard_map/ppermute | solution.py:396

commit v6 on v5

--- a/solution.py
+++ b/solution.py
@@ -94,9 +94,11 @@
 
 def place_lines(part, out_ref, at, wide_ref):
     outs, _, rows, cols = part.shape
-    wide_ref[: outs * rows, :] = part[...].reshape(outs * rows, cols).astype(F32)
+    pitch = rows + 8
+    for o in range(outs):
+        wide_ref[o * pitch : o * pitch + rows, :] = part[o, 0].astype(F32)
     for row in range(rows):
-        line = wide_ref[pl.ds(row, outs, stride=rows), :].astype(BF16)
+        line = wide_ref[pl.ds(row, outs, stride=pitch), :].astype(BF16)
         out_ref[at : at + outs, row * cols : (row + 1) * cols] = line
 
 
@@ -120,6 +122,7 @@
     def grads(lo, hi):
         return jnp.concatenate([ref[:, lo:hi] for ref in line_refs], axis=0)
 
+    pitch = chans + 8
     sums = None
     for lo in range(0, cells, chunk):
         hi = lo + chunk
@@ -134,11 +137,12 @@
         terms = sums[6 * a * chans : 6 * (a + 1) * chans]
         even, odd = terms[: 3 * chans, :channels], terms[3 * chans :]
         for b, block in enumerate((odd[:, channels:], even, odd[:, :channels])):
-            lo = (9 * a + 3 * b) * chans
-            terms_ref[lo : lo + 3 * chans, :] = block
-    terms_ref[27 * chans :, :] = jnp.zeros((5 * chans, channels), F32)
+            for e in range(3):
+                lo = (9 * a + 3 * b + e) * pitch
+                terms_ref[lo : lo + chans, :] = block[e * chans : (e + 1) * chans]
+    terms_ref[27 * pitch :, :] = jnp.zeros((5 * pitch, channels), F32)
     for c in range(chans):
-        placed_ref[32 * c : 32 * c + 32, :] = terms_ref[pl.ds(c, 32, stride=chans), :]
+        placed_ref[32 * c : 32 * c + 32, :] = terms_ref[pl.ds(c, 32, stride=pitch), :]
     turned = placed_ref[...].T
     count = lax.axis_size("chan")
     part = channels // count
@@ -170,6 +174,7 @@
     cells_ref[:, :grid_cells] = matmul(taps_ref[...], grads)
     cells_ref[:, grid_cells:] = jnp.zeros((cells_ref.shape[0], half), F32)
     group = 256 // chans
+    pitch = chans + 8
     weave = one_hot(cols, cols, lambda row, col: col == 2 * (row & (half - 1)) + row // half)
     inner = lax.broadcasted_iota(jnp.int32, (chans, half), 1) < half - 1
 
@@ -191,9 +196,10 @@
         woven = matmul(jnp.concatenate(pieces, axis=0), weave)
         for side in range(2):
             lanes = slice(side * half, (side + 1) * half)
-            lines_ref[side] = woven[:, lanes]
+            for at in range(group):
+                lines_ref[side, at * pitch : at * pitch + chans] = woven[at * chans : (at + 1) * chans, lanes]
             for c in range(chans):
-                line = lines_ref[side, pl.ds(c, group, stride=chans), :].astype(BF16)
+                line = lines_ref[side, pl.ds(c, group, stride=pitch), :].astype(BF16)
                 rows_ref[c, start : start + group, lanes] = line
         place = pl.ds(start, group)
         copies.append(
@@ -329,24 +335,31 @@
     got = {0: grad_out}
     for mask in sorted(range(1, count), key=lambda mask: (mask & (mask - 1) > 0, -mask)):
         low = mask & -mask
+        if mask == 3:
+            got[2], views = lax.optimization_barrier((got[2], views))
         got[mask] = lax.ppermute(got[mask - low], "chan", [(i, i ^ low) for i in range(count)])
     lines = lambda *parts: call(
         lines_kernel,
         jax.ShapeDtypeStruct((sum(part.shape[0] for part in parts), cells), BF16),
         *parts,
-        scratch=(pltpu.VMEM((own_outs * rows, cols), F32),),
+        scratch=(pltpu.VMEM((own_outs * (rows + 8), cols), F32),),
         cost=(1 << 20, 2 << 20),
     )
     behind = lax.ppermute(volume, "depth", farther)
+    next_own = lax.ppermute(grad_out, "depth", nearer)
     behind_views = call(
         behind_views_kernel,
         jax.ShapeDtypeStruct((6 * chans, cells), BF16),
         behind,
         cost=(2 * 2 * cells * chans * 8 * cols, 2 << 20),
     )
-    got[1], views, behind_views = lax.optimization_barrier((got[1], views, behind_views))
-    own_lines = [lines(got[0], got[1])] + [lines(got[mask]) for mask in range(2, count)]
-    next_lines = [lax.ppermute(part, "depth", nearer) for part in own_lines]
+    first_lines, next_first_lines = lines(grad_out), lines(next_own)
+    got[1], views, behind_views, first_lines, next_first_lines = lax.optimization_barrier(
+        (got[1], views, behind_views, first_lines, next_first_lines)
+    )
+    later_lines = [lines(*[got[mask] for mask in range(1, count - 1)]), lines(got[count - 1])]
+    own_lines = [first_lines] + later_lines
+    next_lines = [next_first_lines] + [lax.ppermute(part, "depth", nearer) for part in later_lines]
     outs = channels // depth
     half_terms = jax.ShapeDtypeStruct((channels // 2, 32 * chans), F32)
     keep, send = call(
@@ -356,13 +369,11 @@
         behind_views,
         *own_lines,
         scratch=(
-            pltpu.VMEM((32 * chans, channels), F32),
+            pltpu.VMEM((32 * (chans + 8), channels), F32),
             pltpu.VMEM((32 * chans, channels), F32),
         ),
         cost=(2 * 27 * chans * channels * cells, 8 << 20),
     )
-    chips = depth // 2
-    other = lax.ppermute(send, "depth", [(i, i ^ 1) for i in range(depth)])
     def input_plane(plane, taps, lines, before):
         kernel = functools.partial(input_kernel, plane)
         earlier = [] if before is None else [before]
@@ -374,7 +385,7 @@
             input_output_aliases={} if before is None else {0: 0},
             scratch_shapes=(
                 pltpu.VMEM((9 * chans, cells + cols), F32),
-                pltpu.VMEM((2, 256, cols), F32),
+                pltpu.VMEM((2, 256 // chans * (chans + 8), cols), F32),
                 pltpu.VMEM((chans, 2 * rows, 2 * cols), BF16),
                 pltpu.SemaphoreType.DMA((2 * rows * chans // 256,)),
             ),
@@ -384,11 +395,12 @@
             ),
         )(*earlier, taps, *lines)
 
+    other = lax.ppermute(send, "depth", [(i, i ^ 1) for i in range(depth)])
     half_grad = input_plane(0, even_taps, own_lines, None)
     other, half_grad = lax.optimization_barrier((other, half_grad))
     own_terms, *terms = call(
         pair_kernel,
-        [jax.ShapeDtypeStruct((outs, 32 * chans), F32)] * chips,
+        [jax.ShapeDtypeStruct((outs, 32 * chans), F32)] * (depth // 2),
         keep,
         other,
         cost=(1 << 16, 1 << 19),
@@ -398,7 +410,7 @@
     own_terms, input_grad = lax.optimization_barrier((own_terms, input_grad))
     scale = 1.0 / math.sqrt(depth * cells)
     weight_grad = call(
-        lambda *refs: total_kernel(scale, *refs),
+        functools.partial(total_kernel, scale),
         jax.ShapeDtypeStruct((chans, outs, 27), F32),
         own_terms,
         *terms,
@@ -417,7 +429,7 @@
             grad_out.shape[0] % 32 == 0
             and volume.shape[0] == 16
             and grad_out.shape[1] == 1
-            and ring >= 2
+            and ring >= 4
             and ring & (ring - 1) == 0
             and depth & (depth - 1) == 0
             and depth % (2 * ring) == 0

time: 38.1 us -> 38.1 us (level)
  Pallas kernels: 7.51 us -> 6.49 us
  starting transfers between devices: 14.6 us -> 15.6 us
  waiting for transfers between devices: 13.8 us -> 12.8 us
  local copies, waits for them, and re-layouts: 1.25 us -> 2.24 us
    ppermute x3, waiting for transfers between devices: 11.7 us -> 9.81 us  [shards(): lax.ppermute(got[mask - low], 'chan', [(i, i ^ low) for i in range(count)])]
    ppermute x3, waiting for transfers between devices: 1.04 us -> 2.49 us  [shards(): lax.ppermute(term, 'depth', [(i, i ^ 2 * k + 2) for i in range(depth)])]
    ppermute x3, waiting for transfers between devices: 1.14 us -> 0.01 us  [the longest x2 0.01 us: shards(): lax.ppermute(part, 'depth', nearer)]
    unnamed x6, local copies, waits for them, and re-layouts: 1.23 us -> 2.21 us
    ppermute x3, starting transfers between devices: 3.25 us -> 4.02 us  [the longest x1 2.28 us: shards(): next_own = lax.ppermute(grad_out, 'depth', nearer)]
    pallas_call x8 -> x9, Pallas kernels: 4.05 us -> 3.36 us  [call(): pl.pallas_call(kernel, out_shape=out_shape, in_specs=[VMEM] * len(args),...]
    ppermute x1, waiting for transfers between devices: 0.01 us -> 0.53 us  [shards(): behind = lax.ppermute(volume, 'depth', farther)]
  transfers between devices with their start and end apart: 11 -> 11, of which waited for: 4 -> 5; matrix products, arithmetic and copies ran while one was open for 0% -> 0% of each run, Pallas kernels for 18% -> 15%
where the time goes in v6:
time: 38.1 us; the launch traced here: 37.9 us
  starting transfers between devices  15.6 us (41%)
  waiting for transfers between devices  12.8 us (34%)
  Pallas kernels  6.49 us (17%)
  local copies, waits for them, and re-layouts  2.24 us (6%)
  between operations  0.75 us (2%)
    ppermute x3, waiting for transfers between devices, shards(): lax.ppermute(got[mask - low], 'chan', [(i, i ^ low) for i in range(count)])  9.81 us
    ppermute x3, starting transfers between devices, shards(): lax.ppermute(got[mask - low], 'chan', [(i, i ^ low) for i in range(count)])  7.07 us
    ppermute x3, starting transfers between devices, shards(): lax.ppermute(term, 'depth', [(i, i ^ 2 * k + 2) for i in range(depth)])  3.55 us
    pallas_call x9, Pallas kernels, call(): pl.pallas_call(kernel, out_shape=out_shape, in_specs=[VMEM] * len(args),...  3.36 us
    pallas_call x2, Pallas kernels, input_plane(): pl.pallas_call(kernel if before is None else lambda before, *refs: kernel...  3.13 us
    ppermute x3, waiting for transfers between devices, shards(): lax.ppermute(term, 'depth', [(i, i ^ 2 * k + 2) for i in range(depth)])  2.49 us
    ppermute x1, starting transfers between devices, shards(): next_own = lax.ppermute(grad_out, 'depth', nearer)  2.28 us
    unnamed x6, local copies, waits for them, and re-layouts  2.21 us
  transfers between devices with their start and end apart: 11, of which 5 were waited for; matrix products, arithmetic and copies ran while one was open for 0% of the time, Pallas kernels for 15%

profile of v6, /device:TPU:0, one launch (start us, length us, event | category | flops | bytes accessed | tf_op | source)
XLA Modules:
  0.0 37.9 jit_solution(12154132025653843924)
XLA Ops:
  0.6 0.0 copy-start
  0.6 0.5 %collective-permute-start.2 = (bf16[16,2,64,256]{3,2,1,0:T(8,128)(2,1)}, bf16[16,2,64,256]{3,2,1,0:T(8,128)(2,1)S(1)}, u32[]{:S(2)}, u32[]{:S(2)}) collective-permute-start(bf16[16,2,64,256]{3,2,1,0:T(8,128)(2,1)} %refs_0_.2), channel_id=1, source_target_pairs={{0,4},{4,8},{8,12},{12,16},{16,20},{20,24},{24,28},{28,0},{1,5},{5... | collective-permute-start | bytes 3145736 | tf_op jit(solution)/shard_map/ppermute | solution.py:348
  1.1 3.7 %collective-permute-start.1 = (bf16[32,1,32,128]{3,2,1,0:T(8,128)(2,1)}, bf16[32,1,32,128]{3,2,1,0:T(8,128)(2,1)S(1)}, u32[]{:S(2)}, u32[]{:S(2)}) collective-permute-start(bf16[32,1,32,128]{3,2,1,0:T(8,128)(2,1)} %refs_0_.3), channel_id=1, source_target_pairs={{0,2},{1,3},{2,0},{3,1},{4,6},{5,7},{6,4},{7,5},{8,10},{9,11},{10,... | collective-permute-start | bytes 786440 | tf_op jit(solution)/shard_map/ppermute | solution.py:340
  4.8 2.3 %collective-permute-start.3 = (bf16[32,1,32,128]{3,2,1,0:T(8,128)(2,1)}, bf16[32,1,32,128]{3,2,1,0:T(8,128)(2,1)S(1)}, u32[]{:S(2)}, u32[]{:S(2)}) collective-permute-start(bf16[32,1,32,128]{3,2,1,0:T(8,128)(2,1)} %refs_0_.3), channel_id=1, source_target_pairs={{4,0},{8,4},{12,8},{16,12},{20,16},{24,20},{28,24},{0,28},{5,1},{9... | collective-permute-start | bytes 786440 | tf_op jit(solution)/shard_map/ppermute | solution.py:349
  7.1 1.6 %collective-permute-start = (bf16[32,1,32,128]{3,2,1,0:T(8,128)(2,1)}, bf16[32,1,32,128]{3,2,1,0:T(8,128)(2,1)S(1)}, u32[]{:S(2)}, u32[]{:S(2)}) collective-permute-start(bf16[32,1,32,128]{3,2,1,0:T(8,128)(2,1)} %refs_0_.3), channel_id=1, source_target_pairs={{0,1},{1,0},{2,3},{3,2},{4,5},{5,4},{6,7},{7,6},{8,9},{9,8},{10,11... | collective-permute-start | bytes 786440 | tf_op jit(solution)/shard_map/ppermute | solution.py:340
  8.7 0.0 copy-start.1
  8.7 1.0 %copy-done.1 = bf16[32,1,32,128]{3,2,1,0:T(8,128)(2,1)S(1)} copy-done((bf16[32,1,32,128]{3,2,1,0:T(8,128)(2,1)S(1)}, bf16[32,1,32,128]{3,2,1,0:T(8,128)(2,1)}, u32[]{:S(2)}) %copy-start.1) | copy-done | bytes 262168
  9.7 0.1 shard_map.52.refs_2_.refs_1_.refs_4_
  9.8 0.0 copy-done
  9.8 0.0 copy-start.2
  9.9 1.2 %copy-done.2 = bf16[16,2,64,256]{3,2,1,0:T(8,128)(2,1)S(1)} copy-done((bf16[16,2,64,256]{3,2,1,0:T(8,128)(2,1)S(1)}, bf16[16,2,64,256]{3,2,1,0:T(8,128)(2,1)}, u32[]{:S(2)}) %copy-start.2) | copy-done | bytes 1048600
  11.1 0.9 %shard_map.50 = (bf16[192,4096]{1,0:T(8,128)(2,1)S(1)}, bf16[144,128]{1,0:T(8,128)(2,1)S(1)}, bf16[144,256]{1,0:T(8,128)(2,1)S(1)}) custom-call(bf16[16,2,64,256]{3,2,1,0:T(8,128)(2,1)S(1)} %copy-done.2, bf16[27,16,128]{2,1,0:T(8,128)(2,1)S(1)} %constant_dynamic-slice_fusion.refs_1_), custom_call_target="tpu_custom_call" | custom-call | flops 536870912 | bytes 4194304 | tf_op jit(solution)/shard_map/pallas_call | solution.py:302
  12.0 5.1 %collective-permute-done.1.refs_1_ = bf16[32,1,32,128]{3,2,1,0:T(8,128)(2,1)S(1)} collective-permute-done((bf16[32,1,32,128]{3,2,1,0:T(8,128)(2,1)}, bf16[32,1,32,128]{3,2,1,0:T(8,128)(2,1)S(1)}, u32[]{:S(2)}, u32[]{:S(2)}) %collective-permute-start.1) | collective-permute-done | bytes 262176 | tf_op jit(solution)/shard_map/ppermute | solution.py:340
  17.0 1.8 %collective-permute-start.4 = (bf16[32,1,32,128]{3,2,1,0:T(8,128)(2,1)S(1)}, bf16[32,1,32,128]{3,2,1,0:T(8,128)(2,1)S(1)}, u32[]{:S(2)}, u32[]{:S(2)}) collective-permute-start(bf16[32,1,32,128]{3,2,1,0:T(8,128)(2,1)S(1)} %collective-permute-done.1.refs_1_), channel_id=1, source_target_pairs={{0,1},{1,0},{2,3},{3,2},{4,5},{5,4},{6,7},{7,6},{8,9},{9,8},{10,11... | collective-permute-start | bytes 786440 | tf_op jit(solution)/shard_map/ppermute | solution.py:340
  18.9 0.0 collective-permute-done.3.refs_0_
  18.9 0.1 shard_map.53.refs_1_
  19.0 0.5 %collective-permute-done.2.behind_ref = bf16[16,2,64,256]{3,2,1,0:T(8,128)(2,1)S(1)} collective-permute-done((bf16[16,2,64,256]{3,2,1,0:T(8,128)(2,1)}, bf16[16,2,64,256]{3,2,1,0:T(8,128)(2,1)S(1)}, u32[]{:S(2)}, u32[]{:S(2)}) %collective-permute-start.2) | collective-permute-done | bytes 1048608 | tf_op jit(solution)/shard_map/ppermute | solution.py:348
  19.5 0.1 shard_map.51.refs_1_
  19.6 0.0 collective-permute-done.refs_0_
  19.6 0.3 shard_map.54.refs_3_.refs_2_.refs_5_
  19.9 1.5 %collective-permute-start.6 = (bf16[64,4096]{1,0:T(8,128)(2,1)S(1)}, bf16[64,4096]{1,0:T(8,128)(2,1)S(1)}, u32[]{:S(2)}, u32[]{:S(2)}) collective-permute-start(bf16[64,4096]{1,0:T(8,128)(2,1)S(1)} %shard_map.54.refs_3_.refs_2_.refs_5_), channel_id=1, source_target_pairs={{4,0},{8,4},{12,8},{16,12},{20,16},{24,20},{28,24},{0,28},{5,1},{9... | collective-permute-start | bytes 1572872 | tf_op jit(solution)/shard_map/ppermute | solution.py:362
  21.4 4.8 %collective-permute-done.4.refs_0_ = bf16[32,1,32,128]{3,2,1,0:T(8,128)(2,1)S(1)} collective-permute-done((bf16[32,1,32,128]{3,2,1,0:T(8,128)(2,1)S(1)}, bf16[32,1,32,128]{3,2,1,0:T(8,128)(2,1)S(1)}, u32[]{:S(2)}, u32[]{:S(2)}) %collective-permute-start.4) | collective-permute-done | bytes 262176 | tf_op jit(solution)/shard_map/ppermute | solution.py:340
  26.2 0.1 shard_map.55.refs_4_.refs_3_.refs_6_
  26.3 0.2 collective-permute-start.7
  26.5 0.9 %shard_map.56 = (f32[64,512]{1,0:T(8,128)S(1)}, f32[64,512]{1,0:T(8,128)S(1)}) custom-call(bf16[192,4096]{1,0:T(8,128)(2,1)S(1)} %get-tuple-element.24.refs_0_, bf16[96,4096]{1,0:T(8,128)(2,1)S(1)} %shard_map.51.refs_1_, bf16[32,4096]{1,0:T(8,128)(2,1)S(1)} %shard_map.52.refs_2_.refs_1_.refs_4_, bf16[64,4096]{1,0:T(8,128)(2,1)S(1)} %shard_map.54.refs_3_.refs_2_.refs_5_, ...), custom_call_target="tpu_custom_call" | custom-call | flops 452984832 | bytes 8388608 | tf_op jit(solution)/shard_map/pallas_call | solution.py:302
  27.5 0.4 %collective-permute-start.5 = (f32[64,512]{1,0:T(8,128)S(1)}, f32[64,512]{1,0:T(8,128)S(1)}, u32[]{:S(2)}, u32[]{:S(2)}) collective-permute-start(f32[64,512]{1,0:T(8,128)S(1)} %get-tuple-element.30), channel_id=1, source_target_pairs={{0,4},{4,0},{8,12},{12,8},{16,20},{20,16},{24,28},{28,24},{1,5},{5... | collective-permute-start | bytes 393224 | tf_op jit(solution)/shard_map/ppermute | solution.py:398
  27.9 1.6 %shard_map.57.before = bf16[16,2,64,256]{3,2,1,0:T(8,128)(2,1)} custom-call(bf16[144,128]{1,0:T(8,128)(2,1)S(1)} %get-tuple-element.31.refs_0_, bf16[32,4096]{1,0:T(8,128)(2,1)S(1)} %shard_map.52.refs_2_.refs_1_.refs_4_, bf16[64,4096]{1,0:T(8,128)(2,1)S(1)} %shard_map.54.refs_3_.refs_2_.refs_5_, bf16[32,4096]{1,0:T(8,128)(2,1)S(1)} %shard_map.55.refs_4_.refs_3_.refs_6_), custom_call_target="tpu_custom_call" | custom-call | flops 150994944 | bytes 4194304 | tf_op jit(solution)/shard_map/pallas_call | solution.py:380
  29.5 0.0 collective-permute-done.5.other_ref
  29.5 1.6 %collective-permute-start.8 = (f32[16,512]{1,0:T(8,128)S(1)}, f32[16,512]{1,0:T(8,128)S(1)}, u32[]{:S(2)}, u32[]{:S(2)}) collective-permute-start(f32[16,512]{1,0:T(8,128)S(1)} %get-tuple-element.39), channel_id=1, source_target_pairs={{0,8},{4,12},{8,0},{12,4},{16,24},{20,28},{24,16},{28,20},{1,9},{5... | collective-permute-start | bytes 98312 | tf_op jit(solution)/shard_map/ppermute | solution.py:408
  31.2 1.2 %collective-permute-start.9 = (f32[16,512]{1,0:T(8,128)S(1)}, f32[16,512]{1,0:T(8,128)S(1)}, u32[]{:S(2)}, u32[]{:S(2)}) collective-permute-start(f32[16,512]{1,0:T(8,128)S(1)} %get-tuple-element.40), channel_id=1, source_target_pairs={{0,16},{4,20},{8,24},{12,28},{16,0},{20,4},{24,8},{28,12},{1,17},{... | collective-permute-start | bytes 98312 | tf_op jit(solution)/shard_map/ppermute | solution.py:408
  32.3 0.7 %collective-permute-start.10 = (f32[16,512]{1,0:T(8,128)S(1)}, f32[16,512]{1,0:T(8,128)S(1)}, u32[]{:S(2)}, u32[]{:S(2)}) collective-permute-start(f32[16,512]{1,0:T(8,128)S(1)} %get-tuple-element.41), channel_id=1, source_target_pairs={{0,24},{4,28},{8,16},{12,20},{16,8},{20,12},{24,0},{28,4},{1,25},{... | collective-permute-start | bytes 98312 | tf_op jit(solution)/shard_map/ppermute | solution.py:408
  33.1 0.0 collective-permute-done.7.refs_3_
  33.1 0.0 collective-permute-done.6.refs_2_
  33.1 1.6 %shard_map.59 = bf16[16,2,64,256]{3,2,1,0:T(8,128)(2,1)} custom-call(bf16[16,2,64,256]{3,2,1,0:T(8,128)(2,1)} %shard_map.57.before, bf16[144,256]{1,0:T(8,128)(2,1)S(1)} %get-tuple-element.35.refs_0_, bf16[32,4096]{1,0:T(8,128)(2,1)S(1)} %shard_map.53.refs_1_, bf16[64,4096]{1,0:T(8,128)(2,1)S(1)} %collective-permute-done.6.refs_2_, ...), custom_call_target="tpu_custom_call", output_to_operand_aliasing={{}: (0, {})} | custom-call | flops 301989888 | bytes 4194304 | tf_op jit(solution)/shard_map/pallas_call | solution.py:380
  34.6 0.0 collective-permute-done.8.refs_1_
  34.7 0.4 %collective-permute-done.9.refs_2_ = f32[16,512]{1,0:T(8,128)S(1)} collective-permute-done((f32[16,512]{1,0:T(8,128)S(1)}, f32[16,512]{1,0:T(8,128)S(1)}, u32[]{:S(2)}, u32[]{:S(2)}) %collective-permute-start.9) | collective-permute-done | bytes 32800 | tf_op jit(solution)/shard_map/ppermute | solution.py:408
  35.1 2.1 %collective-permute-done.10.refs_3_ = f32[16,512]{1,0:T(8,128)S(1)} collective-permute-done((f32[16,512]{1,0:T(8,128)S(1)}, f32[16,512]{1,0:T(8,128)S(1)}, u32[]{:S(2)}, u32[]{:S(2)}) %collective-permute-start.10) | collective-permute-done | bytes 32800 | tf_op jit(solution)/shard_map/ppermute | solution.py:408
  37.1 0.8 %shard_map.60 = f32[16,16,27]{2,1,0:T(8,128)} custom-call(f32[16,512]{1,0:T(8,128)S(1)} %get-tuple-element.38.refs_0_, f32[16,512]{1,0:T(8,128)S(1)} %collective-permute-done.8.refs_1_, f32[16,512]{1,0:T(8,128)S(1)} %collective-permute-done.9.refs_2_, f32[16,512]{1,0:T(8,128)S(1)} %collective-permute-done.10.refs_3_), custom_call_target="tpu_custom_call" | custom-call | flops 65536 | bytes 524288 | tf_op jit(solution)/shard_map/pallas_call | solution.py:302
  (2 shorter events, 0.1 us)
Async XLA Ops:
  0.6 9.2 %copy-start = (bf16[27,64,128]{2,1,0:T(8,128)(2,1)S(1)}, bf16[27,64,128]{2,1,0:T(8,128)(2,1)}, u32[]{:S(2)}) copy-start(bf16[27,64,128]{2,1,0:T(8,128)(2,1)} %param.5) | copy-start | bytes 1327108
  0.6 18.9 %collective-permute-start.2 = (bf16[16,2,64,256]{3,2,1,0:T(8,128)(2,1)}, bf16[16,2,64,256]{3,2,1,0:T(8,128)(2,1)S(1)}, u32[]{:S(2)}, u32[]{:S(2)}) collective-permute-start(bf16[16,2,64,256]{3,2,1,0:T(8,128)(2,1)} %refs_0_.2), channel_id=1, source_target_pairs={{0,4},{4,8},{8,12},{12,16},{16,20},{20,24},{24,28},{28,0},{1,5},{5... | collective-permute-start | bytes 3145736 | tf_op jit(solution)/shard_map/ppermute | solution.py:348
  1.1 15.9 %collective-permute-start.1 = (bf16[32,1,32,128]{3,2,1,0:T(8,128)(2,1)}, bf16[32,1,32,128]{3,2,1,0:T(8,128)(2,1)S(1)}, u32[]{:S(2)}, u32[]{:S(2)}) collective-permute-start(bf16[32,1,32,128]{3,2,1,0:T(8,128)(2,1)} %refs_0_.3), channel_id=1, source_target_pairs={{0,2},{1,3},{2,0},{3,1},{4,6},{5,7},{6,4},{7,5},{8,10},{9,11},{10,... | collective-permute-start | bytes 786440 | tf_op jit(solution)/shard_map/ppermute | solution.py:340
  4.8 14.0 %collective-permute-start.3 = (bf16[32,1,32,128]{3,2,1,0:T(8,128)(2,1)}, bf16[32,1,32,128]{3,2,1,0:T(8,128)(2,1)S(1)}, u32[]{:S(2)}, u32[]{:S(2)}) collective-permute-start(bf16[32,1,32,128]{3,2,1,0:T(8,128)(2,1)} %refs_0_.3), channel_id=1, source_target_pairs={{4,0},{8,4},{12,8},{16,12},{20,16},{24,20},{28,24},{0,28},{5,1},{9... | collective-permute-start | bytes 786440 | tf_op jit(solution)/shard_map/ppermute | solution.py:349
  7.1 12.5 %collective-permute-start = (bf16[32,1,32,128]{3,2,1,0:T(8,128)(2,1)}, bf16[32,1,32,128]{3,2,1,0:T(8,128)(2,1)S(1)}, u32[]{:S(2)}, u32[]{:S(2)}) collective-permute-start(bf16[32,1,32,128]{3,2,1,0:T(8,128)(2,1)} %refs_0_.3), channel_id=1, source_target_pairs={{0,1},{1,0},{2,3},{3,2},{4,5},{5,4},{6,7},{7,6},{8,9},{9,8},{10,11... | collective-permute-start | bytes 786440 | tf_op jit(solution)/shard_map/ppermute | solution.py:340
  8.7 1.0 %copy-start.1 = (bf16[32,1,32,128]{3,2,1,0:T(8,128)(2,1)S(1)}, bf16[32,1,32,128]{3,2,1,0:T(8,128)(2,1)}, u32[]{:S(2)}) copy-start(bf16[32,1,32,128]{3,2,1,0:T(8,128)(2,1)} %refs_0_.3) | copy-start | bytes 786436
  9.8 1.2 %copy-start.2 = (bf16[16,2,64,256]{3,2,1,0:T(8,128)(2,1)S(1)}, bf16[16,2,64,256]{3,2,1,0:T(8,128)(2,1)}, u32[]{:S(2)}) copy-start(bf16[16,2,64,256]{3,2,1,0:T(8,128)(2,1)} %refs_0_.2) | copy-start | bytes 3145732
  17.0 9.1 %collective-permute-start.4 = (bf16[32,1,32,128]{3,2,1,0:T(8,128)(2,1)S(1)}, bf16[32,1,32,128]{3,2,1,0:T(8,128)(2,1)S(1)}, u32[]{:S(2)}, u32[]{:S(2)}) collective-permute-start(bf16[32,1,32,128]{3,2,1,0:T(8,128)(2,1)S(1)} %collective-permute-done.1.refs_1_), channel_id=1, source_target_pairs={{0,1},{1,0},{2,3},{3,2},{4,5},{5,4},{6,7},{7,6},{8,9},{9,8},{10,11... | collective-permute-start | bytes 786440 | tf_op jit(solution)/shard_map/ppermute | solution.py:340
  19.9 13.2 %collective-permute-start.6 = (bf16[64,4096]{1,0:T(8,128)(2,1)S(1)}, bf16[64,4096]{1,0:T(8,128)(2,1)S(1)}, u32[]{:S(2)}, u32[]{:S(2)}) collective-permute-start(bf16[64,4096]{1,0:T(8,128)(2,1)S(1)} %shard_map.54.refs_3_.refs_2_.refs_5_), channel_id=1, source_target_pairs={{4,0},{8,4},{12,8},{16,12},{20,16},{24,20},{28,24},{0,28},{5,1},{9... | collective-permute-start | bytes 1572872 | tf_op jit(solution)/shard_map/ppermute | solution.py:362
  26.3 6.7 %collective-permute-start.7 = (bf16[32,4096]{1,0:T(8,128)(2,1)S(1)}, bf16[32,4096]{1,0:T(8,128)(2,1)S(1)}, u32[]{:S(2)}, u32[]{:S(2)}) collective-permute-start(bf16[32,4096]{1,0:T(8,128)(2,1)S(1)} %shard_map.55.refs_4_.refs_3_.refs_6_), channel_id=1, source_target_pairs={{4,0},{8,4},{12,8},{16,12},{20,16},{24,20},{28,24},{0,28},{5,1},{9... | collective-permute-start | bytes 786440 | tf_op jit(solution)/shard_map/ppermute | solution.py:362
  27.5 2.0 %collective-permute-start.5 = (f32[64,512]{1,0:T(8,128)S(1)}, f32[64,512]{1,0:T(8,128)S(1)}, u32[]{:S(2)}, u32[]{:S(2)}) collective-permute-start(f32[64,512]{1,0:T(8,128)S(1)} %get-tuple-element.30), channel_id=1, source_target_pairs={{0,4},{4,0},{8,12},{12,8},{16,20},{20,16},{24,28},{28,24},{1,5},{5... | collective-permute-start | bytes 393224 | tf_op jit(solution)/shard_map/ppermute | solution.py:398
  29.5 5.1 %collective-permute-start.8 = (f32[16,512]{1,0:T(8,128)S(1)}, f32[16,512]{1,0:T(8,128)S(1)}, u32[]{:S(2)}, u32[]{:S(2)}) collective-permute-start(f32[16,512]{1,0:T(8,128)S(1)} %get-tuple-element.39), channel_id=1, source_target_pairs={{0,8},{4,12},{8,0},{12,4},{16,24},{20,28},{24,16},{28,20},{1,9},{5... | collective-permute-start | bytes 98312 | tf_op jit(solution)/shard_map/ppermute | solution.py:408
  31.2 3.9 %collective-permute-start.9 = (f32[16,512]{1,0:T(8,128)S(1)}, f32[16,512]{1,0:T(8,128)S(1)}, u32[]{:S(2)}, u32[]{:S(2)}) collective-permute-start(f32[16,512]{1,0:T(8,128)S(1)} %get-tuple-element.40), channel_id=1, source_target_pairs={{0,16},{4,20},{8,24},{12,28},{16,0},{20,4},{24,8},{28,12},{1,17},{... | collective-permute-start | bytes 98312 | tf_op jit(solution)/shard_map/ppermute | solution.py:408
  32.3 4.8 %collective-permute-start.10 = (f32[16,512]{1,0:T(8,128)S(1)}, f32[16,512]{1,0:T(8,128)S(1)}, u32[]{:S(2)}, u32[]{:S(2)}) collective-permute-start(f32[16,512]{1,0:T(8,128)S(1)} %get-tuple-element.41), channel_id=1, source_target_pairs={{0,24},{4,28},{8,16},{12,20},{16,8},{20,12},{24,0},{28,4},{1,25},{... | collective-permute-start | bytes 98312 | tf_op jit(solution)/shard_map/ppermute | solution.py:408

commit v7 on v6

--- a/solution.py
+++ b/solution.py
@@ -13,6 +13,19 @@
 VMEM = pl.BlockSpec(memory_space=pltpu.VMEM)
 HBM = pl.BlockSpec(memory_space=pltpu.HBM)
 LIMIT = 48 * 1024 * 1024
+
+
+def ring_order(count):
+    return [0] + list(range(1, count, 2)) + list(range(2, count, 2))[::-1]
+
+
+def holder(order, step):
+    here = lax.axis_index("chan")
+    count = len(order)
+    owner = jnp.int32(order[-step % count])
+    for seat in range(1, count):
+        owner = jnp.where(here == order[seat], order[(seat - step) % count], owner)
+    return owner
 
 
 def matmul(left, right):
@@ -55,19 +68,18 @@
                 views_ref[lo : lo + chans, lanes] = views[e][at * chans : (at + 1) * chans]
 
 
-def own_views_kernel(depth, volume_ref, weight_ref, views_ref, even_ref, odd_ref):
+def own_views_kernel(ring, depth, volume_ref, weight_ref, views_ref, even_ref, odd_ref):
     chans = volume_ref.shape[0]
     channels = weight_ref.shape[2]
     place_views(volume_ref.at[:, 0], views_ref, 0)
     place_views(volume_ref.at[:, 1], views_ref, 6 * chans)
-    count = lax.axis_size("chan")
+    count = len(ring)
     part = channels // count
-    here = lax.axis_index("chan")
     row = lax.broadcasted_iota(jnp.int32, (channels, channels), 0)
     col = lax.broadcasted_iota(jnp.int32, (channels, channels), 1)
     order = jnp.zeros((channels, channels), F32)
     for slot in range(count):
-        moved = ((here ^ slot) - slot) * part
+        moved = (holder(ring, slot) - slot) * part
         inside = (col >= slot * part) & (col < (slot + 1) * part)
         order = jnp.where(inside & (row == col + moved), 1.0, order)
     ordered = matmul(weight_ref[...].reshape(27 * chans, channels), order.astype(BF16)).astype(BF16)
@@ -111,7 +123,7 @@
 
 
 def weight_kernel(
-    outs, cols, chunk, own_ref, behind_ref, *refs
+    ring, outs, cols, chunk, own_ref, behind_ref, *refs
 ):
     *line_refs, keep_ref, send_ref, terms_ref, placed_ref = refs
     channels = terms_ref.shape[1]
@@ -144,11 +156,11 @@
     for c in range(chans):
         placed_ref[32 * c : 32 * c + 32, :] = terms_ref[pl.ds(c, 32, stride=pitch), :]
     turned = placed_ref[...].T
-    count = lax.axis_size("chan")
+    count = len(ring)
     part = channels // count
     odd_core = lax.axis_index("depth") % 2 == 1
     for slot in range(count):
-        start = (lax.axis_index("chan") ^ slot) * (part // 2)
+        start = holder(ring, slot) * (part // 2)
         for at in range(0, part // 2, outs):
             lo = slot * part + 2 * at
             even, odd = turned[lo : lo + outs], turned[lo + outs : lo + 2 * outs]
@@ -317,12 +329,14 @@
     chans = volume.shape[0]
     channels = weight.shape[2]
     cells = rows * cols
+    ring = ring_order(count)
+    ahead = [(ring[i], ring[(i + 1) % count]) for i in range(count)]
     farther = [(i, (i + 1) % depth) for i in range(depth)]
     nearer = [(b, a) for a, b in farther]
 
     own_weight = lax.dynamic_slice_in_dim(weight, lax.axis_index("chan") * chans, chans, 1)
     views, even_taps, odd_taps = call(
-        lambda *refs: own_views_kernel(depth, *refs),
+        lambda *refs: own_views_kernel(ring, depth, *refs),
         (
             jax.ShapeDtypeStruct((12 * chans, cells), BF16),
             jax.ShapeDtypeStruct((9 * chans, channels), BF16),
@@ -332,12 +346,11 @@
         own_weight,
         cost=(2 * 2 * 2 * cells * chans * 8 * cols, 4 << 20),
     )
-    got = {0: grad_out}
-    for mask in sorted(range(1, count), key=lambda mask: (mask & (mask - 1) > 0, -mask)):
-        low = mask & -mask
-        if mask == 3:
-            got[2], views = lax.optimization_barrier((got[2], views))
-        got[mask] = lax.ppermute(got[mask - low], "chan", [(i, i ^ low) for i in range(count)])
+    got = [grad_out]
+    for step in range(1, count):
+        got.append(lax.ppermute(got[-1], "chan", ahead))
+        if step == 1:
+            got[1], views = lax.optimization_barrier((got[1], views))
     lines = lambda *parts: call(
         lines_kernel,
         jax.ShapeDtypeStruct((sum(part.shape[0] for part in parts), cells), BF16),
@@ -354,16 +367,16 @@
         cost=(2 * 2 * cells * chans * 8 * cols, 2 << 20),
     )
     first_lines, next_first_lines = lines(grad_out), lines(next_own)
-    got[1], views, behind_views, first_lines, next_first_lines = lax.optimization_barrier(
-        (got[1], views, behind_views, first_lines, next_first_lines)
-    )
-    later_lines = [lines(*[got[mask] for mask in range(1, count - 1)]), lines(got[count - 1])]
+    got[2], views, behind_views, first_lines, next_first_lines = lax.optimization_barrier(
+        (got[2], views, behind_views, first_lines, next_first_lines)
+    )
+    later_lines = [lines(*got[1:-1]), lines(got[-1])]
     own_lines = [first_lines] + later_lines
     next_lines = [next_first_lines] + [lax.ppermute(part, "depth", nearer) for part in later_lines]
     outs = channels // depth
     half_terms = jax.ShapeDtypeStruct((channels // 2, 32 * chans), F32)
     keep, send = call(
-        lambda *refs: weight_kernel(outs, cols, 4 * cols, *refs),
+        lambda *refs: weight_kernel(ring, outs, cols, 4 * cols, *refs),
         (half_terms, half_terms),
         views,
         behind_views,
@@ -430,7 +443,6 @@
             and volume.shape[0] == 16
             and grad_out.shape[1] == 1
             and ring >= 4
-            and ring & (ring - 1) == 0
             and depth & (depth - 1) == 0
             and depth % (2 * ring) == 0
         )

time: 38.1 us -> 41.3 us (1.084)
  waiting for transfers between devices: 12.8 us -> 19.9 us
  starting transfers between devices: 15.6 us -> 12.8 us
  local copies, waits for them, and re-layouts: 2.24 us -> 1.25 us
    ppermute x3, waiting for transfers between devices: 9.81 us -> 18.4 us  [shards(): got.append(lax.ppermute(got[-1], 'chan', ahead))]
    ppermute x3, starting transfers between devices: 7.07 us -> 5.41 us  [shards(): got.append(lax.ppermute(got[-1], 'chan', ahead))]
    ppermute x2, starting transfers between devices: 1.74 us -> 0.5 us  [shards(): lax.ppermute(part, 'depth', nearer)]
    ppermute x3, waiting for transfers between devices: 2.49 us -> 1.38 us  [shards(): lax.ppermute(term, 'depth', [(i, i ^ 2 * k + 2) for i in range(depth)])]
    unnamed x6, local copies, waits for them, and re-layouts: 2.21 us -> 1.23 us
    ppermute x1, waiting for transfers between devices: 0.53 us -> 0.01 us  [shards(): behind = lax.ppermute(volume, 'depth', farther)]
  transfers between devices with their start and end apart: 11 -> 11, of which waited for: 5 -> 5; matrix products, arithmetic and copies ran while one was open for 0% -> 0% of each run, Pallas kernels for 15% -> 14%
where the time goes in v7:
time: 41.3 us; the launch traced here: 41.2 us
  waiting for transfers between devices  19.9 us (48%)
  starting transfers between devices  12.8 us (31%)
  Pallas kernels  6.47 us (16%)
  local copies, waits for them, and re-layouts  1.25 us (3%)
  between operations  0.75 us (2%)
    ppermute x3, waiting for transfers between devices, shards(): got.append(lax.ppermute(got[-1], 'chan', ahead))  18.4 us
    ppermute x3, starting transfers between devices, shards(): got.append(lax.ppermute(got[-1], 'chan', ahead))  5.41 us
    ppermute x3, starting transfers between devices, shards(): lax.ppermute(term, 'depth', [(i, i ^ 2 * k + 2) for i in range(depth)])  3.55 us
    pallas_call x9, Pallas kernels, call(): pl.pallas_call(kernel, out_shape=out_shape, in_specs=[VMEM] * len(args),...  3.35 us
    pallas_call x2, Pallas kernels, input_plane(): pl.pallas_call(kernel if before is None else lambda before, *refs: kernel...  3.12 us
    ppermute x1, starting transfers between devices, shards(): next_own = lax.ppermute(grad_out, 'depth', nearer)  2.3 us
    ppermute x3, waiting for transfers between devices, shards(): lax.ppermute(term, 'depth', [(i, i ^ 2 * k + 2) for i in range(depth)])  1.38 us
    unnamed x6, local copies, waits for them, and re-layouts  1.23 us
  transfers between devices with their start and end apart: 11, of which 5 were waited for; matrix products, arithmetic and copies ran while one was open for 0% of the time, Pallas kernels for 14%

profile of v7, /device:TPU:0, one launch (start us, length us, event | category | flops | bytes accessed | tf_op | source)
XLA Modules:
  0.0 41.2 jit_solution(15570417649271903141)
XLA Ops:
  0.6 0.0 copy-start
  0.6 0.0 copy-start.1
  0.7 0.5 %collective-permute-start.2 = (bf16[16,2,64,256]{3,2,1,0:T(8,128)(2,1)}, bf16[16,2,64,256]{3,2,1,0:T(8,128)(2,1)S(1)}, u32[]{:S(2)}, u32[]{:S(2)}) collective-permute-start(bf16[16,2,64,256]{3,2,1,0:T(8,128)(2,1)} %refs_0_.2), channel_id=1, source_target_pairs={{0,4},{4,8},{8,12},{12,16},{16,20},{20,24},{24,28},{28,0},{1,5},{5... | collective-permute-start | bytes 3145736 | tf_op jit(solution)/shard_map/ppermute | solution.py:361
  1.2 2.6 %collective-permute-start = (bf16[32,1,32,128]{3,2,1,0:T(8,128)(2,1)}, bf16[32,1,32,128]{3,2,1,0:T(8,128)(2,1)S(1)}, u32[]{:S(2)}, u32[]{:S(2)}) collective-permute-start(bf16[32,1,32,128]{3,2,1,0:T(8,128)(2,1)} %refs_0_.3), channel_id=1, source_target_pairs={{0,1},{1,3},{3,2},{2,0},{4,5},{5,7},{7,6},{6,4},{8,9},{9,11},{11,1... | collective-permute-start | bytes 786440 | tf_op jit(solution)/shard_map/ppermute | solution.py:351
  3.8 2.3 %collective-permute-start.3 = (bf16[32,1,32,128]{3,2,1,0:T(8,128)(2,1)}, bf16[32,1,32,128]{3,2,1,0:T(8,128)(2,1)S(1)}, u32[]{:S(2)}, u32[]{:S(2)}) collective-permute-start(bf16[32,1,32,128]{3,2,1,0:T(8,128)(2,1)} %refs_0_.3), channel_id=1, source_target_pairs={{4,0},{8,4},{12,8},{16,12},{20,16},{24,20},{28,24},{0,28},{5,1},{9... | collective-permute-start | bytes 786440 | tf_op jit(solution)/shard_map/ppermute | solution.py:362
  6.1 0.0 copy-done
  6.1 0.0 copy-start.2
  6.1 1.2 %copy-done.2 = bf16[16,2,64,256]{3,2,1,0:T(8,128)(2,1)S(1)} copy-done((bf16[16,2,64,256]{3,2,1,0:T(8,128)(2,1)S(1)}, bf16[16,2,64,256]{3,2,1,0:T(8,128)(2,1)}, u32[]{:S(2)}) %copy-start.2) | copy-done | bytes 1048600
  7.3 0.9 %shard_map.50 = (bf16[192,4096]{1,0:T(8,128)(2,1)S(1)}, bf16[144,128]{1,0:T(8,128)(2,1)S(1)}, bf16[144,256]{1,0:T(8,128)(2,1)S(1)}) custom-call(bf16[16,2,64,256]{3,2,1,0:T(8,128)(2,1)S(1)} %copy-done.2, bf16[27,16,128]{2,1,0:T(8,128)(2,1)S(1)} %constant_dynamic-slice_fusion.refs_1_), custom_call_target="tpu_custom_call" | custom-call | flops 536870912 | bytes 4194304 | tf_op jit(solution)/shard_map/pallas_call | solution.py:314
  8.2 3.1 %collective-permute-done.refs_0_ = bf16[32,1,32,128]{3,2,1,0:T(8,128)(2,1)S(1)} collective-permute-done((bf16[32,1,32,128]{3,2,1,0:T(8,128)(2,1)}, bf16[32,1,32,128]{3,2,1,0:T(8,128)(2,1)S(1)}, u32[]{:S(2)}, u32[]{:S(2)}) %collective-permute-start) | collective-permute-done | bytes 262176 | tf_op jit(solution)/shard_map/ppermute | solution.py:351
  11.3 1.6 %collective-permute-start.1 = (bf16[32,1,32,128]{3,2,1,0:T(8,128)(2,1)S(1)}, bf16[32,1,32,128]{3,2,1,0:T(8,128)(2,1)S(1)}, u32[]{:S(2)}, u32[]{:S(2)}) collective-permute-start(bf16[32,1,32,128]{3,2,1,0:T(8,128)(2,1)S(1)} %collective-permute-done.refs_0_), channel_id=1, source_target_pairs={{0,1},{1,3},{3,2},{2,0},{4,5},{5,7},{7,6},{6,4},{8,9},{9,11},{11,1... | collective-permute-start | bytes 786440 | tf_op jit(solution)/shard_map/ppermute | solution.py:351
  12.9 0.0 copy-done.1
  12.9 0.1 shard_map.52.refs_2_.refs_1_.refs_4_
  13.0 0.1 collective-permute-done.3.refs_0_
  13.2 0.1 shard_map.53.refs_1_
  13.3 8.0 %collective-permute-done.1.refs_1_ = bf16[32,1,32,128]{3,2,1,0:T(8,128)(2,1)S(1)} collective-permute-done((bf16[32,1,32,128]{3,2,1,0:T(8,128)(2,1)S(1)}, bf16[32,1,32,128]{3,2,1,0:T(8,128)(2,1)S(1)}, u32[]{:S(2)}, u32[]{:S(2)}) %collective-permute-start.1) | collective-permute-done | bytes 262176 | tf_op jit(solution)/shard_map/ppermute | solution.py:351
  21.3 1.2 %collective-permute-start.4 = (bf16[32,1,32,128]{3,2,1,0:T(8,128)(2,1)S(1)}, bf16[32,1,32,128]{3,2,1,0:T(8,128)(2,1)S(1)}, u32[]{:S(2)}, u32[]{:S(2)}) collective-permute-start(bf16[32,1,32,128]{3,2,1,0:T(8,128)(2,1)S(1)} %collective-permute-done.1.refs_1_), channel_id=1, source_target_pairs={{0,1},{1,3},{3,2},{2,0},{4,5},{5,7},{7,6},{6,4},{8,9},{9,11},{11,1... | collective-permute-start | bytes 786440 | tf_op jit(solution)/shard_map/ppermute | solution.py:351
  22.5 0.0 collective-permute-done.2.behind_ref
  22.5 0.1 shard_map.51.refs_1_
  22.6 0.3 shard_map.54.refs_3_.refs_2_.refs_5_
  22.9 0.4 %collective-permute-start.6 = (bf16[64,4096]{1,0:T(8,128)(2,1)S(1)}, bf16[64,4096]{1,0:T(8,128)(2,1)S(1)}, u32[]{:S(2)}, u32[]{:S(2)}) collective-permute-start(bf16[64,4096]{1,0:T(8,128)(2,1)S(1)} %shard_map.54.refs_3_.refs_2_.refs_5_), channel_id=1, source_target_pairs={{4,0},{8,4},{12,8},{16,12},{20,16},{24,20},{28,24},{0,28},{5,1},{9... | collective-permute-start | bytes 1572872 | tf_op jit(solution)/shard_map/ppermute | solution.py:375
  23.3 7.3 %collective-permute-done.4.refs_0_ = bf16[32,1,32,128]{3,2,1,0:T(8,128)(2,1)S(1)} collective-permute-done((bf16[32,1,32,128]{3,2,1,0:T(8,128)(2,1)S(1)}, bf16[32,1,32,128]{3,2,1,0:T(8,128)(2,1)S(1)}, u32[]{:S(2)}, u32[]{:S(2)}) %collective-permute-start.4) | collective-permute-done | bytes 262176 | tf_op jit(solution)/shard_map/ppermute | solution.py:351
  30.6 0.1 shard_map.55.refs_4_.refs_3_.refs_6_
  30.7 0.1 collective-permute-start.7
  30.8 0.9 %shard_map.56 = (f32[64,512]{1,0:T(8,128)S(1)}, f32[64,512]{1,0:T(8,128)S(1)}) custom-call(bf16[192,4096]{1,0:T(8,128)(2,1)S(1)} %get-tuple-element.25.refs_0_, bf16[96,4096]{1,0:T(8,128)(2,1)S(1)} %shard_map.51.refs_1_, bf16[32,4096]{1,0:T(8,128)(2,1)S(1)} %shard_map.52.refs_2_.refs_1_.refs_4_, bf16[64,4096]{1,0:T(8,128)(2,1)S(1)} %shard_map.54.refs_3_.refs_2_.refs_5_, ...), custom_call_target="tpu_custom_call" | custom-call | flops 452984832 | bytes 8388608 | tf_op jit(solution)/shard_map/pallas_call | solution.py:314
  31.7 0.6 %collective-permute-start.5 = (f32[64,512]{1,0:T(8,128)S(1)}, f32[64,512]{1,0:T(8,128)S(1)}, u32[]{:S(2)}, u32[]{:S(2)}) collective-permute-start(f32[64,512]{1,0:T(8,128)S(1)} %get-tuple-element.30), channel_id=1, source_target_pairs={{0,4},{4,0},{8,12},{12,8},{16,20},{20,16},{24,28},{28,24},{1,5},{5... | collective-permute-start | bytes 393224 | tf_op jit(solution)/shard_map/ppermute | solution.py:411
  32.3 1.5 %shard_map.57.before = bf16[16,2,64,256]{3,2,1,0:T(8,128)(2,1)} custom-call(bf16[144,128]{1,0:T(8,128)(2,1)S(1)} %get-tuple-element.31.refs_0_, bf16[32,4096]{1,0:T(8,128)(2,1)S(1)} %shard_map.52.refs_2_.refs_1_.refs_4_, bf16[64,4096]{1,0:T(8,128)(2,1)S(1)} %shard_map.54.refs_3_.refs_2_.refs_5_, bf16[32,4096]{1,0:T(8,128)(2,1)S(1)} %shard_map.55.refs_4_.refs_3_.refs_6_), custom_call_target="tpu_custom_call" | custom-call | flops 150994944 | bytes 4194304 | tf_op jit(solution)/shard_map/pallas_call | solution.py:393
  33.8 0.0 collective-permute-done.5.other_ref
  33.9 1.1 %collective-permute-start.8 = (f32[16,512]{1,0:T(8,128)S(1)}, f32[16,512]{1,0:T(8,128)S(1)}, u32[]{:S(2)}, u32[]{:S(2)}) collective-permute-start(f32[16,512]{1,0:T(8,128)S(1)} %get-tuple-element.39), channel_id=1, source_target_pairs={{0,8},{4,12},{8,0},{12,4},{16,24},{20,28},{24,16},{28,20},{1,9},{5... | collective-permute-start | bytes 98312 | tf_op jit(solution)/shard_map/ppermute | solution.py:421
  35.0 0.7 %collective-permute-start.9 = (f32[16,512]{1,0:T(8,128)S(1)}, f32[16,512]{1,0:T(8,128)S(1)}, u32[]{:S(2)}, u32[]{:S(2)}) collective-permute-start(f32[16,512]{1,0:T(8,128)S(1)} %get-tuple-element.40), channel_id=1, source_target_pairs={{0,16},{4,20},{8,24},{12,28},{16,0},{20,4},{24,8},{28,12},{1,17},{... | collective-permute-start | bytes 98312 | tf_op jit(solution)/shard_map/ppermute | solution.py:421
  35.6 1.8 %collective-permute-start.10 = (f32[16,512]{1,0:T(8,128)S(1)}, f32[16,512]{1,0:T(8,128)S(1)}, u32[]{:S(2)}, u32[]{:S(2)}) collective-permute-start(f32[16,512]{1,0:T(8,128)S(1)} %get-tuple-element.41), channel_id=1, source_target_pairs={{0,24},{4,28},{8,16},{12,20},{16,8},{20,12},{24,0},{28,4},{1,25},{... | collective-permute-start | bytes 98312 | tf_op jit(solution)/shard_map/ppermute | solution.py:421
  37.4 0.0 collective-permute-done.7.refs_3_
  37.4 0.0 collective-permute-done.6.refs_2_
  37.5 1.6 %shard_map.59 = bf16[16,2,64,256]{3,2,1,0:T(8,128)(2,1)} custom-call(bf16[16,2,64,256]{3,2,1,0:T(8,128)(2,1)} %shard_map.57.before, bf16[144,256]{1,0:T(8,128)(2,1)S(1)} %get-tuple-element.35.refs_0_, bf16[32,4096]{1,0:T(8,128)(2,1)S(1)} %shard_map.53.refs_1_, bf16[64,4096]{1,0:T(8,128)(2,1)S(1)} %collective-permute-done.6.refs_2_, ...), custom_call_target="tpu_custom_call", output_to_operand_aliasing={{}: (0, {})} | custom-call | flops 301989888 | bytes 4194304 | tf_op jit(solution)/shard_map/pallas_call | solution.py:393
  39.0 0.0 collective-permute-done.8.refs_1_
  39.0 0.0 collective-permute-done.9.refs_2_
  39.1 1.4 %collective-permute-done.10.refs_3_ = f32[16,512]{1,0:T(8,128)S(1)} collective-permute-done((f32[16,512]{1,0:T(8,128)S(1)}, f32[16,512]{1,0:T(8,128)S(1)}, u32[]{:S(2)}, u32[]{:S(2)}) %collective-permute-start.10) | collective-permute-done | bytes 32800 | tf_op jit(solution)/shard_map/ppermute | solution.py:421
  40.4 0.8 %shard_map.60 = f32[16,16,27]{2,1,0:T(8,128)} custom-call(f32[16,512]{1,0:T(8,128)S(1)} %get-tuple-element.38.refs_0_, f32[16,512]{1,0:T(8,128)S(1)} %collective-permute-done.8.refs_1_, f32[16,512]{1,0:T(8,128)S(1)} %collective-permute-done.9.refs_2_, f32[16,512]{1,0:T(8,128)S(1)} %collective-permute-done.10.refs_3_), custom_call_target="tpu_custom_call" | custom-call | flops 65536 | bytes 524288 | tf_op jit(solution)/shard_map/pallas_call | solution.py:314
  (2 shorter events, 0.0 us)
Async XLA Ops:
  0.6 5.5 %copy-start = (bf16[27,64,128]{2,1,0:T(8,128)(2,1)S(1)}, bf16[27,64,128]{2,1,0:T(8,128)(2,1)}, u32[]{:S(2)}) copy-start(bf16[27,64,128]{2,1,0:T(8,128)(2,1)} %param.5) | copy-start | bytes 1327108
  0.6 12.3 %copy-start.1 = (bf16[32,1,32,128]{3,2,1,0:T(8,128)(2,1)S(1)}, bf16[32,1,32,128]{3,2,1,0:T(8,128)(2,1)}, u32[]{:S(2)}) copy-start(bf16[32,1,32,128]{3,2,1,0:T(8,128)(2,1)} %refs_0_.3) | copy-start | bytes 786436
  0.7 21.9 %collective-permute-start.2 = (bf16[16,2,64,256]{3,2,1,0:T(8,128)(2,1)}, bf16[16,2,64,256]{3,2,1,0:T(8,128)(2,1)S(1)}, u32[]{:S(2)}, u32[]{:S(2)}) collective-permute-start(bf16[16,2,64,256]{3,2,1,0:T(8,128)(2,1)} %refs_0_.2), channel_id=1, source_target_pairs={{0,4},{4,8},{8,12},{12,16},{16,20},{20,24},{24,28},{28,0},{1,5},{5... | collective-permute-start | bytes 3145736 | tf_op jit(solution)/shard_map/ppermute | solution.py:361
  1.2 10.1 %collective-permute-start = (bf16[32,1,32,128]{3,2,1,0:T(8,128)(2,1)}, bf16[32,1,32,128]{3,2,1,0:T(8,128)(2,1)S(1)}, u32[]{:S(2)}, u32[]{:S(2)}) collective-permute-start(bf16[32,1,32,128]{3,2,1,0:T(8,128)(2,1)} %refs_0_.3), channel_id=1, source_target_pairs={{0,1},{1,3},{3,2},{2,0},{4,5},{5,7},{7,6},{6,4},{8,9},{9,11},{11,1... | collective-permute-start | bytes 786440 | tf_op jit(solution)/shard_map/ppermute | solution.py:351
  3.8 9.4 %collective-permute-start.3 = (bf16[32,1,32,128]{3,2,1,0:T(8,128)(2,1)}, bf16[32,1,32,128]{3,2,1,0:T(8,128)(2,1)S(1)}, u32[]{:S(2)}, u32[]{:S(2)}) collective-permute-start(bf16[32,1,32,128]{3,2,1,0:T(8,128)(2,1)} %refs_0_.3), channel_id=1, source_target_pairs={{4,0},{8,4},{12,8},{16,12},{20,16},{24,20},{28,24},{0,28},{5,1},{9... | collective-permute-start | bytes 786440 | tf_op jit(solution)/shard_map/ppermute | solution.py:362
  6.1 1.2 %copy-start.2 = (bf16[16,2,64,256]{3,2,1,0:T(8,128)(2,1)S(1)}, bf16[16,2,64,256]{3,2,1,0:T(8,128)(2,1)}, u32[]{:S(2)}) copy-start(bf16[16,2,64,256]{3,2,1,0:T(8,128)(2,1)} %refs_0_.2) | copy-start | bytes 3145732
  11.3 10.0 %collective-permute-start.1 = (bf16[32,1,32,128]{3,2,1,0:T(8,128)(2,1)S(1)}, bf16[32,1,32,128]{3,2,1,0:T(8,128)(2,1)S(1)}, u32[]{:S(2)}, u32[]{:S(2)}) collective-permute-start(bf16[32,1,32,128]{3,2,1,0:T(8,128)(2,1)S(1)} %collective-permute-done.refs_0_), channel_id=1, source_target_pairs={{0,1},{1,3},{3,2},{2,0},{4,5},{5,7},{7,6},{6,4},{8,9},{9,11},{11,1... | collective-permute-start | bytes 786440 | tf_op jit(solution)/shard_map/ppermute | solution.py:351
  21.3 9.2 %collective-permute-start.4 = (bf16[32,1,32,128]{3,2,1,0:T(8,128)(2,1)S(1)}, bf16[32,1,32,128]{3,2,1,0:T(8,128)(2,1)S(1)}, u32[]{:S(2)}, u32[]{:S(2)}) collective-permute-start(bf16[32,1,32,128]{3,2,1,0:T(8,128)(2,1)S(1)} %collective-permute-done.1.refs_1_), channel_id=1, source_target_pairs={{0,1},{1,3},{3,2},{2,0},{4,5},{5,7},{7,6},{6,4},{8,9},{9,11},{11,1... | collective-permute-start | bytes 786440 | tf_op jit(solution)/shard_map/ppermute | solution.py:351
  22.9 14.6 %collective-permute-start.6 = (bf16[64,4096]{1,0:T(8,128)(2,1)S(1)}, bf16[64,4096]{1,0:T(8,128)(2,1)S(1)}, u32[]{:S(2)}, u32[]{:S(2)}) collective-permute-start(bf16[64,4096]{1,0:T(8,128)(2,1)S(1)} %shard_map.54.refs_3_.refs_2_.refs_5_), channel_id=1, source_target_pairs={{4,0},{8,4},{12,8},{16,12},{20,16},{24,20},{28,24},{0,28},{5,1},{9... | collective-permute-start | bytes 1572872 | tf_op jit(solution)/shard_map/ppermute | solution.py:375
  30.7 6.7 %collective-permute-start.7 = (bf16[32,4096]{1,0:T(8,128)(2,1)S(1)}, bf16[32,4096]{1,0:T(8,128)(2,1)S(1)}, u32[]{:S(2)}, u32[]{:S(2)}) collective-permute-start(bf16[32,4096]{1,0:T(8,128)(2,1)S(1)} %shard_map.55.refs_4_.refs_3_.refs_6_), channel_id=1, source_target_pairs={{4,0},{8,4},{12,8},{16,12},{20,16},{24,20},{28,24},{0,28},{5,1},{9... | collective-permute-start | bytes 786440 | tf_op jit(solution)/shard_map/ppermute | solution.py:375
  31.7 2.1 %collective-permute-start.5 = (f32[64,512]{1,0:T(8,128)S(1)}, f32[64,512]{1,0:T(8,128)S(1)}, u32[]{:S(2)}, u32[]{:S(2)}) collective-permute-start(f32[64,512]{1,0:T(8,128)S(1)} %get-tuple-element.30), channel_id=1, source_target_pairs={{0,4},{4,0},{8,12},{12,8},{16,20},{20,16},{24,28},{28,24},{1,5},{5... | collective-permute-start | bytes 393224 | tf_op jit(solution)/shard_map/ppermute | solution.py:411
  33.9 5.1 %collective-permute-start.8 = (f32[16,512]{1,0:T(8,128)S(1)}, f32[16,512]{1,0:T(8,128)S(1)}, u32[]{:S(2)}, u32[]{:S(2)}) collective-permute-start(f32[16,512]{1,0:T(8,128)S(1)} %get-tuple-element.39), channel_id=1, source_target_pairs={{0,8},{4,12},{8,0},{12,4},{16,24},{20,28},{24,16},{28,20},{1,9},{5... | collective-permute-start | bytes 98312 | tf_op jit(solution)/shard_map/ppermute | solution.py:421
  35.0 4.1 %collective-permute-start.9 = (f32[16,512]{1,0:T(8,128)S(1)}, f32[16,512]{1,0:T(8,128)S(1)}, u32[]{:S(2)}, u32[]{:S(2)}) collective-permute-start(f32[16,512]{1,0:T(8,128)S(1)} %get-tuple-element.40), channel_id=1, source_target_pairs={{0,16},{4,20},{8,24},{12,28},{16,0},{20,4},{24,8},{28,12},{1,17},{... | collective-permute-start | bytes 98312 | tf_op jit(solution)/shard_map/ppermute | solution.py:421
  35.6 4.8 %collective-permute-start.10 = (f32[16,512]{1,0:T(8,128)S(1)}, f32[16,512]{1,0:T(8,128)S(1)}, u32[]{:S(2)}, u32[]{:S(2)}) collective-permute-start(f32[16,512]{1,0:T(8,128)S(1)} %get-tuple-element.41), channel_id=1, source_target_pairs={{0,24},{4,28},{8,16},{12,20},{16,8},{20,12},{24,0},{28,4},{1,25},{... | collective-permute-start | bytes 98312 | tf_op jit(solution)/shard_map/ppermute | solution.py:421

commit v8 on v6

--- a/solution.py
+++ b/solution.py
@@ -335,8 +335,8 @@
     got = {0: grad_out}
     for mask in sorted(range(1, count), key=lambda mask: (mask & (mask - 1) > 0, -mask)):
         low = mask & -mask
-        if mask == 3:
-            got[2], views = lax.optimization_barrier((got[2], views))
+        if mask == 1:
+            got[0], views = lax.optimization_barrier((got[0], views))
         got[mask] = lax.ppermute(got[mask - low], "chan", [(i, i ^ low) for i in range(count)])
     lines = lambda *parts: call(
         lines_kernel,
@@ -346,7 +346,7 @@
         cost=(1 << 20, 2 << 20),
     )
     behind = lax.ppermute(volume, "depth", farther)
-    next_own = lax.ppermute(grad_out, "depth", nearer)
+    next_own = lax.ppermute(got[0], "depth", nearer)
     behind_views = call(
         behind_views_kernel,
         jax.ShapeDtypeStruct((6 * chans, cells), BF16),

time: 38.1 us -> 38.4 us (level)
  waiting for transfers between devices: 12.8 us -> 15.1 us
  starting transfers between devices: 15.6 us -> 14.6 us
  local copies, waits for them, and re-layouts: 2.24 us -> 1.25 us
    ppermute x3, waiting for transfers between devices: 9.81 us -> 12.2 us  [shards(): lax.ppermute(got[mask - low], 'chan', [(i, i ^ low) for i in range(count)])]
    unnamed x6, local copies, waits for them, and re-layouts: 2.21 us -> 1.23 us
    ppermute x2, starting transfers between devices: 1.74 us -> 0.87 us  [shards(): lax.ppermute(part, 'depth', nearer)]
  transfers between devices with their start and end apart: 11 -> 11, of which waited for: 5 -> 6; matrix products, arithmetic and copies ran while one was open for 0% -> 0% of each run, Pallas kernels for 15% -> 15%
where the time goes in v8:
time: 38.4 us; the launch traced here: 38.2 us
  waiting for transfers between devices  15.1 us (39%)
  starting transfers between devices  14.6 us (38%)
  Pallas kernels  6.49 us (17%)
  local copies, waits for them, and re-layouts  1.25 us (3%)
  between operations  0.74 us (2%)
    ppermute x3, waiting for transfers between devices, shards(): lax.ppermute(got[mask - low], 'chan', [(i, i ^ low) for i in range(count)])  12.2 us
    ppermute x3, starting transfers between devices, shards(): lax.ppermute(got[mask - low], 'chan', [(i, i ^ low) for i in range(count)])  7.11 us
    ppermute x3, starting transfers between devices, shards(): lax.ppermute(term, 'depth', [(i, i ^ 2 * k + 2) for i in range(depth)])  3.7 us
    pallas_call x9, Pallas kernels, call(): pl.pallas_call(kernel, out_shape=out_shape, in_specs=[VMEM] * len(args),...  3.36 us
    pallas_call x2, Pallas kernels, input_plane(): pl.pallas_call(kernel if before is None else lambda before, *refs: kernel...  3.13 us
    ppermute x3, waiting for transfers between devices, shards(): lax.ppermute(term, 'depth', [(i, i ^ 2 * k + 2) for i in range(depth)])  2.45 us
    ppermute x1, starting transfers between devices, shards(): next_own = lax.ppermute(got[0], 'depth', nearer)  2.34 us
    unnamed x6, local copies, waits for them, and re-layouts  1.23 us
  transfers between devices with their start and end apart: 11, of which 6 were waited for; matrix products, arithmetic and copies ran while one was open for 0% of the time, Pallas kernels for 15%

profile of v8, /device:TPU:0, one launch (start us, length us, event | category | flops | bytes accessed | tf_op | source)
XLA Modules:
  0.0 38.2 jit_solution(15206925101101966017)
XLA Ops:
  0.6 0.0 copy-start
  0.6 0.0 copy-start.1
  0.7 0.5 %collective-permute-start.1 = (bf16[16,2,64,256]{3,2,1,0:T(8,128)(2,1)}, bf16[16,2,64,256]{3,2,1,0:T(8,128)(2,1)S(1)}, u32[]{:S(2)}, u32[]{:S(2)}) collective-permute-start(bf16[16,2,64,256]{3,2,1,0:T(8,128)(2,1)} %refs_0_.2), channel_id=1, source_target_pairs={{0,4},{4,8},{8,12},{12,16},{16,20},{20,24},{24,28},{28,0},{1,5},{5... | collective-permute-start | bytes 3145736 | tf_op jit(solution)/shard_map/ppermute | solution.py:348
  1.2 3.7 %collective-permute-start.3 = (bf16[32,1,32,128]{3,2,1,0:T(8,128)(2,1)}, bf16[32,1,32,128]{3,2,1,0:T(8,128)(2,1)S(1)}, u32[]{:S(2)}, u32[]{:S(2)}) collective-permute-start(bf16[32,1,32,128]{3,2,1,0:T(8,128)(2,1)} %refs_0_.3), channel_id=1, source_target_pairs={{0,2},{1,3},{2,0},{3,1},{4,6},{5,7},{6,4},{7,5},{8,10},{9,11},{10,... | collective-permute-start | bytes 786440 | tf_op jit(solution)/shard_map/ppermute | solution.py:340
  4.8 0.0 copy-done
  4.8 0.0 copy-start.2
  4.9 1.2 %copy-done.2 = bf16[16,2,64,256]{3,2,1,0:T(8,128)(2,1)S(1)} copy-done((bf16[16,2,64,256]{3,2,1,0:T(8,128)(2,1)S(1)}, bf16[16,2,64,256]{3,2,1,0:T(8,128)(2,1)}, u32[]{:S(2)}) %copy-start.2) | copy-done | bytes 1048600
  6.1 0.9 %shard_map.50 = (bf16[192,4096]{1,0:T(8,128)(2,1)S(1)}, bf16[144,128]{1,0:T(8,128)(2,1)S(1)}, bf16[144,256]{1,0:T(8,128)(2,1)S(1)}) custom-call(bf16[16,2,64,256]{3,2,1,0:T(8,128)(2,1)S(1)} %copy-done.2, bf16[27,16,128]{2,1,0:T(8,128)(2,1)S(1)} %constant_dynamic-slice_fusion.refs_1_), custom_call_target="tpu_custom_call" | custom-call | flops 536870912 | bytes 4194304 | tf_op jit(solution)/shard_map/pallas_call | solution.py:302
  7.0 0.0 copy-done.1
  7.0 2.3 %collective-permute-start.2 = (bf16[32,1,32,128]{3,2,1,0:T(8,128)(2,1)S(1)}, bf16[32,1,32,128]{3,2,1,0:T(8,128)(2,1)S(1)}, u32[]{:S(2)}, u32[]{:S(2)}) collective-permute-start(bf16[32,1,32,128]{3,2,1,0:T(8,128)(2,1)S(1)} %copy-done.1), channel_id=1, source_target_pairs={{4,0},{8,4},{12,8},{16,12},{20,16},{24,20},{28,24},{0,28},{5,1},{9... | collective-permute-start | bytes 786440 | tf_op jit(solution)/shard_map/ppermute | solution.py:349
  9.3 1.6 %collective-permute-start = (bf16[32,1,32,128]{3,2,1,0:T(8,128)(2,1)S(1)}, bf16[32,1,32,128]{3,2,1,0:T(8,128)(2,1)S(1)}, u32[]{:S(2)}, u32[]{:S(2)}) collective-permute-start(bf16[32,1,32,128]{3,2,1,0:T(8,128)(2,1)S(1)} %copy-done.1), channel_id=1, source_target_pairs={{0,1},{1,0},{2,3},{3,2},{4,5},{5,4},{6,7},{7,6},{8,9},{9,8},{10,11... | collective-permute-start | bytes 786440 | tf_op jit(solution)/shard_map/ppermute | solution.py:340
  10.9 0.1 shard_map.52.refs_2_.refs_1_.refs_4_
  11.0 6.0 %collective-permute-done.3.refs_1_ = bf16[32,1,32,128]{3,2,1,0:T(8,128)(2,1)S(1)} collective-permute-done((bf16[32,1,32,128]{3,2,1,0:T(8,128)(2,1)}, bf16[32,1,32,128]{3,2,1,0:T(8,128)(2,1)S(1)}, u32[]{:S(2)}, u32[]{:S(2)}) %collective-permute-start.3) | collective-permute-done | bytes 262176 | tf_op jit(solution)/shard_map/ppermute | solution.py:340
  17.0 1.9 %collective-permute-start.4 = (bf16[32,1,32,128]{3,2,1,0:T(8,128)(2,1)S(1)}, bf16[32,1,32,128]{3,2,1,0:T(8,128)(2,1)S(1)}, u32[]{:S(2)}, u32[]{:S(2)}) collective-permute-start(bf16[32,1,32,128]{3,2,1,0:T(8,128)(2,1)S(1)} %collective-permute-done.3.refs_1_), channel_id=1, source_target_pairs={{0,1},{1,0},{2,3},{3,2},{4,5},{5,4},{6,7},{7,6},{8,9},{9,8},{10,11... | collective-permute-start | bytes 786440 | tf_op jit(solution)/shard_map/ppermute | solution.py:340
  18.9 0.0 collective-permute-done.2.refs_0_
  18.9 0.1 shard_map.53.refs_1_
  19.1 0.5 %collective-permute-done.1.behind_ref = bf16[16,2,64,256]{3,2,1,0:T(8,128)(2,1)S(1)} collective-permute-done((bf16[16,2,64,256]{3,2,1,0:T(8,128)(2,1)}, bf16[16,2,64,256]{3,2,1,0:T(8,128)(2,1)S(1)}, u32[]{:S(2)}, u32[]{:S(2)}) %collective-permute-start.1) | collective-permute-done | bytes 1048608 | tf_op jit(solution)/shard_map/ppermute | solution.py:348
  19.5 0.1 shard_map.51.refs_1_
  19.6 1.3 %collective-permute-done.refs_0_ = bf16[32,1,32,128]{3,2,1,0:T(8,128)(2,1)S(1)} collective-permute-done((bf16[32,1,32,128]{3,2,1,0:T(8,128)(2,1)S(1)}, bf16[32,1,32,128]{3,2,1,0:T(8,128)(2,1)S(1)}, u32[]{:S(2)}, u32[]{:S(2)}) %collective-permute-start) | collective-permute-done | bytes 262176 | tf_op jit(solution)/shard_map/ppermute | solution.py:340
  20.9 0.3 shard_map.54.refs_3_.refs_2_.refs_5_
  21.1 0.3 collective-permute-start.6
  21.5 4.9 %collective-permute-done.4.refs_0_ = bf16[32,1,32,128]{3,2,1,0:T(8,128)(2,1)S(1)} collective-permute-done((bf16[32,1,32,128]{3,2,1,0:T(8,128)(2,1)S(1)}, bf16[32,1,32,128]{3,2,1,0:T(8,128)(2,1)S(1)}, u32[]{:S(2)}, u32[]{:S(2)}) %collective-permute-start.4) | collective-permute-done | bytes 262176 | tf_op jit(solution)/shard_map/ppermute | solution.py:340
  26.4 0.1 shard_map.55.refs_4_.refs_3_.refs_6_
  26.5 0.5 %collective-permute-start.7 = (bf16[32,4096]{1,0:T(8,128)(2,1)S(1)}, bf16[32,4096]{1,0:T(8,128)(2,1)S(1)}, u32[]{:S(2)}, u32[]{:S(2)}) collective-permute-start(bf16[32,4096]{1,0:T(8,128)(2,1)S(1)} %shard_map.55.refs_4_.refs_3_.refs_6_), channel_id=1, source_target_pairs={{4,0},{8,4},{12,8},{16,12},{20,16},{24,20},{28,24},{0,28},{5,1},{9... | collective-permute-start | bytes 786440 | tf_op jit(solution)/shard_map/ppermute | solution.py:362
  27.1 0.9 %shard_map.56 = (f32[64,512]{1,0:T(8,128)S(1)}, f32[64,512]{1,0:T(8,128)S(1)}) custom-call(bf16[192,4096]{1,0:T(8,128)(2,1)S(1)} %get-tuple-element.25.refs_0_, bf16[96,4096]{1,0:T(8,128)(2,1)S(1)} %shard_map.51.refs_1_, bf16[32,4096]{1,0:T(8,128)(2,1)S(1)} %shard_map.52.refs_2_.refs_1_.refs_4_, bf16[64,4096]{1,0:T(8,128)(2,1)S(1)} %shard_map.54.refs_3_.refs_2_.refs_5_, ...), custom_call_target="tpu_custom_call" | custom-call | flops 452984832 | bytes 8388608 | tf_op jit(solution)/shard_map/pallas_call | solution.py:302
  28.0 0.1 collective-permute-start.5
  28.1 1.5 %shard_map.57.before = bf16[16,2,64,256]{3,2,1,0:T(8,128)(2,1)} custom-call(bf16[144,128]{1,0:T(8,128)(2,1)S(1)} %get-tuple-element.31.refs_0_, bf16[32,4096]{1,0:T(8,128)(2,1)S(1)} %shard_map.52.refs_2_.refs_1_.refs_4_, bf16[64,4096]{1,0:T(8,128)(2,1)S(1)} %shard_map.54.refs_3_.refs_2_.refs_5_, bf16[32,4096]{1,0:T(8,128)(2,1)S(1)} %shard_map.55.refs_4_.refs_3_.refs_6_), custom_call_target="tpu_custom_call" | custom-call | flops 150994944 | bytes 4194304 | tf_op jit(solution)/shard_map/pallas_call | solution.py:380
  29.6 0.0 collective-permute-done.5.other_ref
  29.7 1.9 %collective-permute-start.8 = (f32[16,512]{1,0:T(8,128)S(1)}, f32[16,512]{1,0:T(8,128)S(1)}, u32[]{:S(2)}, u32[]{:S(2)}) collective-permute-start(f32[16,512]{1,0:T(8,128)S(1)} %get-tuple-element.39), channel_id=1, source_target_pairs={{0,8},{4,12},{8,0},{12,4},{16,24},{20,28},{24,16},{28,20},{1,9},{5... | collective-permute-start | bytes 98312 | tf_op jit(solution)/shard_map/ppermute | solution.py:408
  31.6 1.1 %collective-permute-start.9 = (f32[16,512]{1,0:T(8,128)S(1)}, f32[16,512]{1,0:T(8,128)S(1)}, u32[]{:S(2)}, u32[]{:S(2)}) collective-permute-start(f32[16,512]{1,0:T(8,128)S(1)} %get-tuple-element.40), channel_id=1, source_target_pairs={{0,16},{4,20},{8,24},{12,28},{16,0},{20,4},{24,8},{28,12},{1,17},{... | collective-permute-start | bytes 98312 | tf_op jit(solution)/shard_map/ppermute | solution.py:408
  32.6 0.8 %collective-permute-start.10 = (f32[16,512]{1,0:T(8,128)S(1)}, f32[16,512]{1,0:T(8,128)S(1)}, u32[]{:S(2)}, u32[]{:S(2)}) collective-permute-start(f32[16,512]{1,0:T(8,128)S(1)} %get-tuple-element.41), channel_id=1, source_target_pairs={{0,24},{4,28},{8,16},{12,20},{16,8},{20,12},{24,0},{28,4},{1,25},{... | collective-permute-start | bytes 98312 | tf_op jit(solution)/shard_map/ppermute | solution.py:408
  33.4 0.0 collective-permute-done.7.refs_3_
  33.4 0.0 collective-permute-done.6.refs_2_
  33.4 1.6 %shard_map.59 = bf16[16,2,64,256]{3,2,1,0:T(8,128)(2,1)} custom-call(bf16[16,2,64,256]{3,2,1,0:T(8,128)(2,1)} %shard_map.57.before, bf16[144,256]{1,0:T(8,128)(2,1)S(1)} %get-tuple-element.35.refs_0_, bf16[32,4096]{1,0:T(8,128)(2,1)S(1)} %shard_map.53.refs_1_, bf16[64,4096]{1,0:T(8,128)(2,1)S(1)} %collective-permute-done.6.refs_2_, ...), custom_call_target="tpu_custom_call", output_to_operand_aliasing={{}: (0, {})} | custom-call | flops 301989888 | bytes 4194304 | tf_op jit(solution)/shard_map/pallas_call | solution.py:380
  35.0 0.0 collective-permute-done.8.refs_1_
  35.0 0.5 %collective-permute-done.9.refs_2_ = f32[16,512]{1,0:T(8,128)S(1)} collective-permute-done((f32[16,512]{1,0:T(8,128)S(1)}, f32[16,512]{1,0:T(8,128)S(1)}, u32[]{:S(2)}, u32[]{:S(2)}) %collective-permute-start.9) | collective-permute-done | bytes 32800 | tf_op jit(solution)/shard_map/ppermute | solution.py:408
  35.5 1.9 %collective-permute-done.10.refs_3_ = f32[16,512]{1,0:T(8,128)S(1)} collective-permute-done((f32[16,512]{1,0:T(8,128)S(1)}, f32[16,512]{1,0:T(8,128)S(1)}, u32[]{:S(2)}, u32[]{:S(2)}) %collective-permute-start.10) | collective-permute-done | bytes 32800 | tf_op jit(solution)/shard_map/ppermute | solution.py:408
  37.4 0.8 %shard_map.60 = f32[16,16,27]{2,1,0:T(8,128)} custom-call(f32[16,512]{1,0:T(8,128)S(1)} %get-tuple-element.38.refs_0_, f32[16,512]{1,0:T(8,128)S(1)} %collective-permute-done.8.refs_1_, f32[16,512]{1,0:T(8,128)S(1)} %collective-permute-done.9.refs_2_, f32[16,512]{1,0:T(8,128)S(1)} %collective-permute-done.10.refs_3_), custom_call_target="tpu_custom_call" | custom-call | flops 65536 | bytes 524288 | tf_op jit(solution)/shard_map/pallas_call | solution.py:302
  (2 shorter events, 0.0 us)
Async XLA Ops:
  0.6 4.2 %copy-start = (bf16[27,64,128]{2,1,0:T(8,128)(2,1)S(1)}, bf16[27,64,128]{2,1,0:T(8,128)(2,1)}, u32[]{:S(2)}) copy-start(bf16[27,64,128]{2,1,0:T(8,128)(2,1)} %param.5) | copy-start | bytes 1327108
  0.6 6.3 %copy-start.1 = (bf16[32,1,32,128]{3,2,1,0:T(8,128)(2,1)S(1)}, bf16[32,1,32,128]{3,2,1,0:T(8,128)(2,1)}, u32[]{:S(2)}) copy-start(bf16[32,1,32,128]{3,2,1,0:T(8,128)(2,1)} %refs_0_.3) | copy-start | bytes 786436
  0.7 18.9 %collective-permute-start.1 = (bf16[16,2,64,256]{3,2,1,0:T(8,128)(2,1)}, bf16[16,2,64,256]{3,2,1,0:T(8,128)(2,1)S(1)}, u32[]{:S(2)}, u32[]{:S(2)}) collective-permute-start(bf16[16,2,64,256]{3,2,1,0:T(8,128)(2,1)} %refs_0_.2), channel_id=1, source_target_pairs={{0,4},{4,8},{8,12},{12,16},{16,20},{20,24},{24,28},{28,0},{1,5},{5... | collective-permute-start | bytes 3145736 | tf_op jit(solution)/shard_map/ppermute | solution.py:348
  1.2 15.9 %collective-permute-start.3 = (bf16[32,1,32,128]{3,2,1,0:T(8,128)(2,1)}, bf16[32,1,32,128]{3,2,1,0:T(8,128)(2,1)S(1)}, u32[]{:S(2)}, u32[]{:S(2)}) collective-permute-start(bf16[32,1,32,128]{3,2,1,0:T(8,128)(2,1)} %refs_0_.3), channel_id=1, source_target_pairs={{0,2},{1,3},{2,0},{3,1},{4,6},{5,7},{6,4},{7,5},{8,10},{9,11},{10,... | collective-permute-start | bytes 786440 | tf_op jit(solution)/shard_map/ppermute | solution.py:340
  4.8 1.2 %copy-start.2 = (bf16[16,2,64,256]{3,2,1,0:T(8,128)(2,1)S(1)}, bf16[16,2,64,256]{3,2,1,0:T(8,128)(2,1)}, u32[]{:S(2)}) copy-start(bf16[16,2,64,256]{3,2,1,0:T(8,128)(2,1)} %refs_0_.2) | copy-start | bytes 3145732
  7.0 11.9 %collective-permute-start.2 = (bf16[32,1,32,128]{3,2,1,0:T(8,128)(2,1)S(1)}, bf16[32,1,32,128]{3,2,1,0:T(8,128)(2,1)S(1)}, u32[]{:S(2)}, u32[]{:S(2)}) collective-permute-start(bf16[32,1,32,128]{3,2,1,0:T(8,128)(2,1)S(1)} %copy-done.1), channel_id=1, source_target_pairs={{4,0},{8,4},{12,8},{16,12},{20,16},{24,20},{28,24},{0,28},{5,1},{9... | collective-permute-start | bytes 786440 | tf_op jit(solution)/shard_map/ppermute | solution.py:349
  9.3 11.5 %collective-permute-start = (bf16[32,1,32,128]{3,2,1,0:T(8,128)(2,1)S(1)}, bf16[32,1,32,128]{3,2,1,0:T(8,128)(2,1)S(1)}, u32[]{:S(2)}, u32[]{:S(2)}) collective-permute-start(bf16[32,1,32,128]{3,2,1,0:T(8,128)(2,1)S(1)} %copy-done.1), channel_id=1, source_target_pairs={{0,1},{1,0},{2,3},{3,2},{4,5},{5,4},{6,7},{7,6},{8,9},{9,8},{10,11... | collective-permute-start | bytes 786440 | tf_op jit(solution)/shard_map/ppermute | solution.py:340
  17.0 9.3 %collective-permute-start.4 = (bf16[32,1,32,128]{3,2,1,0:T(8,128)(2,1)S(1)}, bf16[32,1,32,128]{3,2,1,0:T(8,128)(2,1)S(1)}, u32[]{:S(2)}, u32[]{:S(2)}) collective-permute-start(bf16[32,1,32,128]{3,2,1,0:T(8,128)(2,1)S(1)} %collective-permute-done.3.refs_1_), channel_id=1, source_target_pairs={{0,1},{1,0},{2,3},{3,2},{4,5},{5,4},{6,7},{7,6},{8,9},{9,8},{10,11... | collective-permute-start | bytes 786440 | tf_op jit(solution)/shard_map/ppermute | solution.py:340
  21.1 12.3 %collective-permute-start.6 = (bf16[64,4096]{1,0:T(8,128)(2,1)S(1)}, bf16[64,4096]{1,0:T(8,128)(2,1)S(1)}, u32[]{:S(2)}, u32[]{:S(2)}) collective-permute-start(bf16[64,4096]{1,0:T(8,128)(2,1)S(1)} %shard_map.54.refs_3_.refs_2_.refs_5_), channel_id=1, source_target_pairs={{4,0},{8,4},{12,8},{16,12},{20,16},{24,20},{28,24},{0,28},{5,1},{9... | collective-permute-start | bytes 1572872 | tf_op jit(solution)/shard_map/ppermute | solution.py:362
  26.5 6.9 %collective-permute-start.7 = (bf16[32,4096]{1,0:T(8,128)(2,1)S(1)}, bf16[32,4096]{1,0:T(8,128)(2,1)S(1)}, u32[]{:S(2)}, u32[]{:S(2)}) collective-permute-start(bf16[32,4096]{1,0:T(8,128)(2,1)S(1)} %shard_map.55.refs_4_.refs_3_.refs_6_), channel_id=1, source_target_pairs={{4,0},{8,4},{12,8},{16,12},{20,16},{24,20},{28,24},{0,28},{5,1},{9... | collective-permute-start | bytes 786440 | tf_op jit(solution)/shard_map/ppermute | solution.py:362
  28.0 1.6 %collective-permute-start.5 = (f32[64,512]{1,0:T(8,128)S(1)}, f32[64,512]{1,0:T(8,128)S(1)}, u32[]{:S(2)}, u32[]{:S(2)}) collective-permute-start(f32[64,512]{1,0:T(8,128)S(1)} %get-tuple-element.30), channel_id=1, source_target_pairs={{0,4},{4,0},{8,12},{12,8},{16,20},{20,16},{24,28},{28,24},{1,5},{5... | collective-permute-start | bytes 393224 | tf_op jit(solution)/shard_map/ppermute | solution.py:398
  29.7 5.3 %collective-permute-start.8 = (f32[16,512]{1,0:T(8,128)S(1)}, f32[16,512]{1,0:T(8,128)S(1)}, u32[]{:S(2)}, u32[]{:S(2)}) collective-permute-start(f32[16,512]{1,0:T(8,128)S(1)} %get-tuple-element.39), channel_id=1, source_target_pairs={{0,8},{4,12},{8,0},{12,4},{16,24},{20,28},{24,16},{28,20},{1,9},{5... | collective-permute-start | bytes 98312 | tf_op jit(solution)/shard_map/ppermute | solution.py:408
  31.6 3.9 %collective-permute-start.9 = (f32[16,512]{1,0:T(8,128)S(1)}, f32[16,512]{1,0:T(8,128)S(1)}, u32[]{:S(2)}, u32[]{:S(2)}) collective-permute-start(f32[16,512]{1,0:T(8,128)S(1)} %get-tuple-element.40), channel_id=1, source_target_pairs={{0,16},{4,20},{8,24},{12,28},{16,0},{20,4},{24,8},{28,12},{1,17},{... | collective-permute-start | bytes 98312 | tf_op jit(solution)/shard_map/ppermute | solution.py:408
  32.6 4.8 %collective-permute-start.10 = (f32[16,512]{1,0:T(8,128)S(1)}, f32[16,512]{1,0:T(8,128)S(1)}, u32[]{:S(2)}, u32[]{:S(2)}) collective-permute-start(f32[16,512]{1,0:T(8,128)S(1)} %get-tuple-element.41), channel_id=1, source_target_pairs={{0,24},{4,28},{8,16},{12,20},{16,8},{20,12},{24,0},{28,4},{1,25},{... | collective-permute-start | bytes 98312 | tf_op jit(solution)/shard_map/ppermute | solution.py:408

commit v9 on v8

--- a/solution.py
+++ b/solution.py
@@ -332,12 +332,14 @@
         own_weight,
         cost=(2 * 2 * 2 * cells * chans * 8 * cols, 4 << 20),
     )
-    got = {0: grad_out}
-    for mask in sorted(range(1, count), key=lambda mask: (mask & (mask - 1) > 0, -mask)):
-        low = mask & -mask
-        if mask == 1:
-            got[0], views = lax.optimization_barrier((got[0], views))
-        got[mask] = lax.ppermute(got[mask - low], "chan", [(i, i ^ low) for i in range(count)])
+    pairs = lambda mask: [(i, i ^ mask) for i in range(count)]
+    middle = own_outs // 2
+    by_two = lax.ppermute(grad_out[:middle], "chan", pairs(2))
+    by_one = lax.ppermute(grad_out, "chan", pairs(1))
+    own, by_two, views = lax.optimization_barrier((grad_out, by_two, views))
+    by_two_later = lax.ppermute(own[middle:], "chan", pairs(2))
+    by_three = lax.ppermute(by_two, "chan", pairs(1))
+    by_three_later = lax.ppermute(by_two_later, "chan", pairs(1))
     lines = lambda *parts: call(
         lines_kernel,
         jax.ShapeDtypeStruct((sum(part.shape[0] for part in parts), cells), BF16),
@@ -346,7 +348,7 @@
         cost=(1 << 20, 2 << 20),
     )
     behind = lax.ppermute(volume, "depth", farther)
-    next_own = lax.ppermute(got[0], "depth", nearer)
+    next_own = lax.ppermute(own, "depth", nearer)
     behind_views = call(
         behind_views_kernel,
         jax.ShapeDtypeStruct((6 * chans, cells), BF16),
@@ -354,10 +356,11 @@
         cost=(2 * 2 * cells * chans * 8 * cols, 2 << 20),
     )
     first_lines, next_first_lines = lines(grad_out), lines(next_own)
-    got[1], views, behind_views, first_lines, next_first_lines = lax.optimization_barrier(
-        (got[1], views, behind_views, first_lines, next_first_lines)
-    )
-    later_lines = [lines(*[got[mask] for mask in range(1, count - 1)]), lines(got[count - 1])]
+    second_lines = lines(by_one, by_two)
+    by_three, behind_views, first_lines, next_first_lines = lax.optimization_barrier(
+        (by_three, behind_views, first_lines, next_first_lines)
+    )
+    later_lines = [second_lines, lines(by_two_later, by_three), lines(by_three_later)]
     own_lines = [first_lines] + later_lines
     next_lines = [next_first_lines] + [lax.ppermute(part, "depth", nearer) for part in later_lines]
     outs = channels // depth
@@ -429,7 +432,7 @@
             grad_out.shape[0] % 32 == 0
             and volume.shape[0] == 16
             and grad_out.shape[1] == 1
-            and ring >= 4
+            and ring == 4
             and ring & (ring - 1) == 0
             and depth & (depth - 1) == 0
             and depth % (2 * ring) == 0

time: 38.4 us -> 40.2 us (1.047)
  starting transfers between devices: 14.6 us -> 20 us
  waiting for transfers between devices: 15.1 us -> 10.5 us
  local copies, waits for them, and re-layouts: 1.25 us -> 2.2 us
    ppermute x4 -> x6, starting transfers between devices: 9.45 us -> 12.8 us  [the longest x1 3.44 us: shards(): by_two_later = lax.ppermute(own[middle:], 'chan', pairs(2))]
    ppermute x4 -> x6, waiting for transfers between devices: 12.2 us -> 9.48 us  [the longest x1 3.66 us: shards(): by_two_later = lax.ppermute(own[middle:], 'chan', pairs(2))]
    ppermute x2 -> x3, starting transfers between devices: 0.87 us -> 3.14 us  [shards(): lax.ppermute(part, 'depth', nearer)]
    ppermute x3, waiting for transfers between devices: 2.45 us -> 0.91 us  [shards(): lax.ppermute(term, 'depth', [(i, i ^ 2 * k + 2) for i in range(depth)])]
    slice x0 -> x2, local copies, waits for them, and re-layouts: none -> 0.96 us  [the longest x1 0.95 us: shards(): by_two = lax.ppermute(grad_out[:middle], 'chan', pairs(2))]
    ppermute x1, waiting for transfers between devices: 0.49 us -> 0.01 us  [shards(): behind = lax.ppermute(volume, 'depth', farther)]
    pallas_call x9 -> x10, Pallas kernels: 3.36 us -> 3.4 us  [call(): pl.pallas_call(kernel, out_shape=out_shape, in_specs=[VMEM] * len(args),...]
  transfers between devices with their start and end apart: 11 -> 14, of which waited for: 6 -> 5; matrix products, arithmetic and copies ran while one was open for 0% -> 2% of each run, Pallas kernels for 15% -> 14%
where the time goes in v9:
time: 40.2 us; the launch traced here: 40 us
  starting transfers between devices  20 us (50%)
  waiting for transfers between devices  10.5 us (26%)
  Pallas kernels  6.54 us (16%)
  local copies, waits for them, and re-layouts  2.2 us (5%)
  between operations  0.8 us (2%)
    ppermute x1, waiting for transfers between devices, shards(): by_two_later = lax.ppermute(own[middle:], 'chan', pairs(2))  3.66 us
    ppermute x3, starting transfers between devices, shards(): lax.ppermute(term, 'depth', [(i, i ^ 2 * k + 2) for i in range(depth)])  3.5 us
    ppermute x1, waiting for transfers between devices, shards(): by_two = lax.ppermute(grad_out[:middle], 'chan', pairs(2))  3.46 us
    ppermute x1, starting transfers between devices, shards(): by_two_later = lax.ppermute(own[middle:], 'chan', pairs(2))  3.44 us
    pallas_call x10, Pallas kernels, call(): pl.pallas_call(kernel, out_shape=out_shape, in_specs=[VMEM] * len(args),...  3.4 us
    pallas_call x2, Pallas kernels, input_plane(): pl.pallas_call(kernel if before is None else lambda before, *refs: kernel...  3.14 us
    ppermute x3, starting transfers between devices, shards(): lax.ppermute(part, 'depth', nearer)  3.14 us
    ppermute x1, starting transfers between devices, shards(): by_two = lax.ppermute(grad_out[:middle], 'chan', pairs(2))  2.65 us
  transfers between devices with their start and end apart: 14, of which 5 were waited for; matrix products, arithmetic and copies ran while one was open for 2% of the time, Pallas kernels for 14%

profile of v9, /device:TPU:0, one launch (start us, length us, event | category | flops | bytes accessed | tf_op | source)
XLA Modules:
  0.0 40.0 jit_solution(18106503737429845798)
XLA Ops:
  0.6 0.0 copy-start
  0.6 0.0 copy-start.1
  0.7 0.5 %collective-permute-start.2 = (bf16[16,2,64,256]{3,2,1,0:T(8,128)(2,1)}, bf16[16,2,64,256]{3,2,1,0:T(8,128)(2,1)S(1)}, u32[]{:S(2)}, u32[]{:S(2)}) collective-permute-start(bf16[16,2,64,256]{3,2,1,0:T(8,128)(2,1)} %refs_0_.2), channel_id=1, source_target_pairs={{0,4},{4,8},{8,12},{12,16},{16,20},{20,24},{24,28},{28,0},{1,5},{5... | collective-permute-start | bytes 3145736 | tf_op jit(solution)/shard_map/ppermute | solution.py:350
  1.2 2.7 %collective-permute-start.4 = (bf16[32,1,32,128]{3,2,1,0:T(8,128)(2,1)}, bf16[32,1,32,128]{3,2,1,0:T(8,128)(2,1)S(1)}, u32[]{:S(2)}, u32[]{:S(2)}) collective-permute-start(bf16[32,1,32,128]{3,2,1,0:T(8,128)(2,1)} %refs_0_.3), channel_id=1, source_target_pairs={{0,1},{1,0},{2,3},{3,2},{4,5},{5,4},{6,7},{7,6},{8,9},{9,8},{10,11... | collective-permute-start | bytes 786440 | tf_op jit(solution)/shard_map/ppermute | solution.py:338
  3.8 0.9 %slice.6 = bf16[16,1,32,128]{3,2,1,0:T(8,128)(2,1)S(1)} slice(bf16[32,1,32,128]{3,2,1,0:T(8,128)(2,1)} %refs_0_.3), slice={[0:16], [0:1], [0:32], [0:128]} | slice | bytes 262144 | tf_op jit(solution)/shard_map/slice | solution.py:337
  4.8 2.7 %collective-permute-start = (bf16[16,1,32,128]{3,2,1,0:T(8,128)(2,1)S(1)}, bf16[16,1,32,128]{3,2,1,0:T(8,128)(2,1)S(1)}, u32[]{:S(2)}, u32[]{:S(2)}) collective-permute-start(bf16[16,1,32,128]{3,2,1,0:T(8,128)(2,1)S(1)} %slice.6), channel_id=1, source_target_pairs={{0,2},{1,3},{2,0},{3,1},{4,6},{5,7},{6,4},{7,5},{8,10},{9,11},{10,... | collective-permute-start | bytes 393224 | tf_op jit(solution)/shard_map/ppermute | solution.py:337
  7.4 0.0 copy-done
  7.4 0.0 copy-start.2
  7.5 1.2 %copy-done.2 = bf16[16,2,64,256]{3,2,1,0:T(8,128)(2,1)S(1)} copy-done((bf16[16,2,64,256]{3,2,1,0:T(8,128)(2,1)S(1)}, bf16[16,2,64,256]{3,2,1,0:T(8,128)(2,1)}, u32[]{:S(2)}) %copy-start.2) | copy-done | bytes 1048600
  8.7 0.9 %shard_map.50 = (bf16[192,4096]{1,0:T(8,128)(2,1)S(1)}, bf16[144,128]{1,0:T(8,128)(2,1)S(1)}, bf16[144,256]{1,0:T(8,128)(2,1)S(1)}) custom-call(bf16[16,2,64,256]{3,2,1,0:T(8,128)(2,1)S(1)} %copy-done.2, bf16[27,16,128]{2,1,0:T(8,128)(2,1)S(1)} %constant_dynamic-slice_fusion.refs_1_), custom_call_target="tpu_custom_call" | custom-call | flops 536870912 | bytes 4194304 | tf_op jit(solution)/shard_map/pallas_call | solution.py:302
  9.6 3.5 %collective-permute-done.refs_1_ = bf16[16,1,32,128]{3,2,1,0:T(8,128)(2,1)S(1)} collective-permute-done((bf16[16,1,32,128]{3,2,1,0:T(8,128)(2,1)S(1)}, bf16[16,1,32,128]{3,2,1,0:T(8,128)(2,1)S(1)}, u32[]{:S(2)}, u32[]{:S(2)}) %collective-permute-start) | collective-permute-done | bytes 131104 | tf_op jit(solution)/shard_map/ppermute | solution.py:337
  13.0 0.0 copy-done.1
  13.0 1.8 %collective-permute-start.3 = (bf16[32,1,32,128]{3,2,1,0:T(8,128)(2,1)S(1)}, bf16[32,1,32,128]{3,2,1,0:T(8,128)(2,1)S(1)}, u32[]{:S(2)}, u32[]{:S(2)}) collective-permute-start(bf16[32,1,32,128]{3,2,1,0:T(8,128)(2,1)S(1)} %copy-done.1), channel_id=1, source_target_pairs={{4,0},{8,4},{12,8},{16,12},{20,16},{24,20},{28,24},{0,28},{5,1},{9... | collective-permute-start | bytes 786440 | tf_op jit(solution)/shard_map/ppermute | solution.py:351
  14.9 3.4 %collective-permute-start.5 = (bf16[16,1,32,128]{3,2,1,0:T(8,128)(2,1)S(1)}, bf16[16,1,32,128]{3,2,1,0:T(8,128)(2,1)S(1)}, u32[]{:S(2)}, u32[]{:S(2)}) collective-permute-start(bf16[16,1,32,128]{3,2,1,0:T(8,128)(2,1)S(1)} %slice.7), channel_id=1, source_target_pairs={{0,2},{1,3},{2,0},{3,1},{4,6},{5,7},{6,4},{7,5},{8,10},{9,11},{10,... | collective-permute-start | bytes 393224 | tf_op jit(solution)/shard_map/ppermute | solution.py:340
  18.3 0.2 collective-permute-start.1
  18.5 0.0 collective-permute-done.4.refs_0_
  18.5 0.2 shard_map.54.refs_3_.refs_2_.refs_6_
  18.7 0.6 %collective-permute-start.8 = (bf16[48,4096]{1,0:T(8,128)(2,1)S(1)}, bf16[48,4096]{1,0:T(8,128)(2,1)S(1)}, u32[]{:S(2)}, u32[]{:S(2)}) collective-permute-start(bf16[48,4096]{1,0:T(8,128)(2,1)S(1)} %shard_map.54.refs_3_.refs_2_.refs_6_), channel_id=1, source_target_pairs={{4,0},{8,4},{12,8},{16,12},{20,16},{24,20},{28,24},{0,28},{5,1},{9... | collective-permute-start | bytes 1179656 | tf_op jit(solution)/shard_map/ppermute | solution.py:365
  19.3 3.7 %collective-permute-done.5.refs_0_ = bf16[16,1,32,128]{3,2,1,0:T(8,128)(2,1)S(1)} collective-permute-done((bf16[16,1,32,128]{3,2,1,0:T(8,128)(2,1)S(1)}, bf16[16,1,32,128]{3,2,1,0:T(8,128)(2,1)S(1)}, u32[]{:S(2)}, u32[]{:S(2)}) %collective-permute-start.5) | collective-permute-done | bytes 131104 | tf_op jit(solution)/shard_map/ppermute | solution.py:340
  22.9 2.0 %collective-permute-start.6 = (bf16[16,1,32,128]{3,2,1,0:T(8,128)(2,1)S(1)}, bf16[16,1,32,128]{3,2,1,0:T(8,128)(2,1)S(1)}, u32[]{:S(2)}, u32[]{:S(2)}) collective-permute-start(bf16[16,1,32,128]{3,2,1,0:T(8,128)(2,1)S(1)} %collective-permute-done.5.refs_0_), channel_id=1, source_target_pairs={{0,1},{1,0},{2,3},{3,2},{4,5},{5,4},{6,7},{7,6},{8,9},{9,8},{10,11... | collective-permute-start | bytes 393224 | tf_op jit(solution)/shard_map/ppermute | solution.py:342
  25.0 0.1 shard_map.52.refs_2_.refs_1_.refs_5_
  25.1 0.0 collective-permute-done.3.refs_0_
  25.1 0.1 shard_map.53.refs_1_
  25.3 0.0 collective-permute-done.2.behind_ref
  25.3 0.1 shard_map.51.refs_1_
  25.4 0.0 collective-permute-done.1.refs_1_
  25.4 0.1 shard_map.55.refs_4_.refs_3_.refs_7_
  25.5 0.1 collective-permute-start.9
  25.6 2.3 %collective-permute-done.6.refs_0_ = bf16[16,1,32,128]{3,2,1,0:T(8,128)(2,1)S(1)} collective-permute-done((bf16[16,1,32,128]{3,2,1,0:T(8,128)(2,1)S(1)}, bf16[16,1,32,128]{3,2,1,0:T(8,128)(2,1)S(1)}, u32[]{:S(2)}, u32[]{:S(2)}) %collective-permute-start.6) | collective-permute-done | bytes 131104 | tf_op jit(solution)/shard_map/ppermute | solution.py:342
  27.9 0.1 shard_map.56.refs_5_.refs_4_.refs_8_
  28.0 0.9 %shard_map.57 = (f32[64,512]{1,0:T(8,128)S(1)}, f32[64,512]{1,0:T(8,128)S(1)}) custom-call(bf16[192,4096]{1,0:T(8,128)(2,1)S(1)} %get-tuple-element.23.refs_0_, bf16[96,4096]{1,0:T(8,128)(2,1)S(1)} %shard_map.51.refs_1_, bf16[32,4096]{1,0:T(8,128)(2,1)S(1)} %shard_map.52.refs_2_.refs_1_.refs_5_, bf16[48,4096]{1,0:T(8,128)(2,1)S(1)} %shard_map.54.refs_3_.refs_2_.refs_6_, ...), custom_call_target="tpu_custom_call" | custom-call | flops 452984832 | bytes 8388608 | tf_op jit(solution)/shard_map/pallas_call | solution.py:302
  29.0 0.1 collective-permute-start.7
  29.0 2.5 %collective-permute-start.10 = (bf16[16,4096]{1,0:T(8,128)(2,1)S(1)}, bf16[16,4096]{1,0:T(8,128)(2,1)S(1)}, u32[]{:S(2)}, u32[]{:S(2)}) collective-permute-start(bf16[16,4096]{1,0:T(8,128)(2,1)S(1)} %shard_map.56.refs_5_.refs_4_.refs_8_), channel_id=1, source_target_pairs={{4,0},{8,4},{12,8},{16,12},{20,16},{24,20},{28,24},{0,28},{5,1},{9... | collective-permute-start | bytes 393224 | tf_op jit(solution)/shard_map/ppermute | solution.py:365
  31.6 1.6 %shard_map.58.before = bf16[16,2,64,256]{3,2,1,0:T(8,128)(2,1)} custom-call(bf16[144,128]{1,0:T(8,128)(2,1)S(1)} %get-tuple-element.31.refs_0_, bf16[32,4096]{1,0:T(8,128)(2,1)S(1)} %shard_map.52.refs_2_.refs_1_.refs_5_, bf16[48,4096]{1,0:T(8,128)(2,1)S(1)} %shard_map.54.refs_3_.refs_2_.refs_6_, bf16[32,4096]{1,0:T(8,128)(2,1)S(1)} %shard_map.55.refs_4_.refs_3_.refs_7_, ...), custom_call_target="tpu_custom_call" | custom-call | flops 150994944 | bytes 4194304 | tf_op jit(solution)/shard_map/pallas_call | solution.py:383
  33.1 0.0 collective-permute-done.7.other_ref
  33.2 0.1 collective-permute-start.11
  33.3 1.1 %collective-permute-start.12 = (f32[16,512]{1,0:T(8,128)S(1)}, f32[16,512]{1,0:T(8,128)S(1)}, u32[]{:S(2)}, u32[]{:S(2)}) collective-permute-start(f32[16,512]{1,0:T(8,128)S(1)} %get-tuple-element.40), channel_id=1, source_target_pairs={{0,16},{4,20},{8,24},{12,28},{16,0},{20,4},{24,8},{28,12},{1,17},{... | collective-permute-start | bytes 98312 | tf_op jit(solution)/shard_map/ppermute | solution.py:411
  34.3 0.1 collective-permute-done.10.refs_4_
  34.4 2.3 %collective-permute-start.13 = (f32[16,512]{1,0:T(8,128)S(1)}, f32[16,512]{1,0:T(8,128)S(1)}, u32[]{:S(2)}, u32[]{:S(2)}) collective-permute-start(f32[16,512]{1,0:T(8,128)S(1)} %get-tuple-element.41), channel_id=1, source_target_pairs={{0,24},{4,28},{8,16},{12,20},{16,8},{20,12},{24,0},{28,4},{1,25},{... | collective-permute-start | bytes 98312 | tf_op jit(solution)/shard_map/ppermute | solution.py:411
  36.7 0.0 collective-permute-done.8.refs_2_
  36.7 0.0 collective-permute-done.9.refs_3_
  36.7 1.6 %shard_map.60 = bf16[16,2,64,256]{3,2,1,0:T(8,128)(2,1)} custom-call(bf16[16,2,64,256]{3,2,1,0:T(8,128)(2,1)} %shard_map.58.before, bf16[144,256]{1,0:T(8,128)(2,1)S(1)} %get-tuple-element.35.refs_0_, bf16[32,4096]{1,0:T(8,128)(2,1)S(1)} %shard_map.53.refs_1_, bf16[48,4096]{1,0:T(8,128)(2,1)S(1)} %collective-permute-done.8.refs_2_, ...), custom_call_target="tpu_custom_call", output_to_operand_aliasing={{}: (0, {})} | custom-call | flops 301989888 | bytes 4194304 | tf_op jit(solution)/shard_map/pallas_call | solution.py:383
  38.3 0.0 collective-permute-done.11.refs_1_
  38.3 0.0 collective-permute-done.12.refs_2_
  38.4 0.9 %collective-permute-done.13.refs_3_ = f32[16,512]{1,0:T(8,128)S(1)} collective-permute-done((f32[16,512]{1,0:T(8,128)S(1)}, f32[16,512]{1,0:T(8,128)S(1)}, u32[]{:S(2)}, u32[]{:S(2)}) %collective-permute-start.13) | collective-permute-done | bytes 32800 | tf_op jit(solution)/shard_map/ppermute | solution.py:411
  39.3 0.8 %shard_map.61 = f32[16,16,27]{2,1,0:T(8,128)} custom-call(f32[16,512]{1,0:T(8,128)S(1)} %get-tuple-element.38.refs_0_, f32[16,512]{1,0:T(8,128)S(1)} %collective-permute-done.11.refs_1_, f32[16,512]{1,0:T(8,128)S(1)} %collective-permute-done.12.refs_2_, f32[16,512]{1,0:T(8,128)S(1)} %collective-permute-done.13.refs_3_), custom_call_target="tpu_custom_call" | custom-call | flops 65536 | bytes 524288 | tf_op jit(solution)/shard_map/pallas_call | solution.py:302
  (3 shorter events, 0.1 us)
Async XLA Ops:
  0.6 6.8 %copy-start = (bf16[27,64,128]{2,1,0:T(8,128)(2,1)S(1)}, bf16[27,64,128]{2,1,0:T(8,128)(2,1)}, u32[]{:S(2)}) copy-start(bf16[27,64,128]{2,1,0:T(8,128)(2,1)} %param.5) | copy-start | bytes 1327108
  0.6 12.4 %copy-start.1 = (bf16[32,1,32,128]{3,2,1,0:T(8,128)(2,1)S(1)}, bf16[32,1,32,128]{3,2,1,0:T(8,128)(2,1)}, u32[]{:S(2)}) copy-start(bf16[32,1,32,128]{3,2,1,0:T(8,128)(2,1)} %refs_0_.3) | copy-start | bytes 786436
  0.7 24.6 %collective-permute-start.2 = (bf16[16,2,64,256]{3,2,1,0:T(8,128)(2,1)}, bf16[16,2,64,256]{3,2,1,0:T(8,128)(2,1)S(1)}, u32[]{:S(2)}, u32[]{:S(2)}) collective-permute-start(bf16[16,2,64,256]{3,2,1,0:T(8,128)(2,1)} %refs_0_.2), channel_id=1, source_target_pairs={{0,4},{4,8},{8,12},{12,16},{16,20},{20,24},{24,28},{28,0},{1,5},{5... | collective-permute-start | bytes 3145736 | tf_op jit(solution)/shard_map/ppermute | solution.py:350
  1.2 17.4 %collective-permute-start.4 = (bf16[32,1,32,128]{3,2,1,0:T(8,128)(2,1)}, bf16[32,1,32,128]{3,2,1,0:T(8,128)(2,1)S(1)}, u32[]{:S(2)}, u32[]{:S(2)}) collective-permute-start(bf16[32,1,32,128]{3,2,1,0:T(8,128)(2,1)} %refs_0_.3), channel_id=1, source_target_pairs={{0,1},{1,0},{2,3},{3,2},{4,5},{5,4},{6,7},{7,6},{8,9},{9,8},{10,11... | collective-permute-start | bytes 786440 | tf_op jit(solution)/shard_map/ppermute | solution.py:338
  4.8 8.3 %collective-permute-start = (bf16[16,1,32,128]{3,2,1,0:T(8,128)(2,1)S(1)}, bf16[16,1,32,128]{3,2,1,0:T(8,128)(2,1)S(1)}, u32[]{:S(2)}, u32[]{:S(2)}) collective-permute-start(bf16[16,1,32,128]{3,2,1,0:T(8,128)(2,1)S(1)} %slice.6), channel_id=1, source_target_pairs={{0,2},{1,3},{2,0},{3,1},{4,6},{5,7},{6,4},{7,5},{8,10},{9,11},{10,... | collective-permute-start | bytes 393224 | tf_op jit(solution)/shard_map/ppermute | solution.py:337
  7.4 1.2 %copy-start.2 = (bf16[16,2,64,256]{3,2,1,0:T(8,128)(2,1)S(1)}, bf16[16,2,64,256]{3,2,1,0:T(8,128)(2,1)}, u32[]{:S(2)}) copy-start(bf16[16,2,64,256]{3,2,1,0:T(8,128)(2,1)} %refs_0_.2) | copy-start | bytes 3145732
  13.0 12.1 %collective-permute-start.3 = (bf16[32,1,32,128]{3,2,1,0:T(8,128)(2,1)S(1)}, bf16[32,1,32,128]{3,2,1,0:T(8,128)(2,1)S(1)}, u32[]{:S(2)}, u32[]{:S(2)}) collective-permute-start(bf16[32,1,32,128]{3,2,1,0:T(8,128)(2,1)S(1)} %copy-done.1), channel_id=1, source_target_pairs={{4,0},{8,4},{12,8},{16,12},{20,16},{24,20},{28,24},{0,28},{5,1},{9... | collective-permute-start | bytes 786440 | tf_op jit(solution)/shard_map/ppermute | solution.py:351
  14.9 8.1 %collective-permute-start.5 = (bf16[16,1,32,128]{3,2,1,0:T(8,128)(2,1)S(1)}, bf16[16,1,32,128]{3,2,1,0:T(8,128)(2,1)S(1)}, u32[]{:S(2)}, u32[]{:S(2)}) collective-permute-start(bf16[16,1,32,128]{3,2,1,0:T(8,128)(2,1)S(1)} %slice.7), channel_id=1, source_target_pairs={{0,2},{1,3},{2,0},{3,1},{4,6},{5,7},{6,4},{7,5},{8,10},{9,11},{10,... | collective-permute-start | bytes 393224 | tf_op jit(solution)/shard_map/ppermute | solution.py:340
  18.3 7.0 %collective-permute-start.1 = (bf16[16,1,32,128]{3,2,1,0:T(8,128)(2,1)S(1)}, bf16[16,1,32,128]{3,2,1,0:T(8,128)(2,1)S(1)}, u32[]{:S(2)}, u32[]{:S(2)}) collective-permute-start(bf16[16,1,32,128]{3,2,1,0:T(8,128)(2,1)S(1)} %collective-permute-done.refs_1_), channel_id=1, source_target_pairs={{0,1},{1,0},{2,3},{3,2},{4,5},{5,4},{6,7},{7,6},{8,9},{9,8},{10,11... | collective-permute-start | bytes 393224 | tf_op jit(solution)/shard_map/ppermute | solution.py:341
  18.7 18.0 %collective-permute-start.8 = (bf16[48,4096]{1,0:T(8,128)(2,1)S(1)}, bf16[48,4096]{1,0:T(8,128)(2,1)S(1)}, u32[]{:S(2)}, u32[]{:S(2)}) collective-permute-start(bf16[48,4096]{1,0:T(8,128)(2,1)S(1)} %shard_map.54.refs_3_.refs_2_.refs_6_), channel_id=1, source_target_pairs={{4,0},{8,4},{12,8},{16,12},{20,16},{24,20},{28,24},{0,28},{5,1},{9... | collective-permute-start | bytes 1179656 | tf_op jit(solution)/shard_map/ppermute | solution.py:365
  22.9 5.0 %collective-permute-start.6 = (bf16[16,1,32,128]{3,2,1,0:T(8,128)(2,1)S(1)}, bf16[16,1,32,128]{3,2,1,0:T(8,128)(2,1)S(1)}, u32[]{:S(2)}, u32[]{:S(2)}) collective-permute-start(bf16[16,1,32,128]{3,2,1,0:T(8,128)(2,1)S(1)} %collective-permute-done.5.refs_0_), channel_id=1, source_target_pairs={{0,1},{1,0},{2,3},{3,2},{4,5},{5,4},{6,7},{7,6},{8,9},{9,8},{10,11... | collective-permute-start | bytes 393224 | tf_op jit(solution)/shard_map/ppermute | solution.py:342
  25.5 11.2 %collective-permute-start.9 = (bf16[32,4096]{1,0:T(8,128)(2,1)S(1)}, bf16[32,4096]{1,0:T(8,128)(2,1)S(1)}, u32[]{:S(2)}, u32[]{:S(2)}) collective-permute-start(bf16[32,4096]{1,0:T(8,128)(2,1)S(1)} %shard_map.55.refs_4_.refs_3_.refs_7_), channel_id=1, source_target_pairs={{4,0},{8,4},{12,8},{16,12},{20,16},{24,20},{28,24},{0,28},{5,1},{9... | collective-permute-start | bytes 786440 | tf_op jit(solution)/shard_map/ppermute | solution.py:365
  29.0 4.2 %collective-permute-start.7 = (f32[64,512]{1,0:T(8,128)S(1)}, f32[64,512]{1,0:T(8,128)S(1)}, u32[]{:S(2)}, u32[]{:S(2)}) collective-permute-start(f32[64,512]{1,0:T(8,128)S(1)} %get-tuple-element.30), channel_id=1, source_target_pairs={{0,4},{4,0},{8,12},{12,8},{16,20},{20,16},{24,28},{28,24},{1,5},{5... | collective-permute-start | bytes 393224 | tf_op jit(solution)/shard_map/ppermute | solution.py:401
  29.0 5.4 %collective-permute-start.10 = (bf16[16,4096]{1,0:T(8,128)(2,1)S(1)}, bf16[16,4096]{1,0:T(8,128)(2,1)S(1)}, u32[]{:S(2)}, u32[]{:S(2)}) collective-permute-start(bf16[16,4096]{1,0:T(8,128)(2,1)S(1)} %shard_map.56.refs_5_.refs_4_.refs_8_), channel_id=1, source_target_pairs={{4,0},{8,4},{12,8},{16,12},{20,16},{24,20},{28,24},{0,28},{5,1},{9... | collective-permute-start | bytes 393224 | tf_op jit(solution)/shard_map/ppermute | solution.py:365
  33.2 5.2 %collective-permute-start.11 = (f32[16,512]{1,0:T(8,128)S(1)}, f32[16,512]{1,0:T(8,128)S(1)}, u32[]{:S(2)}, u32[]{:S(2)}) collective-permute-start(f32[16,512]{1,0:T(8,128)S(1)} %get-tuple-element.39), channel_id=1, source_target_pairs={{0,8},{4,12},{8,0},{12,4},{16,24},{20,28},{24,16},{28,20},{1,9},{5... | collective-permute-start | bytes 98312 | tf_op jit(solution)/shard_map/ppermute | solution.py:411
  33.3 5.1 %collective-permute-start.12 = (f32[16,512]{1,0:T(8,128)S(1)}, f32[16,512]{1,0:T(8,128)S(1)}, u32[]{:S(2)}, u32[]{:S(2)}) collective-permute-start(f32[16,512]{1,0:T(8,128)S(1)} %get-tuple-element.40), channel_id=1, source_target_pairs={{0,16},{4,20},{8,24},{12,28},{16,0},{20,4},{24,8},{28,12},{1,17},{... | collective-permute-start | bytes 98312 | tf_op jit(solution)/shard_map/ppermute | solution.py:411
  34.4 4.9 %collective-permute-start.13 = (f32[16,512]{1,0:T(8,128)S(1)}, f32[16,512]{1,0:T(8,128)S(1)}, u32[]{:S(2)}, u32[]{:S(2)}) collective-permute-start(f32[16,512]{1,0:T(8,128)S(1)} %get-tuple-element.41), channel_id=1, source_target_pairs={{0,24},{4,28},{8,16},{12,20},{16,8},{20,12},{24,0},{28,4},{1,25},{... | collective-permute-start | bytes 98312 | tf_op jit(solution)/shard_map/ppermute | solution.py:411

commit v10 on v6

--- a/solution.py
+++ b/solution.py
@@ -170,10 +170,15 @@
     chans, rows, cols = rows_ref.shape
     half = cols // 2
     grid_cells = half * rows // 2
-    grads = jnp.concatenate([ref[...] for ref in line_refs], axis=0)
-    cells_ref[:, :grid_cells] = matmul(taps_ref[...], grads)
     cells_ref[:, grid_cells:] = jnp.zeros((cells_ref.shape[0], half), F32)
     group = 256 // chans
+
+    def compute(start):
+        lanes = slice(start // 2 * half, (start + group) // 2 * half)
+        grads = jnp.concatenate([ref[:, lanes] for ref in line_refs], axis=0)
+        cells_ref[:, lanes] = matmul(taps_ref[...], grads)
+
+    compute(0)
     pitch = chans + 8
     weave = one_hot(cols, cols, lambda row, col: col == 2 * (row & (half - 1)) + row // half)
     inner = lax.broadcasted_iota(jnp.int32, (chans, half), 1) < half - 1
@@ -184,6 +189,8 @@
 
     copies = []
     for start in range(0, rows, group):
+        if start + group < rows:
+            compute(start + group)
         pieces = []
         for row in range(start, start + group):
             r = row // 2
@@ -405,7 +412,10 @@
         other,
         cost=(1 << 16, 1 << 19),
     )
-    terms = [lax.ppermute(term, "depth", [(i, i ^ (2 * k + 2)) for i in range(depth)]) for k, term in enumerate(terms)]
+    terms = [
+        lax.ppermute(terms[k - 1], "depth", [(i, i ^ (2 * k)) for i in range(depth)])
+        for k in range(depth // 2 - 1, 0, -1)
+    ]
     input_grad = input_plane(1, odd_taps, next_lines + own_lines, half_grad)
     own_terms, input_grad = lax.optimization_barrier((own_terms, input_grad))
     scale = 1.0 / math.sqrt(depth * cells)

time: 38.1 us -> 37.6 us (0.987)
  waiting for transfers between devices: 12.8 us -> 12.2 us
    ppermute x3, waiting for transfers between devices: 2.49 us -> 1.81 us  [shards(): lax.ppermute(terms[k - 1], 'depth', [(i, i ^ 2 * k) for i in range(depth)])]
  transfers between devices with their start and end apart: 11 -> 11, of which waited for: 5 -> 5; matrix products, arithmetic and copies ran while one was open for 0% -> 0% of each run, Pallas kernels for 15% -> 16%
where the time goes in v10:
time: 37.6 us; the launch traced here: 37.4 us
  starting transfers between devices  15.6 us (41%)
  waiting for transfers between devices  12.2 us (32%)
  Pallas kernels  6.64 us (18%)
  local copies, waits for them, and re-layouts  2.24 us (6%)
  between operations  0.75 us (2%)
    ppermute x3, waiting for transfers between devices, shards(): lax.ppermute(got[mask - low], 'chan', [(i, i ^ low) for i in range(count)])  9.81 us
    ppermute x3, starting transfers between devices, shards(): lax.ppermute(got[mask - low], 'chan', [(i, i ^ low) for i in range(count)])  7.07 us
    ppermute x3, starting transfers between devices, shards(): lax.ppermute(terms[k - 1], 'depth', [(i, i ^ 2 * k) for i in range(depth)])  3.55 us
    pallas_call x9, Pallas kernels, call(): pl.pallas_call(kernel, out_shape=out_shape, in_specs=[VMEM] * len(args),...  3.36 us
    pallas_call x2, Pallas kernels, input_plane(): pl.pallas_call(kernel if before is None else lambda before, *refs: kernel...  3.28 us
    ppermute x1, starting transfers between devices, shards(): next_own = lax.ppermute(grad_out, 'depth', nearer)  2.28 us
    unnamed x6, local copies, waits for them, and re-layouts  2.21 us
    ppermute x3, waiting for transfers between devices, shards(): lax.ppermute(terms[k - 1], 'depth', [(i, i ^ 2 * k) for i in range(depth)])  1.81 us
  transfers between devices with their start and end apart: 11, of which 5 were waited for; matrix products, arithmetic and copies ran while one was open for 0% of the time, Pallas kernels for 16%

profile of v10, /device:TPU:0, one launch (start us, length us, event | category | flops | bytes accessed | tf_op | source)
XLA Modules:
  0.0 37.4 jit_solution(9754419820363403462)
XLA Ops:
  0.6 0.0 copy-start
  0.6 0.5 %collective-permute-start.2 = (bf16[16,2,64,256]{3,2,1,0:T(8,128)(2,1)}, bf16[16,2,64,256]{3,2,1,0:T(8,128)(2,1)S(1)}, u32[]{:S(2)}, u32[]{:S(2)}) collective-permute-start(bf16[16,2,64,256]{3,2,1,0:T(8,128)(2,1)} %refs_0_.2), channel_id=1, source_target_pairs={{0,4},{4,8},{8,12},{12,16},{16,20},{20,24},{24,28},{28,0},{1,5},{5... | collective-permute-start | bytes 3145736 | tf_op jit(solution)/shard_map/ppermute | solution.py:355
  1.1 3.7 %collective-permute-start.1 = (bf16[32,1,32,128]{3,2,1,0:T(8,128)(2,1)}, bf16[32,1,32,128]{3,2,1,0:T(8,128)(2,1)S(1)}, u32[]{:S(2)}, u32[]{:S(2)}) collective-permute-start(bf16[32,1,32,128]{3,2,1,0:T(8,128)(2,1)} %refs_0_.3), channel_id=1, source_target_pairs={{0,2},{1,3},{2,0},{3,1},{4,6},{5,7},{6,4},{7,5},{8,10},{9,11},{10,... | collective-permute-start | bytes 786440 | tf_op jit(solution)/shard_map/ppermute | solution.py:347
  4.8 2.3 %collective-permute-start.3 = (bf16[32,1,32,128]{3,2,1,0:T(8,128)(2,1)}, bf16[32,1,32,128]{3,2,1,0:T(8,128)(2,1)S(1)}, u32[]{:S(2)}, u32[]{:S(2)}) collective-permute-start(bf16[32,1,32,128]{3,2,1,0:T(8,128)(2,1)} %refs_0_.3), channel_id=1, source_target_pairs={{4,0},{8,4},{12,8},{16,12},{20,16},{24,20},{28,24},{0,28},{5,1},{9... | collective-permute-start | bytes 786440 | tf_op jit(solution)/shard_map/ppermute | solution.py:356
  7.1 1.6 %collective-permute-start = (bf16[32,1,32,128]{3,2,1,0:T(8,128)(2,1)}, bf16[32,1,32,128]{3,2,1,0:T(8,128)(2,1)S(1)}, u32[]{:S(2)}, u32[]{:S(2)}) collective-permute-start(bf16[32,1,32,128]{3,2,1,0:T(8,128)(2,1)} %refs_0_.3), channel_id=1, source_target_pairs={{0,1},{1,0},{2,3},{3,2},{4,5},{5,4},{6,7},{7,6},{8,9},{9,8},{10,11... | collective-permute-start | bytes 786440 | tf_op jit(solution)/shard_map/ppermute | solution.py:347
  8.7 0.0 copy-start.1
  8.7 1.0 %copy-done.1 = bf16[32,1,32,128]{3,2,1,0:T(8,128)(2,1)S(1)} copy-done((bf16[32,1,32,128]{3,2,1,0:T(8,128)(2,1)S(1)}, bf16[32,1,32,128]{3,2,1,0:T(8,128)(2,1)}, u32[]{:S(2)}) %copy-start.1) | copy-done | bytes 262168
  9.7 0.1 shard_map.52.refs_2_.refs_1_.refs_4_
  9.8 0.0 copy-done
  9.8 0.0 copy-start.2
  9.9 1.2 %copy-done.2 = bf16[16,2,64,256]{3,2,1,0:T(8,128)(2,1)S(1)} copy-done((bf16[16,2,64,256]{3,2,1,0:T(8,128)(2,1)S(1)}, bf16[16,2,64,256]{3,2,1,0:T(8,128)(2,1)}, u32[]{:S(2)}) %copy-start.2) | copy-done | bytes 1048600
  11.1 0.9 %shard_map.50 = (bf16[192,4096]{1,0:T(8,128)(2,1)S(1)}, bf16[144,128]{1,0:T(8,128)(2,1)S(1)}, bf16[144,256]{1,0:T(8,128)(2,1)S(1)}) custom-call(bf16[16,2,64,256]{3,2,1,0:T(8,128)(2,1)S(1)} %copy-done.2, bf16[27,16,128]{2,1,0:T(8,128)(2,1)S(1)} %constant_dynamic-slice_fusion.refs_1_), custom_call_target="tpu_custom_call" | custom-call | flops 536870912 | bytes 4194304 | tf_op jit(solution)/shard_map/pallas_call | solution.py:309
  12.0 5.1 %collective-permute-done.1.refs_1_ = bf16[32,1,32,128]{3,2,1,0:T(8,128)(2,1)S(1)} collective-permute-done((bf16[32,1,32,128]{3,2,1,0:T(8,128)(2,1)}, bf16[32,1,32,128]{3,2,1,0:T(8,128)(2,1)S(1)}, u32[]{:S(2)}, u32[]{:S(2)}) %collective-permute-start.1) | collective-permute-done | bytes 262176 | tf_op jit(solution)/shard_map/ppermute | solution.py:347
  17.0 1.8 %collective-permute-start.4 = (bf16[32,1,32,128]{3,2,1,0:T(8,128)(2,1)S(1)}, bf16[32,1,32,128]{3,2,1,0:T(8,128)(2,1)S(1)}, u32[]{:S(2)}, u32[]{:S(2)}) collective-permute-start(bf16[32,1,32,128]{3,2,1,0:T(8,128)(2,1)S(1)} %collective-permute-done.1.refs_1_), channel_id=1, source_target_pairs={{0,1},{1,0},{2,3},{3,2},{4,5},{5,4},{6,7},{7,6},{8,9},{9,8},{10,11... | collective-permute-start | bytes 786440 | tf_op jit(solution)/shard_map/ppermute | solution.py:347
  18.9 0.0 collective-permute-done.3.refs_0_
  18.9 0.1 shard_map.53.refs_1_
  19.0 0.5 %collective-permute-done.2.behind_ref = bf16[16,2,64,256]{3,2,1,0:T(8,128)(2,1)S(1)} collective-permute-done((bf16[16,2,64,256]{3,2,1,0:T(8,128)(2,1)}, bf16[16,2,64,256]{3,2,1,0:T(8,128)(2,1)S(1)}, u32[]{:S(2)}, u32[]{:S(2)}) %collective-permute-start.2) | collective-permute-done | bytes 1048608 | tf_op jit(solution)/shard_map/ppermute | solution.py:355
  19.5 0.1 shard_map.51.refs_1_
  19.6 0.0 collective-permute-done.refs_0_
  19.6 0.3 shard_map.54.refs_3_.refs_2_.refs_5_
  19.9 1.5 %collective-permute-start.6 = (bf16[64,4096]{1,0:T(8,128)(2,1)S(1)}, bf16[64,4096]{1,0:T(8,128)(2,1)S(1)}, u32[]{:S(2)}, u32[]{:S(2)}) collective-permute-start(bf16[64,4096]{1,0:T(8,128)(2,1)S(1)} %shard_map.54.refs_3_.refs_2_.refs_5_), channel_id=1, source_target_pairs={{4,0},{8,4},{12,8},{16,12},{20,16},{24,20},{28,24},{0,28},{5,1},{9... | collective-permute-start | bytes 1572872 | tf_op jit(solution)/shard_map/ppermute | solution.py:369
  21.4 4.8 %collective-permute-done.4.refs_0_ = bf16[32,1,32,128]{3,2,1,0:T(8,128)(2,1)S(1)} collective-permute-done((bf16[32,1,32,128]{3,2,1,0:T(8,128)(2,1)S(1)}, bf16[32,1,32,128]{3,2,1,0:T(8,128)(2,1)S(1)}, u32[]{:S(2)}, u32[]{:S(2)}) %collective-permute-start.4) | collective-permute-done | bytes 262176 | tf_op jit(solution)/shard_map/ppermute | solution.py:347
  26.2 0.1 shard_map.55.refs_4_.refs_3_.refs_6_
  26.3 0.2 collective-permute-start.7
  26.5 0.9 %shard_map.56 = (f32[64,512]{1,0:T(8,128)S(1)}, f32[64,512]{1,0:T(8,128)S(1)}) custom-call(bf16[192,4096]{1,0:T(8,128)(2,1)S(1)} %get-tuple-element.24.refs_0_, bf16[96,4096]{1,0:T(8,128)(2,1)S(1)} %shard_map.51.refs_1_, bf16[32,4096]{1,0:T(8,128)(2,1)S(1)} %shard_map.52.refs_2_.refs_1_.refs_4_, bf16[64,4096]{1,0:T(8,128)(2,1)S(1)} %shard_map.54.refs_3_.refs_2_.refs_5_, ...), custom_call_target="tpu_custom_call" | custom-call | flops 452984832 | bytes 8388608 | tf_op jit(solution)/shard_map/pallas_call | solution.py:309
  27.5 0.4 %collective-permute-start.5 = (f32[64,512]{1,0:T(8,128)S(1)}, f32[64,512]{1,0:T(8,128)S(1)}, u32[]{:S(2)}, u32[]{:S(2)}) collective-permute-start(f32[64,512]{1,0:T(8,128)S(1)} %get-tuple-element.30), channel_id=1, source_target_pairs={{0,4},{4,0},{8,12},{12,8},{16,20},{20,16},{24,28},{28,24},{1,5},{5... | collective-permute-start | bytes 393224 | tf_op jit(solution)/shard_map/ppermute | solution.py:405
  27.9 1.6 %shard_map.57.before = bf16[16,2,64,256]{3,2,1,0:T(8,128)(2,1)} custom-call(bf16[144,128]{1,0:T(8,128)(2,1)S(1)} %get-tuple-element.31.refs_0_, bf16[32,4096]{1,0:T(8,128)(2,1)S(1)} %shard_map.52.refs_2_.refs_1_.refs_4_, bf16[64,4096]{1,0:T(8,128)(2,1)S(1)} %shard_map.54.refs_3_.refs_2_.refs_5_, bf16[32,4096]{1,0:T(8,128)(2,1)S(1)} %shard_map.55.refs_4_.refs_3_.refs_6_), custom_call_target="tpu_custom_call" | custom-call | flops 150994944 | bytes 4194304 | tf_op jit(solution)/shard_map/pallas_call | solution.py:387
  29.5 0.0 collective-permute-done.5.other_ref
  29.6 2.3 %collective-permute-start.8 = (f32[16,512]{1,0:T(8,128)S(1)}, f32[16,512]{1,0:T(8,128)S(1)}, u32[]{:S(2)}, u32[]{:S(2)}) collective-permute-start(f32[16,512]{1,0:T(8,128)S(1)} %get-tuple-element.39), channel_id=1, source_target_pairs={{0,24},{4,28},{8,16},{12,20},{16,8},{20,12},{24,0},{28,4},{1,25},{... | collective-permute-start | bytes 98312 | tf_op jit(solution)/shard_map/ppermute | solution.py:416
  31.9 0.8 %collective-permute-start.9 = (f32[16,512]{1,0:T(8,128)S(1)}, f32[16,512]{1,0:T(8,128)S(1)}, u32[]{:S(2)}, u32[]{:S(2)}) collective-permute-start(f32[16,512]{1,0:T(8,128)S(1)} %get-tuple-element.40), channel_id=1, source_target_pairs={{0,16},{4,20},{8,24},{12,28},{16,0},{20,4},{24,8},{28,12},{1,17},{... | collective-permute-start | bytes 98312 | tf_op jit(solution)/shard_map/ppermute | solution.py:416
  32.7 0.4 %collective-permute-start.10 = (f32[16,512]{1,0:T(8,128)S(1)}, f32[16,512]{1,0:T(8,128)S(1)}, u32[]{:S(2)}, u32[]{:S(2)}) collective-permute-start(f32[16,512]{1,0:T(8,128)S(1)} %get-tuple-element.41), channel_id=1, source_target_pairs={{0,8},{4,12},{8,0},{12,4},{16,24},{20,28},{24,16},{28,20},{1,9},{5... | collective-permute-start | bytes 98312 | tf_op jit(solution)/shard_map/ppermute | solution.py:416
  33.1 0.0 collective-permute-done.7.refs_3_
  33.1 0.0 collective-permute-done.6.refs_2_
  33.1 1.6 %shard_map.59 = bf16[16,2,64,256]{3,2,1,0:T(8,128)(2,1)} custom-call(bf16[16,2,64,256]{3,2,1,0:T(8,128)(2,1)} %shard_map.57.before, bf16[144,256]{1,0:T(8,128)(2,1)S(1)} %get-tuple-element.35.refs_0_, bf16[32,4096]{1,0:T(8,128)(2,1)S(1)} %shard_map.53.refs_1_, bf16[64,4096]{1,0:T(8,128)(2,1)S(1)} %collective-permute-done.6.refs_2_, ...), custom_call_target="tpu_custom_call", output_to_operand_aliasing={{}: (0, {})} | custom-call | flops 301989888 | bytes 4194304 | tf_op jit(solution)/shard_map/pallas_call | solution.py:387
  34.8 0.0 collective-permute-done.8.refs_1_
  34.8 1.0 %collective-permute-done.9.refs_2_ = f32[16,512]{1,0:T(8,128)S(1)} collective-permute-done((f32[16,512]{1,0:T(8,128)S(1)}, f32[16,512]{1,0:T(8,128)S(1)}, u32[]{:S(2)}, u32[]{:S(2)}) %collective-permute-start.9) | collective-permute-done | bytes 32800 | tf_op jit(solution)/shard_map/ppermute | solution.py:416
  35.8 0.8 %collective-permute-done.10.refs_3_ = f32[16,512]{1,0:T(8,128)S(1)} collective-permute-done((f32[16,512]{1,0:T(8,128)S(1)}, f32[16,512]{1,0:T(8,128)S(1)}, u32[]{:S(2)}, u32[]{:S(2)}) %collective-permute-start.10) | collective-permute-done | bytes 32800 | tf_op jit(solution)/shard_map/ppermute | solution.py:416
  36.6 0.8 %shard_map.60 = f32[16,16,27]{2,1,0:T(8,128)} custom-call(f32[16,512]{1,0:T(8,128)S(1)} %get-tuple-element.38.refs_0_, f32[16,512]{1,0:T(8,128)S(1)} %collective-permute-done.8.refs_1_, f32[16,512]{1,0:T(8,128)S(1)} %collective-permute-done.9.refs_2_, f32[16,512]{1,0:T(8,128)S(1)} %collective-permute-done.10.refs_3_), custom_call_target="tpu_custom_call" | custom-call | flops 65536 | bytes 524288 | tf_op jit(solution)/shard_map/pallas_call | solution.py:309
  (2 shorter events, 0.1 us)
Async XLA Ops:
  0.6 9.2 %copy-start = (bf16[27,64,128]{2,1,0:T(8,128)(2,1)S(1)}, bf16[27,64,128]{2,1,0:T(8,128)(2,1)}, u32[]{:S(2)}) copy-start(bf16[27,64,128]{2,1,0:T(8,128)(2,1)} %param.5) | copy-start | bytes 1327108
  0.6 18.9 %collective-permute-start.2 = (bf16[16,2,64,256]{3,2,1,0:T(8,128)(2,1)}, bf16[16,2,64,256]{3,2,1,0:T(8,128)(2,1)S(1)}, u32[]{:S(2)}, u32[]{:S(2)}) collective-permute-start(bf16[16,2,64,256]{3,2,1,0:T(8,128)(2,1)} %refs_0_.2), channel_id=1, source_target_pairs={{0,4},{4,8},{8,12},{12,16},{16,20},{20,24},{24,28},{28,0},{1,5},{5... | collective-permute-start | bytes 3145736 | tf_op jit(solution)/shard_map/ppermute | solution.py:355
  1.1 15.9 %collective-permute-start.1 = (bf16[32,1,32,128]{3,2,1,0:T(8,128)(2,1)}, bf16[32,1,32,128]{3,2,1,0:T(8,128)(2,1)S(1)}, u32[]{:S(2)}, u32[]{:S(2)}) collective-permute-start(bf16[32,1,32,128]{3,2,1,0:T(8,128)(2,1)} %refs_0_.3), channel_id=1, source_target_pairs={{0,2},{1,3},{2,0},{3,1},{4,6},{5,7},{6,4},{7,5},{8,10},{9,11},{10,... | collective-permute-start | bytes 786440 | tf_op jit(solution)/shard_map/ppermute | solution.py:347
  4.8 14.0 %collective-permute-start.3 = (bf16[32,1,32,128]{3,2,1,0:T(8,128)(2,1)}, bf16[32,1,32,128]{3,2,1,0:T(8,128)(2,1)S(1)}, u32[]{:S(2)}, u32[]{:S(2)}) collective-permute-start(bf16[32,1,32,128]{3,2,1,0:T(8,128)(2,1)} %refs_0_.3), channel_id=1, source_target_pairs={{4,0},{8,4},{12,8},{16,12},{20,16},{24,20},{28,24},{0,28},{5,1},{9... | collective-permute-start | bytes 786440 | tf_op jit(solution)/shard_map/ppermute | solution.py:356
  7.1 12.5 %collective-permute-start = (bf16[32,1,32,128]{3,2,1,0:T(8,128)(2,1)}, bf16[32,1,32,128]{3,2,1,0:T(8,128)(2,1)S(1)}, u32[]{:S(2)}, u32[]{:S(2)}) collective-permute-start(bf16[32,1,32,128]{3,2,1,0:T(8,128)(2,1)} %refs_0_.3), channel_id=1, source_target_pairs={{0,1},{1,0},{2,3},{3,2},{4,5},{5,4},{6,7},{7,6},{8,9},{9,8},{10,11... | collective-permute-start | bytes 786440 | tf_op jit(solution)/shard_map/ppermute | solution.py:347
  8.7 1.0 %copy-start.1 = (bf16[32,1,32,128]{3,2,1,0:T(8,128)(2,1)S(1)}, bf16[32,1,32,128]{3,2,1,0:T(8,128)(2,1)}, u32[]{:S(2)}) copy-start(bf16[32,1,32,128]{3,2,1,0:T(8,128)(2,1)} %refs_0_.3) | copy-start | bytes 786436
  9.8 1.2 %copy-start.2 = (bf16[16,2,64,256]{3,2,1,0:T(8,128)(2,1)S(1)}, bf16[16,2,64,256]{3,2,1,0:T(8,128)(2,1)}, u32[]{:S(2)}) copy-start(bf16[16,2,64,256]{3,2,1,0:T(8,128)(2,1)} %refs_0_.2) | copy-start | bytes 3145732
  17.0 9.1 %collective-permute-start.4 = (bf16[32,1,32,128]{3,2,1,0:T(8,128)(2,1)S(1)}, bf16[32,1,32,128]{3,2,1,0:T(8,128)(2,1)S(1)}, u32[]{:S(2)}, u32[]{:S(2)}) collective-permute-start(bf16[32,1,32,128]{3,2,1,0:T(8,128)(2,1)S(1)} %collective-permute-done.1.refs_1_), channel_id=1, source_target_pairs={{0,1},{1,0},{2,3},{3,2},{4,5},{5,4},{6,7},{7,6},{8,9},{9,8},{10,11... | collective-permute-start | bytes 786440 | tf_op jit(solution)/shard_map/ppermute | solution.py:347
  19.9 13.3 %collective-permute-start.6 = (bf16[64,4096]{1,0:T(8,128)(2,1)S(1)}, bf16[64,4096]{1,0:T(8,128)(2,1)S(1)}, u32[]{:S(2)}, u32[]{:S(2)}) collective-permute-start(bf16[64,4096]{1,0:T(8,128)(2,1)S(1)} %shard_map.54.refs_3_.refs_2_.refs_5_), channel_id=1, source_target_pairs={{4,0},{8,4},{12,8},{16,12},{20,16},{24,20},{28,24},{0,28},{5,1},{9... | collective-permute-start | bytes 1572872 | tf_op jit(solution)/shard_map/ppermute | solution.py:369
  26.3 6.8 %collective-permute-start.7 = (bf16[32,4096]{1,0:T(8,128)(2,1)S(1)}, bf16[32,4096]{1,0:T(8,128)(2,1)S(1)}, u32[]{:S(2)}, u32[]{:S(2)}) collective-permute-start(bf16[32,4096]{1,0:T(8,128)(2,1)S(1)} %shard_map.55.refs_4_.refs_3_.refs_6_), channel_id=1, source_target_pairs={{4,0},{8,4},{12,8},{16,12},{20,16},{24,20},{28,24},{0,28},{5,1},{9... | collective-permute-start | bytes 786440 | tf_op jit(solution)/shard_map/ppermute | solution.py:369
  27.5 2.1 %collective-permute-start.5 = (f32[64,512]{1,0:T(8,128)S(1)}, f32[64,512]{1,0:T(8,128)S(1)}, u32[]{:S(2)}, u32[]{:S(2)}) collective-permute-start(f32[64,512]{1,0:T(8,128)S(1)} %get-tuple-element.30), channel_id=1, source_target_pairs={{0,4},{4,0},{8,12},{12,8},{16,20},{20,16},{24,28},{28,24},{1,5},{5... | collective-permute-start | bytes 393224 | tf_op jit(solution)/shard_map/ppermute | solution.py:405
  29.6 5.2 %collective-permute-start.8 = (f32[16,512]{1,0:T(8,128)S(1)}, f32[16,512]{1,0:T(8,128)S(1)}, u32[]{:S(2)}, u32[]{:S(2)}) collective-permute-start(f32[16,512]{1,0:T(8,128)S(1)} %get-tuple-element.39), channel_id=1, source_target_pairs={{0,24},{4,28},{8,16},{12,20},{16,8},{20,12},{24,0},{28,4},{1,25},{... | collective-permute-start | bytes 98312 | tf_op jit(solution)/shard_map/ppermute | solution.py:416
  31.9 3.9 %collective-permute-start.9 = (f32[16,512]{1,0:T(8,128)S(1)}, f32[16,512]{1,0:T(8,128)S(1)}, u32[]{:S(2)}, u32[]{:S(2)}) collective-permute-start(f32[16,512]{1,0:T(8,128)S(1)} %get-tuple-element.40), channel_id=1, source_target_pairs={{0,16},{4,20},{8,24},{12,28},{16,0},{20,4},{24,8},{28,12},{1,17},{... | collective-permute-start | bytes 98312 | tf_op jit(solution)/shard_map/ppermute | solution.py:416
  32.7 3.9 %collective-permute-start.10 = (f32[16,512]{1,0:T(8,128)S(1)}, f32[16,512]{1,0:T(8,128)S(1)}, u32[]{:S(2)}, u32[]{:S(2)}) collective-permute-start(f32[16,512]{1,0:T(8,128)S(1)} %get-tuple-element.41), channel_id=1, source_target_pairs={{0,8},{4,12},{8,0},{12,4},{16,24},{20,28},{24,16},{28,20},{1,9},{5... | collective-permute-start | bytes 98312 | tf_op jit(solution)/shard_map/ppermute | solution.py:416

commit v11 on v10

--- a/solution.py
+++ b/solution.py
@@ -165,8 +165,7 @@
         out_ref[...] = keep_ref[place, :] + other_ref[place, :]
 
 
-def input_kernel(plane, *refs):
-    taps_ref, *line_refs, out_ref, cells_ref, lines_ref, rows_ref, sems = refs
+def input_rows(taps_ref, line_refs, rows_ref, cells_ref, lines_ref, finished):
     chans, rows, cols = rows_ref.shape
     half = cols // 2
     grid_cells = half * rows // 2
@@ -187,7 +186,6 @@
         lo = (3 * kind + b) * chans
         return cells_ref[lo : lo + chans, r * half : (r + 1) * half]
 
-    copies = []
     for start in range(0, rows, group):
         if start + group < rows:
             compute(start + group)
@@ -208,13 +206,26 @@
             for c in range(chans):
                 line = lines_ref[side, pl.ds(c, group, stride=pitch), :].astype(BF16)
                 rows_ref[c, start : start + group, lanes] = line
-        place = pl.ds(start, group)
-        copies.append(
-            pltpu.make_async_copy(
-                rows_ref.at[:, place], out_ref.at[:, plane, place], sems.at[start // group]
-            )
-        )
-        copies[-1].start()
+        finished(start, group)
+
+
+def even_kernel(taps_ref, *refs):
+    *line_refs, rows_ref, cells_ref, lines_ref = refs
+    input_rows(taps_ref, line_refs, rows_ref, cells_ref, lines_ref, lambda start, size: None)
+
+
+def odd_kernel(even_ref, taps_ref, *refs):
+    *line_refs, out_ref, cells_ref, lines_ref, rows_ref, even_sem, sems = refs
+    copies = [pltpu.make_async_copy(even_ref, out_ref.at[:, 0], even_sem)]
+    copies[0].start()
+
+    def finished(start, size):
+        place = pl.ds(start, size)
+        copy = pltpu.make_async_copy(rows_ref.at[:, place], out_ref.at[:, 1, place], sems.at[start // size])
+        copy.start()
+        copies.append(copy)
+
+    input_rows(taps_ref, line_refs, rows_ref, cells_ref, lines_ref, finished)
     for copy in copies:
         copy.wait()
 
@@ -304,13 +315,13 @@
     return (input_grad, summed * (1.0 / math.sqrt(cell_count)))
 
 
-def call(kernel, out_shape, *args, scratch=(), cost=None):
+def call(kernel, out_shape, *args, out_spec=VMEM, scratch=(), cost=None):
     flops, moved = cost
     return pl.pallas_call(
         kernel,
         out_shape=out_shape,
         in_specs=[VMEM] * len(args),
-        out_specs=jax.tree.map(lambda _: VMEM, out_shape),
+        out_specs=jax.tree.map(lambda _: out_spec, out_shape),
         scratch_shapes=scratch,
         compiler_params=pltpu.CompilerParams(vmem_limit_bytes=LIMIT),
         cost_estimate=pl.CostEstimate(flops=flops, bytes_accessed=moved, transcendentals=0),
@@ -381,30 +392,21 @@
         ),
         cost=(2 * 27 * chans * channels * cells, 8 << 20),
     )
-    def input_plane(plane, taps, lines, before):
-        kernel = functools.partial(input_kernel, plane)
-        earlier = [] if before is None else [before]
-        return pl.pallas_call(
-            kernel if before is None else lambda before, *refs: kernel(*refs),
-            out_shape=jax.ShapeDtypeStruct(volume.shape, BF16),
-            in_specs=[HBM] * len(earlier) + [VMEM] * (1 + len(lines)),
-            out_specs=HBM,
-            input_output_aliases={} if before is None else {0: 0},
-            scratch_shapes=(
-                pltpu.VMEM((9 * chans, cells + cols), F32),
-                pltpu.VMEM((2, 256 // chans * (chans + 8), cols), F32),
-                pltpu.VMEM((chans, 2 * rows, 2 * cols), BF16),
-                pltpu.SemaphoreType.DMA((2 * rows * chans // 256,)),
-            ),
-            compiler_params=pltpu.CompilerParams(vmem_limit_bytes=LIMIT),
-            cost_estimate=pl.CostEstimate(
-                flops=2 * 9 * chans * taps.shape[1] * cells, bytes_accessed=4 << 20, transcendentals=0
-            ),
-        )(*earlier, taps, *lines)
-
+    cells_scratch = (
+        pltpu.VMEM((9 * chans, cells + cols), F32),
+        pltpu.VMEM((2, 256 // chans * (chans + 8), cols), F32),
+    )
+    plane = jax.ShapeDtypeStruct((chans, 2 * rows, 2 * cols), BF16)
     other = lax.ppermute(send, "depth", [(i, i ^ 1) for i in range(depth)])
-    half_grad = input_plane(0, even_taps, own_lines, None)
-    other, half_grad = lax.optimization_barrier((other, half_grad))
+    even_grad = call(
+        even_kernel,
+        plane,
+        even_taps,
+        *own_lines,
+        scratch=cells_scratch,
+        cost=(2 * 9 * chans * channels * cells, 4 << 20),
+    )
+    other, even_grad = lax.optimization_barrier((other, even_grad))
     own_terms, *terms = call(
         pair_kernel,
         [jax.ShapeDtypeStruct((outs, 32 * chans), F32)] * (depth // 2),
@@ -416,7 +418,22 @@
         lax.ppermute(terms[k - 1], "depth", [(i, i ^ (2 * k)) for i in range(depth)])
         for k in range(depth // 2 - 1, 0, -1)
     ]
-    input_grad = input_plane(1, odd_taps, next_lines + own_lines, half_grad)
+    input_grad = call(
+        odd_kernel,
+        jax.ShapeDtypeStruct(volume.shape, BF16),
+        even_grad,
+        odd_taps,
+        *next_lines,
+        *own_lines,
+        out_spec=HBM,
+        scratch=cells_scratch
+        + (
+            pltpu.VMEM(plane.shape, BF16),
+            pltpu.SemaphoreType.DMA,
+            pltpu.SemaphoreType.DMA((2 * rows * chans // 256,)),
+        ),
+        cost=(4 * 9 * chans * channels * cells, 4 << 20),
+    )
     own_terms, input_grad = lax.optimization_barrier((own_terms, input_grad))
     scale = 1.0 / math.sqrt(depth * cells)
     weight_grad = call(

time: 37.6 us -> 37.3 us (level)
  Pallas kernels: 6.64 us -> 5.94 us
  waiting for transfers between devices: 12.2 us -> 12.6 us
    pallas_call x2 -> x0, Pallas kernels: 3.28 us -> none  [input_plane(): pl.pallas_call(kernel if before is None else lambda before, *refs: kernel...]
    pallas_call x9 -> x11, Pallas kernels: 3.36 us -> 5.94 us  [call(): pl.pallas_call(kernel, out_shape=out_shape, in_specs=[VMEM] * len(args),...]
    ppermute x3, waiting for transfers between devices: 1.81 us -> 2.21 us  [shards(): lax.ppermute(terms[k - 1], 'depth', [(i, i ^ 2 * k) for i in range(depth)])]
  transfers between devices with their start and end apart: 11 -> 11, of which waited for: 5 -> 5; matrix products, arithmetic and copies ran while one was open for 0% -> 0% of each run, Pallas kernels for 16% -> 14%
where the time goes in v11:
time: 37.3 us; the launch traced here: 37.1 us
  starting transfers between devices  15.6 us (42%)
  waiting for transfers between devices  12.6 us (34%)
  Pallas kernels  5.94 us (16%)
  local copies, waits for them, and re-layouts  2.24 us (6%)
  between operations  0.73 us (2%)
    ppermute x3, waiting for transfers between devices, shards(): lax.ppermute(got[mask - low], 'chan', [(i, i ^ low) for i in range(count)])  9.81 us
    ppermute x3, starting transfers between devices, shards(): lax.ppermute(got[mask - low], 'chan', [(i, i ^ low) for i in range(count)])  7.07 us
    pallas_call x11, Pallas kernels, call(): pl.pallas_call(kernel, out_shape=out_shape, in_specs=[VMEM] * len(args),...  5.94 us
    ppermute x3, starting transfers between devices, shards(): lax.ppermute(terms[k - 1], 'depth', [(i, i ^ 2 * k) for i in range(depth)])  3.57 us
    ppermute x1, starting transfers between devices, shards(): next_own = lax.ppermute(grad_out, 'depth', nearer)  2.28 us
    unnamed x6, local copies, waits for them, and re-layouts  2.21 us
    ppermute x3, waiting for transfers between devices, shards(): lax.ppermute(terms[k - 1], 'depth', [(i, i ^ 2 * k) for i in range(depth)])  2.21 us
    ppermute x2, starting transfers between devices, shards(): lax.ppermute(part, 'depth', nearer)  1.74 us
  transfers between devices with their start and end apart: 11, of which 5 were waited for; matrix products, arithmetic and copies ran while one was open for 0% of the time, Pallas kernels for 14%

profile of v11, /device:TPU:0, one launch (start us, length us, event | category | flops | bytes accessed | tf_op | source)
XLA Modules:
  0.0 37.1 jit_solution(10679219680390073807)
XLA Ops:
  0.6 0.0 copy-start
  0.6 0.5 %collective-permute-start.2 = (bf16[16,2,64,256]{3,2,1,0:T(8,128)(2,1)}, bf16[16,2,64,256]{3,2,1,0:T(8,128)(2,1)S(1)}, u32[]{:S(2)}, u32[]{:S(2)}) collective-permute-start(bf16[16,2,64,256]{3,2,1,0:T(8,128)(2,1)} %refs_0_.2), channel_id=1, source_target_pairs={{0,4},{4,8},{8,12},{12,16},{16,20},{20,24},{24,28},{28,0},{1,5},{5... | collective-permute-start | bytes 3145736 | tf_op jit(solution)/shard_map/ppermute | solution.py:366
  1.1 3.7 %collective-permute-start.1 = (bf16[32,1,32,128]{3,2,1,0:T(8,128)(2,1)}, bf16[32,1,32,128]{3,2,1,0:T(8,128)(2,1)S(1)}, u32[]{:S(2)}, u32[]{:S(2)}) collective-permute-start(bf16[32,1,32,128]{3,2,1,0:T(8,128)(2,1)} %refs_0_.3), channel_id=1, source_target_pairs={{0,2},{1,3},{2,0},{3,1},{4,6},{5,7},{6,4},{7,5},{8,10},{9,11},{10,... | collective-permute-start | bytes 786440 | tf_op jit(solution)/shard_map/ppermute | solution.py:358
  4.8 2.3 %collective-permute-start.3 = (bf16[32,1,32,128]{3,2,1,0:T(8,128)(2,1)}, bf16[32,1,32,128]{3,2,1,0:T(8,128)(2,1)S(1)}, u32[]{:S(2)}, u32[]{:S(2)}) collective-permute-start(bf16[32,1,32,128]{3,2,1,0:T(8,128)(2,1)} %refs_0_.3), channel_id=1, source_target_pairs={{4,0},{8,4},{12,8},{16,12},{20,16},{24,20},{28,24},{0,28},{5,1},{9... | collective-permute-start | bytes 786440 | tf_op jit(solution)/shard_map/ppermute | solution.py:367
  7.1 1.6 %collective-permute-start = (bf16[32,1,32,128]{3,2,1,0:T(8,128)(2,1)}, bf16[32,1,32,128]{3,2,1,0:T(8,128)(2,1)S(1)}, u32[]{:S(2)}, u32[]{:S(2)}) collective-permute-start(bf16[32,1,32,128]{3,2,1,0:T(8,128)(2,1)} %refs_0_.3), channel_id=1, source_target_pairs={{0,1},{1,0},{2,3},{3,2},{4,5},{5,4},{6,7},{7,6},{8,9},{9,8},{10,11... | collective-permute-start | bytes 786440 | tf_op jit(solution)/shard_map/ppermute | solution.py:358
  8.7 0.0 copy-start.1
  8.7 1.0 %copy-done.1 = bf16[32,1,32,128]{3,2,1,0:T(8,128)(2,1)S(1)} copy-done((bf16[32,1,32,128]{3,2,1,0:T(8,128)(2,1)S(1)}, bf16[32,1,32,128]{3,2,1,0:T(8,128)(2,1)}, u32[]{:S(2)}) %copy-start.1) | copy-done | bytes 262168
  9.7 0.1 shard_map.52.refs_2_.refs_0_.refs_3_
  9.8 0.0 copy-done
  9.8 0.0 copy-start.2
  9.9 1.2 %copy-done.2 = bf16[16,2,64,256]{3,2,1,0:T(8,128)(2,1)S(1)} copy-done((bf16[16,2,64,256]{3,2,1,0:T(8,128)(2,1)S(1)}, bf16[16,2,64,256]{3,2,1,0:T(8,128)(2,1)}, u32[]{:S(2)}) %copy-start.2) | copy-done | bytes 1048600
  11.1 0.9 %shard_map.50 = (bf16[192,4096]{1,0:T(8,128)(2,1)S(1)}, bf16[144,128]{1,0:T(8,128)(2,1)S(1)}, bf16[144,256]{1,0:T(8,128)(2,1)S(1)}) custom-call(bf16[16,2,64,256]{3,2,1,0:T(8,128)(2,1)S(1)} %copy-done.2, bf16[27,16,128]{2,1,0:T(8,128)(2,1)S(1)} %constant_dynamic-slice_fusion.refs_1_), custom_call_target="tpu_custom_call" | custom-call | flops 536870912 | bytes 4194304 | tf_op jit(solution)/shard_map/pallas_call | solution.py:320
  12.0 5.1 %collective-permute-done.1.refs_1_ = bf16[32,1,32,128]{3,2,1,0:T(8,128)(2,1)S(1)} collective-permute-done((bf16[32,1,32,128]{3,2,1,0:T(8,128)(2,1)}, bf16[32,1,32,128]{3,2,1,0:T(8,128)(2,1)S(1)}, u32[]{:S(2)}, u32[]{:S(2)}) %collective-permute-start.1) | collective-permute-done | bytes 262176 | tf_op jit(solution)/shard_map/ppermute | solution.py:358
  17.0 1.8 %collective-permute-start.4 = (bf16[32,1,32,128]{3,2,1,0:T(8,128)(2,1)S(1)}, bf16[32,1,32,128]{3,2,1,0:T(8,128)(2,1)S(1)}, u32[]{:S(2)}, u32[]{:S(2)}) collective-permute-start(bf16[32,1,32,128]{3,2,1,0:T(8,128)(2,1)S(1)} %collective-permute-done.1.refs_1_), channel_id=1, source_target_pairs={{0,1},{1,0},{2,3},{3,2},{4,5},{5,4},{6,7},{7,6},{8,9},{9,8},{10,11... | collective-permute-start | bytes 786440 | tf_op jit(solution)/shard_map/ppermute | solution.py:358
  18.9 0.0 collective-permute-done.3.refs_0_
  18.9 0.1 shard_map.53.refs_0_
  19.0 0.5 %collective-permute-done.2.behind_ref = bf16[16,2,64,256]{3,2,1,0:T(8,128)(2,1)S(1)} collective-permute-done((bf16[16,2,64,256]{3,2,1,0:T(8,128)(2,1)}, bf16[16,2,64,256]{3,2,1,0:T(8,128)(2,1)S(1)}, u32[]{:S(2)}, u32[]{:S(2)}) %collective-permute-start.2) | collective-permute-done | bytes 1048608 | tf_op jit(solution)/shard_map/ppermute | solution.py:366
  19.5 0.1 shard_map.51.refs_1_
  19.6 0.0 collective-permute-done.refs_0_
  19.6 0.3 shard_map.54.refs_3_.refs_1_.refs_4_
  19.9 1.5 %collective-permute-start.6 = (bf16[64,4096]{1,0:T(8,128)(2,1)S(1)}, bf16[64,4096]{1,0:T(8,128)(2,1)S(1)}, u32[]{:S(2)}, u32[]{:S(2)}) collective-permute-start(bf16[64,4096]{1,0:T(8,128)(2,1)S(1)} %shard_map.54.refs_3_.refs_1_.refs_4_), channel_id=1, source_target_pairs={{4,0},{8,4},{12,8},{16,12},{20,16},{24,20},{28,24},{0,28},{5,1},{9... | collective-permute-start | bytes 1572872 | tf_op jit(solution)/shard_map/ppermute | solution.py:380
  21.4 4.8 %collective-permute-done.4.refs_0_ = bf16[32,1,32,128]{3,2,1,0:T(8,128)(2,1)S(1)} collective-permute-done((bf16[32,1,32,128]{3,2,1,0:T(8,128)(2,1)S(1)}, bf16[32,1,32,128]{3,2,1,0:T(8,128)(2,1)S(1)}, u32[]{:S(2)}, u32[]{:S(2)}) %collective-permute-start.4) | collective-permute-done | bytes 262176 | tf_op jit(solution)/shard_map/ppermute | solution.py:358
  26.2 0.1 shard_map.55.refs_4_.refs_2_.refs_5_
  26.3 0.2 collective-permute-start.7
  26.5 0.9 %shard_map.56 = (f32[64,512]{1,0:T(8,128)S(1)}, f32[64,512]{1,0:T(8,128)S(1)}) custom-call(bf16[192,4096]{1,0:T(8,128)(2,1)S(1)} %get-tuple-element.24.refs_0_, bf16[96,4096]{1,0:T(8,128)(2,1)S(1)} %shard_map.51.refs_1_, bf16[32,4096]{1,0:T(8,128)(2,1)S(1)} %shard_map.52.refs_2_.refs_0_.refs_3_, bf16[64,4096]{1,0:T(8,128)(2,1)S(1)} %shard_map.54.refs_3_.refs_1_.refs_4_, ...), custom_call_target="tpu_custom_call" | custom-call | flops 452984832 | bytes 8388608 | tf_op jit(solution)/shard_map/pallas_call | solution.py:320
  27.5 0.4 %collective-permute-start.5 = (f32[64,512]{1,0:T(8,128)S(1)}, f32[64,512]{1,0:T(8,128)S(1)}, u32[]{:S(2)}, u32[]{:S(2)}) collective-permute-start(f32[64,512]{1,0:T(8,128)S(1)} %get-tuple-element.30), channel_id=1, source_target_pairs={{0,4},{4,0},{8,12},{12,8},{16,20},{20,16},{24,28},{28,24},{1,5},{5... | collective-permute-start | bytes 393224 | tf_op jit(solution)/shard_map/ppermute | solution.py:400
  27.9 0.9 %shard_map.57.even_ref = bf16[16,64,256]{2,1,0:T(8,128)(2,1)S(1)} custom-call(bf16[144,128]{1,0:T(8,128)(2,1)S(1)} %get-tuple-element.31.taps_ref, bf16[32,4096]{1,0:T(8,128)(2,1)S(1)} %shard_map.52.refs_2_.refs_0_.refs_3_, bf16[64,4096]{1,0:T(8,128)(2,1)S(1)} %shard_map.54.refs_3_.refs_1_.refs_4_, bf16[32,4096]{1,0:T(8,128)(2,1)S(1)} %shard_map.55.refs_4_.refs_2_.refs_5_), custom_call_target="tpu_custom_call" | custom-call | flops 150994944 | bytes 4194304 | tf_op jit(solution)/shard_map/pallas_call | solution.py:320
  28.8 0.0 collective-permute-done.5.other_ref
  28.9 1.7 %collective-permute-start.10 = (f32[16,512]{1,0:T(8,128)S(1)}, f32[16,512]{1,0:T(8,128)S(1)}, u32[]{:S(2)}, u32[]{:S(2)}) collective-permute-start(f32[16,512]{1,0:T(8,128)S(1)} %get-tuple-element.41), channel_id=1, source_target_pairs={{0,8},{4,12},{8,0},{12,4},{16,24},{20,28},{24,16},{28,20},{1,9},{5... | collective-permute-start | bytes 98312 | tf_op jit(solution)/shard_map/ppermute | solution.py:418
  30.6 1.9 %collective-permute-start.8 = (f32[16,512]{1,0:T(8,128)S(1)}, f32[16,512]{1,0:T(8,128)S(1)}, u32[]{:S(2)}, u32[]{:S(2)}) collective-permute-start(f32[16,512]{1,0:T(8,128)S(1)} %get-tuple-element.39), channel_id=1, source_target_pairs={{0,24},{4,28},{8,16},{12,20},{16,8},{20,12},{24,0},{28,4},{1,25},{... | collective-permute-start | bytes 98312 | tf_op jit(solution)/shard_map/ppermute | solution.py:418
  32.4 0.0 collective-permute-start.9
  32.5 0.0 collective-permute-done.7.refs_2_
  32.5 0.0 collective-permute-done.6.refs_1_
  32.5 1.7 %shard_map.59 = bf16[16,2,64,256]{3,2,1,0:T(8,128)(2,1)} custom-call(bf16[16,64,256]{2,1,0:T(8,128)(2,1)S(1)} %shard_map.57.even_ref, bf16[144,256]{1,0:T(8,128)(2,1)S(1)} %get-tuple-element.35.taps_ref, bf16[32,4096]{1,0:T(8,128)(2,1)S(1)} %shard_map.53.refs_0_, bf16[64,4096]{1,0:T(8,128)(2,1)S(1)} %collective-permute-done.6.refs_1_, ...), custom_call_target="tpu_custom_call" | custom-call | flops 301989888 | bytes 4194304 | tf_op jit(solution)/shard_map/pallas_call | solution.py:320
  34.1 0.0 collective-permute-done.10.refs_3_
  34.2 1.2 %collective-permute-done.8.refs_1_ = f32[16,512]{1,0:T(8,128)S(1)} collective-permute-done((f32[16,512]{1,0:T(8,128)S(1)}, f32[16,512]{1,0:T(8,128)S(1)}, u32[]{:S(2)}, u32[]{:S(2)}) %collective-permute-start.8) | collective-permute-done | bytes 32800 | tf_op jit(solution)/shard_map/ppermute | solution.py:418
  35.4 1.0 %collective-permute-done.9.refs_2_ = f32[16,512]{1,0:T(8,128)S(1)} collective-permute-done((f32[16,512]{1,0:T(8,128)S(1)}, f32[16,512]{1,0:T(8,128)S(1)}, u32[]{:S(2)}, u32[]{:S(2)}) %collective-permute-start.9) | collective-permute-done | bytes 32800 | tf_op jit(solution)/shard_map/ppermute | solution.py:418
  36.4 0.8 %shard_map.60 = f32[16,16,27]{2,1,0:T(8,128)} custom-call(f32[16,512]{1,0:T(8,128)S(1)} %get-tuple-element.38.refs_0_, f32[16,512]{1,0:T(8,128)S(1)} %collective-permute-done.8.refs_1_, f32[16,512]{1,0:T(8,128)S(1)} %collective-permute-done.9.refs_2_, f32[16,512]{1,0:T(8,128)S(1)} %collective-permute-done.10.refs_3_), custom_call_target="tpu_custom_call" | custom-call | flops 65536 | bytes 524288 | tf_op jit(solution)/shard_map/pallas_call | solution.py:320
  (2 shorter events, 0.0 us)
Async XLA Ops:
  0.6 9.2 %copy-start = (bf16[27,64,128]{2,1,0:T(8,128)(2,1)S(1)}, bf16[27,64,128]{2,1,0:T(8,128)(2,1)}, u32[]{:S(2)}) copy-start(bf16[27,64,128]{2,1,0:T(8,128)(2,1)} %param.5) | copy-start | bytes 1327108
  0.6 18.9 %collective-permute-start.2 = (bf16[16,2,64,256]{3,2,1,0:T(8,128)(2,1)}, bf16[16,2,64,256]{3,2,1,0:T(8,128)(2,1)S(1)}, u32[]{:S(2)}, u32[]{:S(2)}) collective-permute-start(bf16[16,2,64,256]{3,2,1,0:T(8,128)(2,1)} %refs_0_.2), channel_id=1, source_target_pairs={{0,4},{4,8},{8,12},{12,16},{16,20},{20,24},{24,28},{28,0},{1,5},{5... | collective-permute-start | bytes 3145736 | tf_op jit(solution)/shard_map/ppermute | solution.py:366
  1.1 15.9 %collective-permute-start.1 = (bf16[32,1,32,128]{3,2,1,0:T(8,128)(2,1)}, bf16[32,1,32,128]{3,2,1,0:T(8,128)(2,1)S(1)}, u32[]{:S(2)}, u32[]{:S(2)}) collective-permute-start(bf16[32,1,32,128]{3,2,1,0:T(8,128)(2,1)} %refs_0_.3), channel_id=1, source_target_pairs={{0,2},{1,3},{2,0},{3,1},{4,6},{5,7},{6,4},{7,5},{8,10},{9,11},{10,... | collective-permute-start | bytes 786440 | tf_op jit(solution)/shard_map/ppermute | solution.py:358
  4.8 14.0 %collective-permute-start.3 = (bf16[32,1,32,128]{3,2,1,0:T(8,128)(2,1)}, bf16[32,1,32,128]{3,2,1,0:T(8,128)(2,1)S(1)}, u32[]{:S(2)}, u32[]{:S(2)}) collective-permute-start(bf16[32,1,32,128]{3,2,1,0:T(8,128)(2,1)} %refs_0_.3), channel_id=1, source_target_pairs={{4,0},{8,4},{12,8},{16,12},{20,16},{24,20},{28,24},{0,28},{5,1},{9... | collective-permute-start | bytes 786440 | tf_op jit(solution)/shard_map/ppermute | solution.py:367
  7.1 12.5 %collective-permute-start = (bf16[32,1,32,128]{3,2,1,0:T(8,128)(2,1)}, bf16[32,1,32,128]{3,2,1,0:T(8,128)(2,1)S(1)}, u32[]{:S(2)}, u32[]{:S(2)}) collective-permute-start(bf16[32,1,32,128]{3,2,1,0:T(8,128)(2,1)} %refs_0_.3), channel_id=1, source_target_pairs={{0,1},{1,0},{2,3},{3,2},{4,5},{5,4},{6,7},{7,6},{8,9},{9,8},{10,11... | collective-permute-start | bytes 786440 | tf_op jit(solution)/shard_map/ppermute | solution.py:358
  8.7 1.0 %copy-start.1 = (bf16[32,1,32,128]{3,2,1,0:T(8,128)(2,1)S(1)}, bf16[32,1,32,128]{3,2,1,0:T(8,128)(2,1)}, u32[]{:S(2)}) copy-start(bf16[32,1,32,128]{3,2,1,0:T(8,128)(2,1)} %refs_0_.3) | copy-start | bytes 786436
  9.8 1.2 %copy-start.2 = (bf16[16,2,64,256]{3,2,1,0:T(8,128)(2,1)S(1)}, bf16[16,2,64,256]{3,2,1,0:T(8,128)(2,1)}, u32[]{:S(2)}) copy-start(bf16[16,2,64,256]{3,2,1,0:T(8,128)(2,1)} %refs_0_.2) | copy-start | bytes 3145732
  17.0 9.1 %collective-permute-start.4 = (bf16[32,1,32,128]{3,2,1,0:T(8,128)(2,1)S(1)}, bf16[32,1,32,128]{3,2,1,0:T(8,128)(2,1)S(1)}, u32[]{:S(2)}, u32[]{:S(2)}) collective-permute-start(bf16[32,1,32,128]{3,2,1,0:T(8,128)(2,1)S(1)} %collective-permute-done.1.refs_1_), channel_id=1, source_target_pairs={{0,1},{1,0},{2,3},{3,2},{4,5},{5,4},{6,7},{7,6},{8,9},{9,8},{10,11... | collective-permute-start | bytes 786440 | tf_op jit(solution)/shard_map/ppermute | solution.py:358
  19.9 12.6 %collective-permute-start.6 = (bf16[64,4096]{1,0:T(8,128)(2,1)S(1)}, bf16[64,4096]{1,0:T(8,128)(2,1)S(1)}, u32[]{:S(2)}, u32[]{:S(2)}) collective-permute-start(bf16[64,4096]{1,0:T(8,128)(2,1)S(1)} %shard_map.54.refs_3_.refs_1_.refs_4_), channel_id=1, source_target_pairs={{4,0},{8,4},{12,8},{16,12},{20,16},{24,20},{28,24},{0,28},{5,1},{9... | collective-permute-start | bytes 1572872 | tf_op jit(solution)/shard_map/ppermute | solution.py:380
  26.3 6.2 %collective-permute-start.7 = (bf16[32,4096]{1,0:T(8,128)(2,1)S(1)}, bf16[32,4096]{1,0:T(8,128)(2,1)S(1)}, u32[]{:S(2)}, u32[]{:S(2)}) collective-permute-start(bf16[32,4096]{1,0:T(8,128)(2,1)S(1)} %shard_map.55.refs_4_.refs_2_.refs_5_), channel_id=1, source_target_pairs={{4,0},{8,4},{12,8},{16,12},{20,16},{24,20},{28,24},{0,28},{5,1},{9... | collective-permute-start | bytes 786440 | tf_op jit(solution)/shard_map/ppermute | solution.py:380
  27.5 1.4 %collective-permute-start.5 = (f32[64,512]{1,0:T(8,128)S(1)}, f32[64,512]{1,0:T(8,128)S(1)}, u32[]{:S(2)}, u32[]{:S(2)}) collective-permute-start(f32[64,512]{1,0:T(8,128)S(1)} %get-tuple-element.30), channel_id=1, source_target_pairs={{0,4},{4,0},{8,12},{12,8},{16,20},{20,16},{24,28},{28,24},{1,5},{5... | collective-permute-start | bytes 393224 | tf_op jit(solution)/shard_map/ppermute | solution.py:400
  28.9 5.3 %collective-permute-start.10 = (f32[16,512]{1,0:T(8,128)S(1)}, f32[16,512]{1,0:T(8,128)S(1)}, u32[]{:S(2)}, u32[]{:S(2)}) collective-permute-start(f32[16,512]{1,0:T(8,128)S(1)} %get-tuple-element.41), channel_id=1, source_target_pairs={{0,8},{4,12},{8,0},{12,4},{16,24},{20,28},{24,16},{28,20},{1,9},{5... | collective-permute-start | bytes 98312 | tf_op jit(solution)/shard_map/ppermute | solution.py:418
  30.6 4.8 %collective-permute-start.8 = (f32[16,512]{1,0:T(8,128)S(1)}, f32[16,512]{1,0:T(8,128)S(1)}, u32[]{:S(2)}, u32[]{:S(2)}) collective-permute-start(f32[16,512]{1,0:T(8,128)S(1)} %get-tuple-element.39), channel_id=1, source_target_pairs={{0,24},{4,28},{8,16},{12,20},{16,8},{20,12},{24,0},{28,4},{1,25},{... | collective-permute-start | bytes 98312 | tf_op jit(solution)/shard_map/ppermute | solution.py:418
  32.4 3.9 %collective-permute-start.9 = (f32[16,512]{1,0:T(8,128)S(1)}, f32[16,512]{1,0:T(8,128)S(1)}, u32[]{:S(2)}, u32[]{:S(2)}) collective-permute-start(f32[16,512]{1,0:T(8,128)S(1)} %get-tuple-element.40), channel_id=1, source_target_pairs={{0,16},{4,20},{8,24},{12,28},{16,0},{20,4},{24,8},{28,12},{1,17},{... | collective-permute-start | bytes 98312 | tf_op jit(solution)/shard_map/ppermute | solution.py:418

commit v12 on v11

--- a/solution.py
+++ b/solution.py
@@ -157,12 +157,8 @@
             send_ref[place, :] = jnp.where(odd_core, even, odd)
 
 
-def pair_kernel(keep_ref, other_ref, *out_refs):
-    chip = lax.axis_index("depth") // 2
-    outs = out_refs[0].shape[0]
-    for k, out_ref in enumerate(out_refs):
-        place = pl.ds(pl.multiple_of((chip ^ k) * outs, outs), outs)
-        out_ref[...] = keep_ref[place, :] + other_ref[place, :]
+def pair_kernel(keep_ref, other_ref, out_ref):
+    out_ref[...] = keep_ref[...] + other_ref[...]
 
 
 def input_rows(taps_ref, line_refs, rows_ref, cells_ref, lines_ref, finished):
@@ -230,12 +226,11 @@
         copy.wait()
 
 
-def total_kernel(scale, *refs):
-    *term_refs, out_ref = refs
+def total_kernel(scale, terms_ref, out_ref):
     chans, outs, taps = out_ref.shape
-    total = term_refs[0][...]
-    for ref in term_refs[1:]:
-        total = total + ref[...]
+    total = terms_ref[0]
+    for source in range(1, terms_ref.shape[0]):
+        total = total + terms_ref[source]
     total = total * scale
     for c in range(chans):
         out_ref[c] = total[:, 32 * c : 32 * c + taps]
@@ -407,17 +402,11 @@
         cost=(2 * 9 * chans * channels * cells, 4 << 20),
     )
     other, even_grad = lax.optimization_barrier((other, even_grad))
-    own_terms, *terms = call(
-        pair_kernel,
-        [jax.ShapeDtypeStruct((outs, 32 * chans), F32)] * (depth // 2),
-        keep,
-        other,
-        cost=(1 << 16, 1 << 19),
-    )
-    terms = [
-        lax.ppermute(terms[k - 1], "depth", [(i, i ^ (2 * k)) for i in range(depth)])
-        for k in range(depth // 2 - 1, 0, -1)
-    ]
+    pair_terms = call(pair_kernel, half_terms, keep, other, cost=(1 << 16, 1 << 19))
+    chips = [[chip * 2 + core for chip in range(depth // 2)] for core in range(2)]
+    terms = lax.all_to_all(
+        pair_terms, "depth", split_axis=0, concat_axis=0, axis_index_groups=chips, tiled=True
+    )
     input_grad = call(
         odd_kernel,
         jax.ShapeDtypeStruct(volume.shape, BF16),
@@ -434,13 +423,12 @@
         ),
         cost=(4 * 9 * chans * channels * cells, 4 << 20),
     )
-    own_terms, input_grad = lax.optimization_barrier((own_terms, input_grad))
+    terms, input_grad = lax.optimization_barrier((terms, input_grad))
     scale = 1.0 / math.sqrt(depth * cells)
     weight_grad = call(
         functools.partial(total_kernel, scale),
         jax.ShapeDtypeStruct((chans, outs, 27), F32),
-        own_terms,
-        *terms,
+        terms.reshape(depth // 2, outs, 32 * chans),
         cost=(1 << 16, 1 << 19),
     )
     return input_grad, jnp.transpose(weight_grad, (2, 0, 1))

time: 37.3 us -> 39.4 us (1.056)
  waiting for transfers between devices: 12.6 us -> 13.7 us
  Pallas kernels: 5.94 us -> 6.58 us
    all_to_all x0 -> x1, starting transfers between devices: none -> 3.82 us  [shards(): lax.all_to_all(pair_terms, 'depth', split_axis=0, concat_axis=0, axis_ind...]
    ppermute x3 -> x0, starting transfers between devices: 3.57 us -> none  [shards(): lax.ppermute(terms[k - 1], 'depth', [(i, i ^ 2 * k) for i in range(depth)])]
    all_to_all x0 -> x1, waiting for transfers between devices: none -> 3.35 us  [shards(): lax.all_to_all(pair_terms, 'depth', split_axis=0, concat_axis=0, axis_ind...]
    ppermute x3 -> x0, waiting for transfers between devices: 2.21 us -> none  [shards(): lax.ppermute(terms[k - 1], 'depth', [(i, i ^ 2 * k) for i in range(depth)])]
    pallas_call x11, Pallas kernels: 5.94 us -> 6.58 us  [call(): pl.pallas_call(kernel, out_shape=out_shape, in_specs=[VMEM] * len(args),...]
  transfers between devices with their start and end apart: 11 -> 9, of which waited for: 5 -> 4; matrix products, arithmetic and copies ran while one was open for 0% -> 0% of each run, Pallas kernels for 14% -> 15%
where the time goes in v12:
time: 39.4 us; the launch traced here: 39.1 us
  starting transfers between devices  15.8 us (40%)
  waiting for transfers between devices  13.7 us (35%)
  Pallas kernels  6.58 us (17%)
  local copies, waits for them, and re-layouts  2.24 us (6%)
  between operations  0.73 us (2%)
    ppermute x3, waiting for transfers between devices, shards(): lax.ppermute(got[mask - low], 'chan', [(i, i ^ low) for i in range(count)])  9.81 us
    ppermute x3, starting transfers between devices, shards(): lax.ppermute(got[mask - low], 'chan', [(i, i ^ low) for i in range(count)])  7.07 us
    pallas_call x11, Pallas kernels, call(): pl.pallas_call(kernel, out_shape=out_shape, in_specs=[VMEM] * len(args),...  6.58 us
    all_to_all x1, starting transfers between devices, shards(): lax.all_to_all(pair_terms, 'depth', split_axis=0, concat_axis=0, axis_ind...  3.82 us
    all_to_all x1, waiting for transfers between devices, shards(): lax.all_to_all(pair_terms, 'depth', split_axis=0, concat_axis=0, axis_ind...  3.35 us
    ppermute x1, starting transfers between devices, shards(): next_own = lax.ppermute(grad_out, 'depth', nearer)  2.28 us
    unnamed x6, local copies, waits for them, and re-layouts  2.21 us
    ppermute x2, starting transfers between devices, shards(): lax.ppermute(part, 'depth', nearer)  1.74 us
  transfers between devices with their start and end apart: 9, of which 4 were waited for; matrix products, arithmetic and copies ran while one was open for 0% of the time, Pallas kernels for 15%

profile of v12, /device:TPU:0, one launch (start us, length us, event | category | flops | bytes accessed | tf_op | source)
XLA Modules:
  0.0 39.1 jit_solution(8059352951595049675)
XLA Ops:
  0.6 0.0 copy-start
  0.6 0.5 %collective-permute-start.2 = (bf16[16,2,64,256]{3,2,1,0:T(8,128)(2,1)}, bf16[16,2,64,256]{3,2,1,0:T(8,128)(2,1)S(1)}, u32[]{:S(2)}, u32[]{:S(2)}) collective-permute-start(bf16[16,2,64,256]{3,2,1,0:T(8,128)(2,1)} %refs_0_.2), channel_id=1, source_target_pairs={{0,4},{4,8},{8,12},{12,16},{16,20},{20,24},{24,28},{28,0},{1,5},{5... | collective-permute-start | bytes 3145736 | tf_op jit(solution)/shard_map/ppermute | solution.py:361
  1.1 3.7 %collective-permute-start.1 = (bf16[32,1,32,128]{3,2,1,0:T(8,128)(2,1)}, bf16[32,1,32,128]{3,2,1,0:T(8,128)(2,1)S(1)}, u32[]{:S(2)}, u32[]{:S(2)}) collective-permute-start(bf16[32,1,32,128]{3,2,1,0:T(8,128)(2,1)} %refs_0_.3), channel_id=1, source_target_pairs={{0,2},{1,3},{2,0},{3,1},{4,6},{5,7},{6,4},{7,5},{8,10},{9,11},{10,... | collective-permute-start | bytes 786440 | tf_op jit(solution)/shard_map/ppermute | solution.py:353
  4.8 2.3 %collective-permute-start.3 = (bf16[32,1,32,128]{3,2,1,0:T(8,128)(2,1)}, bf16[32,1,32,128]{3,2,1,0:T(8,128)(2,1)S(1)}, u32[]{:S(2)}, u32[]{:S(2)}) collective-permute-start(bf16[32,1,32,128]{3,2,1,0:T(8,128)(2,1)} %refs_0_.3), channel_id=1, source_target_pairs={{4,0},{8,4},{12,8},{16,12},{20,16},{24,20},{28,24},{0,28},{5,1},{9... | collective-permute-start | bytes 786440 | tf_op jit(solution)/shard_map/ppermute | solution.py:362
  7.1 1.6 %collective-permute-start = (bf16[32,1,32,128]{3,2,1,0:T(8,128)(2,1)}, bf16[32,1,32,128]{3,2,1,0:T(8,128)(2,1)S(1)}, u32[]{:S(2)}, u32[]{:S(2)}) collective-permute-start(bf16[32,1,32,128]{3,2,1,0:T(8,128)(2,1)} %refs_0_.3), channel_id=1, source_target_pairs={{0,1},{1,0},{2,3},{3,2},{4,5},{5,4},{6,7},{7,6},{8,9},{9,8},{10,11... | collective-permute-start | bytes 786440 | tf_op jit(solution)/shard_map/ppermute | solution.py:353
  8.7 0.0 copy-start.1
  8.7 1.0 %copy-done.1 = bf16[32,1,32,128]{3,2,1,0:T(8,128)(2,1)S(1)} copy-done((bf16[32,1,32,128]{3,2,1,0:T(8,128)(2,1)S(1)}, bf16[32,1,32,128]{3,2,1,0:T(8,128)(2,1)}, u32[]{:S(2)}) %copy-start.1) | copy-done | bytes 262168
  9.7 0.1 shard_map.52.refs_2_.refs_0_.refs_3_
  9.8 0.0 copy-done
  9.8 0.0 copy-start.2
  9.9 1.2 %copy-done.2 = bf16[16,2,64,256]{3,2,1,0:T(8,128)(2,1)S(1)} copy-done((bf16[16,2,64,256]{3,2,1,0:T(8,128)(2,1)S(1)}, bf16[16,2,64,256]{3,2,1,0:T(8,128)(2,1)}, u32[]{:S(2)}) %copy-start.2) | copy-done | bytes 1048600
  11.1 0.9 %shard_map.50 = (bf16[192,4096]{1,0:T(8,128)(2,1)S(1)}, bf16[144,128]{1,0:T(8,128)(2,1)S(1)}, bf16[144,256]{1,0:T(8,128)(2,1)S(1)}) custom-call(bf16[16,2,64,256]{3,2,1,0:T(8,128)(2,1)S(1)} %copy-done.2, bf16[27,16,128]{2,1,0:T(8,128)(2,1)S(1)} %constant_dynamic-slice_fusion.refs_1_), custom_call_target="tpu_custom_call" | custom-call | flops 536870912 | bytes 4194304 | tf_op jit(solution)/shard_map/pallas_call | solution.py:315
  12.0 5.1 %collective-permute-done.1.refs_1_ = bf16[32,1,32,128]{3,2,1,0:T(8,128)(2,1)S(1)} collective-permute-done((bf16[32,1,32,128]{3,2,1,0:T(8,128)(2,1)}, bf16[32,1,32,128]{3,2,1,0:T(8,128)(2,1)S(1)}, u32[]{:S(2)}, u32[]{:S(2)}) %collective-permute-start.1) | collective-permute-done | bytes 262176 | tf_op jit(solution)/shard_map/ppermute | solution.py:353
  17.0 1.8 %collective-permute-start.4 = (bf16[32,1,32,128]{3,2,1,0:T(8,128)(2,1)S(1)}, bf16[32,1,32,128]{3,2,1,0:T(8,128)(2,1)S(1)}, u32[]{:S(2)}, u32[]{:S(2)}) collective-permute-start(bf16[32,1,32,128]{3,2,1,0:T(8,128)(2,1)S(1)} %collective-permute-done.1.refs_1_), channel_id=1, source_target_pairs={{0,1},{1,0},{2,3},{3,2},{4,5},{5,4},{6,7},{7,6},{8,9},{9,8},{10,11... | collective-permute-start | bytes 786440 | tf_op jit(solution)/shard_map/ppermute | solution.py:353
  18.9 0.0 collective-permute-done.3.refs_0_
  18.9 0.1 shard_map.53.refs_0_
  19.0 0.5 %collective-permute-done.2.behind_ref = bf16[16,2,64,256]{3,2,1,0:T(8,128)(2,1)S(1)} collective-permute-done((bf16[16,2,64,256]{3,2,1,0:T(8,128)(2,1)}, bf16[16,2,64,256]{3,2,1,0:T(8,128)(2,1)S(1)}, u32[]{:S(2)}, u32[]{:S(2)}) %collective-permute-start.2) | collective-permute-done | bytes 1048608 | tf_op jit(solution)/shard_map/ppermute | solution.py:361
  19.5 0.1 shard_map.51.refs_1_
  19.6 0.0 collective-permute-done.refs_0_
  19.6 0.3 shard_map.54.refs_3_.refs_1_.refs_4_
  19.9 1.5 %collective-permute-start.6 = (bf16[64,4096]{1,0:T(8,128)(2,1)S(1)}, bf16[64,4096]{1,0:T(8,128)(2,1)S(1)}, u32[]{:S(2)}, u32[]{:S(2)}) collective-permute-start(bf16[64,4096]{1,0:T(8,128)(2,1)S(1)} %shard_map.54.refs_3_.refs_1_.refs_4_), channel_id=1, source_target_pairs={{4,0},{8,4},{12,8},{16,12},{20,16},{24,20},{28,24},{0,28},{5,1},{9... | collective-permute-start | bytes 1572872 | tf_op jit(solution)/shard_map/ppermute | solution.py:375
  21.4 4.8 %collective-permute-done.4.refs_0_ = bf16[32,1,32,128]{3,2,1,0:T(8,128)(2,1)S(1)} collective-permute-done((bf16[32,1,32,128]{3,2,1,0:T(8,128)(2,1)S(1)}, bf16[32,1,32,128]{3,2,1,0:T(8,128)(2,1)S(1)}, u32[]{:S(2)}, u32[]{:S(2)}) %collective-permute-start.4) | collective-permute-done | bytes 262176 | tf_op jit(solution)/shard_map/ppermute | solution.py:353
  26.2 0.1 shard_map.55.refs_4_.refs_2_.refs_5_
  26.3 0.2 collective-permute-start.7
  26.5 0.9 %shard_map.56 = (f32[64,512]{1,0:T(8,128)S(1)}, f32[64,512]{1,0:T(8,128)S(1)}) custom-call(bf16[192,4096]{1,0:T(8,128)(2,1)S(1)} %get-tuple-element.20.refs_0_, bf16[96,4096]{1,0:T(8,128)(2,1)S(1)} %shard_map.51.refs_1_, bf16[32,4096]{1,0:T(8,128)(2,1)S(1)} %shard_map.52.refs_2_.refs_0_.refs_3_, bf16[64,4096]{1,0:T(8,128)(2,1)S(1)} %shard_map.54.refs_3_.refs_1_.refs_4_, ...), custom_call_target="tpu_custom_call" | custom-call | flops 452984832 | bytes 8388608 | tf_op jit(solution)/shard_map/pallas_call | solution.py:315
  27.5 0.4 %collective-permute-start.5 = (f32[64,512]{1,0:T(8,128)S(1)}, f32[64,512]{1,0:T(8,128)S(1)}, u32[]{:S(2)}, u32[]{:S(2)}) collective-permute-start(f32[64,512]{1,0:T(8,128)S(1)} %get-tuple-element.26), channel_id=1, source_target_pairs={{0,4},{4,0},{8,12},{12,8},{16,20},{20,16},{24,28},{28,24},{1,5},{5... | collective-permute-start | bytes 393224 | tf_op jit(solution)/shard_map/ppermute | solution.py:395
  27.9 0.9 %shard_map.57.even_ref = bf16[16,64,256]{2,1,0:T(8,128)(2,1)S(1)} custom-call(bf16[144,128]{1,0:T(8,128)(2,1)S(1)} %get-tuple-element.27.taps_ref, bf16[32,4096]{1,0:T(8,128)(2,1)S(1)} %shard_map.52.refs_2_.refs_0_.refs_3_, bf16[64,4096]{1,0:T(8,128)(2,1)S(1)} %shard_map.54.refs_3_.refs_1_.refs_4_, bf16[32,4096]{1,0:T(8,128)(2,1)S(1)} %shard_map.55.refs_4_.refs_2_.refs_5_), custom_call_target="tpu_custom_call" | custom-call | flops 150994944 | bytes 4194304 | tf_op jit(solution)/shard_map/pallas_call | solution.py:315
  28.8 0.0 collective-permute-done.5.other_ref
  28.9 0.7 %shard_map.58 = f32[64,512]{1,0:T(8,128)} custom-call(f32[64,512]{1,0:T(8,128)S(1)} %get-tuple-element.25.keep_ref, f32[64,512]{1,0:T(8,128)S(1)} %collective-permute-done.5.other_ref), custom_call_target="tpu_custom_call" | custom-call | flops 65536 | bytes 524288 | tf_op jit(solution)/shard_map/pallas_call | solution.py:315
  29.5 3.8 %all-to-all-start = ((f32[4,16,512]{2,1,0:T(8,128)}), f32[4,16,512]{2,1,0:T(8,128)S(1)}, u32[]{:S(2)}, u32[]{:S(2)}) async-start(f32[4,16,512]{2,1,0:T(8,128)} %bitcast), calls=%async_computation | async-start | bytes 262144 | tf_op jit(solution)/shard_map/all_to_all | solution.py:407
  33.4 0.0 collective-permute-done.7.refs_2_
  33.4 0.0 collective-permute-done.6.refs_1_
  33.4 1.7 %shard_map.59 = bf16[16,2,64,256]{3,2,1,0:T(8,128)(2,1)} custom-call(bf16[16,64,256]{2,1,0:T(8,128)(2,1)S(1)} %shard_map.57.even_ref, bf16[144,256]{1,0:T(8,128)(2,1)S(1)} %get-tuple-element.30.taps_ref, bf16[32,4096]{1,0:T(8,128)(2,1)S(1)} %shard_map.53.refs_0_, bf16[64,4096]{1,0:T(8,128)(2,1)S(1)} %collective-permute-done.6.refs_1_, ...), custom_call_target="tpu_custom_call" | custom-call | flops 301989888 | bytes 4194304 | tf_op jit(solution)/shard_map/pallas_call | solution.py:315
  35.0 3.3 %all-to-all-done = f32[4,16,512]{2,1,0:T(8,128)S(1)} async-done(((f32[4,16,512]{2,1,0:T(8,128)}), f32[4,16,512]{2,1,0:T(8,128)S(1)}, u32[]{:S(2)}, u32[]{:S(2)}) %all-to-all-start) | async-done | bytes 131104 | tf_op jit(solution)/shard_map/all_to_all | solution.py:407
  38.4 0.8 %shard_map.60 = f32[16,16,27]{2,1,0:T(8,128)} custom-call(f32[4,16,512]{2,1,0:T(8,128)S(1)} %all-to-all-done), custom_call_target="tpu_custom_call" | custom-call | flops 65536 | bytes 524288 | tf_op jit(solution)/shard_map/pallas_call | solution.py:315
  (1 shorter events, 0.0 us)
Async XLA Ops:
  0.6 9.2 %copy-start = (bf16[27,64,128]{2,1,0:T(8,128)(2,1)S(1)}, bf16[27,64,128]{2,1,0:T(8,128)(2,1)}, u32[]{:S(2)}) copy-start(bf16[27,64,128]{2,1,0:T(8,128)(2,1)} %param.5) | copy-start | bytes 1327108
  0.6 18.9 %collective-permute-start.2 = (bf16[16,2,64,256]{3,2,1,0:T(8,128)(2,1)}, bf16[16,2,64,256]{3,2,1,0:T(8,128)(2,1)S(1)}, u32[]{:S(2)}, u32[]{:S(2)}) collective-permute-start(bf16[16,2,64,256]{3,2,1,0:T(8,128)(2,1)} %refs_0_.2), channel_id=1, source_target_pairs={{0,4},{4,8},{8,12},{12,16},{16,20},{20,24},{24,28},{28,0},{1,5},{5... | collective-permute-start | bytes 3145736 | tf_op jit(solution)/shard_map/ppermute | solution.py:361
  1.1 15.9 %collective-permute-start.1 = (bf16[32,1,32,128]{3,2,1,0:T(8,128)(2,1)}, bf16[32,1,32,128]{3,2,1,0:T(8,128)(2,1)S(1)}, u32[]{:S(2)}, u32[]{:S(2)}) collective-permute-start(bf16[32,1,32,128]{3,2,1,0:T(8,128)(2,1)} %refs_0_.3), channel_id=1, source_target_pairs={{0,2},{1,3},{2,0},{3,1},{4,6},{5,7},{6,4},{7,5},{8,10},{9,11},{10,... | collective-permute-start | bytes 786440 | tf_op jit(solution)/shard_map/ppermute | solution.py:353
  4.8 14.0 %collective-permute-start.3 = (bf16[32,1,32,128]{3,2,1,0:T(8,128)(2,1)}, bf16[32,1,32,128]{3,2,1,0:T(8,128)(2,1)S(1)}, u32[]{:S(2)}, u32[]{:S(2)}) collective-permute-start(bf16[32,1,32,128]{3,2,1,0:T(8,128)(2,1)} %refs_0_.3), channel_id=1, source_target_pairs={{4,0},{8,4},{12,8},{16,12},{20,16},{24,20},{28,24},{0,28},{5,1},{9... | collective-permute-start | bytes 786440 | tf_op jit(solution)/shard_map/ppermute | solution.py:362
  7.1 12.5 %collective-permute-start = (bf16[32,1,32,128]{3,2,1,0:T(8,128)(2,1)}, bf16[32,1,32,128]{3,2,1,0:T(8,128)(2,1)S(1)}, u32[]{:S(2)}, u32[]{:S(2)}) collective-permute-start(bf16[32,1,32,128]{3,2,1,0:T(8,128)(2,1)} %refs_0_.3), channel_id=1, source_target_pairs={{0,1},{1,0},{2,3},{3,2},{4,5},{5,4},{6,7},{7,6},{8,9},{9,8},{10,11... | collective-permute-start | bytes 786440 | tf_op jit(solution)/shard_map/ppermute | solution.py:353
  8.7 1.0 %copy-start.1 = (bf16[32,1,32,128]{3,2,1,0:T(8,128)(2,1)S(1)}, bf16[32,1,32,128]{3,2,1,0:T(8,128)(2,1)}, u32[]{:S(2)}) copy-start(bf16[32,1,32,128]{3,2,1,0:T(8,128)(2,1)} %refs_0_.3) | copy-start | bytes 786436
  9.8 1.2 %copy-start.2 = (bf16[16,2,64,256]{3,2,1,0:T(8,128)(2,1)S(1)}, bf16[16,2,64,256]{3,2,1,0:T(8,128)(2,1)}, u32[]{:S(2)}) copy-start(bf16[16,2,64,256]{3,2,1,0:T(8,128)(2,1)} %refs_0_.2) | copy-start | bytes 3145732
  17.0 9.1 %collective-permute-start.4 = (bf16[32,1,32,128]{3,2,1,0:T(8,128)(2,1)S(1)}, bf16[32,1,32,128]{3,2,1,0:T(8,128)(2,1)S(1)}, u32[]{:S(2)}, u32[]{:S(2)}) collective-permute-start(bf16[32,1,32,128]{3,2,1,0:T(8,128)(2,1)S(1)} %collective-permute-done.1.refs_1_), channel_id=1, source_target_pairs={{0,1},{1,0},{2,3},{3,2},{4,5},{5,4},{6,7},{7,6},{8,9},{9,8},{10,11... | collective-permute-start | bytes 786440 | tf_op jit(solution)/shard_map/ppermute | solution.py:353
  19.9 13.5 %collective-permute-start.6 = (bf16[64,4096]{1,0:T(8,128)(2,1)S(1)}, bf16[64,4096]{1,0:T(8,128)(2,1)S(1)}, u32[]{:S(2)}, u32[]{:S(2)}) collective-permute-start(bf16[64,4096]{1,0:T(8,128)(2,1)S(1)} %shard_map.54.refs_3_.refs_1_.refs_4_), channel_id=1, source_target_pairs={{4,0},{8,4},{12,8},{16,12},{20,16},{24,20},{28,24},{0,28},{5,1},{9... | collective-permute-start | bytes 1572872 | tf_op jit(solution)/shard_map/ppermute | solution.py:375
  26.3 7.1 %collective-permute-start.7 = (bf16[32,4096]{1,0:T(8,128)(2,1)S(1)}, bf16[32,4096]{1,0:T(8,128)(2,1)S(1)}, u32[]{:S(2)}, u32[]{:S(2)}) collective-permute-start(bf16[32,4096]{1,0:T(8,128)(2,1)S(1)} %shard_map.55.refs_4_.refs_2_.refs_5_), channel_id=1, source_target_pairs={{4,0},{8,4},{12,8},{16,12},{20,16},{24,20},{28,24},{0,28},{5,1},{9... | collective-permute-start | bytes 786440 | tf_op jit(solution)/shard_map/ppermute | solution.py:375
  27.5 1.4 %collective-permute-start.5 = (f32[64,512]{1,0:T(8,128)S(1)}, f32[64,512]{1,0:T(8,128)S(1)}, u32[]{:S(2)}, u32[]{:S(2)}) collective-permute-start(f32[64,512]{1,0:T(8,128)S(1)} %get-tuple-element.26), channel_id=1, source_target_pairs={{0,4},{4,0},{8,12},{12,8},{16,20},{20,16},{24,28},{28,24},{1,5},{5... | collective-permute-start | bytes 393224 | tf_op jit(solution)/shard_map/ppermute | solution.py:395
  29.5 8.8 %all-to-all-start = ((f32[4,16,512]{2,1,0:T(8,128)}), f32[4,16,512]{2,1,0:T(8,128)S(1)}, u32[]{:S(2)}, u32[]{:S(2)}) async-start(f32[4,16,512]{2,1,0:T(8,128)} %bitcast), calls=%async_computation | async-start | bytes 262144 | tf_op jit(solution)/shard_map/all_to_all | solution.py:407

commit v13 on v11

--- a/solution.py
+++ b/solution.py
@@ -140,7 +140,7 @@
             for e in range(3):
                 lo = (9 * a + 3 * b + e) * pitch
                 terms_ref[lo : lo + chans, :] = block[e * chans : (e + 1) * chans]
-    terms_ref[27 * pitch :, :] = jnp.zeros((5 * pitch, channels), F32)
+    terms_ref[27 * pitch :, :] = jnp.zeros((6 * pitch, channels), F32)
     for c in range(chans):
         placed_ref[32 * c : 32 * c + 32, :] = terms_ref[pl.ds(c, 32, stride=pitch), :]
     turned = placed_ref[...].T
@@ -360,7 +360,7 @@
         lines_kernel,
         jax.ShapeDtypeStruct((sum(part.shape[0] for part in parts), cells), BF16),
         *parts,
-        scratch=(pltpu.VMEM((own_outs * (rows + 8), cols), F32),),
+        scratch=(pltpu.VMEM(((own_outs + 1) * (rows + 8), cols), F32),),
         cost=(1 << 20, 2 << 20),
     )
     behind = lax.ppermute(volume, "depth", farther)
@@ -377,7 +377,7 @@
     )
     later_lines = [lines(*[got[mask] for mask in range(1, count - 1)]), lines(got[count - 1])]
     own_lines = [first_lines] + later_lines
-    next_lines = [next_first_lines] + [lax.ppermute(part, "depth", nearer) for part in later_lines]
+    next_lines = [next_first_lines] + [lax.ppermute(part, "depth", nearer) for part in later_lines[:-1]]
     outs = channels // depth
     half_terms = jax.ShapeDtypeStruct((channels // 2, 32 * chans), F32)
     keep, send = call(
@@ -387,37 +387,39 @@
         behind_views,
         *own_lines,
         scratch=(
-            pltpu.VMEM((32 * (chans + 8), channels), F32),
+            pltpu.VMEM((33 * (chans + 8), channels), F32),
             pltpu.VMEM((32 * chans, channels), F32),
         ),
         cost=(2 * 27 * chans * channels * cells, 8 << 20),
     )
     cells_scratch = (
         pltpu.VMEM((9 * chans, cells + cols), F32),
-        pltpu.VMEM((2, 256 // chans * (chans + 8), cols), F32),
+        pltpu.VMEM((2, (256 // chans + 1) * (chans + 8), cols), F32),
     )
     plane = jax.ShapeDtypeStruct((chans, 2 * rows, 2 * cols), BF16)
+    last_lines, send = lax.optimization_barrier((later_lines[-1], send))
+    next_lines.append(lax.ppermute(last_lines, "depth", nearer))
     other = lax.ppermute(send, "depth", [(i, i ^ 1) for i in range(depth)])
+    own_terms, *terms = call(
+        pair_kernel,
+        [jax.ShapeDtypeStruct((outs, 32 * chans), F32)] * (depth // 2),
+        keep,
+        other,
+        cost=(1 << 16, 1 << 19),
+    )
+    terms = [
+        lax.ppermute(terms[k - 1], "depth", [(i, i ^ (2 * k)) for i in range(depth)])
+        for k in range(depth // 2 - 1, 0, -1)
+    ]
+    even_taps, own_terms = lax.optimization_barrier((even_taps, own_terms))
     even_grad = call(
         even_kernel,
         plane,
         even_taps,
         *own_lines,
         scratch=cells_scratch,
-        cost=(2 * 9 * chans * channels * cells, 4 << 20),
-    )
-    other, even_grad = lax.optimization_barrier((other, even_grad))
-    own_terms, *terms = call(
-        pair_kernel,
-        [jax.ShapeDtypeStruct((outs, 32 * chans), F32)] * (depth // 2),
-        keep,
-        other,
-        cost=(1 << 16, 1 << 19),
-    )
-    terms = [
-        lax.ppermute(terms[k - 1], "depth", [(i, i ^ (2 * k)) for i in range(depth)])
-        for k in range(depth // 2 - 1, 0, -1)
-    ]
+        cost=(24 * 9 * chans * channels * cells, 4 << 20),
+    )
     input_grad = call(
         odd_kernel,
         jax.ShapeDtypeStruct(volume.shape, BF16),

time: 37.3 us -> 37.4 us (level)
  starting transfers between devices: 15.6 us -> 17.1 us
  local copies, waits for them, and re-layouts: 2.24 us -> 1.25 us
  waiting for transfers between devices: 12.6 us -> 12.2 us
    ppermute x0 -> x1, starting transfers between devices: none -> 1.87 us  [shards(): next_lines.append(lax.ppermute(last_lines, 'depth', nearer))]
    ppermute x3, waiting for transfers between devices: 2.21 us -> 0.93 us  [shards(): lax.ppermute(terms[k - 1], 'depth', [(i, i ^ 2 * k) for i in range(depth)])]
    ppermute x3, waiting for transfers between devices: 9.81 us -> 10.8 us  [shards(): lax.ppermute(got[mask - low], 'chan', [(i, i ^ low) for i in range(count)])]
    unnamed x6, local copies, waits for them, and re-layouts: 2.21 us -> 1.23 us
    ppermute x2 -> x1, starting transfers between devices: 1.74 us -> 1.7 us  [shards(): lax.ppermute(part, 'depth', nearer)]
where the time goes in v13:
time: 37.4 us; the launch traced here: 37.3 us
  starting transfers between devices  17.1 us (46%)
  waiting for transfers between devices  12.2 us (33%)
  Pallas kernels  5.94 us (16%)
  local copies, waits for them, and re-layouts  1.25 us (3%)
  between operations  0.74 us (2%)
    ppermute x3, waiting for transfers between devices, shards(): lax.ppermute(got[mask - low], 'chan', [(i, i ^ low) for i in range(count)])  10.8 us
    ppermute x3, starting transfers between devices, shards(): lax.ppermute(got[mask - low], 'chan', [(i, i ^ low) for i in range(count)])  7.07 us
    pallas_call x11, Pallas kernels, call(): pl.pallas_call(kernel, out_shape=out_shape, in_specs=[VMEM] * len(args),...  5.94 us
    ppermute x3, starting transfers between devices, shards(): lax.ppermute(terms[k - 1], 'depth', [(i, i ^ 2 * k) for i in range(depth)])  3.55 us
    ppermute x1, starting transfers between devices, shards(): next_own = lax.ppermute(grad_out, 'depth', nearer)  2.28 us
    ppermute x1, starting transfers between devices, shards(): next_lines.append(lax.ppermute(last_lines, 'depth', nearer))  1.87 us
    ppermute x1, starting transfers between devices, shards(): lax.ppermute(part, 'depth', nearer)  1.7 us
    unnamed x6, local copies, waits for them, and re-layouts  1.23 us
  transfers between devices with their start and end apart: 11, of which 5 were waited for; matrix products, arithmetic and copies ran while one was open for 0% of the time, Pallas kernels for 14%

profile of v13, /device:TPU:0, one launch (start us, length us, event | category | flops | bytes accessed | tf_op | source)
XLA Modules:
  0.0 37.3 jit_solution(16172460926957458211)
XLA Ops:
  0.6 0.0 copy-start
  0.6 0.0 copy-start.1
  0.7 0.5 %collective-permute-start.2 = (bf16[16,2,64,256]{3,2,1,0:T(8,128)(2,1)}, bf16[16,2,64,256]{3,2,1,0:T(8,128)(2,1)S(1)}, u32[]{:S(2)}, u32[]{:S(2)}) collective-permute-start(bf16[16,2,64,256]{3,2,1,0:T(8,128)(2,1)} %refs_0_.2), channel_id=1, source_target_pairs={{0,4},{4,8},{8,12},{12,16},{16,20},{20,24},{24,28},{28,0},{1,5},{5... | collective-permute-start | bytes 3145736 | tf_op jit(solution)/shard_map/ppermute | solution.py:366
  1.2 3.7 %collective-permute-start.1 = (bf16[32,1,32,128]{3,2,1,0:T(8,128)(2,1)}, bf16[32,1,32,128]{3,2,1,0:T(8,128)(2,1)S(1)}, u32[]{:S(2)}, u32[]{:S(2)}) collective-permute-start(bf16[32,1,32,128]{3,2,1,0:T(8,128)(2,1)} %refs_0_.3), channel_id=1, source_target_pairs={{0,2},{1,3},{2,0},{3,1},{4,6},{5,7},{6,4},{7,5},{8,10},{9,11},{10,... | collective-permute-start | bytes 786440 | tf_op jit(solution)/shard_map/ppermute | solution.py:358
  4.8 2.3 %collective-permute-start.3 = (bf16[32,1,32,128]{3,2,1,0:T(8,128)(2,1)}, bf16[32,1,32,128]{3,2,1,0:T(8,128)(2,1)S(1)}, u32[]{:S(2)}, u32[]{:S(2)}) collective-permute-start(bf16[32,1,32,128]{3,2,1,0:T(8,128)(2,1)} %refs_0_.3), channel_id=1, source_target_pairs={{4,0},{8,4},{12,8},{16,12},{20,16},{24,20},{28,24},{0,28},{5,1},{9... | collective-permute-start | bytes 786440 | tf_op jit(solution)/shard_map/ppermute | solution.py:367
  7.1 1.6 %collective-permute-start = (bf16[32,1,32,128]{3,2,1,0:T(8,128)(2,1)}, bf16[32,1,32,128]{3,2,1,0:T(8,128)(2,1)S(1)}, u32[]{:S(2)}, u32[]{:S(2)}) collective-permute-start(bf16[32,1,32,128]{3,2,1,0:T(8,128)(2,1)} %refs_0_.3), channel_id=1, source_target_pairs={{0,1},{1,0},{2,3},{3,2},{4,5},{5,4},{6,7},{7,6},{8,9},{9,8},{10,11... | collective-permute-start | bytes 786440 | tf_op jit(solution)/shard_map/ppermute | solution.py:358
  8.7 0.0 copy-done
  8.7 0.0 copy-start.2
  8.7 1.2 %copy-done.2 = bf16[16,2,64,256]{3,2,1,0:T(8,128)(2,1)S(1)} copy-done((bf16[16,2,64,256]{3,2,1,0:T(8,128)(2,1)S(1)}, bf16[16,2,64,256]{3,2,1,0:T(8,128)(2,1)}, u32[]{:S(2)}) %copy-start.2) | copy-done | bytes 1048600
  9.9 0.9 %shard_map.50 = (bf16[192,4096]{1,0:T(8,128)(2,1)S(1)}, bf16[144,128]{1,0:T(8,128)(2,1)S(1)}, bf16[144,256]{1,0:T(8,128)(2,1)S(1)}) custom-call(bf16[16,2,64,256]{3,2,1,0:T(8,128)(2,1)S(1)} %copy-done.2, bf16[27,16,128]{2,1,0:T(8,128)(2,1)S(1)} %constant_dynamic-slice_fusion.refs_1_), custom_call_target="tpu_custom_call" | custom-call | flops 536870912 | bytes 4194304 | tf_op jit(solution)/shard_map/pallas_call | solution.py:320
  10.8 6.2 %collective-permute-done.1.refs_1_ = bf16[32,1,32,128]{3,2,1,0:T(8,128)(2,1)S(1)} collective-permute-done((bf16[32,1,32,128]{3,2,1,0:T(8,128)(2,1)}, bf16[32,1,32,128]{3,2,1,0:T(8,128)(2,1)S(1)}, u32[]{:S(2)}, u32[]{:S(2)}) %collective-permute-start.1) | collective-permute-done | bytes 262176 | tf_op jit(solution)/shard_map/ppermute | solution.py:358
  17.0 1.8 %collective-permute-start.4 = (bf16[32,1,32,128]{3,2,1,0:T(8,128)(2,1)S(1)}, bf16[32,1,32,128]{3,2,1,0:T(8,128)(2,1)S(1)}, u32[]{:S(2)}, u32[]{:S(2)}) collective-permute-start(bf16[32,1,32,128]{3,2,1,0:T(8,128)(2,1)S(1)} %collective-permute-done.1.refs_1_), channel_id=1, source_target_pairs={{0,1},{1,0},{2,3},{3,2},{4,5},{5,4},{6,7},{7,6},{8,9},{9,8},{10,11... | collective-permute-start | bytes 786440 | tf_op jit(solution)/shard_map/ppermute | solution.py:358
  18.9 0.0 copy-done.1
  18.9 0.1 shard_map.52.refs_2_.refs_0_.refs_3_
  19.0 0.0 collective-permute-done.3.refs_0_
  19.0 0.1 shard_map.53.refs_0_
  19.2 0.4 %collective-permute-done.2.behind_ref = bf16[16,2,64,256]{3,2,1,0:T(8,128)(2,1)S(1)} collective-permute-done((bf16[16,2,64,256]{3,2,1,0:T(8,128)(2,1)}, bf16[16,2,64,256]{3,2,1,0:T(8,128)(2,1)S(1)}, u32[]{:S(2)}, u32[]{:S(2)}) %collective-permute-start.2) | collective-permute-done | bytes 1048608 | tf_op jit(solution)/shard_map/ppermute | solution.py:366
  19.5 0.1 shard_map.51.refs_1_
  19.6 0.0 collective-permute-done.refs_0_
  19.6 0.3 shard_map.54.refs_3_.refs_1_.refs_4_
  19.9 1.7 %collective-permute-start.6 = (bf16[64,4096]{1,0:T(8,128)(2,1)S(1)}, bf16[64,4096]{1,0:T(8,128)(2,1)S(1)}, u32[]{:S(2)}, u32[]{:S(2)}) collective-permute-start(bf16[64,4096]{1,0:T(8,128)(2,1)S(1)} %shard_map.54.refs_3_.refs_1_.refs_4_), channel_id=1, source_target_pairs={{4,0},{8,4},{12,8},{16,12},{20,16},{24,20},{28,24},{0,28},{5,1},{9... | collective-permute-start | bytes 1572872 | tf_op jit(solution)/shard_map/ppermute | solution.py:380
  21.6 4.6 %collective-permute-done.4.refs_0_ = bf16[32,1,32,128]{3,2,1,0:T(8,128)(2,1)S(1)} collective-permute-done((bf16[32,1,32,128]{3,2,1,0:T(8,128)(2,1)S(1)}, bf16[32,1,32,128]{3,2,1,0:T(8,128)(2,1)S(1)}, u32[]{:S(2)}, u32[]{:S(2)}) %collective-permute-start.4) | collective-permute-done | bytes 262176 | tf_op jit(solution)/shard_map/ppermute | solution.py:358
  26.2 0.1 shard_map.55.refs_4_.refs_2_.refs_5_
  26.3 0.9 %shard_map.56 = (f32[64,512]{1,0:T(8,128)S(1)}, f32[64,512]{1,0:T(8,128)S(1)}) custom-call(bf16[192,4096]{1,0:T(8,128)(2,1)S(1)} %get-tuple-element.27.refs_0_, bf16[96,4096]{1,0:T(8,128)(2,1)S(1)} %shard_map.51.refs_1_, bf16[32,4096]{1,0:T(8,128)(2,1)S(1)} %shard_map.52.refs_2_.refs_0_.refs_3_, bf16[64,4096]{1,0:T(8,128)(2,1)S(1)} %shard_map.54.refs_3_.refs_1_.refs_4_, ...), custom_call_target="tpu_custom_call" | custom-call | flops 452984832 | bytes 8388608 | tf_op jit(solution)/shard_map/pallas_call | solution.py:320
  27.3 0.1 collective-permute-start.5
  27.4 1.9 %collective-permute-start.7 = (bf16[32,4096]{1,0:T(8,128)(2,1)S(1)}, bf16[32,4096]{1,0:T(8,128)(2,1)S(1)}, u32[]{:S(2)}, u32[]{:S(2)}) collective-permute-start(bf16[32,4096]{1,0:T(8,128)(2,1)S(1)} %shard_map.55.refs_4_.refs_2_.refs_5_), channel_id=1, source_target_pairs={{4,0},{8,4},{12,8},{16,12},{20,16},{24,20},{28,24},{0,28},{5,1},{9... | collective-permute-start | bytes 786440 | tf_op jit(solution)/shard_map/ppermute | solution.py:401
  29.3 0.0 collective-permute-done.5.other_ref
  29.3 1.1 %collective-permute-start.10 = (f32[16,512]{1,0:T(8,128)S(1)}, f32[16,512]{1,0:T(8,128)S(1)}, u32[]{:S(2)}, u32[]{:S(2)}) collective-permute-start(f32[16,512]{1,0:T(8,128)S(1)} %get-tuple-element.45), channel_id=1, source_target_pairs={{0,8},{4,12},{8,0},{12,4},{16,24},{20,28},{24,16},{28,20},{1,9},{5... | collective-permute-start | bytes 98312 | tf_op jit(solution)/shard_map/ppermute | solution.py:411
  30.4 1.7 %collective-permute-start.8 = (f32[16,512]{1,0:T(8,128)S(1)}, f32[16,512]{1,0:T(8,128)S(1)}, u32[]{:S(2)}, u32[]{:S(2)}) collective-permute-start(f32[16,512]{1,0:T(8,128)S(1)} %get-tuple-element.43), channel_id=1, source_target_pairs={{0,24},{4,28},{8,16},{12,20},{16,8},{20,12},{24,0},{28,4},{1,25},{... | collective-permute-start | bytes 98312 | tf_op jit(solution)/shard_map/ppermute | solution.py:411
  32.1 0.8 %collective-permute-start.9 = (f32[16,512]{1,0:T(8,128)S(1)}, f32[16,512]{1,0:T(8,128)S(1)}, u32[]{:S(2)}, u32[]{:S(2)}) collective-permute-start(f32[16,512]{1,0:T(8,128)S(1)} %get-tuple-element.44), channel_id=1, source_target_pairs={{0,16},{4,20},{8,24},{12,28},{16,0},{20,4},{24,8},{28,12},{1,17},{... | collective-permute-start | bytes 98312 | tf_op jit(solution)/shard_map/ppermute | solution.py:411
  32.9 0.9 %shard_map.58.even_ref = bf16[16,64,256]{2,1,0:T(8,128)(2,1)S(1)} custom-call(bf16[144,128]{1,0:T(8,128)(2,1)S(1)} %get-tuple-element.37.taps_ref, bf16[32,4096]{1,0:T(8,128)(2,1)S(1)} %shard_map.52.refs_2_.refs_0_.refs_3_, bf16[64,4096]{1,0:T(8,128)(2,1)S(1)} %shard_map.54.refs_3_.refs_1_.refs_4_, bf16[32,4096]{1,0:T(8,128)(2,1)S(1)} %shard_map.55.refs_4_.refs_2_.refs_5_), custom_call_target="tpu_custom_call" | custom-call | flops 1811939328 | bytes 4194304 | tf_op jit(solution)/shard_map/pallas_call | solution.py:320
  33.8 0.1 collective-permute-done.7.refs_2_
  33.9 0.0 collective-permute-done.6.refs_1_
  33.9 1.7 %shard_map.59 = bf16[16,2,64,256]{3,2,1,0:T(8,128)(2,1)} custom-call(bf16[16,64,256]{2,1,0:T(8,128)(2,1)S(1)} %shard_map.58.even_ref, bf16[144,256]{1,0:T(8,128)(2,1)S(1)} %get-tuple-element.38.taps_ref, bf16[32,4096]{1,0:T(8,128)(2,1)S(1)} %shard_map.53.refs_0_, bf16[64,4096]{1,0:T(8,128)(2,1)S(1)} %collective-permute-done.6.refs_1_, ...), custom_call_target="tpu_custom_call" | custom-call | flops 301989888 | bytes 4194304 | tf_op jit(solution)/shard_map/pallas_call | solution.py:320
  35.6 0.0 collective-permute-done.10.refs_3_
  35.6 0.9 %collective-permute-done.8.refs_1_ = f32[16,512]{1,0:T(8,128)S(1)} collective-permute-done((f32[16,512]{1,0:T(8,128)S(1)}, f32[16,512]{1,0:T(8,128)S(1)}, u32[]{:S(2)}, u32[]{:S(2)}) %collective-permute-start.8) | collective-permute-done | bytes 32800 | tf_op jit(solution)/shard_map/ppermute | solution.py:411
  36.5 0.0 collective-permute-done.9.refs_2_
  36.5 0.8 %shard_map.60 = f32[16,16,27]{2,1,0:T(8,128)} custom-call(f32[16,512]{1,0:T(8,128)S(1)} %get-tuple-element.42.refs_0_, f32[16,512]{1,0:T(8,128)S(1)} %collective-permute-done.8.refs_1_, f32[16,512]{1,0:T(8,128)S(1)} %collective-permute-done.9.refs_2_, f32[16,512]{1,0:T(8,128)S(1)} %collective-permute-done.10.refs_3_), custom_call_target="tpu_custom_call" | custom-call | flops 65536 | bytes 524288 | tf_op jit(solution)/shard_map/pallas_call | solution.py:320
  (2 shorter events, 0.0 us)
Async XLA Ops:
  0.6 8.1 %copy-start = (bf16[27,64,128]{2,1,0:T(8,128)(2,1)S(1)}, bf16[27,64,128]{2,1,0:T(8,128)(2,1)}, u32[]{:S(2)}) copy-start(bf16[27,64,128]{2,1,0:T(8,128)(2,1)} %param.5) | copy-start | bytes 1327108
  0.6 18.2 %copy-start.1 = (bf16[32,1,32,128]{3,2,1,0:T(8,128)(2,1)S(1)}, bf16[32,1,32,128]{3,2,1,0:T(8,128)(2,1)}, u32[]{:S(2)}) copy-start(bf16[32,1,32,128]{3,2,1,0:T(8,128)(2,1)} %refs_0_.3) | copy-start | bytes 786436
  0.7 18.9 %collective-permute-start.2 = (bf16[16,2,64,256]{3,2,1,0:T(8,128)(2,1)}, bf16[16,2,64,256]{3,2,1,0:T(8,128)(2,1)S(1)}, u32[]{:S(2)}, u32[]{:S(2)}) collective-permute-start(bf16[16,2,64,256]{3,2,1,0:T(8,128)(2,1)} %refs_0_.2), channel_id=1, source_target_pairs={{0,4},{4,8},{8,12},{12,16},{16,20},{20,24},{24,28},{28,0},{1,5},{5... | collective-permute-start | bytes 3145736 | tf_op jit(solution)/shard_map/ppermute | solution.py:366
  1.2 15.9 %collective-permute-start.1 = (bf16[32,1,32,128]{3,2,1,0:T(8,128)(2,1)}, bf16[32,1,32,128]{3,2,1,0:T(8,128)(2,1)S(1)}, u32[]{:S(2)}, u32[]{:S(2)}) collective-permute-start(bf16[32,1,32,128]{3,2,1,0:T(8,128)(2,1)} %refs_0_.3), channel_id=1, source_target_pairs={{0,2},{1,3},{2,0},{3,1},{4,6},{5,7},{6,4},{7,5},{8,10},{9,11},{10,... | collective-permute-start | bytes 786440 | tf_op jit(solution)/shard_map/ppermute | solution.py:358
  4.8 14.2 %collective-permute-start.3 = (bf16[32,1,32,128]{3,2,1,0:T(8,128)(2,1)}, bf16[32,1,32,128]{3,2,1,0:T(8,128)(2,1)S(1)}, u32[]{:S(2)}, u32[]{:S(2)}) collective-permute-start(bf16[32,1,32,128]{3,2,1,0:T(8,128)(2,1)} %refs_0_.3), channel_id=1, source_target_pairs={{4,0},{8,4},{12,8},{16,12},{20,16},{24,20},{28,24},{0,28},{5,1},{9... | collective-permute-start | bytes 786440 | tf_op jit(solution)/shard_map/ppermute | solution.py:367
  7.1 12.5 %collective-permute-start = (bf16[32,1,32,128]{3,2,1,0:T(8,128)(2,1)}, bf16[32,1,32,128]{3,2,1,0:T(8,128)(2,1)S(1)}, u32[]{:S(2)}, u32[]{:S(2)}) collective-permute-start(bf16[32,1,32,128]{3,2,1,0:T(8,128)(2,1)} %refs_0_.3), channel_id=1, source_target_pairs={{0,1},{1,0},{2,3},{3,2},{4,5},{5,4},{6,7},{7,6},{8,9},{9,8},{10,11... | collective-permute-start | bytes 786440 | tf_op jit(solution)/shard_map/ppermute | solution.py:358
  8.7 1.2 %copy-start.2 = (bf16[16,2,64,256]{3,2,1,0:T(8,128)(2,1)S(1)}, bf16[16,2,64,256]{3,2,1,0:T(8,128)(2,1)}, u32[]{:S(2)}) copy-start(bf16[16,2,64,256]{3,2,1,0:T(8,128)(2,1)} %refs_0_.2) | copy-start | bytes 3145732
  17.0 9.1 %collective-permute-start.4 = (bf16[32,1,32,128]{3,2,1,0:T(8,128)(2,1)S(1)}, bf16[32,1,32,128]{3,2,1,0:T(8,128)(2,1)S(1)}, u32[]{:S(2)}, u32[]{:S(2)}) collective-permute-start(bf16[32,1,32,128]{3,2,1,0:T(8,128)(2,1)S(1)} %collective-permute-done.1.refs_1_), channel_id=1, source_target_pairs={{0,1},{1,0},{2,3},{3,2},{4,5},{5,4},{6,7},{7,6},{8,9},{9,8},{10,11... | collective-permute-start | bytes 786440 | tf_op jit(solution)/shard_map/ppermute | solution.py:358
  19.9 14.0 %collective-permute-start.6 = (bf16[64,4096]{1,0:T(8,128)(2,1)S(1)}, bf16[64,4096]{1,0:T(8,128)(2,1)S(1)}, u32[]{:S(2)}, u32[]{:S(2)}) collective-permute-start(bf16[64,4096]{1,0:T(8,128)(2,1)S(1)} %shard_map.54.refs_3_.refs_1_.refs_4_), channel_id=1, source_target_pairs={{4,0},{8,4},{12,8},{16,12},{20,16},{24,20},{28,24},{0,28},{5,1},{9... | collective-permute-start | bytes 1572872 | tf_op jit(solution)/shard_map/ppermute | solution.py:380
  27.3 2.0 %collective-permute-start.5 = (f32[64,512]{1,0:T(8,128)S(1)}, f32[64,512]{1,0:T(8,128)S(1)}, u32[]{:S(2)}, u32[]{:S(2)}) collective-permute-start(f32[64,512]{1,0:T(8,128)S(1)} %get-tuple-element.34), channel_id=1, source_target_pairs={{0,4},{4,0},{8,12},{12,8},{16,20},{20,16},{24,28},{28,24},{1,5},{5... | collective-permute-start | bytes 393224 | tf_op jit(solution)/shard_map/ppermute | solution.py:402
  27.4 6.5 %collective-permute-start.7 = (bf16[32,4096]{1,0:T(8,128)(2,1)S(1)}, bf16[32,4096]{1,0:T(8,128)(2,1)S(1)}, u32[]{:S(2)}, u32[]{:S(2)}) collective-permute-start(bf16[32,4096]{1,0:T(8,128)(2,1)S(1)} %shard_map.55.refs_4_.refs_2_.refs_5_), channel_id=1, source_target_pairs={{4,0},{8,4},{12,8},{16,12},{20,16},{24,20},{28,24},{0,28},{5,1},{9... | collective-permute-start | bytes 786440 | tf_op jit(solution)/shard_map/ppermute | solution.py:401
  29.3 6.3 %collective-permute-start.10 = (f32[16,512]{1,0:T(8,128)S(1)}, f32[16,512]{1,0:T(8,128)S(1)}, u32[]{:S(2)}, u32[]{:S(2)}) collective-permute-start(f32[16,512]{1,0:T(8,128)S(1)} %get-tuple-element.45), channel_id=1, source_target_pairs={{0,8},{4,12},{8,0},{12,4},{16,24},{20,28},{24,16},{28,20},{1,9},{5... | collective-permute-start | bytes 98312 | tf_op jit(solution)/shard_map/ppermute | solution.py:411
  30.4 6.2 %collective-permute-start.8 = (f32[16,512]{1,0:T(8,128)S(1)}, f32[16,512]{1,0:T(8,128)S(1)}, u32[]{:S(2)}, u32[]{:S(2)}) collective-permute-start(f32[16,512]{1,0:T(8,128)S(1)} %get-tuple-element.43), channel_id=1, source_target_pairs={{0,24},{4,28},{8,16},{12,20},{16,8},{20,12},{24,0},{28,4},{1,25},{... | collective-permute-start | bytes 98312 | tf_op jit(solution)/shard_map/ppermute | solution.py:411
  32.1 4.4 %collective-permute-start.9 = (f32[16,512]{1,0:T(8,128)S(1)}, f32[16,512]{1,0:T(8,128)S(1)}, u32[]{:S(2)}, u32[]{:S(2)}) collective-permute-start(f32[16,512]{1,0:T(8,128)S(1)} %get-tuple-element.44), channel_id=1, source_target_pairs={{0,16},{4,20},{8,24},{12,28},{16,0},{20,4},{24,8},{28,12},{1,17},{... | collective-permute-start | bytes 98312 | tf_op jit(solution)/shard_map/ppermute | solution.py:411

commit v14 on v11

--- a/solution.py
+++ b/solution.py
@@ -140,7 +140,7 @@
             for e in range(3):
                 lo = (9 * a + 3 * b + e) * pitch
                 terms_ref[lo : lo + chans, :] = block[e * chans : (e + 1) * chans]
-    terms_ref[27 * pitch :, :] = jnp.zeros((5 * pitch, channels), F32)
+    terms_ref[27 * pitch :, :] = jnp.zeros((6 * pitch, channels), F32)
     for c in range(chans):
         placed_ref[32 * c : 32 * c + 32, :] = terms_ref[pl.ds(c, 32, stride=pitch), :]
     turned = placed_ref[...].T
@@ -360,7 +360,7 @@
         lines_kernel,
         jax.ShapeDtypeStruct((sum(part.shape[0] for part in parts), cells), BF16),
         *parts,
-        scratch=(pltpu.VMEM((own_outs * (rows + 8), cols), F32),),
+        scratch=(pltpu.VMEM(((own_outs + 1) * (rows + 8), cols), F32),),
         cost=(1 << 20, 2 << 20),
     )
     behind = lax.ppermute(volume, "depth", farther)
@@ -381,20 +381,20 @@
     outs = channels // depth
     half_terms = jax.ShapeDtypeStruct((channels // 2, 32 * chans), F32)
     keep, send = call(
-        lambda *refs: weight_kernel(outs, cols, 4 * cols, *refs),
+        lambda *refs: weight_kernel(outs, cols, 8 * cols, *refs),
         (half_terms, half_terms),
         views,
         behind_views,
         *own_lines,
         scratch=(
-            pltpu.VMEM((32 * (chans + 8), channels), F32),
+            pltpu.VMEM((33 * (chans + 8), channels), F32),
             pltpu.VMEM((32 * chans, channels), F32),
         ),
         cost=(2 * 27 * chans * channels * cells, 8 << 20),
     )
     cells_scratch = (
         pltpu.VMEM((9 * chans, cells + cols), F32),
-        pltpu.VMEM((2, 256 // chans * (chans + 8), cols), F32),
+        pltpu.VMEM((2, (256 // chans + 1) * (chans + 8), cols), F32),
     )
     plane = jax.ShapeDtypeStruct((chans, 2 * rows, 2 * cols), BF16)
     other = lax.ppermute(send, "depth", [(i, i ^ 1) for i in range(depth)])

time: 37.3 us -> 37.3 us (level)
  no operation moved by 1% of the time
where the time goes in v14:
time: 37.3 us; the launch traced here: 37.1 us
  starting transfers between devices  15.6 us (42%)
  waiting for transfers between devices  12.6 us (34%)
  Pallas kernels  5.95 us (16%)
  local copies, waits for them, and re-layouts  2.24 us (6%)
  between operations  0.73 us (2%)
    ppermute x3, waiting for transfers between devices, shards(): lax.ppermute(got[mask - low], 'chan', [(i, i ^ low) for i in range(count)])  9.81 us
    ppermute x3, starting transfers between devices, shards(): lax.ppermute(got[mask - low], 'chan', [(i, i ^ low) for i in range(count)])  7.07 us
    pallas_call x11, Pallas kernels, call(): pl.pallas_call(kernel, out_shape=out_shape, in_specs=[VMEM] * len(args),...  5.95 us
    ppermute x3, starting transfers between devices, shards(): lax.ppermute(terms[k - 1], 'depth', [(i, i ^ 2 * k) for i in range(depth)])  3.57 us
    ppermute x1, starting transfers between devices, shards(): next_own = lax.ppermute(grad_out, 'depth', nearer)  2.28 us
    unnamed x6, local copies, waits for them, and re-layouts  2.21 us
    ppermute x3, waiting for transfers between devices, shards(): lax.ppermute(terms[k - 1], 'depth', [(i, i ^ 2 * k) for i in range(depth)])  2.2 us
    ppermute x2, starting transfers between devices, shards(): lax.ppermute(part, 'depth', nearer)  1.74 us
  transfers between devices with their start and end apart: 11, of which 5 were waited for; matrix products, arithmetic and copies ran while one was open for 0% of the time, Pallas kernels for 14%

profile of v14, /device:TPU:0, one launch (start us, length us, event | category | flops | bytes accessed | tf_op | source)
XLA Modules:
  0.0 37.1 jit_solution(14244191681765934762)
XLA Ops:
  0.6 0.0 copy-start
  0.6 0.5 %collective-permute-start.2 = (bf16[16,2,64,256]{3,2,1,0:T(8,128)(2,1)}, bf16[16,2,64,256]{3,2,1,0:T(8,128)(2,1)S(1)}, u32[]{:S(2)}, u32[]{:S(2)}) collective-permute-start(bf16[16,2,64,256]{3,2,1,0:T(8,128)(2,1)} %refs_0_.2), channel_id=1, source_target_pairs={{0,4},{4,8},{8,12},{12,16},{16,20},{20,24},{24,28},{28,0},{1,5},{5... | collective-permute-start | bytes 3145736 | tf_op jit(solution)/shard_map/ppermute | solution.py:366
  1.1 3.7 %collective-permute-start.1 = (bf16[32,1,32,128]{3,2,1,0:T(8,128)(2,1)}, bf16[32,1,32,128]{3,2,1,0:T(8,128)(2,1)S(1)}, u32[]{:S(2)}, u32[]{:S(2)}) collective-permute-start(bf16[32,1,32,128]{3,2,1,0:T(8,128)(2,1)} %refs_0_.3), channel_id=1, source_target_pairs={{0,2},{1,3},{2,0},{3,1},{4,6},{5,7},{6,4},{7,5},{8,10},{9,11},{10,... | collective-permute-start | bytes 786440 | tf_op jit(solution)/shard_map/ppermute | solution.py:358
  4.8 2.3 %collective-permute-start.3 = (bf16[32,1,32,128]{3,2,1,0:T(8,128)(2,1)}, bf16[32,1,32,128]{3,2,1,0:T(8,128)(2,1)S(1)}, u32[]{:S(2)}, u32[]{:S(2)}) collective-permute-start(bf16[32,1,32,128]{3,2,1,0:T(8,128)(2,1)} %refs_0_.3), channel_id=1, source_target_pairs={{4,0},{8,4},{12,8},{16,12},{20,16},{24,20},{28,24},{0,28},{5,1},{9... | collective-permute-start | bytes 786440 | tf_op jit(solution)/shard_map/ppermute | solution.py:367
  7.1 1.6 %collective-permute-start = (bf16[32,1,32,128]{3,2,1,0:T(8,128)(2,1)}, bf16[32,1,32,128]{3,2,1,0:T(8,128)(2,1)S(1)}, u32[]{:S(2)}, u32[]{:S(2)}) collective-permute-start(bf16[32,1,32,128]{3,2,1,0:T(8,128)(2,1)} %refs_0_.3), channel_id=1, source_target_pairs={{0,1},{1,0},{2,3},{3,2},{4,5},{5,4},{6,7},{7,6},{8,9},{9,8},{10,11... | collective-permute-start | bytes 786440 | tf_op jit(solution)/shard_map/ppermute | solution.py:358
  8.7 0.0 copy-start.1
  8.7 1.0 %copy-done.1 = bf16[32,1,32,128]{3,2,1,0:T(8,128)(2,1)S(1)} copy-done((bf16[32,1,32,128]{3,2,1,0:T(8,128)(2,1)S(1)}, bf16[32,1,32,128]{3,2,1,0:T(8,128)(2,1)}, u32[]{:S(2)}) %copy-start.1) | copy-done | bytes 262168
  9.7 0.1 shard_map.52.refs_2_.refs_0_.refs_3_
  9.8 0.0 copy-done
  9.8 0.0 copy-start.2
  9.9 1.2 %copy-done.2 = bf16[16,2,64,256]{3,2,1,0:T(8,128)(2,1)S(1)} copy-done((bf16[16,2,64,256]{3,2,1,0:T(8,128)(2,1)S(1)}, bf16[16,2,64,256]{3,2,1,0:T(8,128)(2,1)}, u32[]{:S(2)}) %copy-start.2) | copy-done | bytes 1048600
  11.1 0.9 %shard_map.50 = (bf16[192,4096]{1,0:T(8,128)(2,1)S(1)}, bf16[144,128]{1,0:T(8,128)(2,1)S(1)}, bf16[144,256]{1,0:T(8,128)(2,1)S(1)}) custom-call(bf16[16,2,64,256]{3,2,1,0:T(8,128)(2,1)S(1)} %copy-done.2, bf16[27,16,128]{2,1,0:T(8,128)(2,1)S(1)} %constant_dynamic-slice_fusion.refs_1_), custom_call_target="tpu_custom_call" | custom-call | flops 536870912 | bytes 4194304 | tf_op jit(solution)/shard_map/pallas_call | solution.py:320
  12.0 5.1 %collective-permute-done.1.refs_1_ = bf16[32,1,32,128]{3,2,1,0:T(8,128)(2,1)S(1)} collective-permute-done((bf16[32,1,32,128]{3,2,1,0:T(8,128)(2,1)}, bf16[32,1,32,128]{3,2,1,0:T(8,128)(2,1)S(1)}, u32[]{:S(2)}, u32[]{:S(2)}) %collective-permute-start.1) | collective-permute-done | bytes 262176 | tf_op jit(solution)/shard_map/ppermute | solution.py:358
  17.0 1.8 %collective-permute-start.4 = (bf16[32,1,32,128]{3,2,1,0:T(8,128)(2,1)S(1)}, bf16[32,1,32,128]{3,2,1,0:T(8,128)(2,1)S(1)}, u32[]{:S(2)}, u32[]{:S(2)}) collective-permute-start(bf16[32,1,32,128]{3,2,1,0:T(8,128)(2,1)S(1)} %collective-permute-done.1.refs_1_), channel_id=1, source_target_pairs={{0,1},{1,0},{2,3},{3,2},{4,5},{5,4},{6,7},{7,6},{8,9},{9,8},{10,11... | collective-permute-start | bytes 786440 | tf_op jit(solution)/shard_map/ppermute | solution.py:358
  18.9 0.0 collective-permute-done.3.refs_0_
  18.9 0.1 shard_map.53.refs_0_
  19.0 0.5 %collective-permute-done.2.behind_ref = bf16[16,2,64,256]{3,2,1,0:T(8,128)(2,1)S(1)} collective-permute-done((bf16[16,2,64,256]{3,2,1,0:T(8,128)(2,1)}, bf16[16,2,64,256]{3,2,1,0:T(8,128)(2,1)S(1)}, u32[]{:S(2)}, u32[]{:S(2)}) %collective-permute-start.2) | collective-permute-done | bytes 1048608 | tf_op jit(solution)/shard_map/ppermute | solution.py:366
  19.5 0.1 shard_map.51.refs_1_
  19.6 0.0 collective-permute-done.refs_0_
  19.6 0.3 shard_map.54.refs_3_.refs_1_.refs_4_
  19.9 1.5 %collective-permute-start.6 = (bf16[64,4096]{1,0:T(8,128)(2,1)S(1)}, bf16[64,4096]{1,0:T(8,128)(2,1)S(1)}, u32[]{:S(2)}, u32[]{:S(2)}) collective-permute-start(bf16[64,4096]{1,0:T(8,128)(2,1)S(1)} %shard_map.54.refs_3_.refs_1_.refs_4_), channel_id=1, source_target_pairs={{4,0},{8,4},{12,8},{16,12},{20,16},{24,20},{28,24},{0,28},{5,1},{9... | collective-permute-start | bytes 1572872 | tf_op jit(solution)/shard_map/ppermute | solution.py:380
  21.4 4.8 %collective-permute-done.4.refs_0_ = bf16[32,1,32,128]{3,2,1,0:T(8,128)(2,1)S(1)} collective-permute-done((bf16[32,1,32,128]{3,2,1,0:T(8,128)(2,1)S(1)}, bf16[32,1,32,128]{3,2,1,0:T(8,128)(2,1)S(1)}, u32[]{:S(2)}, u32[]{:S(2)}) %collective-permute-start.4) | collective-permute-done | bytes 262176 | tf_op jit(solution)/shard_map/ppermute | solution.py:358
  26.2 0.1 shard_map.55.refs_4_.refs_2_.refs_5_
  26.3 0.2 collective-permute-start.7
  26.5 0.9 %shard_map.56 = (f32[64,512]{1,0:T(8,128)S(1)}, f32[64,512]{1,0:T(8,128)S(1)}) custom-call(bf16[192,4096]{1,0:T(8,128)(2,1)S(1)} %get-tuple-element.24.refs_0_, bf16[96,4096]{1,0:T(8,128)(2,1)S(1)} %shard_map.51.refs_1_, bf16[32,4096]{1,0:T(8,128)(2,1)S(1)} %shard_map.52.refs_2_.refs_0_.refs_3_, bf16[64,4096]{1,0:T(8,128)(2,1)S(1)} %shard_map.54.refs_3_.refs_1_.refs_4_, ...), custom_call_target="tpu_custom_call" | custom-call | flops 452984832 | bytes 8388608 | tf_op jit(solution)/shard_map/pallas_call | solution.py:320
  27.5 0.4 %collective-permute-start.5 = (f32[64,512]{1,0:T(8,128)S(1)}, f32[64,512]{1,0:T(8,128)S(1)}, u32[]{:S(2)}, u32[]{:S(2)}) collective-permute-start(f32[64,512]{1,0:T(8,128)S(1)} %get-tuple-element.30), channel_id=1, source_target_pairs={{0,4},{4,0},{8,12},{12,8},{16,20},{20,16},{24,28},{28,24},{1,5},{5... | collective-permute-start | bytes 393224 | tf_op jit(solution)/shard_map/ppermute | solution.py:400
  27.9 0.9 %shard_map.57.even_ref = bf16[16,64,256]{2,1,0:T(8,128)(2,1)S(1)} custom-call(bf16[144,128]{1,0:T(8,128)(2,1)S(1)} %get-tuple-element.31.taps_ref, bf16[32,4096]{1,0:T(8,128)(2,1)S(1)} %shard_map.52.refs_2_.refs_0_.refs_3_, bf16[64,4096]{1,0:T(8,128)(2,1)S(1)} %shard_map.54.refs_3_.refs_1_.refs_4_, bf16[32,4096]{1,0:T(8,128)(2,1)S(1)} %shard_map.55.refs_4_.refs_2_.refs_5_), custom_call_target="tpu_custom_call" | custom-call | flops 150994944 | bytes 4194304 | tf_op jit(solution)/shard_map/pallas_call | solution.py:320
  28.8 0.0 collective-permute-done.5.other_ref
  28.9 1.7 %collective-permute-start.10 = (f32[16,512]{1,0:T(8,128)S(1)}, f32[16,512]{1,0:T(8,128)S(1)}, u32[]{:S(2)}, u32[]{:S(2)}) collective-permute-start(f32[16,512]{1,0:T(8,128)S(1)} %get-tuple-element.41), channel_id=1, source_target_pairs={{0,8},{4,12},{8,0},{12,4},{16,24},{20,28},{24,16},{28,20},{1,9},{5... | collective-permute-start | bytes 98312 | tf_op jit(solution)/shard_map/ppermute | solution.py:418
  30.6 1.9 %collective-permute-start.8 = (f32[16,512]{1,0:T(8,128)S(1)}, f32[16,512]{1,0:T(8,128)S(1)}, u32[]{:S(2)}, u32[]{:S(2)}) collective-permute-start(f32[16,512]{1,0:T(8,128)S(1)} %get-tuple-element.39), channel_id=1, source_target_pairs={{0,24},{4,28},{8,16},{12,20},{16,8},{20,12},{24,0},{28,4},{1,25},{... | collective-permute-start | bytes 98312 | tf_op jit(solution)/shard_map/ppermute | solution.py:418
  32.4 0.0 collective-permute-start.9
  32.5 0.0 collective-permute-done.7.refs_2_
  32.5 0.0 collective-permute-done.6.refs_1_
  32.5 1.7 %shard_map.59 = bf16[16,2,64,256]{3,2,1,0:T(8,128)(2,1)} custom-call(bf16[16,64,256]{2,1,0:T(8,128)(2,1)S(1)} %shard_map.57.even_ref, bf16[144,256]{1,0:T(8,128)(2,1)S(1)} %get-tuple-element.35.taps_ref, bf16[32,4096]{1,0:T(8,128)(2,1)S(1)} %shard_map.53.refs_0_, bf16[64,4096]{1,0:T(8,128)(2,1)S(1)} %collective-permute-done.6.refs_1_, ...), custom_call_target="tpu_custom_call" | custom-call | flops 301989888 | bytes 4194304 | tf_op jit(solution)/shard_map/pallas_call | solution.py:320
  34.2 0.0 collective-permute-done.10.refs_3_
  34.2 1.2 %collective-permute-done.8.refs_1_ = f32[16,512]{1,0:T(8,128)S(1)} collective-permute-done((f32[16,512]{1,0:T(8,128)S(1)}, f32[16,512]{1,0:T(8,128)S(1)}, u32[]{:S(2)}, u32[]{:S(2)}) %collective-permute-start.8) | collective-permute-done | bytes 32800 | tf_op jit(solution)/shard_map/ppermute | solution.py:418
  35.4 1.0 %collective-permute-done.9.refs_2_ = f32[16,512]{1,0:T(8,128)S(1)} collective-permute-done((f32[16,512]{1,0:T(8,128)S(1)}, f32[16,512]{1,0:T(8,128)S(1)}, u32[]{:S(2)}, u32[]{:S(2)}) %collective-permute-start.9) | collective-permute-done | bytes 32800 | tf_op jit(solution)/shard_map/ppermute | solution.py:418
  36.4 0.8 %shard_map.60 = f32[16,16,27]{2,1,0:T(8,128)} custom-call(f32[16,512]{1,0:T(8,128)S(1)} %get-tuple-element.38.refs_0_, f32[16,512]{1,0:T(8,128)S(1)} %collective-permute-done.8.refs_1_, f32[16,512]{1,0:T(8,128)S(1)} %collective-permute-done.9.refs_2_, f32[16,512]{1,0:T(8,128)S(1)} %collective-permute-done.10.refs_3_), custom_call_target="tpu_custom_call" | custom-call | flops 65536 | bytes 524288 | tf_op jit(solution)/shard_map/pallas_call | solution.py:320
  (2 shorter events, 0.0 us)
Async XLA Ops:
  0.6 9.2 %copy-start = (bf16[27,64,128]{2,1,0:T(8,128)(2,1)S(1)}, bf16[27,64,128]{2,1,0:T(8,128)(2,1)}, u32[]{:S(2)}) copy-start(bf16[27,64,128]{2,1,0:T(8,128)(2,1)} %param.5) | copy-start | bytes 1327108
  0.6 18.9 %collective-permute-start.2 = (bf16[16,2,64,256]{3,2,1,0:T(8,128)(2,1)}, bf16[16,2,64,256]{3,2,1,0:T(8,128)(2,1)S(1)}, u32[]{:S(2)}, u32[]{:S(2)}) collective-permute-start(bf16[16,2,64,256]{3,2,1,0:T(8,128)(2,1)} %refs_0_.2), channel_id=1, source_target_pairs={{0,4},{4,8},{8,12},{12,16},{16,20},{20,24},{24,28},{28,0},{1,5},{5... | collective-permute-start | bytes 3145736 | tf_op jit(solution)/shard_map/ppermute | solution.py:366
  1.1 15.9 %collective-permute-start.1 = (bf16[32,1,32,128]{3,2,1,0:T(8,128)(2,1)}, bf16[32,1,32,128]{3,2,1,0:T(8,128)(2,1)S(1)}, u32[]{:S(2)}, u32[]{:S(2)}) collective-permute-start(bf16[32,1,32,128]{3,2,1,0:T(8,128)(2,1)} %refs_0_.3), channel_id=1, source_target_pairs={{0,2},{1,3},{2,0},{3,1},{4,6},{5,7},{6,4},{7,5},{8,10},{9,11},{10,... | collective-permute-start | bytes 786440 | tf_op jit(solution)/shard_map/ppermute | solution.py:358
  4.8 14.0 %collective-permute-start.3 = (bf16[32,1,32,128]{3,2,1,0:T(8,128)(2,1)}, bf16[32,1,32,128]{3,2,1,0:T(8,128)(2,1)S(1)}, u32[]{:S(2)}, u32[]{:S(2)}) collective-permute-start(bf16[32,1,32,128]{3,2,1,0:T(8,128)(2,1)} %refs_0_.3), channel_id=1, source_target_pairs={{4,0},{8,4},{12,8},{16,12},{20,16},{24,20},{28,24},{0,28},{5,1},{9... | collective-permute-start | bytes 786440 | tf_op jit(solution)/shard_map/ppermute | solution.py:367
  7.1 12.5 %collective-permute-start = (bf16[32,1,32,128]{3,2,1,0:T(8,128)(2,1)}, bf16[32,1,32,128]{3,2,1,0:T(8,128)(2,1)S(1)}, u32[]{:S(2)}, u32[]{:S(2)}) collective-permute-start(bf16[32,1,32,128]{3,2,1,0:T(8,128)(2,1)} %refs_0_.3), channel_id=1, source_target_pairs={{0,1},{1,0},{2,3},{3,2},{4,5},{5,4},{6,7},{7,6},{8,9},{9,8},{10,11... | collective-permute-start | bytes 786440 | tf_op jit(solution)/shard_map/ppermute | solution.py:358
  8.7 1.0 %copy-start.1 = (bf16[32,1,32,128]{3,2,1,0:T(8,128)(2,1)S(1)}, bf16[32,1,32,128]{3,2,1,0:T(8,128)(2,1)}, u32[]{:S(2)}) copy-start(bf16[32,1,32,128]{3,2,1,0:T(8,128)(2,1)} %refs_0_.3) | copy-start | bytes 786436
  9.8 1.2 %copy-start.2 = (bf16[16,2,64,256]{3,2,1,0:T(8,128)(2,1)S(1)}, bf16[16,2,64,256]{3,2,1,0:T(8,128)(2,1)}, u32[]{:S(2)}) copy-start(bf16[16,2,64,256]{3,2,1,0:T(8,128)(2,1)} %refs_0_.2) | copy-start | bytes 3145732
  17.0 9.1 %collective-permute-start.4 = (bf16[32,1,32,128]{3,2,1,0:T(8,128)(2,1)S(1)}, bf16[32,1,32,128]{3,2,1,0:T(8,128)(2,1)S(1)}, u32[]{:S(2)}, u32[]{:S(2)}) collective-permute-start(bf16[32,1,32,128]{3,2,1,0:T(8,128)(2,1)S(1)} %collective-permute-done.1.refs_1_), channel_id=1, source_target_pairs={{0,1},{1,0},{2,3},{3,2},{4,5},{5,4},{6,7},{7,6},{8,9},{9,8},{10,11... | collective-permute-start | bytes 786440 | tf_op jit(solution)/shard_map/ppermute | solution.py:358
  19.9 12.6 %collective-permute-start.6 = (bf16[64,4096]{1,0:T(8,128)(2,1)S(1)}, bf16[64,4096]{1,0:T(8,128)(2,1)S(1)}, u32[]{:S(2)}, u32[]{:S(2)}) collective-permute-start(bf16[64,4096]{1,0:T(8,128)(2,1)S(1)} %shard_map.54.refs_3_.refs_1_.refs_4_), channel_id=1, source_target_pairs={{4,0},{8,4},{12,8},{16,12},{20,16},{24,20},{28,24},{0,28},{5,1},{9... | collective-permute-start | bytes 1572872 | tf_op jit(solution)/shard_map/ppermute | solution.py:380
  26.3 6.2 %collective-permute-start.7 = (bf16[32,4096]{1,0:T(8,128)(2,1)S(1)}, bf16[32,4096]{1,0:T(8,128)(2,1)S(1)}, u32[]{:S(2)}, u32[]{:S(2)}) collective-permute-start(bf16[32,4096]{1,0:T(8,128)(2,1)S(1)} %shard_map.55.refs_4_.refs_2_.refs_5_), channel_id=1, source_target_pairs={{4,0},{8,4},{12,8},{16,12},{20,16},{24,20},{28,24},{0,28},{5,1},{9... | collective-permute-start | bytes 786440 | tf_op jit(solution)/shard_map/ppermute | solution.py:380
  27.5 1.4 %collective-permute-start.5 = (f32[64,512]{1,0:T(8,128)S(1)}, f32[64,512]{1,0:T(8,128)S(1)}, u32[]{:S(2)}, u32[]{:S(2)}) collective-permute-start(f32[64,512]{1,0:T(8,128)S(1)} %get-tuple-element.30), channel_id=1, source_target_pairs={{0,4},{4,0},{8,12},{12,8},{16,20},{20,16},{24,28},{28,24},{1,5},{5... | collective-permute-start | bytes 393224 | tf_op jit(solution)/shard_map/ppermute | solution.py:400
  28.9 5.3 %collective-permute-start.10 = (f32[16,512]{1,0:T(8,128)S(1)}, f32[16,512]{1,0:T(8,128)S(1)}, u32[]{:S(2)}, u32[]{:S(2)}) collective-permute-start(f32[16,512]{1,0:T(8,128)S(1)} %get-tuple-element.41), channel_id=1, source_target_pairs={{0,8},{4,12},{8,0},{12,4},{16,24},{20,28},{24,16},{28,20},{1,9},{5... | collective-permute-start | bytes 98312 | tf_op jit(solution)/shard_map/ppermute | solution.py:418
  30.6 4.8 %collective-permute-start.8 = (f32[16,512]{1,0:T(8,128)S(1)}, f32[16,512]{1,0:T(8,128)S(1)}, u32[]{:S(2)}, u32[]{:S(2)}) collective-permute-start(f32[16,512]{1,0:T(8,128)S(1)} %get-tuple-element.39), channel_id=1, source_target_pairs={{0,24},{4,28},{8,16},{12,20},{16,8},{20,12},{24,0},{28,4},{1,25},{... | collective-permute-start | bytes 98312 | tf_op jit(solution)/shard_map/ppermute | solution.py:418
  32.4 3.9 %collective-permute-start.9 = (f32[16,512]{1,0:T(8,128)S(1)}, f32[16,512]{1,0:T(8,128)S(1)}, u32[]{:S(2)}, u32[]{:S(2)}) collective-permute-start(f32[16,512]{1,0:T(8,128)S(1)} %get-tuple-element.40), channel_id=1, source_target_pairs={{0,16},{4,20},{8,24},{12,28},{16,0},{20,4},{24,8},{28,12},{1,17},{... | collective-permute-start | bytes 98312 | tf_op jit(solution)/shard_map/ppermute | solution.py:418

commit v15 on v14

--- a/solution.py
+++ b/solution.py
@@ -364,7 +364,8 @@
         cost=(1 << 20, 2 << 20),
     )
     behind = lax.ppermute(volume, "depth", farther)
-    next_own = lax.ppermute(grad_out, "depth", nearer)
+    own, views = lax.optimization_barrier((grad_out, views))
+    next_own = lax.ppermute(own, "depth", nearer)
     behind_views = call(
         behind_views_kernel,
         jax.ShapeDtypeStruct((6 * chans, cells), BF16),
@@ -381,7 +382,7 @@
     outs = channels // depth
     half_terms = jax.ShapeDtypeStruct((channels // 2, 32 * chans), F32)
     keep, send = call(
-        lambda *refs: weight_kernel(outs, cols, 8 * cols, *refs),
+        lambda *refs: weight_kernel(outs, cols, 4 * cols, *refs),
         (half_terms, half_terms),
         views,
         behind_views,

time: 37.3 us -> 42.6 us (1.14)
  waiting for transfers between devices: 12.6 us -> 20.3 us
  starting transfers between devices: 15.6 us -> 14.2 us
  local copies, waits for them, and re-layouts: 2.24 us -> 1.25 us
    ppermute x3, waiting for transfers between devices: 9.81 us -> 17.6 us  [shards(): lax.ppermute(got[mask - low], 'chan', [(i, i ^ low) for i in range(count)])]
    ppermute x1, waiting for transfers between devices: 0.01 us -> 1.66 us  [shards(): next_own = lax.ppermute(own, 'depth', nearer)]
    ppermute x3, waiting for transfers between devices: 2.2 us -> 0.61 us  [shards(): lax.ppermute(terms[k - 1], 'depth', [(i, i ^ 2 * k) for i in range(depth)])]
    ppermute x3, starting transfers between devices: 7.07 us -> 5.76 us  [shards(): lax.ppermute(got[mask - low], 'chan', [(i, i ^ low) for i in range(count)])]
    unnamed x6, local copies, waits for them, and re-layouts: 2.21 us -> 1.23 us
    ppermute x1, waiting for transfers between devices: 0.53 us -> 0.01 us  [shards(): behind = lax.ppermute(volume, 'depth', farther)]
  transfers between devices with their start and end apart: 11 -> 11, of which waited for: 5 -> 7; matrix products, arithmetic and copies ran while one was open for 0% -> 0% of each run, Pallas kernels for 14% -> 12%
where the time goes in v15:
time: 42.6 us; the launch traced here: 42.4 us
  waiting for transfers between devices  20.3 us (48%)
  starting transfers between devices  14.2 us (33%)
  Pallas kernels  5.97 us (14%)
  local copies, waits for them, and re-layouts  1.25 us (3%)
  between operations  0.75 us (2%)
    ppermute x3, waiting for transfers between devices, shards(): lax.ppermute(got[mask - low], 'chan', [(i, i ^ low) for i in range(count)])  17.6 us
    pallas_call x11, Pallas kernels, call(): pl.pallas_call(kernel, out_shape=out_shape, in_specs=[VMEM] * len(args),...  5.97 us
    ppermute x3, starting transfers between devices, shards(): lax.ppermute(got[mask - low], 'chan', [(i, i ^ low) for i in range(count)])  5.76 us
    ppermute x3, starting transfers between devices, shards(): lax.ppermute(terms[k - 1], 'depth', [(i, i ^ 2 * k) for i in range(depth)])  3.55 us
    ppermute x1, starting transfers between devices, shards(): next_own = lax.ppermute(own, 'depth', nearer)  2.42 us
    ppermute x2, starting transfers between devices, shards(): lax.ppermute(part, 'depth', nearer)  1.86 us
    ppermute x1, waiting for transfers between devices, shards(): next_own = lax.ppermute(own, 'depth', nearer)  1.66 us
    unnamed x6, local copies, waits for them, and re-layouts  1.23 us
  transfers between devices with their start and end apart: 11, of which 7 were waited for; matrix products, arithmetic and copies ran while one was open for 0% of the time, Pallas kernels for 12%

profile of v15, /device:TPU:0, one launch (start us, length us, event | category | flops | bytes accessed | tf_op | source)
XLA Modules:
  0.0 42.4 jit_solution(1690547538063297115)
XLA Ops:
  0.6 0.0 copy-start
  0.6 0.0 copy-start.1
  0.7 0.5 %collective-permute-start.2 = (bf16[16,2,64,256]{3,2,1,0:T(8,128)(2,1)}, bf16[16,2,64,256]{3,2,1,0:T(8,128)(2,1)S(1)}, u32[]{:S(2)}, u32[]{:S(2)}) collective-permute-start(bf16[16,2,64,256]{3,2,1,0:T(8,128)(2,1)} %refs_0_.2), channel_id=1, source_target_pairs={{0,4},{4,8},{8,12},{12,16},{16,20},{20,24},{24,28},{28,0},{1,5},{5... | collective-permute-start | bytes 3145736 | tf_op jit(solution)/shard_map/ppermute | solution.py:366
  1.2 3.7 %collective-permute-start.1 = (bf16[32,1,32,128]{3,2,1,0:T(8,128)(2,1)}, bf16[32,1,32,128]{3,2,1,0:T(8,128)(2,1)S(1)}, u32[]{:S(2)}, u32[]{:S(2)}) collective-permute-start(bf16[32,1,32,128]{3,2,1,0:T(8,128)(2,1)} %refs_0_.3), channel_id=1, source_target_pairs={{0,2},{1,3},{2,0},{3,1},{4,6},{5,7},{6,4},{7,5},{8,10},{9,11},{10,... | collective-permute-start | bytes 786440 | tf_op jit(solution)/shard_map/ppermute | solution.py:358
  4.8 0.0 copy-done
  4.8 0.0 copy-start.2
  4.9 1.2 %copy-done.2 = bf16[16,2,64,256]{3,2,1,0:T(8,128)(2,1)S(1)} copy-done((bf16[16,2,64,256]{3,2,1,0:T(8,128)(2,1)S(1)}, bf16[16,2,64,256]{3,2,1,0:T(8,128)(2,1)}, u32[]{:S(2)}) %copy-start.2) | copy-done | bytes 1048600
  6.1 0.9 %shard_map.50 = (bf16[192,4096]{1,0:T(8,128)(2,1)S(1)}, bf16[144,128]{1,0:T(8,128)(2,1)S(1)}, bf16[144,256]{1,0:T(8,128)(2,1)S(1)}) custom-call(bf16[16,2,64,256]{3,2,1,0:T(8,128)(2,1)S(1)} %copy-done.2, bf16[27,16,128]{2,1,0:T(8,128)(2,1)S(1)} %constant_dynamic-slice_fusion.refs_1_), custom_call_target="tpu_custom_call" | custom-call | flops 536870912 | bytes 4194304 | tf_op jit(solution)/shard_map/pallas_call | solution.py:320
  7.0 10.0 %collective-permute-done.1.refs_1_ = bf16[32,1,32,128]{3,2,1,0:T(8,128)(2,1)S(1)} collective-permute-done((bf16[32,1,32,128]{3,2,1,0:T(8,128)(2,1)}, bf16[32,1,32,128]{3,2,1,0:T(8,128)(2,1)S(1)}, u32[]{:S(2)}, u32[]{:S(2)}) %collective-permute-start.1) | collective-permute-done | bytes 262176 | tf_op jit(solution)/shard_map/ppermute | solution.py:358
  16.9 0.0 copy-done.1
  16.9 2.4 %collective-permute-start.3 = (bf16[32,1,32,128]{3,2,1,0:T(8,128)(2,1)S(1)}, bf16[32,1,32,128]{3,2,1,0:T(8,128)(2,1)S(1)}, u32[]{:S(2)}, u32[]{:S(2)}) collective-permute-start(bf16[32,1,32,128]{3,2,1,0:T(8,128)(2,1)S(1)} %copy-done.1), channel_id=1, source_target_pairs={{4,0},{8,4},{12,8},{16,12},{20,16},{24,20},{28,24},{0,28},{5,1},{9... | collective-permute-start | bytes 786440 | tf_op jit(solution)/shard_map/ppermute | solution.py:368
  19.4 1.2 %collective-permute-start = (bf16[32,1,32,128]{3,2,1,0:T(8,128)(2,1)S(1)}, bf16[32,1,32,128]{3,2,1,0:T(8,128)(2,1)S(1)}, u32[]{:S(2)}, u32[]{:S(2)}) collective-permute-start(bf16[32,1,32,128]{3,2,1,0:T(8,128)(2,1)S(1)} %copy-done.1), channel_id=1, source_target_pairs={{0,1},{1,0},{2,3},{3,2},{4,5},{5,4},{6,7},{7,6},{8,9},{9,8},{10,11... | collective-permute-start | bytes 786440 | tf_op jit(solution)/shard_map/ppermute | solution.py:358
  20.6 0.1 shard_map.52.refs_2_.refs_0_.refs_3_
  20.7 0.9 %collective-permute-start.4 = (bf16[32,1,32,128]{3,2,1,0:T(8,128)(2,1)S(1)}, bf16[32,1,32,128]{3,2,1,0:T(8,128)(2,1)S(1)}, u32[]{:S(2)}, u32[]{:S(2)}) collective-permute-start(bf16[32,1,32,128]{3,2,1,0:T(8,128)(2,1)S(1)} %collective-permute-done.1.refs_1_), channel_id=1, source_target_pairs={{0,1},{1,0},{2,3},{3,2},{4,5},{5,4},{6,7},{7,6},{8,9},{9,8},{10,11... | collective-permute-start | bytes 786440 | tf_op jit(solution)/shard_map/ppermute | solution.py:358
  21.6 1.7 %collective-permute-done.3.refs_0_ = bf16[32,1,32,128]{3,2,1,0:T(8,128)(2,1)S(1)} collective-permute-done((bf16[32,1,32,128]{3,2,1,0:T(8,128)(2,1)S(1)}, bf16[32,1,32,128]{3,2,1,0:T(8,128)(2,1)S(1)}, u32[]{:S(2)}, u32[]{:S(2)}) %collective-permute-start.3) | collective-permute-done | bytes 262176 | tf_op jit(solution)/shard_map/ppermute | solution.py:368
  23.3 0.1 shard_map.53.refs_0_
  23.4 0.0 collective-permute-done.2.behind_ref
  23.4 0.1 shard_map.51.refs_1_
  23.5 5.1 %collective-permute-done.refs_0_ = bf16[32,1,32,128]{3,2,1,0:T(8,128)(2,1)S(1)} collective-permute-done((bf16[32,1,32,128]{3,2,1,0:T(8,128)(2,1)S(1)}, bf16[32,1,32,128]{3,2,1,0:T(8,128)(2,1)S(1)}, u32[]{:S(2)}, u32[]{:S(2)}) %collective-permute-start) | collective-permute-done | bytes 262176 | tf_op jit(solution)/shard_map/ppermute | solution.py:358
  28.6 0.3 shard_map.54.refs_3_.refs_1_.refs_4_
  28.9 0.1 collective-permute-start.6
  28.9 2.5 %collective-permute-done.4.refs_0_ = bf16[32,1,32,128]{3,2,1,0:T(8,128)(2,1)S(1)} collective-permute-done((bf16[32,1,32,128]{3,2,1,0:T(8,128)(2,1)S(1)}, bf16[32,1,32,128]{3,2,1,0:T(8,128)(2,1)S(1)}, u32[]{:S(2)}, u32[]{:S(2)}) %collective-permute-start.4) | collective-permute-done | bytes 262176 | tf_op jit(solution)/shard_map/ppermute | solution.py:358
  31.5 0.1 shard_map.55.refs_4_.refs_2_.refs_5_
  31.6 1.8 %collective-permute-start.7 = (bf16[32,4096]{1,0:T(8,128)(2,1)S(1)}, bf16[32,4096]{1,0:T(8,128)(2,1)S(1)}, u32[]{:S(2)}, u32[]{:S(2)}) collective-permute-start(bf16[32,4096]{1,0:T(8,128)(2,1)S(1)} %shard_map.55.refs_4_.refs_2_.refs_5_), channel_id=1, source_target_pairs={{4,0},{8,4},{12,8},{16,12},{20,16},{24,20},{28,24},{0,28},{5,1},{9... | collective-permute-start | bytes 786440 | tf_op jit(solution)/shard_map/ppermute | solution.py:381
  33.4 0.9 %shard_map.56 = (f32[64,512]{1,0:T(8,128)S(1)}, f32[64,512]{1,0:T(8,128)S(1)}) custom-call(bf16[192,4096]{1,0:T(8,128)(2,1)S(1)} %get-tuple-element.28.refs_0_, bf16[96,4096]{1,0:T(8,128)(2,1)S(1)} %shard_map.51.refs_1_, bf16[32,4096]{1,0:T(8,128)(2,1)S(1)} %shard_map.52.refs_2_.refs_0_.refs_3_, bf16[64,4096]{1,0:T(8,128)(2,1)S(1)} %shard_map.54.refs_3_.refs_1_.refs_4_, ...), custom_call_target="tpu_custom_call" | custom-call | flops 452984832 | bytes 8388608 | tf_op jit(solution)/shard_map/pallas_call | solution.py:320
  34.4 0.1 collective-permute-start.5
  34.4 0.9 %shard_map.57.even_ref = bf16[16,64,256]{2,1,0:T(8,128)(2,1)S(1)} custom-call(bf16[144,128]{1,0:T(8,128)(2,1)S(1)} %get-tuple-element.35.taps_ref, bf16[32,4096]{1,0:T(8,128)(2,1)S(1)} %shard_map.52.refs_2_.refs_0_.refs_3_, bf16[64,4096]{1,0:T(8,128)(2,1)S(1)} %shard_map.54.refs_3_.refs_1_.refs_4_, bf16[32,4096]{1,0:T(8,128)(2,1)S(1)} %shard_map.55.refs_4_.refs_2_.refs_5_), custom_call_target="tpu_custom_call" | custom-call | flops 150994944 | bytes 4194304 | tf_op jit(solution)/shard_map/pallas_call | solution.py:320
  35.4 0.4 collective-permute-done.5.other_ref
  35.8 1.4 %collective-permute-start.8 = (f32[16,512]{1,0:T(8,128)S(1)}, f32[16,512]{1,0:T(8,128)S(1)}, u32[]{:S(2)}, u32[]{:S(2)}) collective-permute-start(f32[16,512]{1,0:T(8,128)S(1)} %get-tuple-element.43), channel_id=1, source_target_pairs={{0,24},{4,28},{8,16},{12,20},{16,8},{20,12},{24,0},{28,4},{1,25},{... | collective-permute-start | bytes 98312 | tf_op jit(solution)/shard_map/ppermute | solution.py:419
  37.2 0.5 %collective-permute-start.9 = (f32[16,512]{1,0:T(8,128)S(1)}, f32[16,512]{1,0:T(8,128)S(1)}, u32[]{:S(2)}, u32[]{:S(2)}) collective-permute-start(f32[16,512]{1,0:T(8,128)S(1)} %get-tuple-element.44), channel_id=1, source_target_pairs={{0,16},{4,20},{8,24},{12,28},{16,0},{20,4},{24,8},{28,12},{1,17},{... | collective-permute-start | bytes 98312 | tf_op jit(solution)/shard_map/ppermute | solution.py:419
  37.7 1.6 %collective-permute-start.10 = (f32[16,512]{1,0:T(8,128)S(1)}, f32[16,512]{1,0:T(8,128)S(1)}, u32[]{:S(2)}, u32[]{:S(2)}) collective-permute-start(f32[16,512]{1,0:T(8,128)S(1)} %get-tuple-element.45), channel_id=1, source_target_pairs={{0,8},{4,12},{8,0},{12,4},{16,24},{20,28},{24,16},{28,20},{1,9},{5... | collective-permute-start | bytes 98312 | tf_op jit(solution)/shard_map/ppermute | solution.py:419
  39.4 0.0 collective-permute-done.7.refs_2_
  39.4 0.0 collective-permute-done.6.refs_1_
  39.4 1.7 %shard_map.59 = bf16[16,2,64,256]{3,2,1,0:T(8,128)(2,1)} custom-call(bf16[16,64,256]{2,1,0:T(8,128)(2,1)S(1)} %shard_map.57.even_ref, bf16[144,256]{1,0:T(8,128)(2,1)S(1)} %get-tuple-element.39.taps_ref, bf16[32,4096]{1,0:T(8,128)(2,1)S(1)} %shard_map.53.refs_0_, bf16[64,4096]{1,0:T(8,128)(2,1)S(1)} %collective-permute-done.6.refs_1_, ...), custom_call_target="tpu_custom_call" | custom-call | flops 301989888 | bytes 4194304 | tf_op jit(solution)/shard_map/pallas_call | solution.py:320
  41.0 0.0 collective-permute-done.8.refs_1_
  41.1 0.1 collective-permute-done.9.refs_2_
  41.1 0.5 %collective-permute-done.10.refs_3_ = f32[16,512]{1,0:T(8,128)S(1)} collective-permute-done((f32[16,512]{1,0:T(8,128)S(1)}, f32[16,512]{1,0:T(8,128)S(1)}, u32[]{:S(2)}, u32[]{:S(2)}) %collective-permute-start.10) | collective-permute-done | bytes 32800 | tf_op jit(solution)/shard_map/ppermute | solution.py:419
  41.7 0.8 %shard_map.60 = f32[16,16,27]{2,1,0:T(8,128)} custom-call(f32[16,512]{1,0:T(8,128)S(1)} %get-tuple-element.42.refs_0_, f32[16,512]{1,0:T(8,128)S(1)} %collective-permute-done.8.refs_1_, f32[16,512]{1,0:T(8,128)S(1)} %collective-permute-done.9.refs_2_, f32[16,512]{1,0:T(8,128)S(1)} %collective-permute-done.10.refs_3_), custom_call_target="tpu_custom_call" | custom-call | flops 65536 | bytes 524288 | tf_op jit(solution)/shard_map/pallas_call | solution.py:320
  (2 shorter events, 0.0 us)
Async XLA Ops:
  0.6 4.2 %copy-start = (bf16[27,64,128]{2,1,0:T(8,128)(2,1)S(1)}, bf16[27,64,128]{2,1,0:T(8,128)(2,1)}, u32[]{:S(2)}) copy-start(bf16[27,64,128]{2,1,0:T(8,128)(2,1)} %param.5) | copy-start | bytes 1327108
  0.6 16.3 %copy-start.1 = (bf16[32,1,32,128]{3,2,1,0:T(8,128)(2,1)S(1)}, bf16[32,1,32,128]{3,2,1,0:T(8,128)(2,1)}, u32[]{:S(2)}) copy-start(bf16[32,1,32,128]{3,2,1,0:T(8,128)(2,1)} %refs_0_.3) | copy-start | bytes 786436
  0.7 22.7 %collective-permute-start.2 = (bf16[16,2,64,256]{3,2,1,0:T(8,128)(2,1)}, bf16[16,2,64,256]{3,2,1,0:T(8,128)(2,1)S(1)}, u32[]{:S(2)}, u32[]{:S(2)}) collective-permute-start(bf16[16,2,64,256]{3,2,1,0:T(8,128)(2,1)} %refs_0_.2), channel_id=1, source_target_pairs={{0,4},{4,8},{8,12},{12,16},{16,20},{20,24},{24,28},{28,0},{1,5},{5... | collective-permute-start | bytes 3145736 | tf_op jit(solution)/shard_map/ppermute | solution.py:366
  1.2 15.8 %collective-permute-start.1 = (bf16[32,1,32,128]{3,2,1,0:T(8,128)(2,1)}, bf16[32,1,32,128]{3,2,1,0:T(8,128)(2,1)S(1)}, u32[]{:S(2)}, u32[]{:S(2)}) collective-permute-start(bf16[32,1,32,128]{3,2,1,0:T(8,128)(2,1)} %refs_0_.3), channel_id=1, source_target_pairs={{0,2},{1,3},{2,0},{3,1},{4,6},{5,7},{6,4},{7,5},{8,10},{9,11},{10,... | collective-permute-start | bytes 786440 | tf_op jit(solution)/shard_map/ppermute | solution.py:358
  4.8 1.2 %copy-start.2 = (bf16[16,2,64,256]{3,2,1,0:T(8,128)(2,1)S(1)}, bf16[16,2,64,256]{3,2,1,0:T(8,128)(2,1)}, u32[]{:S(2)}) copy-start(bf16[16,2,64,256]{3,2,1,0:T(8,128)(2,1)} %refs_0_.2) | copy-start | bytes 3145732
  16.9 6.3 %collective-permute-start.3 = (bf16[32,1,32,128]{3,2,1,0:T(8,128)(2,1)S(1)}, bf16[32,1,32,128]{3,2,1,0:T(8,128)(2,1)S(1)}, u32[]{:S(2)}, u32[]{:S(2)}) collective-permute-start(bf16[32,1,32,128]{3,2,1,0:T(8,128)(2,1)S(1)} %copy-done.1), channel_id=1, source_target_pairs={{4,0},{8,4},{12,8},{16,12},{20,16},{24,20},{28,24},{0,28},{5,1},{9... | collective-permute-start | bytes 786440 | tf_op jit(solution)/shard_map/ppermute | solution.py:368
  19.4 9.2 %collective-permute-start = (bf16[32,1,32,128]{3,2,1,0:T(8,128)(2,1)S(1)}, bf16[32,1,32,128]{3,2,1,0:T(8,128)(2,1)S(1)}, u32[]{:S(2)}, u32[]{:S(2)}) collective-permute-start(bf16[32,1,32,128]{3,2,1,0:T(8,128)(2,1)S(1)} %copy-done.1), channel_id=1, source_target_pairs={{0,1},{1,0},{2,3},{3,2},{4,5},{5,4},{6,7},{7,6},{8,9},{9,8},{10,11... | collective-permute-start | bytes 786440 | tf_op jit(solution)/shard_map/ppermute | solution.py:358
  20.7 10.7 %collective-permute-start.4 = (bf16[32,1,32,128]{3,2,1,0:T(8,128)(2,1)S(1)}, bf16[32,1,32,128]{3,2,1,0:T(8,128)(2,1)S(1)}, u32[]{:S(2)}, u32[]{:S(2)}) collective-permute-start(bf16[32,1,32,128]{3,2,1,0:T(8,128)(2,1)S(1)} %collective-permute-done.1.refs_1_), channel_id=1, source_target_pairs={{0,1},{1,0},{2,3},{3,2},{4,5},{5,4},{6,7},{7,6},{8,9},{9,8},{10,11... | collective-permute-start | bytes 786440 | tf_op jit(solution)/shard_map/ppermute | solution.py:358
  28.9 10.5 %collective-permute-start.6 = (bf16[64,4096]{1,0:T(8,128)(2,1)S(1)}, bf16[64,4096]{1,0:T(8,128)(2,1)S(1)}, u32[]{:S(2)}, u32[]{:S(2)}) collective-permute-start(bf16[64,4096]{1,0:T(8,128)(2,1)S(1)} %shard_map.54.refs_3_.refs_1_.refs_4_), channel_id=1, source_target_pairs={{4,0},{8,4},{12,8},{16,12},{20,16},{24,20},{28,24},{0,28},{5,1},{9... | collective-permute-start | bytes 1572872 | tf_op jit(solution)/shard_map/ppermute | solution.py:381
  31.6 7.7 %collective-permute-start.7 = (bf16[32,4096]{1,0:T(8,128)(2,1)S(1)}, bf16[32,4096]{1,0:T(8,128)(2,1)S(1)}, u32[]{:S(2)}, u32[]{:S(2)}) collective-permute-start(bf16[32,4096]{1,0:T(8,128)(2,1)S(1)} %shard_map.55.refs_4_.refs_2_.refs_5_), channel_id=1, source_target_pairs={{4,0},{8,4},{12,8},{16,12},{20,16},{24,20},{28,24},{0,28},{5,1},{9... | collective-permute-start | bytes 786440 | tf_op jit(solution)/shard_map/ppermute | solution.py:381
  34.4 1.4 %collective-permute-start.5 = (f32[64,512]{1,0:T(8,128)S(1)}, f32[64,512]{1,0:T(8,128)S(1)}, u32[]{:S(2)}, u32[]{:S(2)}) collective-permute-start(f32[64,512]{1,0:T(8,128)S(1)} %get-tuple-element.34), channel_id=1, source_target_pairs={{0,4},{4,0},{8,12},{12,8},{16,20},{20,16},{24,28},{28,24},{1,5},{5... | collective-permute-start | bytes 393224 | tf_op jit(solution)/shard_map/ppermute | solution.py:401
  35.8 5.2 %collective-permute-start.8 = (f32[16,512]{1,0:T(8,128)S(1)}, f32[16,512]{1,0:T(8,128)S(1)}, u32[]{:S(2)}, u32[]{:S(2)}) collective-permute-start(f32[16,512]{1,0:T(8,128)S(1)} %get-tuple-element.43), channel_id=1, source_target_pairs={{0,24},{4,28},{8,16},{12,20},{16,8},{20,12},{24,0},{28,4},{1,25},{... | collective-permute-start | bytes 98312 | tf_op jit(solution)/shard_map/ppermute | solution.py:419
  37.2 3.9 %collective-permute-start.9 = (f32[16,512]{1,0:T(8,128)S(1)}, f32[16,512]{1,0:T(8,128)S(1)}, u32[]{:S(2)}, u32[]{:S(2)}) collective-permute-start(f32[16,512]{1,0:T(8,128)S(1)} %get-tuple-element.44), channel_id=1, source_target_pairs={{0,16},{4,20},{8,24},{12,28},{16,0},{20,4},{24,8},{28,12},{1,17},{... | collective-permute-start | bytes 98312 | tf_op jit(solution)/shard_map/ppermute | solution.py:419
  37.7 3.9 %collective-permute-start.10 = (f32[16,512]{1,0:T(8,128)S(1)}, f32[16,512]{1,0:T(8,128)S(1)}, u32[]{:S(2)}, u32[]{:S(2)}) collective-permute-start(f32[16,512]{1,0:T(8,128)S(1)} %get-tuple-element.45), channel_id=1, source_target_pairs={{0,8},{4,12},{8,0},{12,4},{16,24},{20,28},{24,16},{28,20},{1,9},{5... | collective-permute-start | bytes 98312 | tf_op jit(solution)/shard_map/ppermute | solution.py:419

commit v16 on v15

--- a/solution.py
+++ b/solution.py
@@ -350,12 +350,15 @@
         own_weight,
         cost=(2 * 2 * 2 * cells * chans * 8 * cols, 4 << 20),
     )
-    got = {0: grad_out}
-    for mask in sorted(range(1, count), key=lambda mask: (mask & (mask - 1) > 0, -mask)):
-        low = mask & -mask
-        if mask == 3:
-            got[2], views = lax.optimization_barrier((got[2], views))
-        got[mask] = lax.ppermute(got[mask - low], "chan", [(i, i ^ low) for i in range(count)])
+    pairs = lambda mask: [(i, i ^ mask) for i in range(count)]
+    middle = own_outs // 2
+    by_two = lax.ppermute(grad_out[:middle], "chan", pairs(2))
+    own, views = lax.optimization_barrier((grad_out, views))
+    by_one = lax.ppermute(own, "chan", pairs(1))
+    by_two, rest = lax.optimization_barrier((by_two, own[middle:]))
+    by_two_later = lax.ppermute(rest, "chan", pairs(2))
+    by_three = lax.ppermute(by_two, "chan", pairs(1))
+    by_three_later = lax.ppermute(by_two_later, "chan", pairs(1))
     lines = lambda *parts: call(
         lines_kernel,
         jax.ShapeDtypeStruct((sum(part.shape[0] for part in parts), cells), BF16),
@@ -364,7 +367,6 @@
         cost=(1 << 20, 2 << 20),
     )
     behind = lax.ppermute(volume, "depth", farther)
-    own, views = lax.optimization_barrier((grad_out, views))
     next_own = lax.ppermute(own, "depth", nearer)
     behind_views = call(
         behind_views_kernel,
@@ -373,10 +375,11 @@
         cost=(2 * 2 * cells * chans * 8 * cols, 2 << 20),
     )
     first_lines, next_first_lines = lines(grad_out), lines(next_own)
-    got[1], views, behind_views, first_lines, next_first_lines = lax.optimization_barrier(
-        (got[1], views, behind_views, first_lines, next_first_lines)
-    )
-    later_lines = [lines(*[got[mask] for mask in range(1, count - 1)]), lines(got[count - 1])]
+    second_lines = lines(by_one, by_two)
+    by_three, behind_views, first_lines, next_first_lines = lax.optimization_barrier(
+        (by_three, behind_views, first_lines, next_first_lines)
+    )
+    later_lines = [second_lines, lines(by_two_later, by_three), lines(by_three_later)]
     own_lines = [first_lines] + later_lines
     next_lines = [next_first_lines] + [lax.ppermute(part, "depth", nearer) for part in later_lines]
     outs = channels // depth
@@ -457,7 +460,7 @@
             grad_out.shape[0] % 32 == 0
             and volume.shape[0] == 16
             and grad_out.shape[1] == 1
-            and ring >= 4
+            and ring == 4
             and ring & (ring - 1) == 0
             and depth & (depth - 1) == 0
             and depth % (2 * ring) == 0

time: 42.6 us -> 40.9 us (0.960)
  waiting for transfers between devices: 20.3 us -> 14.5 us
  starting transfers between devices: 14.2 us -> 17.5 us
  local copies, waits for them, and re-layouts: 1.25 us -> 1.75 us
    ppermute x3 -> x5, starting transfers between devices: 5.76 us -> 10.9 us  [the longest x1 3.38 us: shards(): by_two_later = lax.ppermute(rest, 'chan', pairs(2))]
    ppermute x3 -> x5, waiting for transfers between devices: 17.6 us -> 13.2 us  [the longest x1 5.32 us: shards(): by_two_later = lax.ppermute(rest, 'chan', pairs(2))]
    ppermute x1, waiting for transfers between devices: 1.66 us -> 0.01 us  [shards(): next_own = lax.ppermute(own, 'depth', nearer)]
    ppermute x1, starting transfers between devices: 2.42 us -> 1.33 us  [shards(): next_own = lax.ppermute(own, 'depth', nearer)]
    ppermute x2 -> x3, starting transfers between devices: 1.86 us -> 0.91 us  [shards(): lax.ppermute(part, 'depth', nearer)]
    ppermute x3, waiting for transfers between devices: 0.61 us -> 1.28 us  [shards(): lax.ppermute(terms[k - 1], 'depth', [(i, i ^ 2 * k) for i in range(depth)])]
    unnamed x6, local copies, waits for them, and re-layouts: 1.23 us -> 1.72 us
    pallas_call x11 -> x12, Pallas kernels: 5.97 us -> 5.99 us  [call(): pl.pallas_call(kernel, out_shape=out_shape, in_specs=[VMEM] * len(args),...]
  transfers between devices with their start and end apart: 11 -> 14, of which waited for: 7 -> 5; matrix products, arithmetic and copies ran while one was open for 0% -> 0% of each run, Pallas kernels for 12% -> 13%
where the time goes in v16:
time: 40.9 us; the launch traced here: 40.6 us
  starting transfers between devices  17.5 us (43%)
  waiting for transfers between devices  14.5 us (35%)
  Pallas kernels  5.99 us (15%)
  local copies, waits for them, and re-layouts  1.75 us (4%)
  between operations  0.8 us (2%)
    pallas_call x12, Pallas kernels, call(): pl.pallas_call(kernel, out_shape=out_shape, in_specs=[VMEM] * len(args),...  5.99 us
    ppermute x1, waiting for transfers between devices, shards(): by_two_later = lax.ppermute(rest, 'chan', pairs(2))  5.32 us
    ppermute x1, waiting for transfers between devices, shards(): by_two = lax.ppermute(grad_out[:middle], 'chan', pairs(2))  5.21 us
    ppermute x3, starting transfers between devices, shards(): lax.ppermute(terms[k - 1], 'depth', [(i, i ^ 2 * k) for i in range(depth)])  3.8 us
    ppermute x1, starting transfers between devices, shards(): by_two_later = lax.ppermute(rest, 'chan', pairs(2))  3.38 us
    ppermute x1, starting transfers between devices, shards(): by_one = lax.ppermute(own, 'chan', pairs(1))  3.09 us
    ppermute x1, waiting for transfers between devices, shards(): by_three_later = lax.ppermute(by_two_later, 'chan', pairs(1))  2.69 us
    ppermute x1, starting transfers between devices, shards(): by_two = lax.ppermute(grad_out[:middle], 'chan', pairs(2))  2.65 us
  transfers between devices with their start and end apart: 14, of which 5 were waited for; matrix products, arithmetic and copies ran while one was open for 0% of the time, Pallas kernels for 13%

profile of v16, /device:TPU:0, one launch (start us, length us, event | category | flops | bytes accessed | tf_op | source)
XLA Modules:
  0.0 40.6 jit_solution(11177568995880973684)
XLA Ops:
  0.6 0.0 copy-start
  0.6 0.0 copy-start.1
  0.7 0.5 %collective-permute-start.2 = (bf16[16,2,64,256]{3,2,1,0:T(8,128)(2,1)}, bf16[16,2,64,256]{3,2,1,0:T(8,128)(2,1)S(1)}, u32[]{:S(2)}, u32[]{:S(2)}) collective-permute-start(bf16[16,2,64,256]{3,2,1,0:T(8,128)(2,1)} %refs_0_.2), channel_id=1, source_target_pairs={{0,4},{4,8},{8,12},{12,16},{16,20},{20,24},{24,28},{28,0},{1,5},{5... | collective-permute-start | bytes 3145736 | tf_op jit(solution)/shard_map/ppermute | solution.py:369
  1.2 0.5 %copy-done = bf16[27,64,128]{2,1,0:T(8,128)(2,1)S(1)} copy-done((bf16[27,64,128]{2,1,0:T(8,128)(2,1)S(1)}, bf16[27,64,128]{2,1,0:T(8,128)(2,1)}, u32[]{:S(2)}) %copy-start) | copy-done | bytes 442392
  1.7 0.0 copy-start.2
  1.7 1.2 %copy-done.2 = bf16[16,2,64,256]{3,2,1,0:T(8,128)(2,1)S(1)} copy-done((bf16[16,2,64,256]{3,2,1,0:T(8,128)(2,1)S(1)}, bf16[16,2,64,256]{3,2,1,0:T(8,128)(2,1)}, u32[]{:S(2)}) %copy-start.2) | copy-done | bytes 1048600
  2.9 0.9 %shard_map.50 = (bf16[192,4096]{1,0:T(8,128)(2,1)S(1)}, bf16[144,128]{1,0:T(8,128)(2,1)S(1)}, bf16[144,256]{1,0:T(8,128)(2,1)S(1)}) custom-call(bf16[16,2,64,256]{3,2,1,0:T(8,128)(2,1)S(1)} %copy-done.2, bf16[27,16,128]{2,1,0:T(8,128)(2,1)S(1)} %constant_dynamic-slice_fusion.refs_1_), custom_call_target="tpu_custom_call" | custom-call | flops 536870912 | bytes 4194304 | tf_op jit(solution)/shard_map/pallas_call | solution.py:320
  3.8 0.0 copy-done.1
  3.8 3.1 %collective-permute-start.4 = (bf16[32,1,32,128]{3,2,1,0:T(8,128)(2,1)S(1)}, bf16[32,1,32,128]{3,2,1,0:T(8,128)(2,1)S(1)}, u32[]{:S(2)}, u32[]{:S(2)}) collective-permute-start(bf16[32,1,32,128]{3,2,1,0:T(8,128)(2,1)S(1)} %copy-done.1), channel_id=1, source_target_pairs={{0,1},{1,0},{2,3},{3,2},{4,5},{5,4},{6,7},{7,6},{8,9},{9,8},{10,11... | collective-permute-start | bytes 786440 | tf_op jit(solution)/shard_map/ppermute | solution.py:357
  6.9 2.7 %collective-permute-start = (bf16[16,1,32,128]{3,2,1,0:T(8,128)(2,1)S(1)}, bf16[16,1,32,128]{3,2,1,0:T(8,128)(2,1)S(1)}, u32[]{:S(2)}, u32[]{:S(2)}) collective-permute-start(bf16[16,1,32,128]{3,2,1,0:T(8,128)(2,1)S(1)} %slice.6), channel_id=1, source_target_pairs={{0,2},{1,3},{2,0},{3,1},{4,6},{5,7},{6,4},{7,5},{8,10},{9,11},{10,... | collective-permute-start | bytes 393224 | tf_op jit(solution)/shard_map/ppermute | solution.py:355
  9.6 1.3 %collective-permute-start.3 = (bf16[32,1,32,128]{3,2,1,0:T(8,128)(2,1)S(1)}, bf16[32,1,32,128]{3,2,1,0:T(8,128)(2,1)S(1)}, u32[]{:S(2)}, u32[]{:S(2)}) collective-permute-start(bf16[32,1,32,128]{3,2,1,0:T(8,128)(2,1)S(1)} %copy-done.1), channel_id=1, source_target_pairs={{4,0},{8,4},{12,8},{16,12},{20,16},{24,20},{28,24},{0,28},{5,1},{9... | collective-permute-start | bytes 786440 | tf_op jit(solution)/shard_map/ppermute | solution.py:370
  10.9 5.2 %collective-permute-done.refs_1_ = bf16[16,1,32,128]{3,2,1,0:T(8,128)(2,1)S(1)} collective-permute-done((bf16[16,1,32,128]{3,2,1,0:T(8,128)(2,1)S(1)}, bf16[16,1,32,128]{3,2,1,0:T(8,128)(2,1)S(1)}, u32[]{:S(2)}, u32[]{:S(2)}) %collective-permute-start) | collective-permute-done | bytes 131104 | tf_op jit(solution)/shard_map/ppermute | solution.py:355
  16.1 3.4 %collective-permute-start.5 = (bf16[16,1,32,128]{3,2,1,0:T(8,128)(2,1)S(1)}, bf16[16,1,32,128]{3,2,1,0:T(8,128)(2,1)S(1)}, u32[]{:S(2)}, u32[]{:S(2)}) collective-permute-start(bf16[16,1,32,128]{3,2,1,0:T(8,128)(2,1)S(1)} %slice.7), channel_id=1, source_target_pairs={{0,2},{1,3},{2,0},{3,1},{4,6},{5,7},{6,4},{7,5},{8,10},{9,11},{10,... | collective-permute-start | bytes 393224 | tf_op jit(solution)/shard_map/ppermute | solution.py:359
  19.5 0.1 collective-permute-start.1
  19.6 0.0 collective-permute-done.4.refs_0_
  19.6 0.2 shard_map.54.refs_3_.refs_1_.refs_5_
  19.8 0.1 collective-permute-start.8
  19.9 5.3 %collective-permute-done.5.refs_0_ = bf16[16,1,32,128]{3,2,1,0:T(8,128)(2,1)S(1)} collective-permute-done((bf16[16,1,32,128]{3,2,1,0:T(8,128)(2,1)S(1)}, bf16[16,1,32,128]{3,2,1,0:T(8,128)(2,1)S(1)}, u32[]{:S(2)}, u32[]{:S(2)}) %collective-permute-start.5) | collective-permute-done | bytes 131104 | tf_op jit(solution)/shard_map/ppermute | solution.py:359
  25.2 1.7 %collective-permute-start.6 = (bf16[16,1,32,128]{3,2,1,0:T(8,128)(2,1)S(1)}, bf16[16,1,32,128]{3,2,1,0:T(8,128)(2,1)S(1)}, u32[]{:S(2)}, u32[]{:S(2)}) collective-permute-start(bf16[16,1,32,128]{3,2,1,0:T(8,128)(2,1)S(1)} %collective-permute-done.5.refs_0_), channel_id=1, source_target_pairs={{0,1},{1,0},{2,3},{3,2},{4,5},{5,4},{6,7},{7,6},{8,9},{9,8},{10,11... | collective-permute-start | bytes 393224 | tf_op jit(solution)/shard_map/ppermute | solution.py:361
  26.9 0.1 shard_map.52.refs_2_.refs_0_.refs_4_
  27.0 0.0 collective-permute-done.3.refs_0_
  27.0 0.1 shard_map.53.refs_0_
  27.2 0.0 collective-permute-done.2.behind_ref
  27.2 0.1 shard_map.51.refs_1_
  27.3 0.0 collective-permute-done.1.refs_1_
  27.3 0.1 shard_map.55.refs_4_.refs_2_.refs_6_
  27.4 0.1 collective-permute-start.9
  27.5 2.7 %collective-permute-done.6.refs_0_ = bf16[16,1,32,128]{3,2,1,0:T(8,128)(2,1)S(1)} collective-permute-done((bf16[16,1,32,128]{3,2,1,0:T(8,128)(2,1)S(1)}, bf16[16,1,32,128]{3,2,1,0:T(8,128)(2,1)S(1)}, u32[]{:S(2)}, u32[]{:S(2)}) %collective-permute-start.6) | collective-permute-done | bytes 131104 | tf_op jit(solution)/shard_map/ppermute | solution.py:361
  30.2 0.1 shard_map.56.refs_5_.refs_3_.refs_7_
  30.3 0.9 %shard_map.57 = (f32[64,512]{1,0:T(8,128)S(1)}, f32[64,512]{1,0:T(8,128)S(1)}) custom-call(bf16[192,4096]{1,0:T(8,128)(2,1)S(1)} %get-tuple-element.24.refs_0_, bf16[96,4096]{1,0:T(8,128)(2,1)S(1)} %shard_map.51.refs_1_, bf16[32,4096]{1,0:T(8,128)(2,1)S(1)} %shard_map.52.refs_2_.refs_0_.refs_4_, bf16[48,4096]{1,0:T(8,128)(2,1)S(1)} %shard_map.54.refs_3_.refs_1_.refs_5_, ...), custom_call_target="tpu_custom_call" | custom-call | flops 452984832 | bytes 8388608 | tf_op jit(solution)/shard_map/pallas_call | solution.py:320
  31.2 0.1 collective-permute-start.7
  31.3 0.8 %collective-permute-start.10 = (bf16[16,4096]{1,0:T(8,128)(2,1)S(1)}, bf16[16,4096]{1,0:T(8,128)(2,1)S(1)}, u32[]{:S(2)}, u32[]{:S(2)}) collective-permute-start(bf16[16,4096]{1,0:T(8,128)(2,1)S(1)} %shard_map.56.refs_5_.refs_3_.refs_7_), channel_id=1, source_target_pairs={{4,0},{8,4},{12,8},{16,12},{20,16},{24,20},{28,24},{0,28},{5,1},{9... | collective-permute-start | bytes 393224 | tf_op jit(solution)/shard_map/ppermute | solution.py:384
  32.1 0.9 %shard_map.58.even_ref = bf16[16,64,256]{2,1,0:T(8,128)(2,1)S(1)} custom-call(bf16[144,128]{1,0:T(8,128)(2,1)S(1)} %get-tuple-element.33.taps_ref, bf16[32,4096]{1,0:T(8,128)(2,1)S(1)} %shard_map.52.refs_2_.refs_0_.refs_4_, bf16[48,4096]{1,0:T(8,128)(2,1)S(1)} %shard_map.54.refs_3_.refs_1_.refs_5_, bf16[32,4096]{1,0:T(8,128)(2,1)S(1)} %shard_map.55.refs_4_.refs_2_.refs_6_, ...), custom_call_target="tpu_custom_call" | custom-call | flops 150994944 | bytes 4194304 | tf_op jit(solution)/shard_map/pallas_call | solution.py:320
  33.0 0.0 collective-permute-done.7.other_ref
  33.1 2.4 %collective-permute-start.11 = (f32[16,512]{1,0:T(8,128)S(1)}, f32[16,512]{1,0:T(8,128)S(1)}, u32[]{:S(2)}, u32[]{:S(2)}) collective-permute-start(f32[16,512]{1,0:T(8,128)S(1)} %get-tuple-element.41), channel_id=1, source_target_pairs={{0,24},{4,28},{8,16},{12,20},{16,8},{20,12},{24,0},{28,4},{1,25},{... | collective-permute-start | bytes 98312 | tf_op jit(solution)/shard_map/ppermute | solution.py:422
  35.4 0.5 %collective-permute-start.12 = (f32[16,512]{1,0:T(8,128)S(1)}, f32[16,512]{1,0:T(8,128)S(1)}, u32[]{:S(2)}, u32[]{:S(2)}) collective-permute-start(f32[16,512]{1,0:T(8,128)S(1)} %get-tuple-element.42), channel_id=1, source_target_pairs={{0,16},{4,20},{8,24},{12,28},{16,0},{20,4},{24,8},{28,12},{1,17},{... | collective-permute-start | bytes 98312 | tf_op jit(solution)/shard_map/ppermute | solution.py:422
  35.9 0.0 collective-permute-done.10.refs_3_
  35.9 0.9 %collective-permute-start.13 = (f32[16,512]{1,0:T(8,128)S(1)}, f32[16,512]{1,0:T(8,128)S(1)}, u32[]{:S(2)}, u32[]{:S(2)}) collective-permute-start(f32[16,512]{1,0:T(8,128)S(1)} %get-tuple-element.43), channel_id=1, source_target_pairs={{0,8},{4,12},{8,0},{12,4},{16,24},{20,28},{24,16},{28,20},{1,9},{5... | collective-permute-start | bytes 98312 | tf_op jit(solution)/shard_map/ppermute | solution.py:422
  36.9 0.0 collective-permute-done.8.refs_1_
  36.9 0.0 collective-permute-done.9.refs_2_
  36.9 1.7 %shard_map.60 = bf16[16,2,64,256]{3,2,1,0:T(8,128)(2,1)} custom-call(bf16[16,64,256]{2,1,0:T(8,128)(2,1)S(1)} %shard_map.58.even_ref, bf16[144,256]{1,0:T(8,128)(2,1)S(1)} %get-tuple-element.37.taps_ref, bf16[32,4096]{1,0:T(8,128)(2,1)S(1)} %shard_map.53.refs_0_, bf16[48,4096]{1,0:T(8,128)(2,1)S(1)} %collective-permute-done.8.refs_1_, ...), custom_call_target="tpu_custom_call" | custom-call | flops 301989888 | bytes 4194304 | tf_op jit(solution)/shard_map/pallas_call | solution.py:320
  38.6 0.0 collective-permute-done.11.refs_1_
  38.6 0.8 %collective-permute-done.12.refs_2_ = f32[16,512]{1,0:T(8,128)S(1)} collective-permute-done((f32[16,512]{1,0:T(8,128)S(1)}, f32[16,512]{1,0:T(8,128)S(1)}, u32[]{:S(2)}, u32[]{:S(2)}) %collective-permute-start.12) | collective-permute-done | bytes 32800 | tf_op jit(solution)/shard_map/ppermute | solution.py:422
  39.4 0.5 %collective-permute-done.13.refs_3_ = f32[16,512]{1,0:T(8,128)S(1)} collective-permute-done((f32[16,512]{1,0:T(8,128)S(1)}, f32[16,512]{1,0:T(8,128)S(1)}, u32[]{:S(2)}, u32[]{:S(2)}) %collective-permute-start.13) | collective-permute-done | bytes 32800 | tf_op jit(solution)/shard_map/ppermute | solution.py:422
  39.8 0.8 %shard_map.61 = f32[16,16,27]{2,1,0:T(8,128)} custom-call(f32[16,512]{1,0:T(8,128)S(1)} %get-tuple-element.40.refs_0_, f32[16,512]{1,0:T(8,128)S(1)} %collective-permute-done.11.refs_1_, f32[16,512]{1,0:T(8,128)S(1)} %collective-permute-done.12.refs_2_, f32[16,512]{1,0:T(8,128)S(1)} %collective-permute-done.13.refs_3_), custom_call_target="tpu_custom_call" | custom-call | flops 65536 | bytes 524288 | tf_op jit(solution)/shard_map/pallas_call | solution.py:320
  (4 shorter events, 0.1 us)
Async XLA Ops:
  0.6 1.0 %copy-start = (bf16[27,64,128]{2,1,0:T(8,128)(2,1)S(1)}, bf16[27,64,128]{2,1,0:T(8,128)(2,1)}, u32[]{:S(2)}) copy-start(bf16[27,64,128]{2,1,0:T(8,128)(2,1)} %param.5) | copy-start | bytes 1327108
  0.6 3.2 %copy-start.1 = (bf16[32,1,32,128]{3,2,1,0:T(8,128)(2,1)S(1)}, bf16[32,1,32,128]{3,2,1,0:T(8,128)(2,1)}, u32[]{:S(2)}) copy-start(bf16[32,1,32,128]{3,2,1,0:T(8,128)(2,1)} %refs_0_.3) | copy-start | bytes 786436
  0.7 26.5 %collective-permute-start.2 = (bf16[16,2,64,256]{3,2,1,0:T(8,128)(2,1)}, bf16[16,2,64,256]{3,2,1,0:T(8,128)(2,1)S(1)}, u32[]{:S(2)}, u32[]{:S(2)}) collective-permute-start(bf16[16,2,64,256]{3,2,1,0:T(8,128)(2,1)} %refs_0_.2), channel_id=1, source_target_pairs={{0,4},{4,8},{8,12},{12,16},{16,20},{20,24},{24,28},{28,0},{1,5},{5... | collective-permute-start | bytes 3145736 | tf_op jit(solution)/shard_map/ppermute | solution.py:369
  1.7 1.2 %copy-start.2 = (bf16[16,2,64,256]{3,2,1,0:T(8,128)(2,1)S(1)}, bf16[16,2,64,256]{3,2,1,0:T(8,128)(2,1)}, u32[]{:S(2)}) copy-start(bf16[16,2,64,256]{3,2,1,0:T(8,128)(2,1)} %refs_0_.2) | copy-start | bytes 3145732
  3.8 15.8 %collective-permute-start.4 = (bf16[32,1,32,128]{3,2,1,0:T(8,128)(2,1)S(1)}, bf16[32,1,32,128]{3,2,1,0:T(8,128)(2,1)S(1)}, u32[]{:S(2)}, u32[]{:S(2)}) collective-permute-start(bf16[32,1,32,128]{3,2,1,0:T(8,128)(2,1)S(1)} %copy-done.1), channel_id=1, source_target_pairs={{0,1},{1,0},{2,3},{3,2},{4,5},{5,4},{6,7},{7,6},{8,9},{9,8},{10,11... | collective-permute-start | bytes 786440 | tf_op jit(solution)/shard_map/ppermute | solution.py:357
  6.9 9.2 %collective-permute-start = (bf16[16,1,32,128]{3,2,1,0:T(8,128)(2,1)S(1)}, bf16[16,1,32,128]{3,2,1,0:T(8,128)(2,1)S(1)}, u32[]{:S(2)}, u32[]{:S(2)}) collective-permute-start(bf16[16,1,32,128]{3,2,1,0:T(8,128)(2,1)S(1)} %slice.6), channel_id=1, source_target_pairs={{0,2},{1,3},{2,0},{3,1},{4,6},{5,7},{6,4},{7,5},{8,10},{9,11},{10,... | collective-permute-start | bytes 393224 | tf_op jit(solution)/shard_map/ppermute | solution.py:355
  9.6 17.5 %collective-permute-start.3 = (bf16[32,1,32,128]{3,2,1,0:T(8,128)(2,1)S(1)}, bf16[32,1,32,128]{3,2,1,0:T(8,128)(2,1)S(1)}, u32[]{:S(2)}, u32[]{:S(2)}) collective-permute-start(bf16[32,1,32,128]{3,2,1,0:T(8,128)(2,1)S(1)} %copy-done.1), channel_id=1, source_target_pairs={{4,0},{8,4},{12,8},{16,12},{20,16},{24,20},{28,24},{0,28},{5,1},{9... | collective-permute-start | bytes 786440 | tf_op jit(solution)/shard_map/ppermute | solution.py:370
  16.1 9.1 %collective-permute-start.5 = (bf16[16,1,32,128]{3,2,1,0:T(8,128)(2,1)S(1)}, bf16[16,1,32,128]{3,2,1,0:T(8,128)(2,1)S(1)}, u32[]{:S(2)}, u32[]{:S(2)}) collective-permute-start(bf16[16,1,32,128]{3,2,1,0:T(8,128)(2,1)S(1)} %slice.7), channel_id=1, source_target_pairs={{0,2},{1,3},{2,0},{3,1},{4,6},{5,7},{6,4},{7,5},{8,10},{9,11},{10,... | collective-permute-start | bytes 393224 | tf_op jit(solution)/shard_map/ppermute | solution.py:359
  19.5 7.8 %collective-permute-start.1 = (bf16[16,1,32,128]{3,2,1,0:T(8,128)(2,1)S(1)}, bf16[16,1,32,128]{3,2,1,0:T(8,128)(2,1)S(1)}, u32[]{:S(2)}, u32[]{:S(2)}) collective-permute-start(bf16[16,1,32,128]{3,2,1,0:T(8,128)(2,1)S(1)} %collective-permute-done.refs_1_), channel_id=1, source_target_pairs={{0,1},{1,0},{2,3},{3,2},{4,5},{5,4},{6,7},{7,6},{8,9},{9,8},{10,11... | collective-permute-start | bytes 393224 | tf_op jit(solution)/shard_map/ppermute | solution.py:360
  19.8 17.1 %collective-permute-start.8 = (bf16[48,4096]{1,0:T(8,128)(2,1)S(1)}, bf16[48,4096]{1,0:T(8,128)(2,1)S(1)}, u32[]{:S(2)}, u32[]{:S(2)}) collective-permute-start(bf16[48,4096]{1,0:T(8,128)(2,1)S(1)} %shard_map.54.refs_3_.refs_1_.refs_5_), channel_id=1, source_target_pairs={{4,0},{8,4},{12,8},{16,12},{20,16},{24,20},{28,24},{0,28},{5,1},{9... | collective-permute-start | bytes 1179656 | tf_op jit(solution)/shard_map/ppermute | solution.py:384
  25.2 5.0 %collective-permute-start.6 = (bf16[16,1,32,128]{3,2,1,0:T(8,128)(2,1)S(1)}, bf16[16,1,32,128]{3,2,1,0:T(8,128)(2,1)S(1)}, u32[]{:S(2)}, u32[]{:S(2)}) collective-permute-start(bf16[16,1,32,128]{3,2,1,0:T(8,128)(2,1)S(1)} %collective-permute-done.5.refs_0_), channel_id=1, source_target_pairs={{0,1},{1,0},{2,3},{3,2},{4,5},{5,4},{6,7},{7,6},{8,9},{9,8},{10,11... | collective-permute-start | bytes 393224 | tf_op jit(solution)/shard_map/ppermute | solution.py:361
  27.4 9.5 %collective-permute-start.9 = (bf16[32,4096]{1,0:T(8,128)(2,1)S(1)}, bf16[32,4096]{1,0:T(8,128)(2,1)S(1)}, u32[]{:S(2)}, u32[]{:S(2)}) collective-permute-start(bf16[32,4096]{1,0:T(8,128)(2,1)S(1)} %shard_map.55.refs_4_.refs_2_.refs_6_), channel_id=1, source_target_pairs={{4,0},{8,4},{12,8},{16,12},{20,16},{24,20},{28,24},{0,28},{5,1},{9... | collective-permute-start | bytes 786440 | tf_op jit(solution)/shard_map/ppermute | solution.py:384
  31.2 1.8 %collective-permute-start.7 = (f32[64,512]{1,0:T(8,128)S(1)}, f32[64,512]{1,0:T(8,128)S(1)}, u32[]{:S(2)}, u32[]{:S(2)}) collective-permute-start(f32[64,512]{1,0:T(8,128)S(1)} %get-tuple-element.32), channel_id=1, source_target_pairs={{0,4},{4,0},{8,12},{12,8},{16,20},{20,16},{24,28},{28,24},{1,5},{5... | collective-permute-start | bytes 393224 | tf_op jit(solution)/shard_map/ppermute | solution.py:404
  31.3 4.6 %collective-permute-start.10 = (bf16[16,4096]{1,0:T(8,128)(2,1)S(1)}, bf16[16,4096]{1,0:T(8,128)(2,1)S(1)}, u32[]{:S(2)}, u32[]{:S(2)}) collective-permute-start(bf16[16,4096]{1,0:T(8,128)(2,1)S(1)} %shard_map.56.refs_5_.refs_3_.refs_7_), channel_id=1, source_target_pairs={{4,0},{8,4},{12,8},{16,12},{20,16},{24,20},{28,24},{0,28},{5,1},{9... | collective-permute-start | bytes 393224 | tf_op jit(solution)/shard_map/ppermute | solution.py:384
  33.1 5.5 %collective-permute-start.11 = (f32[16,512]{1,0:T(8,128)S(1)}, f32[16,512]{1,0:T(8,128)S(1)}, u32[]{:S(2)}, u32[]{:S(2)}) collective-permute-start(f32[16,512]{1,0:T(8,128)S(1)} %get-tuple-element.41), channel_id=1, source_target_pairs={{0,24},{4,28},{8,16},{12,20},{16,8},{20,12},{24,0},{28,4},{1,25},{... | collective-permute-start | bytes 98312 | tf_op jit(solution)/shard_map/ppermute | solution.py:422
  35.4 3.9 %collective-permute-start.12 = (f32[16,512]{1,0:T(8,128)S(1)}, f32[16,512]{1,0:T(8,128)S(1)}, u32[]{:S(2)}, u32[]{:S(2)}) collective-permute-start(f32[16,512]{1,0:T(8,128)S(1)} %get-tuple-element.42), channel_id=1, source_target_pairs={{0,16},{4,20},{8,24},{12,28},{16,0},{20,4},{24,8},{28,12},{1,17},{... | collective-permute-start | bytes 98312 | tf_op jit(solution)/shard_map/ppermute | solution.py:422
  35.9 3.9 %collective-permute-start.13 = (f32[16,512]{1,0:T(8,128)S(1)}, f32[16,512]{1,0:T(8,128)S(1)}, u32[]{:S(2)}, u32[]{:S(2)}) collective-permute-start(f32[16,512]{1,0:T(8,128)S(1)} %get-tuple-element.43), channel_id=1, source_target_pairs={{0,8},{4,12},{8,0},{12,4},{16,24},{20,28},{24,16},{28,20},{1,9},{5... | collective-permute-start | bytes 98312 | tf_op jit(solution)/shard_map/ppermute | solution.py:422

commit v17 on v14

--- a/solution.py
+++ b/solution.py
@@ -381,7 +381,7 @@
     outs = channels // depth
     half_terms = jax.ShapeDtypeStruct((channels // 2, 32 * chans), F32)
     keep, send = call(
-        lambda *refs: weight_kernel(outs, cols, 8 * cols, *refs),
+        lambda *refs: weight_kernel(outs, cols, 4 * cols, *refs),
         (half_terms, half_terms),
         views,
         behind_views,

time: 37.3 us -> 37.3 us (level)
  transfers between devices with their start and end apart: 11 -> 11, of which waited for: 5 -> 6; matrix products, arithmetic and copies ran while one was open for 0% -> 0% of each run, Pallas kernels for 14% -> 14%
where the time goes in v17:
time: 37.3 us; the launch traced here: 37.1 us
  starting transfers between devices  15.6 us (42%)
  waiting for transfers between devices  12.6 us (34%)
  Pallas kernels  5.94 us (16%)
  local copies, waits for them, and re-layouts  2.24 us (6%)
  between operations  0.73 us (2%)
    ppermute x3, waiting for transfers between devices, shards(): lax.ppermute(got[mask - low], 'chan', [(i, i ^ low) for i in range(count)])  9.81 us
    ppermute x3, starting transfers between devices, shards(): lax.ppermute(got[mask - low], 'chan', [(i, i ^ low) for i in range(count)])  7.07 us
    pallas_call x11, Pallas kernels, call(): pl.pallas_call(kernel, out_shape=out_shape, in_specs=[VMEM] * len(args),...  5.94 us
    ppermute x3, starting transfers between devices, shards(): lax.ppermute(terms[k - 1], 'depth', [(i, i ^ 2 * k) for i in range(depth)])  3.57 us
    ppermute x1, starting transfers between devices, shards(): next_own = lax.ppermute(grad_out, 'depth', nearer)  2.28 us
    unnamed x6, local copies, waits for them, and re-layouts  2.21 us
    ppermute x3, waiting for transfers between devices, shards(): lax.ppermute(terms[k - 1], 'depth', [(i, i ^ 2 * k) for i in range(depth)])  2.2 us
    ppermute x2, starting transfers between devices, shards(): lax.ppermute(part, 'depth', nearer)  1.74 us
  transfers between devices with their start and end apart: 11, of which 6 were waited for; matrix products, arithmetic and copies ran while one was open for 0% of the time, Pallas kernels for 14%

profile of v17, /device:TPU:0, one launch (start us, length us, event | category | flops | bytes accessed | tf_op | source)
XLA Modules:
  0.0 37.1 jit_solution(16665082814572273362)
XLA Ops:
  0.6 0.0 copy-start
  0.6 0.5 %collective-permute-start.2 = (bf16[16,2,64,256]{3,2,1,0:T(8,128)(2,1)}, bf16[16,2,64,256]{3,2,1,0:T(8,128)(2,1)S(1)}, u32[]{:S(2)}, u32[]{:S(2)}) collective-permute-start(bf16[16,2,64,256]{3,2,1,0:T(8,128)(2,1)} %refs_0_.2), channel_id=1, source_target_pairs={{0,4},{4,8},{8,12},{12,16},{16,20},{20,24},{24,28},{28,0},{1,5},{5... | collective-permute-start | bytes 3145736 | tf_op jit(solution)/shard_map/ppermute | solution.py:366
  1.1 3.7 %collective-permute-start.1 = (bf16[32,1,32,128]{3,2,1,0:T(8,128)(2,1)}, bf16[32,1,32,128]{3,2,1,0:T(8,128)(2,1)S(1)}, u32[]{:S(2)}, u32[]{:S(2)}) collective-permute-start(bf16[32,1,32,128]{3,2,1,0:T(8,128)(2,1)} %refs_0_.3), channel_id=1, source_target_pairs={{0,2},{1,3},{2,0},{3,1},{4,6},{5,7},{6,4},{7,5},{8,10},{9,11},{10,... | collective-permute-start | bytes 786440 | tf_op jit(solution)/shard_map/ppermute | solution.py:358
  4.8 2.3 %collective-permute-start.3 = (bf16[32,1,32,128]{3,2,1,0:T(8,128)(2,1)}, bf16[32,1,32,128]{3,2,1,0:T(8,128)(2,1)S(1)}, u32[]{:S(2)}, u32[]{:S(2)}) collective-permute-start(bf16[32,1,32,128]{3,2,1,0:T(8,128)(2,1)} %refs_0_.3), channel_id=1, source_target_pairs={{4,0},{8,4},{12,8},{16,12},{20,16},{24,20},{28,24},{0,28},{5,1},{9... | collective-permute-start | bytes 786440 | tf_op jit(solution)/shard_map/ppermute | solution.py:367
  7.1 1.6 %collective-permute-start = (bf16[32,1,32,128]{3,2,1,0:T(8,128)(2,1)}, bf16[32,1,32,128]{3,2,1,0:T(8,128)(2,1)S(1)}, u32[]{:S(2)}, u32[]{:S(2)}) collective-permute-start(bf16[32,1,32,128]{3,2,1,0:T(8,128)(2,1)} %refs_0_.3), channel_id=1, source_target_pairs={{0,1},{1,0},{2,3},{3,2},{4,5},{5,4},{6,7},{7,6},{8,9},{9,8},{10,11... | collective-permute-start | bytes 786440 | tf_op jit(solution)/shard_map/ppermute | solution.py:358
  8.7 0.0 copy-start.1
  8.7 1.0 %copy-done.1 = bf16[32,1,32,128]{3,2,1,0:T(8,128)(2,1)S(1)} copy-done((bf16[32,1,32,128]{3,2,1,0:T(8,128)(2,1)S(1)}, bf16[32,1,32,128]{3,2,1,0:T(8,128)(2,1)}, u32[]{:S(2)}) %copy-start.1) | copy-done | bytes 262168
  9.7 0.1 shard_map.52.refs_2_.refs_0_.refs_3_
  9.8 0.0 copy-done
  9.8 0.0 copy-start.2
  9.9 1.2 %copy-done.2 = bf16[16,2,64,256]{3,2,1,0:T(8,128)(2,1)S(1)} copy-done((bf16[16,2,64,256]{3,2,1,0:T(8,128)(2,1)S(1)}, bf16[16,2,64,256]{3,2,1,0:T(8,128)(2,1)}, u32[]{:S(2)}) %copy-start.2) | copy-done | bytes 1048600
  11.1 0.9 %shard_map.50 = (bf16[192,4096]{1,0:T(8,128)(2,1)S(1)}, bf16[144,128]{1,0:T(8,128)(2,1)S(1)}, bf16[144,256]{1,0:T(8,128)(2,1)S(1)}) custom-call(bf16[16,2,64,256]{3,2,1,0:T(8,128)(2,1)S(1)} %copy-done.2, bf16[27,16,128]{2,1,0:T(8,128)(2,1)S(1)} %constant_dynamic-slice_fusion.refs_1_), custom_call_target="tpu_custom_call" | custom-call | flops 536870912 | bytes 4194304 | tf_op jit(solution)/shard_map/pallas_call | solution.py:320
  12.0 5.1 %collective-permute-done.1.refs_1_ = bf16[32,1,32,128]{3,2,1,0:T(8,128)(2,1)S(1)} collective-permute-done((bf16[32,1,32,128]{3,2,1,0:T(8,128)(2,1)}, bf16[32,1,32,128]{3,2,1,0:T(8,128)(2,1)S(1)}, u32[]{:S(2)}, u32[]{:S(2)}) %collective-permute-start.1) | collective-permute-done | bytes 262176 | tf_op jit(solution)/shard_map/ppermute | solution.py:358
  17.0 1.8 %collective-permute-start.4 = (bf16[32,1,32,128]{3,2,1,0:T(8,128)(2,1)S(1)}, bf16[32,1,32,128]{3,2,1,0:T(8,128)(2,1)S(1)}, u32[]{:S(2)}, u32[]{:S(2)}) collective-permute-start(bf16[32,1,32,128]{3,2,1,0:T(8,128)(2,1)S(1)} %collective-permute-done.1.refs_1_), channel_id=1, source_target_pairs={{0,1},{1,0},{2,3},{3,2},{4,5},{5,4},{6,7},{7,6},{8,9},{9,8},{10,11... | collective-permute-start | bytes 786440 | tf_op jit(solution)/shard_map/ppermute | solution.py:358
  18.9 0.0 collective-permute-done.3.refs_0_
  18.9 0.1 shard_map.53.refs_0_
  19.0 0.5 %collective-permute-done.2.behind_ref = bf16[16,2,64,256]{3,2,1,0:T(8,128)(2,1)S(1)} collective-permute-done((bf16[16,2,64,256]{3,2,1,0:T(8,128)(2,1)}, bf16[16,2,64,256]{3,2,1,0:T(8,128)(2,1)S(1)}, u32[]{:S(2)}, u32[]{:S(2)}) %collective-permute-start.2) | collective-permute-done | bytes 1048608 | tf_op jit(solution)/shard_map/ppermute | solution.py:366
  19.5 0.1 shard_map.51.refs_1_
  19.6 0.0 collective-permute-done.refs_0_
  19.6 0.3 shard_map.54.refs_3_.refs_1_.refs_4_
  19.9 1.5 %collective-permute-start.6 = (bf16[64,4096]{1,0:T(8,128)(2,1)S(1)}, bf16[64,4096]{1,0:T(8,128)(2,1)S(1)}, u32[]{:S(2)}, u32[]{:S(2)}) collective-permute-start(bf16[64,4096]{1,0:T(8,128)(2,1)S(1)} %shard_map.54.refs_3_.refs_1_.refs_4_), channel_id=1, source_target_pairs={{4,0},{8,4},{12,8},{16,12},{20,16},{24,20},{28,24},{0,28},{5,1},{9... | collective-permute-start | bytes 1572872 | tf_op jit(solution)/shard_map/ppermute | solution.py:380
  21.4 4.8 %collective-permute-done.4.refs_0_ = bf16[32,1,32,128]{3,2,1,0:T(8,128)(2,1)S(1)} collective-permute-done((bf16[32,1,32,128]{3,2,1,0:T(8,128)(2,1)S(1)}, bf16[32,1,32,128]{3,2,1,0:T(8,128)(2,1)S(1)}, u32[]{:S(2)}, u32[]{:S(2)}) %collective-permute-start.4) | collective-permute-done | bytes 262176 | tf_op jit(solution)/shard_map/ppermute | solution.py:358
  26.2 0.1 shard_map.55.refs_4_.refs_2_.refs_5_
  26.3 0.2 collective-permute-start.7
  26.5 0.9 %shard_map.56 = (f32[64,512]{1,0:T(8,128)S(1)}, f32[64,512]{1,0:T(8,128)S(1)}) custom-call(bf16[192,4096]{1,0:T(8,128)(2,1)S(1)} %get-tuple-element.24.refs_0_, bf16[96,4096]{1,0:T(8,128)(2,1)S(1)} %shard_map.51.refs_1_, bf16[32,4096]{1,0:T(8,128)(2,1)S(1)} %shard_map.52.refs_2_.refs_0_.refs_3_, bf16[64,4096]{1,0:T(8,128)(2,1)S(1)} %shard_map.54.refs_3_.refs_1_.refs_4_, ...), custom_call_target="tpu_custom_call" | custom-call | flops 452984832 | bytes 8388608 | tf_op jit(solution)/shard_map/pallas_call | solution.py:320
  27.5 0.4 %collective-permute-start.5 = (f32[64,512]{1,0:T(8,128)S(1)}, f32[64,512]{1,0:T(8,128)S(1)}, u32[]{:S(2)}, u32[]{:S(2)}) collective-permute-start(f32[64,512]{1,0:T(8,128)S(1)} %get-tuple-element.30), channel_id=1, source_target_pairs={{0,4},{4,0},{8,12},{12,8},{16,20},{20,16},{24,28},{28,24},{1,5},{5... | collective-permute-start | bytes 393224 | tf_op jit(solution)/shard_map/ppermute | solution.py:400
  27.9 0.9 %shard_map.57.even_ref = bf16[16,64,256]{2,1,0:T(8,128)(2,1)S(1)} custom-call(bf16[144,128]{1,0:T(8,128)(2,1)S(1)} %get-tuple-element.31.taps_ref, bf16[32,4096]{1,0:T(8,128)(2,1)S(1)} %shard_map.52.refs_2_.refs_0_.refs_3_, bf16[64,4096]{1,0:T(8,128)(2,1)S(1)} %shard_map.54.refs_3_.refs_1_.refs_4_, bf16[32,4096]{1,0:T(8,128)(2,1)S(1)} %shard_map.55.refs_4_.refs_2_.refs_5_), custom_call_target="tpu_custom_call" | custom-call | flops 150994944 | bytes 4194304 | tf_op jit(solution)/shard_map/pallas_call | solution.py:320
  28.8 0.1 collective-permute-done.5.other_ref
  28.9 1.7 %collective-permute-start.10 = (f32[16,512]{1,0:T(8,128)S(1)}, f32[16,512]{1,0:T(8,128)S(1)}, u32[]{:S(2)}, u32[]{:S(2)}) collective-permute-start(f32[16,512]{1,0:T(8,128)S(1)} %get-tuple-element.41), channel_id=1, source_target_pairs={{0,8},{4,12},{8,0},{12,4},{16,24},{20,28},{24,16},{28,20},{1,9},{5... | collective-permute-start | bytes 98312 | tf_op jit(solution)/shard_map/ppermute | solution.py:418
  30.6 1.9 %collective-permute-start.8 = (f32[16,512]{1,0:T(8,128)S(1)}, f32[16,512]{1,0:T(8,128)S(1)}, u32[]{:S(2)}, u32[]{:S(2)}) collective-permute-start(f32[16,512]{1,0:T(8,128)S(1)} %get-tuple-element.39), channel_id=1, source_target_pairs={{0,24},{4,28},{8,16},{12,20},{16,8},{20,12},{24,0},{28,4},{1,25},{... | collective-permute-start | bytes 98312 | tf_op jit(solution)/shard_map/ppermute | solution.py:418
  32.4 0.0 collective-permute-start.9
  32.5 0.0 collective-permute-done.7.refs_2_
  32.5 0.0 collective-permute-done.6.refs_1_
  32.5 1.7 %shard_map.59 = bf16[16,2,64,256]{3,2,1,0:T(8,128)(2,1)} custom-call(bf16[16,64,256]{2,1,0:T(8,128)(2,1)S(1)} %shard_map.57.even_ref, bf16[144,256]{1,0:T(8,128)(2,1)S(1)} %get-tuple-element.35.taps_ref, bf16[32,4096]{1,0:T(8,128)(2,1)S(1)} %shard_map.53.refs_0_, bf16[64,4096]{1,0:T(8,128)(2,1)S(1)} %collective-permute-done.6.refs_1_, ...), custom_call_target="tpu_custom_call" | custom-call | flops 301989888 | bytes 4194304 | tf_op jit(solution)/shard_map/pallas_call | solution.py:320
  34.2 0.0 collective-permute-done.10.refs_3_
  34.2 1.2 %collective-permute-done.8.refs_1_ = f32[16,512]{1,0:T(8,128)S(1)} collective-permute-done((f32[16,512]{1,0:T(8,128)S(1)}, f32[16,512]{1,0:T(8,128)S(1)}, u32[]{:S(2)}, u32[]{:S(2)}) %collective-permute-start.8) | collective-permute-done | bytes 32800 | tf_op jit(solution)/shard_map/ppermute | solution.py:418
  35.4 1.0 %collective-permute-done.9.refs_2_ = f32[16,512]{1,0:T(8,128)S(1)} collective-permute-done((f32[16,512]{1,0:T(8,128)S(1)}, f32[16,512]{1,0:T(8,128)S(1)}, u32[]{:S(2)}, u32[]{:S(2)}) %collective-permute-start.9) | collective-permute-done | bytes 32800 | tf_op jit(solution)/shard_map/ppermute | solution.py:418
  36.4 0.8 %shard_map.60 = f32[16,16,27]{2,1,0:T(8,128)} custom-call(f32[16,512]{1,0:T(8,128)S(1)} %get-tuple-element.38.refs_0_, f32[16,512]{1,0:T(8,128)S(1)} %collective-permute-done.8.refs_1_, f32[16,512]{1,0:T(8,128)S(1)} %collective-permute-done.9.refs_2_, f32[16,512]{1,0:T(8,128)S(1)} %collective-permute-done.10.refs_3_), custom_call_target="tpu_custom_call" | custom-call | flops 65536 | bytes 524288 | tf_op jit(solution)/shard_map/pallas_call | solution.py:320
  (2 shorter events, 0.0 us)
Async XLA Ops:
  0.6 9.2 %copy-start = (bf16[27,64,128]{2,1,0:T(8,128)(2,1)S(1)}, bf16[27,64,128]{2,1,0:T(8,128)(2,1)}, u32[]{:S(2)}) copy-start(bf16[27,64,128]{2,1,0:T(8,128)(2,1)} %param.5) | copy-start | bytes 1327108
  0.6 18.9 %collective-permute-start.2 = (bf16[16,2,64,256]{3,2,1,0:T(8,128)(2,1)}, bf16[16,2,64,256]{3,2,1,0:T(8,128)(2,1)S(1)}, u32[]{:S(2)}, u32[]{:S(2)}) collective-permute-start(bf16[16,2,64,256]{3,2,1,0:T(8,128)(2,1)} %refs_0_.2), channel_id=1, source_target_pairs={{0,4},{4,8},{8,12},{12,16},{16,20},{20,24},{24,28},{28,0},{1,5},{5... | collective-permute-start | bytes 3145736 | tf_op jit(solution)/shard_map/ppermute | solution.py:366
  1.1 15.9 %collective-permute-start.1 = (bf16[32,1,32,128]{3,2,1,0:T(8,128)(2,1)}, bf16[32,1,32,128]{3,2,1,0:T(8,128)(2,1)S(1)}, u32[]{:S(2)}, u32[]{:S(2)}) collective-permute-start(bf16[32,1,32,128]{3,2,1,0:T(8,128)(2,1)} %refs_0_.3), channel_id=1, source_target_pairs={{0,2},{1,3},{2,0},{3,1},{4,6},{5,7},{6,4},{7,5},{8,10},{9,11},{10,... | collective-permute-start | bytes 786440 | tf_op jit(solution)/shard_map/ppermute | solution.py:358
  4.8 14.0 %collective-permute-start.3 = (bf16[32,1,32,128]{3,2,1,0:T(8,128)(2,1)}, bf16[32,1,32,128]{3,2,1,0:T(8,128)(2,1)S(1)}, u32[]{:S(2)}, u32[]{:S(2)}) collective-permute-start(bf16[32,1,32,128]{3,2,1,0:T(8,128)(2,1)} %refs_0_.3), channel_id=1, source_target_pairs={{4,0},{8,4},{12,8},{16,12},{20,16},{24,20},{28,24},{0,28},{5,1},{9... | collective-permute-start | bytes 786440 | tf_op jit(solution)/shard_map/ppermute | solution.py:367
  7.1 12.5 %collective-permute-start = (bf16[32,1,32,128]{3,2,1,0:T(8,128)(2,1)}, bf16[32,1,32,128]{3,2,1,0:T(8,128)(2,1)S(1)}, u32[]{:S(2)}, u32[]{:S(2)}) collective-permute-start(bf16[32,1,32,128]{3,2,1,0:T(8,128)(2,1)} %refs_0_.3), channel_id=1, source_target_pairs={{0,1},{1,0},{2,3},{3,2},{4,5},{5,4},{6,7},{7,6},{8,9},{9,8},{10,11... | collective-permute-start | bytes 786440 | tf_op jit(solution)/shard_map/ppermute | solution.py:358
  8.7 1.0 %copy-start.1 = (bf16[32,1,32,128]{3,2,1,0:T(8,128)(2,1)S(1)}, bf16[32,1,32,128]{3,2,1,0:T(8,128)(2,1)}, u32[]{:S(2)}) copy-start(bf16[32,1,32,128]{3,2,1,0:T(8,128)(2,1)} %refs_0_.3) | copy-start | bytes 786436
  9.8 1.2 %copy-start.2 = (bf16[16,2,64,256]{3,2,1,0:T(8,128)(2,1)S(1)}, bf16[16,2,64,256]{3,2,1,0:T(8,128)(2,1)}, u32[]{:S(2)}) copy-start(bf16[16,2,64,256]{3,2,1,0:T(8,128)(2,1)} %refs_0_.2) | copy-start | bytes 3145732
  17.0 9.1 %collective-permute-start.4 = (bf16[32,1,32,128]{3,2,1,0:T(8,128)(2,1)S(1)}, bf16[32,1,32,128]{3,2,1,0:T(8,128)(2,1)S(1)}, u32[]{:S(2)}, u32[]{:S(2)}) collective-permute-start(bf16[32,1,32,128]{3,2,1,0:T(8,128)(2,1)S(1)} %collective-permute-done.1.refs_1_), channel_id=1, source_target_pairs={{0,1},{1,0},{2,3},{3,2},{4,5},{5,4},{6,7},{7,6},{8,9},{9,8},{10,11... | collective-permute-start | bytes 786440 | tf_op jit(solution)/shard_map/ppermute | solution.py:358
  19.9 12.6 %collective-permute-start.6 = (bf16[64,4096]{1,0:T(8,128)(2,1)S(1)}, bf16[64,4096]{1,0:T(8,128)(2,1)S(1)}, u32[]{:S(2)}, u32[]{:S(2)}) collective-permute-start(bf16[64,4096]{1,0:T(8,128)(2,1)S(1)} %shard_map.54.refs_3_.refs_1_.refs_4_), channel_id=1, source_target_pairs={{4,0},{8,4},{12,8},{16,12},{20,16},{24,20},{28,24},{0,28},{5,1},{9... | collective-permute-start | bytes 1572872 | tf_op jit(solution)/shard_map/ppermute | solution.py:380
  26.3 6.2 %collective-permute-start.7 = (bf16[32,4096]{1,0:T(8,128)(2,1)S(1)}, bf16[32,4096]{1,0:T(8,128)(2,1)S(1)}, u32[]{:S(2)}, u32[]{:S(2)}) collective-permute-start(bf16[32,4096]{1,0:T(8,128)(2,1)S(1)} %shard_map.55.refs_4_.refs_2_.refs_5_), channel_id=1, source_target_pairs={{4,0},{8,4},{12,8},{16,12},{20,16},{24,20},{28,24},{0,28},{5,1},{9... | collective-permute-start | bytes 786440 | tf_op jit(solution)/shard_map/ppermute | solution.py:380
  27.5 1.4 %collective-permute-start.5 = (f32[64,512]{1,0:T(8,128)S(1)}, f32[64,512]{1,0:T(8,128)S(1)}, u32[]{:S(2)}, u32[]{:S(2)}) collective-permute-start(f32[64,512]{1,0:T(8,128)S(1)} %get-tuple-element.30), channel_id=1, source_target_pairs={{0,4},{4,0},{8,12},{12,8},{16,20},{20,16},{24,28},{28,24},{1,5},{5... | collective-permute-start | bytes 393224 | tf_op jit(solution)/shard_map/ppermute | solution.py:400
  28.9 5.3 %collective-permute-start.10 = (f32[16,512]{1,0:T(8,128)S(1)}, f32[16,512]{1,0:T(8,128)S(1)}, u32[]{:S(2)}, u32[]{:S(2)}) collective-permute-start(f32[16,512]{1,0:T(8,128)S(1)} %get-tuple-element.41), channel_id=1, source_target_pairs={{0,8},{4,12},{8,0},{12,4},{16,24},{20,28},{24,16},{28,20},{1,9},{5... | collective-permute-start | bytes 98312 | tf_op jit(solution)/shard_map/ppermute | solution.py:418
  30.6 4.8 %collective-permute-start.8 = (f32[16,512]{1,0:T(8,128)S(1)}, f32[16,512]{1,0:T(8,128)S(1)}, u32[]{:S(2)}, u32[]{:S(2)}) collective-permute-start(f32[16,512]{1,0:T(8,128)S(1)} %get-tuple-element.39), channel_id=1, source_target_pairs={{0,24},{4,28},{8,16},{12,20},{16,8},{20,12},{24,0},{28,4},{1,25},{... | collective-permute-start | bytes 98312 | tf_op jit(solution)/shard_map/ppermute | solution.py:418
  32.4 3.9 %collective-permute-start.9 = (f32[16,512]{1,0:T(8,128)S(1)}, f32[16,512]{1,0:T(8,128)S(1)}, u32[]{:S(2)}, u32[]{:S(2)}) collective-permute-start(f32[16,512]{1,0:T(8,128)S(1)} %get-tuple-element.40), channel_id=1, source_target_pairs={{0,16},{4,20},{8,24},{12,28},{16,0},{20,4},{24,8},{28,12},{1,17},{... | collective-permute-start | bytes 98312 | tf_op jit(solution)/shard_map/ppermute | solution.py:418

commit v18 on v17

--- a/solution.py
+++ b/solution.py
@@ -67,7 +67,7 @@
     col = lax.broadcasted_iota(jnp.int32, (channels, channels), 1)
     order = jnp.zeros((channels, channels), F32)
     for slot in range(count):
-        moved = ((here ^ slot) - slot) * part
+        moved = ((here ^ slot ^ (slot >> 1)) - slot) * part
         inside = (col >= slot * part) & (col < (slot + 1) * part)
         order = jnp.where(inside & (row == col + moved), 1.0, order)
     ordered = matmul(weight_ref[...].reshape(27 * chans, channels), order.astype(BF16)).astype(BF16)
@@ -148,7 +148,7 @@
     part = channels // count
     odd_core = lax.axis_index("depth") % 2 == 1
     for slot in range(count):
-        start = (lax.axis_index("chan") ^ slot) * (part // 2)
+        start = (lax.axis_index("chan") ^ slot ^ (slot >> 1)) * (part // 2)
         for at in range(0, part // 2, outs):
             lo = slot * part + 2 * at
             even, odd = turned[lo : lo + outs], turned[lo + outs : lo + 2 * outs]
@@ -350,12 +350,11 @@
         own_weight,
         cost=(2 * 2 * 2 * cells * chans * 8 * cols, 4 << 20),
     )
-    got = {0: grad_out}
-    for mask in sorted(range(1, count), key=lambda mask: (mask & (mask - 1) > 0, -mask)):
-        low = mask & -mask
-        if mask == 3:
-            got[2], views = lax.optimization_barrier((got[2], views))
-        got[mask] = lax.ppermute(got[mask - low], "chan", [(i, i ^ low) for i in range(count)])
+    pairs = lambda mask: [(i, i ^ mask) for i in range(count)]
+    far = lax.ppermute(grad_out, "chan", pairs(3))
+    near = lax.ppermute(grad_out, "chan", pairs(1))
+    far, views = lax.optimization_barrier((far, views))
+    forwarded = lax.ppermute(far, "chan", pairs(1))
     lines = lambda *parts: call(
         lines_kernel,
         jax.ShapeDtypeStruct((sum(part.shape[0] for part in parts), cells), BF16),
@@ -372,10 +371,10 @@
         cost=(2 * 2 * cells * chans * 8 * cols, 2 << 20),
     )
     first_lines, next_first_lines = lines(grad_out), lines(next_own)
-    got[1], views, behind_views, first_lines, next_first_lines = lax.optimization_barrier(
-        (got[1], views, behind_views, first_lines, next_first_lines)
-    )
-    later_lines = [lines(*[got[mask] for mask in range(1, count - 1)]), lines(got[count - 1])]
+    near, views, behind_views, first_lines, next_first_lines = lax.optimization_barrier(
+        (near, views, behind_views, first_lines, next_first_lines)
+    )
+    later_lines = [lines(near, far), lines(forwarded)]
     own_lines = [first_lines] + later_lines
     next_lines = [next_first_lines] + [lax.ppermute(part, "depth", nearer) for part in later_lines]
     outs = channels // depth
@@ -456,7 +455,7 @@
             grad_out.shape[0] % 32 == 0
             and volume.shape[0] == 16
             and grad_out.shape[1] == 1
-            and ring >= 4
+            and ring == 4
             and ring & (ring - 1) == 0
             and depth & (depth - 1) == 0
             and depth % (2 * ring) == 0

time: 37.3 us -> 36.9 us (0.989)
  waiting for transfers between devices: 12.6 us -> 8.98 us
  starting transfers between devices: 15.6 us -> 18.8 us
    ppermute x3, waiting for transfers between devices: 9.81 us -> 5.41 us  [the longest x1 4.26 us: shards(): forwarded = lax.ppermute(far, 'chan', pairs(1))]
    ppermute x3, starting transfers between devices: 7.07 us -> 10.4 us  [the longest x1 5.73 us: shards(): forwarded = lax.ppermute(far, 'chan', pairs(1))]
    ppermute x1, waiting for transfers between devices: 0.53 us -> 1.07 us  [shards(): behind = lax.ppermute(volume, 'depth', farther)]
where the time goes in v18:
time: 36.9 us; the launch traced here: 36.8 us
  starting transfers between devices  18.8 us (51%)
  waiting for transfers between devices  8.98 us (24%)
  Pallas kernels  5.94 us (16%)
  local copies, waits for them, and re-layouts  2.27 us (6%)
  between operations  0.74 us (2%)
    pallas_call x11, Pallas kernels, call(): pl.pallas_call(kernel, out_shape=out_shape, in_specs=[VMEM] * len(args),...  5.94 us
    ppermute x1, starting transfers between devices, shards(): forwarded = lax.ppermute(far, 'chan', pairs(1))  5.73 us
    ppermute x1, starting transfers between devices, shards(): far = lax.ppermute(grad_out, 'chan', pairs(3))  4.68 us
    ppermute x1, waiting for transfers between devices, shards(): forwarded = lax.ppermute(far, 'chan', pairs(1))  4.26 us
    ppermute x3, starting transfers between devices, shards(): lax.ppermute(terms[k - 1], 'depth', [(i, i ^ 2 * k) for i in range(depth)])  3.76 us
    ppermute x1, starting transfers between devices, shards(): next_own = lax.ppermute(grad_out, 'depth', nearer)  2.28 us
    unnamed x6, local copies, waits for them, and re-layouts  2.24 us
    ppermute x3, waiting for transfers between devices, shards(): lax.ppermute(terms[k - 1], 'depth', [(i, i ^ 2 * k) for i in range(depth)])  2.21 us
  transfers between devices with their start and end apart: 11, of which 6 were waited for; matrix products, arithmetic and copies ran while one was open for 0% of the time, Pallas kernels for 14%

profile of v18, /device:TPU:0, one launch (start us, length us, event | category | flops | bytes accessed | tf_op | source)
XLA Modules:
  0.0 36.8 jit_solution(3327614319977778360)
XLA Ops:
  0.6 0.0 copy-start
  0.6 0.5 %collective-permute-start.2 = (bf16[16,2,64,256]{3,2,1,0:T(8,128)(2,1)}, bf16[16,2,64,256]{3,2,1,0:T(8,128)(2,1)S(1)}, u32[]{:S(2)}, u32[]{:S(2)}) collective-permute-start(bf16[16,2,64,256]{3,2,1,0:T(8,128)(2,1)} %refs_0_.2), channel_id=1, source_target_pairs={{0,4},{4,8},{8,12},{12,16},{16,20},{20,24},{24,28},{28,0},{1,5},{5... | collective-permute-start | bytes 3145736 | tf_op jit(solution)/shard_map/ppermute | solution.py:365
  1.1 4.7 %collective-permute-start.1 = (bf16[32,1,32,128]{3,2,1,0:T(8,128)(2,1)}, bf16[32,1,32,128]{3,2,1,0:T(8,128)(2,1)S(1)}, u32[]{:S(2)}, u32[]{:S(2)}) collective-permute-start(bf16[32,1,32,128]{3,2,1,0:T(8,128)(2,1)} %refs_0_.3), channel_id=1, source_target_pairs={{0,3},{1,2},{2,1},{3,0},{4,7},{5,6},{6,5},{7,4},{8,11},{9,10},{10,... | collective-permute-start | bytes 786440 | tf_op jit(solution)/shard_map/ppermute | solution.py:354
  5.8 2.3 %collective-permute-start.3 = (bf16[32,1,32,128]{3,2,1,0:T(8,128)(2,1)}, bf16[32,1,32,128]{3,2,1,0:T(8,128)(2,1)S(1)}, u32[]{:S(2)}, u32[]{:S(2)}) collective-permute-start(bf16[32,1,32,128]{3,2,1,0:T(8,128)(2,1)} %refs_0_.3), channel_id=1, source_target_pairs={{4,0},{8,4},{12,8},{16,12},{20,16},{24,20},{28,24},{0,28},{5,1},{9... | collective-permute-start | bytes 786440 | tf_op jit(solution)/shard_map/ppermute | solution.py:366
  8.1 0.0 collective-permute-start
  8.1 0.0 copy-start.1
  8.1 1.0 %copy-done.1 = bf16[32,1,32,128]{3,2,1,0:T(8,128)(2,1)S(1)} copy-done((bf16[32,1,32,128]{3,2,1,0:T(8,128)(2,1)S(1)}, bf16[32,1,32,128]{3,2,1,0:T(8,128)(2,1)}, u32[]{:S(2)}) %copy-start.1) | copy-done | bytes 262168
  9.1 0.1 shard_map.52.refs_2_.refs_0_.refs_3_
  9.3 0.0 copy-done
  9.3 0.0 copy-start.2
  9.3 1.2 %copy-done.2 = bf16[16,2,64,256]{3,2,1,0:T(8,128)(2,1)S(1)} copy-done((bf16[16,2,64,256]{3,2,1,0:T(8,128)(2,1)S(1)}, bf16[16,2,64,256]{3,2,1,0:T(8,128)(2,1)}, u32[]{:S(2)}) %copy-start.2) | copy-done | bytes 1048600
  10.5 0.9 %shard_map.50 = (bf16[192,4096]{1,0:T(8,128)(2,1)S(1)}, bf16[144,128]{1,0:T(8,128)(2,1)S(1)}, bf16[144,256]{1,0:T(8,128)(2,1)S(1)}) custom-call(bf16[16,2,64,256]{3,2,1,0:T(8,128)(2,1)S(1)} %copy-done.2, bf16[27,16,128]{2,1,0:T(8,128)(2,1)S(1)} %constant_dynamic-slice_fusion.refs_1_), custom_call_target="tpu_custom_call" | custom-call | flops 536870912 | bytes 4194304 | tf_op jit(solution)/shard_map/pallas_call | solution.py:320
  11.5 1.1 %collective-permute-done.1.refs_1_ = bf16[32,1,32,128]{3,2,1,0:T(8,128)(2,1)S(1)} collective-permute-done((bf16[32,1,32,128]{3,2,1,0:T(8,128)(2,1)}, bf16[32,1,32,128]{3,2,1,0:T(8,128)(2,1)S(1)}, u32[]{:S(2)}, u32[]{:S(2)}) %collective-permute-start.1) | collective-permute-done | bytes 262176 | tf_op jit(solution)/shard_map/ppermute | solution.py:354
  12.6 5.7 %collective-permute-start.4 = (bf16[32,1,32,128]{3,2,1,0:T(8,128)(2,1)S(1)}, bf16[32,1,32,128]{3,2,1,0:T(8,128)(2,1)S(1)}, u32[]{:S(2)}, u32[]{:S(2)}) collective-permute-start(bf16[32,1,32,128]{3,2,1,0:T(8,128)(2,1)S(1)} %collective-permute-done.1.refs_1_), channel_id=1, source_target_pairs={{0,1},{1,0},{2,3},{3,2},{4,5},{5,4},{6,7},{7,6},{8,9},{9,8},{10,11... | collective-permute-start | bytes 786440 | tf_op jit(solution)/shard_map/ppermute | solution.py:357
  18.3 0.0 collective-permute-done.3.refs_0_
  18.3 0.1 shard_map.53.refs_0_
  18.5 1.1 %collective-permute-done.2.behind_ref = bf16[16,2,64,256]{3,2,1,0:T(8,128)(2,1)S(1)} collective-permute-done((bf16[16,2,64,256]{3,2,1,0:T(8,128)(2,1)}, bf16[16,2,64,256]{3,2,1,0:T(8,128)(2,1)S(1)}, u32[]{:S(2)}, u32[]{:S(2)}) %collective-permute-start.2) | collective-permute-done | bytes 1048608 | tf_op jit(solution)/shard_map/ppermute | solution.py:365
  19.5 0.1 shard_map.51.refs_1_
  19.6 0.0 collective-permute-done.refs_0_
  19.6 0.3 shard_map.54.refs_3_.refs_1_.refs_4_
  19.9 1.3 %collective-permute-start.6 = (bf16[64,4096]{1,0:T(8,128)(2,1)S(1)}, bf16[64,4096]{1,0:T(8,128)(2,1)S(1)}, u32[]{:S(2)}, u32[]{:S(2)}) collective-permute-start(bf16[64,4096]{1,0:T(8,128)(2,1)S(1)} %shard_map.54.refs_3_.refs_1_.refs_4_), channel_id=1, source_target_pairs={{4,0},{8,4},{12,8},{16,12},{20,16},{24,20},{28,24},{0,28},{5,1},{9... | collective-permute-start | bytes 1572872 | tf_op jit(solution)/shard_map/ppermute | solution.py:379
  21.1 4.3 %collective-permute-done.4.refs_0_ = bf16[32,1,32,128]{3,2,1,0:T(8,128)(2,1)S(1)} collective-permute-done((bf16[32,1,32,128]{3,2,1,0:T(8,128)(2,1)S(1)}, bf16[32,1,32,128]{3,2,1,0:T(8,128)(2,1)S(1)}, u32[]{:S(2)}, u32[]{:S(2)}) %collective-permute-start.4) | collective-permute-done | bytes 262176 | tf_op jit(solution)/shard_map/ppermute | solution.py:357
  25.4 0.1 shard_map.55.refs_4_.refs_2_.refs_5_
  25.5 0.4 %collective-permute-start.7 = (bf16[32,4096]{1,0:T(8,128)(2,1)S(1)}, bf16[32,4096]{1,0:T(8,128)(2,1)S(1)}, u32[]{:S(2)}, u32[]{:S(2)}) collective-permute-start(bf16[32,4096]{1,0:T(8,128)(2,1)S(1)} %shard_map.55.refs_4_.refs_2_.refs_5_), channel_id=1, source_target_pairs={{4,0},{8,4},{12,8},{16,12},{20,16},{24,20},{28,24},{0,28},{5,1},{9... | collective-permute-start | bytes 786440 | tf_op jit(solution)/shard_map/ppermute | solution.py:379
  26.0 0.9 %shard_map.56 = (f32[64,512]{1,0:T(8,128)S(1)}, f32[64,512]{1,0:T(8,128)S(1)}) custom-call(bf16[192,4096]{1,0:T(8,128)(2,1)S(1)} %get-tuple-element.24.refs_0_, bf16[96,4096]{1,0:T(8,128)(2,1)S(1)} %shard_map.51.refs_1_, bf16[32,4096]{1,0:T(8,128)(2,1)S(1)} %shard_map.52.refs_2_.refs_0_.refs_3_, bf16[64,4096]{1,0:T(8,128)(2,1)S(1)} %shard_map.54.refs_3_.refs_1_.refs_4_, ...), custom_call_target="tpu_custom_call" | custom-call | flops 452984832 | bytes 8388608 | tf_op jit(solution)/shard_map/pallas_call | solution.py:320
  26.9 0.2 collective-permute-start.5
  27.1 0.9 %shard_map.57.even_ref = bf16[16,64,256]{2,1,0:T(8,128)(2,1)S(1)} custom-call(bf16[144,128]{1,0:T(8,128)(2,1)S(1)} %get-tuple-element.31.taps_ref, bf16[32,4096]{1,0:T(8,128)(2,1)S(1)} %shard_map.52.refs_2_.refs_0_.refs_3_, bf16[64,4096]{1,0:T(8,128)(2,1)S(1)} %shard_map.54.refs_3_.refs_1_.refs_4_, bf16[32,4096]{1,0:T(8,128)(2,1)S(1)} %shard_map.55.refs_4_.refs_2_.refs_5_), custom_call_target="tpu_custom_call" | custom-call | flops 150994944 | bytes 4194304 | tf_op jit(solution)/shard_map/pallas_call | solution.py:320
  28.0 0.3 collective-permute-done.5.other_ref
  28.3 1.4 %collective-permute-start.10 = (f32[16,512]{1,0:T(8,128)S(1)}, f32[16,512]{1,0:T(8,128)S(1)}, u32[]{:S(2)}, u32[]{:S(2)}) collective-permute-start(f32[16,512]{1,0:T(8,128)S(1)} %get-tuple-element.41), channel_id=1, source_target_pairs={{0,8},{4,12},{8,0},{12,4},{16,24},{20,28},{24,16},{28,20},{1,9},{5... | collective-permute-start | bytes 98312 | tf_op jit(solution)/shard_map/ppermute | solution.py:417
  29.7 2.4 %collective-permute-start.8 = (f32[16,512]{1,0:T(8,128)S(1)}, f32[16,512]{1,0:T(8,128)S(1)}, u32[]{:S(2)}, u32[]{:S(2)}) collective-permute-start(f32[16,512]{1,0:T(8,128)S(1)} %get-tuple-element.39), channel_id=1, source_target_pairs={{0,24},{4,28},{8,16},{12,20},{16,8},{20,12},{24,0},{28,4},{1,25},{... | collective-permute-start | bytes 98312 | tf_op jit(solution)/shard_map/ppermute | solution.py:417
  32.1 0.0 collective-permute-start.9
  32.1 0.0 collective-permute-done.7.refs_2_
  32.1 0.0 collective-permute-done.6.refs_1_
  32.1 1.7 %shard_map.59 = bf16[16,2,64,256]{3,2,1,0:T(8,128)(2,1)} custom-call(bf16[16,64,256]{2,1,0:T(8,128)(2,1)S(1)} %shard_map.57.even_ref, bf16[144,256]{1,0:T(8,128)(2,1)S(1)} %get-tuple-element.35.taps_ref, bf16[32,4096]{1,0:T(8,128)(2,1)S(1)} %shard_map.53.refs_0_, bf16[64,4096]{1,0:T(8,128)(2,1)S(1)} %collective-permute-done.6.refs_1_, ...), custom_call_target="tpu_custom_call" | custom-call | flops 301989888 | bytes 4194304 | tf_op jit(solution)/shard_map/pallas_call | solution.py:320
  33.8 0.0 collective-permute-done.10.refs_3_
  33.8 0.7 %collective-permute-done.8.refs_1_ = f32[16,512]{1,0:T(8,128)S(1)} collective-permute-done((f32[16,512]{1,0:T(8,128)S(1)}, f32[16,512]{1,0:T(8,128)S(1)}, u32[]{:S(2)}, u32[]{:S(2)}) %collective-permute-start.8) | collective-permute-done | bytes 32800 | tf_op jit(solution)/shard_map/ppermute | solution.py:417
  34.5 1.5 %collective-permute-done.9.refs_2_ = f32[16,512]{1,0:T(8,128)S(1)} collective-permute-done((f32[16,512]{1,0:T(8,128)S(1)}, f32[16,512]{1,0:T(8,128)S(1)}, u32[]{:S(2)}, u32[]{:S(2)}) %collective-permute-start.9) | collective-permute-done | bytes 32800 | tf_op jit(solution)/shard_map/ppermute | solution.py:417
  36.0 0.8 %shard_map.60 = f32[16,16,27]{2,1,0:T(8,128)} custom-call(f32[16,512]{1,0:T(8,128)S(1)} %get-tuple-element.38.refs_0_, f32[16,512]{1,0:T(8,128)S(1)} %collective-permute-done.8.refs_1_, f32[16,512]{1,0:T(8,128)S(1)} %collective-permute-done.9.refs_2_, f32[16,512]{1,0:T(8,128)S(1)} %collective-permute-done.10.refs_3_), custom_call_target="tpu_custom_call" | custom-call | flops 65536 | bytes 524288 | tf_op jit(solution)/shard_map/pallas_call | solution.py:320
  (2 shorter events, 0.0 us)
Async XLA Ops:
  0.6 8.6 %copy-start = (bf16[27,64,128]{2,1,0:T(8,128)(2,1)S(1)}, bf16[27,64,128]{2,1,0:T(8,128)(2,1)}, u32[]{:S(2)}) copy-start(bf16[27,64,128]{2,1,0:T(8,128)(2,1)} %param.5) | copy-start | bytes 1327108
  0.6 18.9 %collective-permute-start.2 = (bf16[16,2,64,256]{3,2,1,0:T(8,128)(2,1)}, bf16[16,2,64,256]{3,2,1,0:T(8,128)(2,1)S(1)}, u32[]{:S(2)}, u32[]{:S(2)}) collective-permute-start(bf16[16,2,64,256]{3,2,1,0:T(8,128)(2,1)} %refs_0_.2), channel_id=1, source_target_pairs={{0,4},{4,8},{8,12},{12,16},{16,20},{20,24},{24,28},{28,0},{1,5},{5... | collective-permute-start | bytes 3145736 | tf_op jit(solution)/shard_map/ppermute | solution.py:365
  1.1 11.4 %collective-permute-start.1 = (bf16[32,1,32,128]{3,2,1,0:T(8,128)(2,1)}, bf16[32,1,32,128]{3,2,1,0:T(8,128)(2,1)S(1)}, u32[]{:S(2)}, u32[]{:S(2)}) collective-permute-start(bf16[32,1,32,128]{3,2,1,0:T(8,128)(2,1)} %refs_0_.3), channel_id=1, source_target_pairs={{0,3},{1,2},{2,1},{3,0},{4,7},{5,6},{6,5},{7,4},{8,11},{9,10},{10,... | collective-permute-start | bytes 786440 | tf_op jit(solution)/shard_map/ppermute | solution.py:354
  5.8 12.5 %collective-permute-start.3 = (bf16[32,1,32,128]{3,2,1,0:T(8,128)(2,1)}, bf16[32,1,32,128]{3,2,1,0:T(8,128)(2,1)S(1)}, u32[]{:S(2)}, u32[]{:S(2)}) collective-permute-start(bf16[32,1,32,128]{3,2,1,0:T(8,128)(2,1)} %refs_0_.3), channel_id=1, source_target_pairs={{4,0},{8,4},{12,8},{16,12},{20,16},{24,20},{28,24},{0,28},{5,1},{9... | collective-permute-start | bytes 786440 | tf_op jit(solution)/shard_map/ppermute | solution.py:366
  8.1 11.5 %collective-permute-start = (bf16[32,1,32,128]{3,2,1,0:T(8,128)(2,1)}, bf16[32,1,32,128]{3,2,1,0:T(8,128)(2,1)S(1)}, u32[]{:S(2)}, u32[]{:S(2)}) collective-permute-start(bf16[32,1,32,128]{3,2,1,0:T(8,128)(2,1)} %refs_0_.3), channel_id=1, source_target_pairs={{0,1},{1,0},{2,3},{3,2},{4,5},{5,4},{6,7},{7,6},{8,9},{9,8},{10,11... | collective-permute-start | bytes 786440 | tf_op jit(solution)/shard_map/ppermute | solution.py:355
  8.1 1.0 %copy-start.1 = (bf16[32,1,32,128]{3,2,1,0:T(8,128)(2,1)S(1)}, bf16[32,1,32,128]{3,2,1,0:T(8,128)(2,1)}, u32[]{:S(2)}) copy-start(bf16[32,1,32,128]{3,2,1,0:T(8,128)(2,1)} %refs_0_.3) | copy-start | bytes 786436
  9.3 1.2 %copy-start.2 = (bf16[16,2,64,256]{3,2,1,0:T(8,128)(2,1)S(1)}, bf16[16,2,64,256]{3,2,1,0:T(8,128)(2,1)}, u32[]{:S(2)}) copy-start(bf16[16,2,64,256]{3,2,1,0:T(8,128)(2,1)} %refs_0_.2) | copy-start | bytes 3145732
  12.6 12.8 %collective-permute-start.4 = (bf16[32,1,32,128]{3,2,1,0:T(8,128)(2,1)S(1)}, bf16[32,1,32,128]{3,2,1,0:T(8,128)(2,1)S(1)}, u32[]{:S(2)}, u32[]{:S(2)}) collective-permute-start(bf16[32,1,32,128]{3,2,1,0:T(8,128)(2,1)S(1)} %collective-permute-done.1.refs_1_), channel_id=1, source_target_pairs={{0,1},{1,0},{2,3},{3,2},{4,5},{5,4},{6,7},{7,6},{8,9},{9,8},{10,11... | collective-permute-start | bytes 786440 | tf_op jit(solution)/shard_map/ppermute | solution.py:357
  19.9 12.2 %collective-permute-start.6 = (bf16[64,4096]{1,0:T(8,128)(2,1)S(1)}, bf16[64,4096]{1,0:T(8,128)(2,1)S(1)}, u32[]{:S(2)}, u32[]{:S(2)}) collective-permute-start(bf16[64,4096]{1,0:T(8,128)(2,1)S(1)} %shard_map.54.refs_3_.refs_1_.refs_4_), channel_id=1, source_target_pairs={{4,0},{8,4},{12,8},{16,12},{20,16},{24,20},{28,24},{0,28},{5,1},{9... | collective-permute-start | bytes 1572872 | tf_op jit(solution)/shard_map/ppermute | solution.py:379
  25.5 6.6 %collective-permute-start.7 = (bf16[32,4096]{1,0:T(8,128)(2,1)S(1)}, bf16[32,4096]{1,0:T(8,128)(2,1)S(1)}, u32[]{:S(2)}, u32[]{:S(2)}) collective-permute-start(bf16[32,4096]{1,0:T(8,128)(2,1)S(1)} %shard_map.55.refs_4_.refs_2_.refs_5_), channel_id=1, source_target_pairs={{4,0},{8,4},{12,8},{16,12},{20,16},{24,20},{28,24},{0,28},{5,1},{9... | collective-permute-start | bytes 786440 | tf_op jit(solution)/shard_map/ppermute | solution.py:379
  26.9 1.4 %collective-permute-start.5 = (f32[64,512]{1,0:T(8,128)S(1)}, f32[64,512]{1,0:T(8,128)S(1)}, u32[]{:S(2)}, u32[]{:S(2)}) collective-permute-start(f32[64,512]{1,0:T(8,128)S(1)} %get-tuple-element.30), channel_id=1, source_target_pairs={{0,4},{4,0},{8,12},{12,8},{16,20},{20,16},{24,28},{28,24},{1,5},{5... | collective-permute-start | bytes 393224 | tf_op jit(solution)/shard_map/ppermute | solution.py:399
  28.3 5.5 %collective-permute-start.10 = (f32[16,512]{1,0:T(8,128)S(1)}, f32[16,512]{1,0:T(8,128)S(1)}, u32[]{:S(2)}, u32[]{:S(2)}) collective-permute-start(f32[16,512]{1,0:T(8,128)S(1)} %get-tuple-element.41), channel_id=1, source_target_pairs={{0,8},{4,12},{8,0},{12,4},{16,24},{20,28},{24,16},{28,20},{1,9},{5... | collective-permute-start | bytes 98312 | tf_op jit(solution)/shard_map/ppermute | solution.py:417
  29.7 4.8 %collective-permute-start.8 = (f32[16,512]{1,0:T(8,128)S(1)}, f32[16,512]{1,0:T(8,128)S(1)}, u32[]{:S(2)}, u32[]{:S(2)}) collective-permute-start(f32[16,512]{1,0:T(8,128)S(1)} %get-tuple-element.39), channel_id=1, source_target_pairs={{0,24},{4,28},{8,16},{12,20},{16,8},{20,12},{24,0},{28,4},{1,25},{... | collective-permute-start | bytes 98312 | tf_op jit(solution)/shard_map/ppermute | solution.py:417
  32.1 3.9 %collective-permute-start.9 = (f32[16,512]{1,0:T(8,128)S(1)}, f32[16,512]{1,0:T(8,128)S(1)}, u32[]{:S(2)}, u32[]{:S(2)}) collective-permute-start(f32[16,512]{1,0:T(8,128)S(1)} %get-tuple-element.40), channel_id=1, source_target_pairs={{0,16},{4,20},{8,24},{12,28},{16,0},{20,4},{24,8},{28,12},{1,17},{... | collective-permute-start | bytes 98312 | tf_op jit(solution)/shard_map/ppermute | solution.py:417

commit v19 on v18

--- a/solution.py
+++ b/solution.py
@@ -352,8 +352,8 @@
     )
     pairs = lambda mask: [(i, i ^ mask) for i in range(count)]
     far = lax.ppermute(grad_out, "chan", pairs(3))
-    near = lax.ppermute(grad_out, "chan", pairs(1))
-    far, views = lax.optimization_barrier((far, views))
+    own, views = lax.optimization_barrier((grad_out, views))
+    near = lax.ppermute(own, "chan", pairs(1))
     forwarded = lax.ppermute(far, "chan", pairs(1))
     lines = lambda *parts: call(
         lines_kernel,
@@ -363,7 +363,7 @@
         cost=(1 << 20, 2 << 20),
     )
     behind = lax.ppermute(volume, "depth", farther)
-    next_own = lax.ppermute(grad_out, "depth", nearer)
+    next_own = lax.ppermute(own, "depth", nearer)
     behind_views = call(
         behind_views_kernel,
         jax.ShapeDtypeStruct((6 * chans, cells), BF16),

time: 36.9 us -> 36 us (0.976)
  local copies, waits for them, and re-layouts: 2.27 us -> 1.25 us
    unnamed x6, local copies, waits for them, and re-layouts: 2.24 us -> 1.23 us
    ppermute x1, waiting for transfers between devices: 1.14 us -> 2.07 us  [shards(): far = lax.ppermute(grad_out, 'chan', pairs(3))]
    ppermute x3, waiting for transfers between devices: 2.21 us -> 1.29 us  [shards(): lax.ppermute(terms[k - 1], 'depth', [(i, i ^ 2 * k) for i in range(depth)])]
  transfers between devices with their start and end apart: 11 -> 11, of which waited for: 6 -> 6; matrix products, arithmetic and copies ran while one was open for 0% -> 0% of each run, Pallas kernels for 14% -> 15%
where the time goes in v19:
time: 36 us; the launch traced here: 35.8 us
  starting transfers between devices  18.9 us (52%)
  waiting for transfers between devices  8.98 us (25%)
  Pallas kernels  5.95 us (17%)
  local copies, waits for them, and re-layouts  1.25 us (3%)
  between operations  0.74 us (2%)
    pallas_call x11, Pallas kernels, call(): pl.pallas_call(kernel, out_shape=out_shape, in_specs=[VMEM] * len(args),...  5.95 us
    ppermute x1, starting transfers between devices, shards(): forwarded = lax.ppermute(far, 'chan', pairs(1))  5.77 us
    ppermute x1, starting transfers between devices, shards(): far = lax.ppermute(grad_out, 'chan', pairs(3))  4.68 us
    ppermute x1, waiting for transfers between devices, shards(): forwarded = lax.ppermute(far, 'chan', pairs(1))  4.26 us
    ppermute x3, starting transfers between devices, shards(): lax.ppermute(terms[k - 1], 'depth', [(i, i ^ 2 * k) for i in range(depth)])  3.75 us
    ppermute x1, starting transfers between devices, shards(): next_own = lax.ppermute(own, 'depth', nearer)  2.33 us
    ppermute x1, waiting for transfers between devices, shards(): far = lax.ppermute(grad_out, 'chan', pairs(3))  2.07 us
    ppermute x2, starting transfers between devices, shards(): lax.ppermute(part, 'depth', nearer)  1.68 us
  transfers between devices with their start and end apart: 11, of which 6 were waited for; matrix products, arithmetic and copies ran while one was open for 0% of the time, Pallas kernels for 15%

profile of v19, /device:TPU:0, one launch (start us, length us, event | category | flops | bytes accessed | tf_op | source)
XLA Modules:
  0.0 35.8 jit_solution(15148878329986931872)
XLA Ops:
  0.6 0.0 copy-start
  0.6 0.0 copy-start.1
  0.7 0.5 %collective-permute-start.1 = (bf16[16,2,64,256]{3,2,1,0:T(8,128)(2,1)}, bf16[16,2,64,256]{3,2,1,0:T(8,128)(2,1)S(1)}, u32[]{:S(2)}, u32[]{:S(2)}) collective-permute-start(bf16[16,2,64,256]{3,2,1,0:T(8,128)(2,1)} %refs_0_.2), channel_id=1, source_target_pairs={{0,4},{4,8},{8,12},{12,16},{16,20},{20,24},{24,28},{28,0},{1,5},{5... | collective-permute-start | bytes 3145736 | tf_op jit(solution)/shard_map/ppermute | solution.py:365
  1.2 4.7 %collective-permute-start.3 = (bf16[32,1,32,128]{3,2,1,0:T(8,128)(2,1)}, bf16[32,1,32,128]{3,2,1,0:T(8,128)(2,1)S(1)}, u32[]{:S(2)}, u32[]{:S(2)}) collective-permute-start(bf16[32,1,32,128]{3,2,1,0:T(8,128)(2,1)} %refs_0_.3), channel_id=1, source_target_pairs={{0,3},{1,2},{2,1},{3,0},{4,7},{5,6},{6,5},{7,4},{8,11},{9,10},{10,... | collective-permute-start | bytes 786440 | tf_op jit(solution)/shard_map/ppermute | solution.py:354
  5.8 0.0 copy-done
  5.9 0.0 copy-start.2
  5.9 1.2 %copy-done.2 = bf16[16,2,64,256]{3,2,1,0:T(8,128)(2,1)S(1)} copy-done((bf16[16,2,64,256]{3,2,1,0:T(8,128)(2,1)S(1)}, bf16[16,2,64,256]{3,2,1,0:T(8,128)(2,1)}, u32[]{:S(2)}) %copy-start.2) | copy-done | bytes 1048600
  7.1 0.9 %shard_map.50 = (bf16[192,4096]{1,0:T(8,128)(2,1)S(1)}, bf16[144,128]{1,0:T(8,128)(2,1)S(1)}, bf16[144,256]{1,0:T(8,128)(2,1)S(1)}) custom-call(bf16[16,2,64,256]{3,2,1,0:T(8,128)(2,1)S(1)} %copy-done.2, bf16[27,16,128]{2,1,0:T(8,128)(2,1)S(1)} %constant_dynamic-slice_fusion.refs_1_), custom_call_target="tpu_custom_call" | custom-call | flops 536870912 | bytes 4194304 | tf_op jit(solution)/shard_map/pallas_call | solution.py:320
  8.0 0.0 copy-done.1
  8.0 2.3 %collective-permute-start.2 = (bf16[32,1,32,128]{3,2,1,0:T(8,128)(2,1)S(1)}, bf16[32,1,32,128]{3,2,1,0:T(8,128)(2,1)S(1)}, u32[]{:S(2)}, u32[]{:S(2)}) collective-permute-start(bf16[32,1,32,128]{3,2,1,0:T(8,128)(2,1)S(1)} %copy-done.1), channel_id=1, source_target_pairs={{4,0},{8,4},{12,8},{16,12},{20,16},{24,20},{28,24},{0,28},{5,1},{9... | collective-permute-start | bytes 786440 | tf_op jit(solution)/shard_map/ppermute | solution.py:366
  10.3 0.0 collective-permute-start
  10.3 0.1 shard_map.52.refs_2_.refs_0_.refs_3_
  10.5 2.1 %collective-permute-done.3.refs_1_ = bf16[32,1,32,128]{3,2,1,0:T(8,128)(2,1)S(1)} collective-permute-done((bf16[32,1,32,128]{3,2,1,0:T(8,128)(2,1)}, bf16[32,1,32,128]{3,2,1,0:T(8,128)(2,1)S(1)}, u32[]{:S(2)}, u32[]{:S(2)}) %collective-permute-start.3) | collective-permute-done | bytes 262176 | tf_op jit(solution)/shard_map/ppermute | solution.py:354
  12.6 5.8 %collective-permute-start.4 = (bf16[32,1,32,128]{3,2,1,0:T(8,128)(2,1)S(1)}, bf16[32,1,32,128]{3,2,1,0:T(8,128)(2,1)S(1)}, u32[]{:S(2)}, u32[]{:S(2)}) collective-permute-start(bf16[32,1,32,128]{3,2,1,0:T(8,128)(2,1)S(1)} %collective-permute-done.3.refs_1_), channel_id=1, source_target_pairs={{0,1},{1,0},{2,3},{3,2},{4,5},{5,4},{6,7},{7,6},{8,9},{9,8},{10,11... | collective-permute-start | bytes 786440 | tf_op jit(solution)/shard_map/ppermute | solution.py:357
  18.3 0.0 collective-permute-done.2.refs_0_
  18.3 0.1 shard_map.53.refs_0_
  18.5 1.1 %collective-permute-done.1.behind_ref = bf16[16,2,64,256]{3,2,1,0:T(8,128)(2,1)S(1)} collective-permute-done((bf16[16,2,64,256]{3,2,1,0:T(8,128)(2,1)}, bf16[16,2,64,256]{3,2,1,0:T(8,128)(2,1)S(1)}, u32[]{:S(2)}, u32[]{:S(2)}) %collective-permute-start.1) | collective-permute-done | bytes 1048608 | tf_op jit(solution)/shard_map/ppermute | solution.py:365
  19.5 0.1 shard_map.51.refs_1_
  19.6 0.0 collective-permute-done.refs_0_
  19.6 0.3 shard_map.54.refs_3_.refs_1_.refs_4_
  19.9 1.3 %collective-permute-start.6 = (bf16[64,4096]{1,0:T(8,128)(2,1)S(1)}, bf16[64,4096]{1,0:T(8,128)(2,1)S(1)}, u32[]{:S(2)}, u32[]{:S(2)}) collective-permute-start(bf16[64,4096]{1,0:T(8,128)(2,1)S(1)} %shard_map.54.refs_3_.refs_1_.refs_4_), channel_id=1, source_target_pairs={{4,0},{8,4},{12,8},{16,12},{20,16},{24,20},{28,24},{0,28},{5,1},{9... | collective-permute-start | bytes 1572872 | tf_op jit(solution)/shard_map/ppermute | solution.py:379
  21.1 4.3 %collective-permute-done.4.refs_0_ = bf16[32,1,32,128]{3,2,1,0:T(8,128)(2,1)S(1)} collective-permute-done((bf16[32,1,32,128]{3,2,1,0:T(8,128)(2,1)S(1)}, bf16[32,1,32,128]{3,2,1,0:T(8,128)(2,1)S(1)}, u32[]{:S(2)}, u32[]{:S(2)}) %collective-permute-start.4) | collective-permute-done | bytes 262176 | tf_op jit(solution)/shard_map/ppermute | solution.py:357
  25.4 0.1 shard_map.55.refs_4_.refs_2_.refs_5_
  25.5 0.4 %collective-permute-start.7 = (bf16[32,4096]{1,0:T(8,128)(2,1)S(1)}, bf16[32,4096]{1,0:T(8,128)(2,1)S(1)}, u32[]{:S(2)}, u32[]{:S(2)}) collective-permute-start(bf16[32,4096]{1,0:T(8,128)(2,1)S(1)} %shard_map.55.refs_4_.refs_2_.refs_5_), channel_id=1, source_target_pairs={{4,0},{8,4},{12,8},{16,12},{20,16},{24,20},{28,24},{0,28},{5,1},{9... | collective-permute-start | bytes 786440 | tf_op jit(solution)/shard_map/ppermute | solution.py:379
  26.0 0.9 %shard_map.56 = (f32[64,512]{1,0:T(8,128)S(1)}, f32[64,512]{1,0:T(8,128)S(1)}) custom-call(bf16[192,4096]{1,0:T(8,128)(2,1)S(1)} %get-tuple-element.25.refs_0_, bf16[96,4096]{1,0:T(8,128)(2,1)S(1)} %shard_map.51.refs_1_, bf16[32,4096]{1,0:T(8,128)(2,1)S(1)} %shard_map.52.refs_2_.refs_0_.refs_3_, bf16[64,4096]{1,0:T(8,128)(2,1)S(1)} %shard_map.54.refs_3_.refs_1_.refs_4_, ...), custom_call_target="tpu_custom_call" | custom-call | flops 452984832 | bytes 8388608 | tf_op jit(solution)/shard_map/pallas_call | solution.py:320
  26.9 0.2 collective-permute-start.5
  27.1 0.9 %shard_map.57.even_ref = bf16[16,64,256]{2,1,0:T(8,128)(2,1)S(1)} custom-call(bf16[144,128]{1,0:T(8,128)(2,1)S(1)} %get-tuple-element.31.taps_ref, bf16[32,4096]{1,0:T(8,128)(2,1)S(1)} %shard_map.52.refs_2_.refs_0_.refs_3_, bf16[64,4096]{1,0:T(8,128)(2,1)S(1)} %shard_map.54.refs_3_.refs_1_.refs_4_, bf16[32,4096]{1,0:T(8,128)(2,1)S(1)} %shard_map.55.refs_4_.refs_2_.refs_5_), custom_call_target="tpu_custom_call" | custom-call | flops 150994944 | bytes 4194304 | tf_op jit(solution)/shard_map/pallas_call | solution.py:320
  28.1 0.3 collective-permute-done.5.other_ref
  28.4 2.3 %collective-permute-start.8 = (f32[16,512]{1,0:T(8,128)S(1)}, f32[16,512]{1,0:T(8,128)S(1)}, u32[]{:S(2)}, u32[]{:S(2)}) collective-permute-start(f32[16,512]{1,0:T(8,128)S(1)} %get-tuple-element.39), channel_id=1, source_target_pairs={{0,24},{4,28},{8,16},{12,20},{16,8},{20,12},{24,0},{28,4},{1,25},{... | collective-permute-start | bytes 98312 | tf_op jit(solution)/shard_map/ppermute | solution.py:417
  30.7 0.5 %collective-permute-start.9 = (f32[16,512]{1,0:T(8,128)S(1)}, f32[16,512]{1,0:T(8,128)S(1)}, u32[]{:S(2)}, u32[]{:S(2)}) collective-permute-start(f32[16,512]{1,0:T(8,128)S(1)} %get-tuple-element.40), channel_id=1, source_target_pairs={{0,16},{4,20},{8,24},{12,28},{16,0},{20,4},{24,8},{28,12},{1,17},{... | collective-permute-start | bytes 98312 | tf_op jit(solution)/shard_map/ppermute | solution.py:417
  31.2 0.9 %collective-permute-start.10 = (f32[16,512]{1,0:T(8,128)S(1)}, f32[16,512]{1,0:T(8,128)S(1)}, u32[]{:S(2)}, u32[]{:S(2)}) collective-permute-start(f32[16,512]{1,0:T(8,128)S(1)} %get-tuple-element.41), channel_id=1, source_target_pairs={{0,8},{4,12},{8,0},{12,4},{16,24},{20,28},{24,16},{28,20},{1,9},{5... | collective-permute-start | bytes 98312 | tf_op jit(solution)/shard_map/ppermute | solution.py:417
  32.1 0.0 collective-permute-done.7.refs_2_
  32.1 0.0 collective-permute-done.6.refs_1_
  32.1 1.7 %shard_map.59 = bf16[16,2,64,256]{3,2,1,0:T(8,128)(2,1)} custom-call(bf16[16,64,256]{2,1,0:T(8,128)(2,1)S(1)} %shard_map.57.even_ref, bf16[144,256]{1,0:T(8,128)(2,1)S(1)} %get-tuple-element.35.taps_ref, bf16[32,4096]{1,0:T(8,128)(2,1)S(1)} %shard_map.53.refs_0_, bf16[64,4096]{1,0:T(8,128)(2,1)S(1)} %collective-permute-done.6.refs_1_, ...), custom_call_target="tpu_custom_call" | custom-call | flops 301989888 | bytes 4194304 | tf_op jit(solution)/shard_map/pallas_call | solution.py:320
  33.8 0.0 collective-permute-done.8.refs_1_
  33.8 0.8 %collective-permute-done.9.refs_2_ = f32[16,512]{1,0:T(8,128)S(1)} collective-permute-done((f32[16,512]{1,0:T(8,128)S(1)}, f32[16,512]{1,0:T(8,128)S(1)}, u32[]{:S(2)}, u32[]{:S(2)}) %collective-permute-start.9) | collective-permute-done | bytes 32800 | tf_op jit(solution)/shard_map/ppermute | solution.py:417
  34.6 0.5 %collective-permute-done.10.refs_3_ = f32[16,512]{1,0:T(8,128)S(1)} collective-permute-done((f32[16,512]{1,0:T(8,128)S(1)}, f32[16,512]{1,0:T(8,128)S(1)}, u32[]{:S(2)}, u32[]{:S(2)}) %collective-permute-start.10) | collective-permute-done | bytes 32800 | tf_op jit(solution)/shard_map/ppermute | solution.py:417
  35.1 0.8 %shard_map.60 = f32[16,16,27]{2,1,0:T(8,128)} custom-call(f32[16,512]{1,0:T(8,128)S(1)} %get-tuple-element.38.refs_0_, f32[16,512]{1,0:T(8,128)S(1)} %collective-permute-done.8.refs_1_, f32[16,512]{1,0:T(8,128)S(1)} %collective-permute-done.9.refs_2_, f32[16,512]{1,0:T(8,128)S(1)} %collective-permute-done.10.refs_3_), custom_call_target="tpu_custom_call" | custom-call | flops 65536 | bytes 524288 | tf_op jit(solution)/shard_map/pallas_call | solution.py:320
  (2 shorter events, 0.0 us)
Async XLA Ops:
  0.6 5.2 %copy-start = (bf16[27,64,128]{2,1,0:T(8,128)(2,1)S(1)}, bf16[27,64,128]{2,1,0:T(8,128)(2,1)}, u32[]{:S(2)}) copy-start(bf16[27,64,128]{2,1,0:T(8,128)(2,1)} %param.5) | copy-start | bytes 1327108
  0.6 7.4 %copy-start.1 = (bf16[32,1,32,128]{3,2,1,0:T(8,128)(2,1)S(1)}, bf16[32,1,32,128]{3,2,1,0:T(8,128)(2,1)}, u32[]{:S(2)}) copy-start(bf16[32,1,32,128]{3,2,1,0:T(8,128)(2,1)} %refs_0_.3) | copy-start | bytes 786436
  0.7 18.9 %collective-permute-start.1 = (bf16[16,2,64,256]{3,2,1,0:T(8,128)(2,1)}, bf16[16,2,64,256]{3,2,1,0:T(8,128)(2,1)S(1)}, u32[]{:S(2)}, u32[]{:S(2)}) collective-permute-start(bf16[16,2,64,256]{3,2,1,0:T(8,128)(2,1)} %refs_0_.2), channel_id=1, source_target_pairs={{0,4},{4,8},{8,12},{12,16},{16,20},{20,24},{24,28},{28,0},{1,5},{5... | collective-permute-start | bytes 3145736 | tf_op jit(solution)/shard_map/ppermute | solution.py:365
  1.2 11.4 %collective-permute-start.3 = (bf16[32,1,32,128]{3,2,1,0:T(8,128)(2,1)}, bf16[32,1,32,128]{3,2,1,0:T(8,128)(2,1)S(1)}, u32[]{:S(2)}, u32[]{:S(2)}) collective-permute-start(bf16[32,1,32,128]{3,2,1,0:T(8,128)(2,1)} %refs_0_.3), channel_id=1, source_target_pairs={{0,3},{1,2},{2,1},{3,0},{4,7},{5,6},{6,5},{7,4},{8,11},{9,10},{10,... | collective-permute-start | bytes 786440 | tf_op jit(solution)/shard_map/ppermute | solution.py:354
  5.9 1.2 %copy-start.2 = (bf16[16,2,64,256]{3,2,1,0:T(8,128)(2,1)S(1)}, bf16[16,2,64,256]{3,2,1,0:T(8,128)(2,1)}, u32[]{:S(2)}) copy-start(bf16[16,2,64,256]{3,2,1,0:T(8,128)(2,1)} %refs_0_.2) | copy-start | bytes 3145732
  8.0 10.3 %collective-permute-start.2 = (bf16[32,1,32,128]{3,2,1,0:T(8,128)(2,1)S(1)}, bf16[32,1,32,128]{3,2,1,0:T(8,128)(2,1)S(1)}, u32[]{:S(2)}, u32[]{:S(2)}) collective-permute-start(bf16[32,1,32,128]{3,2,1,0:T(8,128)(2,1)S(1)} %copy-done.1), channel_id=1, source_target_pairs={{4,0},{8,4},{12,8},{16,12},{20,16},{24,20},{28,24},{0,28},{5,1},{9... | collective-permute-start | bytes 786440 | tf_op jit(solution)/shard_map/ppermute | solution.py:366
  10.3 9.3 %collective-permute-start = (bf16[32,1,32,128]{3,2,1,0:T(8,128)(2,1)S(1)}, bf16[32,1,32,128]{3,2,1,0:T(8,128)(2,1)S(1)}, u32[]{:S(2)}, u32[]{:S(2)}) collective-permute-start(bf16[32,1,32,128]{3,2,1,0:T(8,128)(2,1)S(1)} %copy-done.1), channel_id=1, source_target_pairs={{0,1},{1,0},{2,3},{3,2},{4,5},{5,4},{6,7},{7,6},{8,9},{9,8},{10,11... | collective-permute-start | bytes 786440 | tf_op jit(solution)/shard_map/ppermute | solution.py:356
  12.6 12.8 %collective-permute-start.4 = (bf16[32,1,32,128]{3,2,1,0:T(8,128)(2,1)S(1)}, bf16[32,1,32,128]{3,2,1,0:T(8,128)(2,1)S(1)}, u32[]{:S(2)}, u32[]{:S(2)}) collective-permute-start(bf16[32,1,32,128]{3,2,1,0:T(8,128)(2,1)S(1)} %collective-permute-done.3.refs_1_), channel_id=1, source_target_pairs={{0,1},{1,0},{2,3},{3,2},{4,5},{5,4},{6,7},{7,6},{8,9},{9,8},{10,11... | collective-permute-start | bytes 786440 | tf_op jit(solution)/shard_map/ppermute | solution.py:357
  19.9 12.2 %collective-permute-start.6 = (bf16[64,4096]{1,0:T(8,128)(2,1)S(1)}, bf16[64,4096]{1,0:T(8,128)(2,1)S(1)}, u32[]{:S(2)}, u32[]{:S(2)}) collective-permute-start(bf16[64,4096]{1,0:T(8,128)(2,1)S(1)} %shard_map.54.refs_3_.refs_1_.refs_4_), channel_id=1, source_target_pairs={{4,0},{8,4},{12,8},{16,12},{20,16},{24,20},{28,24},{0,28},{5,1},{9... | collective-permute-start | bytes 1572872 | tf_op jit(solution)/shard_map/ppermute | solution.py:379
  25.5 6.6 %collective-permute-start.7 = (bf16[32,4096]{1,0:T(8,128)(2,1)S(1)}, bf16[32,4096]{1,0:T(8,128)(2,1)S(1)}, u32[]{:S(2)}, u32[]{:S(2)}) collective-permute-start(bf16[32,4096]{1,0:T(8,128)(2,1)S(1)} %shard_map.55.refs_4_.refs_2_.refs_5_), channel_id=1, source_target_pairs={{4,0},{8,4},{12,8},{16,12},{20,16},{24,20},{28,24},{0,28},{5,1},{9... | collective-permute-start | bytes 786440 | tf_op jit(solution)/shard_map/ppermute | solution.py:379
  26.9 1.4 %collective-permute-start.5 = (f32[64,512]{1,0:T(8,128)S(1)}, f32[64,512]{1,0:T(8,128)S(1)}, u32[]{:S(2)}, u32[]{:S(2)}) collective-permute-start(f32[64,512]{1,0:T(8,128)S(1)} %get-tuple-element.30), channel_id=1, source_target_pairs={{0,4},{4,0},{8,12},{12,8},{16,20},{20,16},{24,28},{28,24},{1,5},{5... | collective-permute-start | bytes 393224 | tf_op jit(solution)/shard_map/ppermute | solution.py:399
  28.4 5.4 %collective-permute-start.8 = (f32[16,512]{1,0:T(8,128)S(1)}, f32[16,512]{1,0:T(8,128)S(1)}, u32[]{:S(2)}, u32[]{:S(2)}) collective-permute-start(f32[16,512]{1,0:T(8,128)S(1)} %get-tuple-element.39), channel_id=1, source_target_pairs={{0,24},{4,28},{8,16},{12,20},{16,8},{20,12},{24,0},{28,4},{1,25},{... | collective-permute-start | bytes 98312 | tf_op jit(solution)/shard_map/ppermute | solution.py:417
  30.7 3.9 %collective-permute-start.9 = (f32[16,512]{1,0:T(8,128)S(1)}, f32[16,512]{1,0:T(8,128)S(1)}, u32[]{:S(2)}, u32[]{:S(2)}) collective-permute-start(f32[16,512]{1,0:T(8,128)S(1)} %get-tuple-element.40), channel_id=1, source_target_pairs={{0,16},{4,20},{8,24},{12,28},{16,0},{20,4},{24,8},{28,12},{1,17},{... | collective-permute-start | bytes 98312 | tf_op jit(solution)/shard_map/ppermute | solution.py:417
  31.2 3.9 %collective-permute-start.10 = (f32[16,512]{1,0:T(8,128)S(1)}, f32[16,512]{1,0:T(8,128)S(1)}, u32[]{:S(2)}, u32[]{:S(2)}) collective-permute-start(f32[16,512]{1,0:T(8,128)S(1)} %get-tuple-element.41), channel_id=1, source_target_pairs={{0,8},{4,12},{8,0},{12,4},{16,24},{20,28},{24,16},{28,20},{1,9},{5... | collective-permute-start | bytes 98312 | tf_op jit(solution)/shard_map/ppermute | solution.py:417

commit v20 on v19

--- a/solution.py
+++ b/solution.py
@@ -415,7 +415,7 @@
     )
     terms = [
         lax.ppermute(terms[k - 1], "depth", [(i, i ^ (2 * k)) for i in range(depth)])
-        for k in range(depth // 2 - 1, 0, -1)
+        for k in [depth // 2 - 1, *range(1, depth // 2 - 1)]
     ]
     input_grad = call(
         odd_kernel,

time: 36 us -> 36.9 us (1.025)
  waiting for transfers between devices: 8.98 us -> 9.91 us
    ppermute x3, waiting for transfers between devices: 1.29 us -> 2.21 us  [shards(): lax.ppermute(terms[k - 1], 'depth', [(i, i ^ 2 * k) for i in range(depth)])]
  transfers between devices with their start and end apart: 11 -> 11, of which waited for: 6 -> 6; matrix products, arithmetic and copies ran while one was open for 0% -> 0% of each run, Pallas kernels for 15% -> 14%
where the time goes in v20:
time: 36.9 us; the launch traced here: 36.8 us
  starting transfers between devices  18.9 us (51%)
  waiting for transfers between devices  9.91 us (27%)
  Pallas kernels  5.95 us (16%)
  local copies, waits for them, and re-layouts  1.25 us (3%)
  between operations  0.74 us (2%)
    pallas_call x11, Pallas kernels, call(): pl.pallas_call(kernel, out_shape=out_shape, in_specs=[VMEM] * len(args),...  5.95 us
    ppermute x1, starting transfers between devices, shards(): forwarded = lax.ppermute(far, 'chan', pairs(1))  5.77 us
    ppermute x1, starting transfers between devices, shards(): far = lax.ppermute(grad_out, 'chan', pairs(3))  4.68 us
    ppermute x1, waiting for transfers between devices, shards(): forwarded = lax.ppermute(far, 'chan', pairs(1))  4.26 us
    ppermute x3, starting transfers between devices, shards(): lax.ppermute(terms[k - 1], 'depth', [(i, i ^ 2 * k) for i in range(depth)])  3.75 us
    ppermute x1, starting transfers between devices, shards(): next_own = lax.ppermute(own, 'depth', nearer)  2.33 us
    ppermute x3, waiting for transfers between devices, shards(): lax.ppermute(terms[k - 1], 'depth', [(i, i ^ 2 * k) for i in range(depth)])  2.21 us
    ppermute x1, waiting for transfers between devices, shards(): far = lax.ppermute(grad_out, 'chan', pairs(3))  2.07 us
  transfers between devices with their start and end apart: 11, of which 6 were waited for; matrix products, arithmetic and copies ran while one was open for 0% of the time, Pallas kernels for 14%

profile of v20, /device:TPU:0, one launch (start us, length us, event | category | flops | bytes accessed | tf_op | source)
XLA Modules:
  0.0 36.8 jit_solution(11130838523267229036)
XLA Ops:
  0.6 0.0 copy-start
  0.6 0.0 copy-start.1
  0.7 0.5 %collective-permute-start.1 = (bf16[16,2,64,256]{3,2,1,0:T(8,128)(2,1)}, bf16[16,2,64,256]{3,2,1,0:T(8,128)(2,1)S(1)}, u32[]{:S(2)}, u32[]{:S(2)}) collective-permute-start(bf16[16,2,64,256]{3,2,1,0:T(8,128)(2,1)} %refs_0_.2), channel_id=1, source_target_pairs={{0,4},{4,8},{8,12},{12,16},{16,20},{20,24},{24,28},{28,0},{1,5},{5... | collective-permute-start | bytes 3145736 | tf_op jit(solution)/shard_map/ppermute | solution.py:365
  1.2 4.7 %collective-permute-start.3 = (bf16[32,1,32,128]{3,2,1,0:T(8,128)(2,1)}, bf16[32,1,32,128]{3,2,1,0:T(8,128)(2,1)S(1)}, u32[]{:S(2)}, u32[]{:S(2)}) collective-permute-start(bf16[32,1,32,128]{3,2,1,0:T(8,128)(2,1)} %refs_0_.3), channel_id=1, source_target_pairs={{0,3},{1,2},{2,1},{3,0},{4,7},{5,6},{6,5},{7,4},{8,11},{9,10},{10,... | collective-permute-start | bytes 786440 | tf_op jit(solution)/shard_map/ppermute | solution.py:354
  5.8 0.0 copy-done
  5.9 0.0 copy-start.2
  5.9 1.2 %copy-done.2 = bf16[16,2,64,256]{3,2,1,0:T(8,128)(2,1)S(1)} copy-done((bf16[16,2,64,256]{3,2,1,0:T(8,128)(2,1)S(1)}, bf16[16,2,64,256]{3,2,1,0:T(8,128)(2,1)}, u32[]{:S(2)}) %copy-start.2) | copy-done | bytes 1048600
  7.1 0.9 %shard_map.50 = (bf16[192,4096]{1,0:T(8,128)(2,1)S(1)}, bf16[144,128]{1,0:T(8,128)(2,1)S(1)}, bf16[144,256]{1,0:T(8,128)(2,1)S(1)}) custom-call(bf16[16,2,64,256]{3,2,1,0:T(8,128)(2,1)S(1)} %copy-done.2, bf16[27,16,128]{2,1,0:T(8,128)(2,1)S(1)} %constant_dynamic-slice_fusion.refs_1_), custom_call_target="tpu_custom_call" | custom-call | flops 536870912 | bytes 4194304 | tf_op jit(solution)/shard_map/pallas_call | solution.py:320
  8.0 0.0 copy-done.1
  8.0 2.3 %collective-permute-start.2 = (bf16[32,1,32,128]{3,2,1,0:T(8,128)(2,1)S(1)}, bf16[32,1,32,128]{3,2,1,0:T(8,128)(2,1)S(1)}, u32[]{:S(2)}, u32[]{:S(2)}) collective-permute-start(bf16[32,1,32,128]{3,2,1,0:T(8,128)(2,1)S(1)} %copy-done.1), channel_id=1, source_target_pairs={{4,0},{8,4},{12,8},{16,12},{20,16},{24,20},{28,24},{0,28},{5,1},{9... | collective-permute-start | bytes 786440 | tf_op jit(solution)/shard_map/ppermute | solution.py:366
  10.3 0.0 collective-permute-start
  10.3 0.1 shard_map.52.refs_2_.refs_0_.refs_3_
  10.5 2.1 %collective-permute-done.3.refs_1_ = bf16[32,1,32,128]{3,2,1,0:T(8,128)(2,1)S(1)} collective-permute-done((bf16[32,1,32,128]{3,2,1,0:T(8,128)(2,1)}, bf16[32,1,32,128]{3,2,1,0:T(8,128)(2,1)S(1)}, u32[]{:S(2)}, u32[]{:S(2)}) %collective-permute-start.3) | collective-permute-done | bytes 262176 | tf_op jit(solution)/shard_map/ppermute | solution.py:354
  12.6 5.8 %collective-permute-start.4 = (bf16[32,1,32,128]{3,2,1,0:T(8,128)(2,1)S(1)}, bf16[32,1,32,128]{3,2,1,0:T(8,128)(2,1)S(1)}, u32[]{:S(2)}, u32[]{:S(2)}) collective-permute-start(bf16[32,1,32,128]{3,2,1,0:T(8,128)(2,1)S(1)} %collective-permute-done.3.refs_1_), channel_id=1, source_target_pairs={{0,1},{1,0},{2,3},{3,2},{4,5},{5,4},{6,7},{7,6},{8,9},{9,8},{10,11... | collective-permute-start | bytes 786440 | tf_op jit(solution)/shard_map/ppermute | solution.py:357
  18.3 0.0 collective-permute-done.2.refs_0_
  18.3 0.1 shard_map.53.refs_0_
  18.5 1.1 %collective-permute-done.1.behind_ref = bf16[16,2,64,256]{3,2,1,0:T(8,128)(2,1)S(1)} collective-permute-done((bf16[16,2,64,256]{3,2,1,0:T(8,128)(2,1)}, bf16[16,2,64,256]{3,2,1,0:T(8,128)(2,1)S(1)}, u32[]{:S(2)}, u32[]{:S(2)}) %collective-permute-start.1) | collective-permute-done | bytes 1048608 | tf_op jit(solution)/shard_map/ppermute | solution.py:365
  19.5 0.1 shard_map.51.refs_1_
  19.6 0.0 collective-permute-done.refs_0_
  19.6 0.3 shard_map.54.refs_3_.refs_1_.refs_4_
  19.9 1.3 %collective-permute-start.6 = (bf16[64,4096]{1,0:T(8,128)(2,1)S(1)}, bf16[64,4096]{1,0:T(8,128)(2,1)S(1)}, u32[]{:S(2)}, u32[]{:S(2)}) collective-permute-start(bf16[64,4096]{1,0:T(8,128)(2,1)S(1)} %shard_map.54.refs_3_.refs_1_.refs_4_), channel_id=1, source_target_pairs={{4,0},{8,4},{12,8},{16,12},{20,16},{24,20},{28,24},{0,28},{5,1},{9... | collective-permute-start | bytes 1572872 | tf_op jit(solution)/shard_map/ppermute | solution.py:379
  21.1 4.3 %collective-permute-done.4.refs_0_ = bf16[32,1,32,128]{3,2,1,0:T(8,128)(2,1)S(1)} collective-permute-done((bf16[32,1,32,128]{3,2,1,0:T(8,128)(2,1)S(1)}, bf16[32,1,32,128]{3,2,1,0:T(8,128)(2,1)S(1)}, u32[]{:S(2)}, u32[]{:S(2)}) %collective-permute-start.4) | collective-permute-done | bytes 262176 | tf_op jit(solution)/shard_map/ppermute | solution.py:357
  25.4 0.1 shard_map.55.refs_4_.refs_2_.refs_5_
  25.5 0.4 %collective-permute-start.7 = (bf16[32,4096]{1,0:T(8,128)(2,1)S(1)}, bf16[32,4096]{1,0:T(8,128)(2,1)S(1)}, u32[]{:S(2)}, u32[]{:S(2)}) collective-permute-start(bf16[32,4096]{1,0:T(8,128)(2,1)S(1)} %shard_map.55.refs_4_.refs_2_.refs_5_), channel_id=1, source_target_pairs={{4,0},{8,4},{12,8},{16,12},{20,16},{24,20},{28,24},{0,28},{5,1},{9... | collective-permute-start | bytes 786440 | tf_op jit(solution)/shard_map/ppermute | solution.py:379
  26.0 0.9 %shard_map.56 = (f32[64,512]{1,0:T(8,128)S(1)}, f32[64,512]{1,0:T(8,128)S(1)}) custom-call(bf16[192,4096]{1,0:T(8,128)(2,1)S(1)} %get-tuple-element.25.refs_0_, bf16[96,4096]{1,0:T(8,128)(2,1)S(1)} %shard_map.51.refs_1_, bf16[32,4096]{1,0:T(8,128)(2,1)S(1)} %shard_map.52.refs_2_.refs_0_.refs_3_, bf16[64,4096]{1,0:T(8,128)(2,1)S(1)} %shard_map.54.refs_3_.refs_1_.refs_4_, ...), custom_call_target="tpu_custom_call" | custom-call | flops 452984832 | bytes 8388608 | tf_op jit(solution)/shard_map/pallas_call | solution.py:320
  26.9 0.2 collective-permute-start.5
  27.1 0.9 %shard_map.57.even_ref = bf16[16,64,256]{2,1,0:T(8,128)(2,1)S(1)} custom-call(bf16[144,128]{1,0:T(8,128)(2,1)S(1)} %get-tuple-element.31.taps_ref, bf16[32,4096]{1,0:T(8,128)(2,1)S(1)} %shard_map.52.refs_2_.refs_0_.refs_3_, bf16[64,4096]{1,0:T(8,128)(2,1)S(1)} %shard_map.54.refs_3_.refs_1_.refs_4_, bf16[32,4096]{1,0:T(8,128)(2,1)S(1)} %shard_map.55.refs_4_.refs_2_.refs_5_), custom_call_target="tpu_custom_call" | custom-call | flops 150994944 | bytes 4194304 | tf_op jit(solution)/shard_map/pallas_call | solution.py:320
  28.1 0.3 collective-permute-done.5.other_ref
  28.4 2.3 %collective-permute-start.8 = (f32[16,512]{1,0:T(8,128)S(1)}, f32[16,512]{1,0:T(8,128)S(1)}, u32[]{:S(2)}, u32[]{:S(2)}) collective-permute-start(f32[16,512]{1,0:T(8,128)S(1)} %get-tuple-element.39), channel_id=1, source_target_pairs={{0,24},{4,28},{8,16},{12,20},{16,8},{20,12},{24,0},{28,4},{1,25},{... | collective-permute-start | bytes 98312 | tf_op jit(solution)/shard_map/ppermute | solution.py:417
  30.7 1.4 %collective-permute-start.9 = (f32[16,512]{1,0:T(8,128)S(1)}, f32[16,512]{1,0:T(8,128)S(1)}, u32[]{:S(2)}, u32[]{:S(2)}) collective-permute-start(f32[16,512]{1,0:T(8,128)S(1)} %get-tuple-element.40), channel_id=1, source_target_pairs={{0,8},{4,12},{8,0},{12,4},{16,24},{20,28},{24,16},{28,20},{1,9},{5... | collective-permute-start | bytes 98312 | tf_op jit(solution)/shard_map/ppermute | solution.py:417
  32.1 0.0 collective-permute-start.10
  32.1 0.0 collective-permute-done.7.refs_2_
  32.1 0.0 collective-permute-done.6.refs_1_
  32.1 1.7 %shard_map.59 = bf16[16,2,64,256]{3,2,1,0:T(8,128)(2,1)} custom-call(bf16[16,64,256]{2,1,0:T(8,128)(2,1)S(1)} %shard_map.57.even_ref, bf16[144,256]{1,0:T(8,128)(2,1)S(1)} %get-tuple-element.35.taps_ref, bf16[32,4096]{1,0:T(8,128)(2,1)S(1)} %shard_map.53.refs_0_, bf16[64,4096]{1,0:T(8,128)(2,1)S(1)} %collective-permute-done.6.refs_1_, ...), custom_call_target="tpu_custom_call" | custom-call | flops 301989888 | bytes 4194304 | tf_op jit(solution)/shard_map/pallas_call | solution.py:320
  33.8 0.0 collective-permute-done.8.refs_1_
  33.8 0.8 %collective-permute-done.9.refs_2_ = f32[16,512]{1,0:T(8,128)S(1)} collective-permute-done((f32[16,512]{1,0:T(8,128)S(1)}, f32[16,512]{1,0:T(8,128)S(1)}, u32[]{:S(2)}, u32[]{:S(2)}) %collective-permute-start.9) | collective-permute-done | bytes 32800 | tf_op jit(solution)/shard_map/ppermute | solution.py:417
  34.6 1.4 %collective-permute-done.10.refs_3_ = f32[16,512]{1,0:T(8,128)S(1)} collective-permute-done((f32[16,512]{1,0:T(8,128)S(1)}, f32[16,512]{1,0:T(8,128)S(1)}, u32[]{:S(2)}, u32[]{:S(2)}) %collective-permute-start.10) | collective-permute-done | bytes 32800 | tf_op jit(solution)/shard_map/ppermute | solution.py:417
  36.0 0.8 %shard_map.60 = f32[16,16,27]{2,1,0:T(8,128)} custom-call(f32[16,512]{1,0:T(8,128)S(1)} %get-tuple-element.38.refs_0_, f32[16,512]{1,0:T(8,128)S(1)} %collective-permute-done.8.refs_1_, f32[16,512]{1,0:T(8,128)S(1)} %collective-permute-done.9.refs_2_, f32[16,512]{1,0:T(8,128)S(1)} %collective-permute-done.10.refs_3_), custom_call_target="tpu_custom_call" | custom-call | flops 65536 | bytes 524288 | tf_op jit(solution)/shard_map/pallas_call | solution.py:320
  (2 shorter events, 0.0 us)
Async XLA Ops:
  0.6 5.2 %copy-start = (bf16[27,64,128]{2,1,0:T(8,128)(2,1)S(1)}, bf16[27,64,128]{2,1,0:T(8,128)(2,1)}, u32[]{:S(2)}) copy-start(bf16[27,64,128]{2,1,0:T(8,128)(2,1)} %param.5) | copy-start | bytes 1327108
  0.6 7.4 %copy-start.1 = (bf16[32,1,32,128]{3,2,1,0:T(8,128)(2,1)S(1)}, bf16[32,1,32,128]{3,2,1,0:T(8,128)(2,1)}, u32[]{:S(2)}) copy-start(bf16[32,1,32,128]{3,2,1,0:T(8,128)(2,1)} %refs_0_.3) | copy-start | bytes 786436
  0.7 18.9 %collective-permute-start.1 = (bf16[16,2,64,256]{3,2,1,0:T(8,128)(2,1)}, bf16[16,2,64,256]{3,2,1,0:T(8,128)(2,1)S(1)}, u32[]{:S(2)}, u32[]{:S(2)}) collective-permute-start(bf16[16,2,64,256]{3,2,1,0:T(8,128)(2,1)} %refs_0_.2), channel_id=1, source_target_pairs={{0,4},{4,8},{8,12},{12,16},{16,20},{20,24},{24,28},{28,0},{1,5},{5... | collective-permute-start | bytes 3145736 | tf_op jit(solution)/shard_map/ppermute | solution.py:365
  1.2 11.4 %collective-permute-start.3 = (bf16[32,1,32,128]{3,2,1,0:T(8,128)(2,1)}, bf16[32,1,32,128]{3,2,1,0:T(8,128)(2,1)S(1)}, u32[]{:S(2)}, u32[]{:S(2)}) collective-permute-start(bf16[32,1,32,128]{3,2,1,0:T(8,128)(2,1)} %refs_0_.3), channel_id=1, source_target_pairs={{0,3},{1,2},{2,1},{3,0},{4,7},{5,6},{6,5},{7,4},{8,11},{9,10},{10,... | collective-permute-start | bytes 786440 | tf_op jit(solution)/shard_map/ppermute | solution.py:354
  5.9 1.2 %copy-start.2 = (bf16[16,2,64,256]{3,2,1,0:T(8,128)(2,1)S(1)}, bf16[16,2,64,256]{3,2,1,0:T(8,128)(2,1)}, u32[]{:S(2)}) copy-start(bf16[16,2,64,256]{3,2,1,0:T(8,128)(2,1)} %refs_0_.2) | copy-start | bytes 3145732
  8.0 10.3 %collective-permute-start.2 = (bf16[32,1,32,128]{3,2,1,0:T(8,128)(2,1)S(1)}, bf16[32,1,32,128]{3,2,1,0:T(8,128)(2,1)S(1)}, u32[]{:S(2)}, u32[]{:S(2)}) collective-permute-start(bf16[32,1,32,128]{3,2,1,0:T(8,128)(2,1)S(1)} %copy-done.1), channel_id=1, source_target_pairs={{4,0},{8,4},{12,8},{16,12},{20,16},{24,20},{28,24},{0,28},{5,1},{9... | collective-permute-start | bytes 786440 | tf_op jit(solution)/shard_map/ppermute | solution.py:366
  10.3 9.3 %collective-permute-start = (bf16[32,1,32,128]{3,2,1,0:T(8,128)(2,1)S(1)}, bf16[32,1,32,128]{3,2,1,0:T(8,128)(2,1)S(1)}, u32[]{:S(2)}, u32[]{:S(2)}) collective-permute-start(bf16[32,1,32,128]{3,2,1,0:T(8,128)(2,1)S(1)} %copy-done.1), channel_id=1, source_target_pairs={{0,1},{1,0},{2,3},{3,2},{4,5},{5,4},{6,7},{7,6},{8,9},{9,8},{10,11... | collective-permute-start | bytes 786440 | tf_op jit(solution)/shard_map/ppermute | solution.py:356
  12.6 12.8 %collective-permute-start.4 = (bf16[32,1,32,128]{3,2,1,0:T(8,128)(2,1)S(1)}, bf16[32,1,32,128]{3,2,1,0:T(8,128)(2,1)S(1)}, u32[]{:S(2)}, u32[]{:S(2)}) collective-permute-start(bf16[32,1,32,128]{3,2,1,0:T(8,128)(2,1)S(1)} %collective-permute-done.3.refs_1_), channel_id=1, source_target_pairs={{0,1},{1,0},{2,3},{3,2},{4,5},{5,4},{6,7},{7,6},{8,9},{9,8},{10,11... | collective-permute-start | bytes 786440 | tf_op jit(solution)/shard_map/ppermute | solution.py:357
  19.9 12.2 %collective-permute-start.6 = (bf16[64,4096]{1,0:T(8,128)(2,1)S(1)}, bf16[64,4096]{1,0:T(8,128)(2,1)S(1)}, u32[]{:S(2)}, u32[]{:S(2)}) collective-permute-start(bf16[64,4096]{1,0:T(8,128)(2,1)S(1)} %shard_map.54.refs_3_.refs_1_.refs_4_), channel_id=1, source_target_pairs={{4,0},{8,4},{12,8},{16,12},{20,16},{24,20},{28,24},{0,28},{5,1},{9... | collective-permute-start | bytes 1572872 | tf_op jit(solution)/shard_map/ppermute | solution.py:379
  25.5 6.6 %collective-permute-start.7 = (bf16[32,4096]{1,0:T(8,128)(2,1)S(1)}, bf16[32,4096]{1,0:T(8,128)(2,1)S(1)}, u32[]{:S(2)}, u32[]{:S(2)}) collective-permute-start(bf16[32,4096]{1,0:T(8,128)(2,1)S(1)} %shard_map.55.refs_4_.refs_2_.refs_5_), channel_id=1, source_target_pairs={{4,0},{8,4},{12,8},{16,12},{20,16},{24,20},{28,24},{0,28},{5,1},{9... | collective-permute-start | bytes 786440 | tf_op jit(solution)/shard_map/ppermute | solution.py:379
  26.9 1.4 %collective-permute-start.5 = (f32[64,512]{1,0:T(8,128)S(1)}, f32[64,512]{1,0:T(8,128)S(1)}, u32[]{:S(2)}, u32[]{:S(2)}) collective-permute-start(f32[64,512]{1,0:T(8,128)S(1)} %get-tuple-element.30), channel_id=1, source_target_pairs={{0,4},{4,0},{8,12},{12,8},{16,20},{20,16},{24,28},{28,24},{1,5},{5... | collective-permute-start | bytes 393224 | tf_op jit(solution)/shard_map/ppermute | solution.py:399
  28.4 5.4 %collective-permute-start.8 = (f32[16,512]{1,0:T(8,128)S(1)}, f32[16,512]{1,0:T(8,128)S(1)}, u32[]{:S(2)}, u32[]{:S(2)}) collective-permute-start(f32[16,512]{1,0:T(8,128)S(1)} %get-tuple-element.39), channel_id=1, source_target_pairs={{0,24},{4,28},{8,16},{12,20},{16,8},{20,12},{24,0},{28,4},{1,25},{... | collective-permute-start | bytes 98312 | tf_op jit(solution)/shard_map/ppermute | solution.py:417
  30.7 3.9 %collective-permute-start.9 = (f32[16,512]{1,0:T(8,128)S(1)}, f32[16,512]{1,0:T(8,128)S(1)}, u32[]{:S(2)}, u32[]{:S(2)}) collective-permute-start(f32[16,512]{1,0:T(8,128)S(1)} %get-tuple-element.40), channel_id=1, source_target_pairs={{0,8},{4,12},{8,0},{12,4},{16,24},{20,28},{24,16},{28,20},{1,9},{5... | collective-permute-start | bytes 98312 | tf_op jit(solution)/shard_map/ppermute | solution.py:417
  32.1 3.9 %collective-permute-start.10 = (f32[16,512]{1,0:T(8,128)S(1)}, f32[16,512]{1,0:T(8,128)S(1)}, u32[]{:S(2)}, u32[]{:S(2)}) collective-permute-start(f32[16,512]{1,0:T(8,128)S(1)} %get-tuple-element.41), channel_id=1, source_target_pairs={{0,16},{4,20},{8,24},{12,28},{16,0},{20,4},{24,8},{28,12},{1,17},{... | collective-permute-start | bytes 98312 | tf_op jit(solution)/shard_map/ppermute | solution.py:417
